TPU v7x, 32 devices: a whole 2x2x4 slice. The times are simulated.
32 devices in a mesh: dom: 16 (over z, y, x), rep: 2 (over core).
Axes of the slice: x: 2, y: 2, z: 4, core: 2. Of those that a mesh axis runs over, the one named last changes fastest.
Arguments:
- features: bfloat16 [131072, 256], P('dom'), may hold values from -6 to 6
- node_order: int32 [16, 8192], P('dom'), may hold values from 0 to 8191, each once within a row
- section_owner: int32 [4], replicated, may hold values from 0 to 15, as said below
- send_blocks: int32 [4, 32], replicated, may hold values from 0 to 63, as said below
- tile_rows: int32 [16, 4, 32], P('dom', None, 'rep'), may hold values from 0 to 63
- tile_cols: int32 [16, 4, 32], P('dom', None, 'rep'), may hold values from 0 to 31
- tiles: bfloat16 [16, 4, 32, 128, 128], P('dom', None, 'rep'), may hold values from -0.375 to 0.375
- weight: bfloat16 [256, 256], replicated, may hold values from -0.375 to 0.375
Outputs:
- hidden: bfloat16 [131072, 256], P(('dom', 'rep'))
Inputs may be any that keep to these rules, and one draw needn't show every extreme that they name: `section_owner`: 4 different partitions; partitions 0 and 15 are always among them. `send_blocks`: each row holds 32 different block numbers in rising order, always including 0 and 63.
All inputs are finite; a program needn't handle non-finite values.
Results may differ from a plain program's by a relative error of at most 0.014.
Values may be sent and summed in bfloat16 or wider, within the bound.
No kernel may reach another device: no remote copies, remote signals or barrier semaphores. Data moves between devices by JAX's collectives and lax.ppermute only.
A program may use at most 64 MiB of HBM per device.

v0:
```python
import jax
import jax.numpy as jnp
from jax import lax
from jax.sharding import PartitionSpec as P


def spread(value, axis, source):
    kept = jnp.where(lax.axis_index(axis) == source, value, 0).astype(value.dtype)
    return lax.psum(kept, axis)


def body(features, node_order, section_owner, send_blocks, tile_rows, tile_cols, tiles, weight):
    width = features.shape[1]
    tile_len = tiles.shape[3]
    blocks = features.shape[0] // tile_len
    curve = jnp.take(features, node_order[0], axis=0).reshape(blocks, tile_len, width)
    total = jnp.zeros((blocks, tile_len, width), jnp.float32)
    for s in range(tiles.shape[1]):
        owner = section_owner[s]
        picks = send_blocks[s]
        share = picks.shape[0] // lax.axis_size("rep")
        my_picks = lax.dynamic_slice_in_dim(picks, lax.axis_index("rep") * share, share)
        mine = jnp.take(curve, my_picks, axis=0)
        landed = spread(mine, "dom", owner)
        arrived = lax.all_gather(landed, "rep", axis=0, tiled=True)
        chosen = jnp.take(arrived, tile_cols[0, s], axis=0)
        product = jnp.einsum(
            "kij,kjf->kif", tiles[0, s], chosen, preferred_element_type=jnp.float32
        )
        total = total.at[tile_rows[0, s]].add(product)
    summed = lax.psum_scatter(
        total.reshape(blocks * tile_len, width).astype(jnp.bfloat16),
        "rep",
        scatter_dimension=0,
        tiled=True,
    )
    mixed = jnp.dot(summed, weight, preferred_element_type=jnp.float32)
    return jnp.maximum(mixed, 0.0).astype(jnp.bfloat16)


def solution(mesh):
    return jax.shard_map(
        body,
        mesh=mesh,
        in_specs=(
            P("dom", None),
            P("dom", None),
            P(),
            P(),
            P("dom", None, "rep"),
            P("dom", None, "rep"),
            P("dom", None, "rep", None, None),
            P(),
        ),
        out_specs=P(("dom", "rep"), None),
        check_vma=False,
    )
```

profile of v0, /device:TPU:1, one launch (start us, length us, event | category | flops | bytes accessed | tf_op | source)
XLA Modules:
  0.0 354.2 jit_solution(11071251288874709248)
XLA Ops:
  6.5 0.0 copy-start
  6.5 0.0 all-reduce.3.cloned.1.call-start
  6.5 0.8 fusion.33
  7.4 0.1 compare_and_fusion.2
  7.5 0.8 compare_select_fusion
  8.3 0.8 compare_and_fusion
  9.1 1.5 fusion.34
  10.5 33.6 %gather_fusion = bf16[8192,256]{1,0:T(8,128)(2,1)} fusion(bf16[8192,256]{1,0:T(8,128)(2,1)} %param.12, s32[8192]{0:T(1024)S(1)} %broadcast_clamp_fusion), kind=kCustom, calls=%fused_computation.8 | custom fusion | bytes 8421376 | tf_op jit(solution)/shard_map/jit(_take)/gather | solution.py:16
  44.2 5.3 %broadcast_select_fusion = bf16[64,128,256]{2,1,0:T(8,128)(2,1)} fusion(bf16[64,128,256]{2,1,0:T(8,128)(2,1)} %bitcast.81, pred[64,128]{1,0:T(8,128)(4,1)S(1)} %compare_and_fusion), kind=kLoop, calls=%fused_computation.15 | loop fusion | flops 2097152 | bytes 8396800 | tf_op jit(solution)/shard_map/jit(_take)/select_n | solution.py:16
  49.4 2.8 gather_fusion.7
  52.2 2.8 gather_fusion.5
  56.3 0.1 compare_and_fusion.6
  56.4 2.8 gather_fusion.3
  59.8 3.8 %gather_fusion.1 = bf16[16,128,256]{2,1,0:T(8,128)(2,1)} fusion(bf16[64,128,256]{2,1,0:T(8,128)(2,1)} %broadcast_select_fusion, s32[1024]{0:T(1024)S(1)} %pad_clamp_fusion.7), kind=kCustom, calls=%fused_computation.clone | custom fusion | bytes 2097216 | tf_op jit(solution)/shard_map/jit(_take)/gather | solution.py:23
  64.2 1.2 select_select_fusion
  65.3 0.0 copy-start.2
  65.3 1.2 select_select_fusion.1
  66.5 1.2 select_select_fusion.2
  67.7 0.0 copy-done.2
  67.7 1.2 select_select_fusion.3
  68.9 0.0 all-reduce.3.cloned.1.call-update
  68.9 0.0 all-gather.5.cloned.1.call-start
  68.9 172.0 %all-reduce.3.cloned.1.call-done = (bf16[16,128,256]{2,1,0:T(8,128)(2,1)}, bf16[16,128,256]{2,1,0:T(8,128)(2,1)}, bf16[16,128,256]{2,1,0:T(8,128)(2,1)}, bf16[16,128,256]{2,1,0:T(8,128)(2,1)}) async-done(((bf16[16,128,256]{2,1,0:T(8,128)(2,1)}, bf16[16,128,256]{2,1,0:T(8,128)(2,1)}, bf16[16,128,256]{2,1,0:T(8,128)(2,1)}, bf16[16,128,256]{2,1,0:T(8,128)(2,1)}), (bf16[16,128,256]{2,1,0:T(8,128)(2,1)}, ...) | async-done | bytes 4194320 | tf_op jit(solution)/shard_map/psum | solution.py:9
  240.9 0.0 copy-start.3
  240.9 0.0 copy-start.4
  240.9 0.0 all-gather.5.cloned.1.call-update
  240.9 0.0 all-gather.7.cloned.1.call-start
  241.0 0.7 all-gather.7.cloned.1.call-update
  241.7 0.0 all-gather.9.cloned.1.call-start
  241.7 0.5 all-gather.9.cloned.1.call-update
  242.2 0.0 all-gather.11.cloned.1.call-start
  242.3 0.5 all-gather.11.cloned.1.call-update
  242.8 0.2 reduce-scatter.2.cloned.1.call-start
  243.1 0.0 copy-done.3
  243.1 0.0 copy-done.4
  243.2 9.3 %all-gather.5.cloned.1.call-done = bf16[32,128,256]{2,1,0:T(8,128)(2,1)} async-done(((bf16[16,128,256]{2,1,0:T(8,128)(2,1)}), bf16[32,128,256]{2,1,0:T(8,128)(2,1)}) %all-gather.5.cloned.1.call-update) | async-done | bytes 2097168 | tf_op jit(solution)/shard_map/all_gather | solution.py:25
  252.5 2.2 gather_fusion.2
  254.7 2.9 convolution_bitcast_fusion.3
  257.6 1.9 copy.22
  259.5 6.4 %all-gather.7.cloned.1.call-done = bf16[32,128,256]{2,1,0:T(8,128)(2,1)} async-done(((bf16[16,128,256]{2,1,0:T(8,128)(2,1)}), bf16[32,128,256]{2,1,0:T(8,128)(2,1)}) %all-gather.7.cloned.1.call-update) | async-done | bytes 2097168 | tf_op jit(solution)/shard_map/all_gather | solution.py:25
  265.9 2.2 gather_fusion.4
  268.1 2.9 convolution_bitcast_fusion.2
  271.0 2.9 copy.24
  273.9 5.2 %all-gather.9.cloned.1.call-done = bf16[32,128,256]{2,1,0:T(8,128)(2,1)} async-done(((bf16[16,128,256]{2,1,0:T(8,128)(2,1)}), bf16[32,128,256]{2,1,0:T(8,128)(2,1)}) %all-gather.9.cloned.1.call-update) | async-done | bytes 2097168 | tf_op jit(solution)/shard_map/all_gather | solution.py:25
  279.1 2.2 gather_fusion.6
  281.3 2.9 convolution_bitcast_fusion.1
  284.2 2.9 copy.26
  287.1 5.2 %all-gather.11.cloned.1.call-done = bf16[32,128,256]{2,1,0:T(8,128)(2,1)} async-done(((bf16[16,128,256]{2,1,0:T(8,128)(2,1)}), bf16[32,128,256]{2,1,0:T(8,128)(2,1)}) %all-gather.11.cloned.1.call-update) | async-done | bytes 2097168 | tf_op jit(solution)/shard_map/all_gather | solution.py:25
  292.4 2.2 gather_fusion.8
  294.6 2.9 convolution_bitcast_fusion
  297.5 2.9 copy.28
  300.4 4.3 %broadcast_in_dim.42 = f32[64,128,256]{2,1,0:T(8,128)} broadcast(f32[]{:T(128)} %constant.34.clone.1), dimensions={} | broadcast | bytes 8388612 | tf_op jit(solution)/shard_map/broadcast_in_dim | solution.py:17
  304.7 4.5 %scatter_fusion = f32[64,128,256]{2,1,0:T(8,128)} fusion(f32[64,128,256]{2,1,0:T(8,128)} %broadcast_in_dim.42, s32[16]{0:T(128)S(1)} %get-tuple-element.35, f32[16,128,256]{2,1,0:T(8,128)S(1)} %copy.22), kind=kCustom, calls=%fused_computation.9 | custom fusion | flops 524288 | bytes 6291520 | tf_op jit(solution)/shard_map/scatter-add | solution.py:30
  309.2 0.0 copy-start.1
  309.2 5.3 %scatter_fusion.1 = f32[64,128,256]{2,1,0:T(8,128)} fusion(f32[64,128,256]{2,1,0:T(8,128)} %scatter_fusion, s32[16]{0:T(128)S(1)} %get-tuple-element.34, f32[16,128,256]{2,1,0:T(8,128)} %copy.24), kind=kCustom, calls=%fused_computation.10 | custom fusion | flops 524288 | bytes 6291520 | tf_op jit(solution)/shard_map/scatter-add | solution.py:30
  314.5 0.0 copy-done.1
  314.5 4.4 %scatter_fusion.2 = f32[64,128,256]{2,1,0:T(8,128)} fusion(f32[64,128,256]{2,1,0:T(8,128)} %scatter_fusion.1, s32[16]{0:T(128)S(1)} %get-tuple-element.36, f32[16,128,256]{2,1,0:T(8,128)S(1)} %copy-done.1), kind=kCustom, calls=%fused_computation.11 | custom fusion | flops 524288 | bytes 6291520 | tf_op jit(solution)/shard_map/scatter-add | solution.py:30
  318.9 5.3 %scatter_fusion.3 = f32[64,128,256]{2,1,0:T(8,128)} fusion(f32[64,128,256]{2,1,0:T(8,128)} %scatter_fusion.2, s32[16]{0:T(128)S(1)} %get-tuple-element.33, f32[16,128,256]{2,1,0:T(8,128)} %copy.28), kind=kCustom, calls=%fused_computation.12 | custom fusion | flops 524288 | bytes 6291520 | tf_op jit(solution)/shard_map/scatter-add | solution.py:30
  324.2 6.0 %convert_element_type.14 = bf16[64,128,256]{2,1,0:T(8,128)(2,1)} convert(f32[64,128,256]{2,1,0:T(8,128)} %scatter_fusion.3) | non-fusion elementwise | flops 2097152 | bytes 12582912 | tf_op jit(solution)/shard_map/convert_element_type | solution.py:32
  330.2 0.0 reduce-scatter.2.cloned.1.call-update
  330.2 13.5 %reduce-scatter.2.cloned.1.call-done = bf16[4096,256]{1,0:T(8,128)(2,1)} async-done(((bf16[8192,256]{1,0:T(8,128)(2,1)}), bf16[4096,256]{1,0:T(8,128)(2,1)}) %reduce-scatter.2.cloned.1.call-update) | async-done | bytes 2097168 | tf_op jit(solution)/shard_map/reduce_scatter | solution.py:31
  343.7 0.0 copy-done
  343.7 3.6 %fusion = bf16[4096,256]{1,0:T(8,128)(2,1)} fusion(bf16[4096,256]{1,0:T(8,128)(2,1)} %reduce-scatter.2.cloned.1.call-done, bf16[256,256]{1,0:T(8,128)(2,1)S(1)} %copy-done), kind=kOutput, calls=%fused_computation.14 | convolution fusion | flops 538968064 | bytes 4325376 | tf_op jit(solution)/shard_map/dot_general | solution.py:37
  (11 shorter events, 0.1 us)
Async XLA Ops:
  6.5 337.2 %copy-start = (bf16[256,256]{1,0:T(8,128)(2,1)S(1)}, bf16[256,256]{1,0:T(8,128)(2,1)}, u32[]{:S(2)}) copy-start(bf16[256,256]{1,0:T(8,128)(2,1)} %param.19) | copy-start | bytes 393220
  6.5 234.4 %all-reduce.3.cloned.1.call-start = ((), (), s32[]{:S(2)}) async-start(), calls=%async_computation.6 | async-start | bytes 8388608 | tf_op jit(solution)/shard_map/psum | solution.py:9
  65.3 2.3 copy-start.2
  68.9 183.6 %all-gather.5.cloned.1.call-start = ((), (), s32[]{:S(2)}) async-start(), calls=%async_computation.1 | async-start | bytes 3145728 | tf_op jit(solution)/shard_map/all_gather | solution.py:25
  240.9 2.2 copy-start.3
  240.9 2.2 copy-start.4
  240.9 24.9 %all-gather.7.cloned.1.call-start = ((), (), s32[]{:S(2)}) async-start(), calls=%async_computation.2 | async-start | bytes 3145728 | tf_op jit(solution)/shard_map/all_gather | solution.py:25
  241.7 37.5 %all-gather.9.cloned.1.call-start = ((), (), s32[]{:S(2)}) async-start(), calls=%async_computation.3 | async-start | bytes 3145728 | tf_op jit(solution)/shard_map/all_gather | solution.py:25
  242.2 50.1 %all-gather.11.cloned.1.call-start = ((), (), s32[]{:S(2)}) async-start(), calls=%async_computation.4 | async-start | bytes 3145728 | tf_op jit(solution)/shard_map/all_gather | solution.py:25
  242.8 100.9 %reduce-scatter.2.cloned.1.call-start = ((), (), s32[]{:S(2)}) async-start(), calls=%async_computation.5 | async-start | bytes 6291456 | tf_op jit(solution)/shard_map/reduce_scatter | solution.py:31
  309.2 5.3 %copy-start.1 = (f32[16,128,256]{2,1,0:T(8,128)S(1)}, f32[16,128,256]{2,1,0:T(8,128)}, u32[]{:S(2)}) copy-start(f32[16,128,256]{2,1,0:T(8,128)} %copy.26) | copy-start | bytes 6291460
Sparse Core Ops, SparseCore 0:
  69.0 171.8 all-reduce.2
  242.5 9.8 all-gather.4
  254.1 11.7 all-gather.6
  267.3 11.7 all-gather.8
  280.6 11.7 all-gather.10
  330.3 13.3 reduce-scatter.1
where the time goes:
time: 355 us; the launch traced here: 354 us
  waiting for transfers between devices  213 us (60%)
  local copies, waits for them, and re-layouts  71.8 us (20%)
  other arithmetic  37.2 us (10%)
  between operations  16.1 us (5%)
  matrix products  15.3 us (4%)
    psum x1, waiting for transfers between devices, spread(): return lax.psum(kept, axis)  172 us
    gather x1, local copies, waits for them, and re-layouts, body(): jnp.take(features, node_order[0], axis=0).reshape(blocks, tile_len, width)  33.6 us
    all_gather x4, waiting for transfers between devices, body(): arrived = lax.all_gather(landed, 'rep', axis=0, tiled=True)  26.1 us
    scatter-add x4, other arithmetic, body(): total = total.at[tile_rows[0, s]].add(product)  19.5 us
    reduce_scatter x1, waiting for transfers between devices, body(): lax.psum_scatter(total.reshape(blocks * tile_len, width).astype(jnp.bfloa...  13.5 us
    gather x4, local copies, waits for them, and re-layouts, body(): mine = jnp.take(curve, my_picks, axis=0)  12.2 us
    dot_general x4, matrix products, body(): jnp.einsum('kij,kjf->kif', tiles[0, s], chosen, preferred_element_type=jn...  11.7 us
    dot_general x4, local copies, waits for them, and re-layouts, body(): jnp.einsum('kij,kjf->kif', tiles[0, s], chosen, preferred_element_type=jn...  10.7 us
  transfers between devices with their start and end apart: 6, of which 6 were waited for; matrix products, arithmetic and copies ran while one was open for 7% of the time, Pallas kernels for 0%

commit v1 on v0

v1 whole, which is shorter than its diff:
```python
import functools

import jax
import jax.numpy as jnp
from jax import lax
from jax.experimental import pallas as pl
from jax.experimental.pallas import tpu as pltpu
from jax.sharding import PartitionSpec as P


def kernel(places, tile_parts, rows_ref, cols_ref, *refs):
    n_pieces = len(places)
    pieces = refs[:n_pieces]
    tile_refs = refs[n_pieces : n_pieces + tile_parts]
    weight_ref, out_ref = refs[n_pieces + tile_parts : n_pieces + tile_parts + 2]
    sent, tiles, acc, stage, mine, sem, tile_sem, out_sem = refs[n_pieces + tile_parts + 2 :]
    n_tiles = rows_ref.shape[0]
    tile_len = tiles.shape[1]
    n_blocks = acc.shape[0]

    copies = []
    for i, place in enumerate(places):
        count = pieces[i].shape[0]
        copies.append(
            pltpu.make_async_copy(pieces[i], sent.at[pl.ds(place, count)], sem.at[i])
        )
    per = n_tiles // tile_parts
    for i in range(tile_parts):
        copies.append(
            pltpu.make_async_copy(tile_refs[i], tiles.at[pl.ds(i * per, per)], tile_sem.at[i])
        )
    for copy in copies:
        copy.start()

    acc[...] = jnp.zeros_like(acc)

    def pick(t, count):
        here = jnp.logical_and(rows_ref[t] >= 0, rows_ref[t] < n_blocks)

        @pl.when(here)
        def _():
            mine[count] = t

        return count + here.astype(jnp.int32)

    n_mine = lax.fori_loop(0, n_tiles, pick, jnp.int32(0))

    for copy in copies:
        copy.wait()

    def step(i, carry):
        t = mine[i]
        acc[rows_ref[t]] += jnp.dot(
            tiles[t], sent[cols_ref[t]], preferred_element_type=jnp.float32
        )
        return carry

    lax.fori_loop(0, n_mine, step, 0)

    group = stage.shape[1]
    steps = n_blocks // group
    outs = []
    for i in range(steps):
        if i >= 2:
            outs[i - 2].wait()
        total = acc[pl.ds(i * group, group)].reshape(group * tile_len, acc.shape[2])
        mixed = jnp.dot(
            total.astype(jnp.bfloat16), weight_ref[...], preferred_element_type=jnp.float32
        )
        stage[i % 2] = (
            jnp.maximum(mixed, 0.0).astype(out_ref.dtype).reshape(stage.shape[1:])
        )
        copy = pltpu.make_async_copy(
            stage.at[i % 2], out_ref.at[pl.ds(i * group, group)], out_sem.at[i % 2]
        )
        copy.start()
        outs.append(copy)
    for copy in outs[max(steps - 2, 0) :]:
        copy.wait()


def products(pieces, places, tile_list, rows, cols, weight, n_sent, n_blocks):
    tile_len = tile_list[0].shape[1]
    width = weight.shape[0]
    n_tiles = rows.shape[0]
    group = min(4, n_blocks)
    any_spec = pl.BlockSpec(memory_space=pl.ANY)
    smem = pl.BlockSpec(memory_space=pltpu.SMEM)
    return pl.pallas_call(
        functools.partial(kernel, tuple(places), len(tile_list)),
        out_shape=jax.ShapeDtypeStruct((n_blocks, tile_len, weight.shape[1]), jnp.bfloat16),
        in_specs=[smem, smem]
        + [any_spec] * (len(pieces) + len(tile_list))
        + [pl.BlockSpec(memory_space=pltpu.VMEM)],
        out_specs=any_spec,
        scratch_shapes=[
            pltpu.VMEM((n_sent, tile_len, width), jnp.bfloat16),
            pltpu.VMEM((n_tiles, tile_len, tile_len), jnp.bfloat16),
            pltpu.VMEM((n_blocks, tile_len, width), jnp.float32),
            pltpu.VMEM((2, group, tile_len, weight.shape[1]), jnp.bfloat16),
            pltpu.SMEM((n_tiles,), jnp.int32),
            pltpu.SemaphoreType.DMA((len(pieces),)),
            pltpu.SemaphoreType.DMA((len(tile_list),)),
            pltpu.SemaphoreType.DMA((2,)),
        ],
        compiler_params=pltpu.CompilerParams(vmem_limit_bytes=40 * 1024 * 1024),
        cost_estimate=pl.CostEstimate(
            flops=2 * n_tiles * tile_len * tile_len * width, bytes_accessed=16 << 20, transcendentals=0
        ),
    )(rows, cols, *pieces, *tile_list, weight)


def candidate(features, node_order, section_owner, send_blocks, tile_len):
    me = lax.axis_index("dom")
    section = jnp.argmax(section_owner == me)
    share = send_blocks.shape[1] // lax.axis_size("rep")
    picks = lax.dynamic_slice(
        send_blocks, (section, lax.axis_index("rep") * share), (1, share)
    )[0]
    order = node_order[0].reshape(-1, tile_len)
    rows = order.at[picks].get(mode="promise_in_bounds").reshape(-1)
    return features.at[rows].get(mode="promise_in_bounds")


def gather_small(shard):
    sections = shard.shape[0]
    ring = {
        k: [(z * 4 + q, ((z - k) % 4) * 4 + q) for z in range(4) for q in range(4)]
        for k in (1, 2, 3)
    }
    flip = {k: [(i, i ^ k) for i in range(16)] for k in (1, 2)}

    def move(value, pairs):
        return lax.ppermute(value, "dom", pairs)

    shifted = [shard] + [move(shard, ring[k]) for k in (1, 2, 3)]
    pieces = list(shifted)
    places = [k * sections for k in range(4)]
    for first in (0, 2):
        pair = jnp.concatenate(shifted[first : first + 2])
        by_x = move(pair, flip[1])
        by_y = move(pair, flip[2])
        pieces += [by_x, by_y, move(by_x[:sections], flip[2]), move(by_y[sections:], flip[1])]
        places += [
            (4 + first) * sections,
            (8 + first) * sections,
            (12 + first) * sections,
            (13 + first) * sections,
        ]
    return pieces, places


def body(features, node_order, section_owner, send_blocks, tile_rows, tile_cols, tiles, weight):
    width = features.shape[1]
    tile_len = tiles.shape[3]
    blocks = features.shape[0] // tile_len
    n_dom, n_rep = lax.axis_size("dom"), lax.axis_size("rep")
    sections, n_send = send_blocks.shape
    me, rep = lax.axis_index("dom"), lax.axis_index("rep")
    n_blocks = blocks // n_rep
    small = n_dom == 16 and n_rep == 2 and n_send == n_dom * n_rep

    own_tiles = tiles[0].reshape(-1, tile_len, tile_len)
    numbers = jnp.stack([tile_rows[0], tile_cols[0]])
    section_of = jnp.broadcast_to(jnp.arange(sections)[:, None], tile_rows.shape[1:])
    if small:
        swap = [(0, 1), (1, 0)]
        tile_list = [own_tiles, lax.ppermute(own_tiles, "rep", swap)]
        numbers = jnp.stack([numbers, lax.ppermute(numbers, "rep", swap)])
    else:
        tile_list = [lax.all_gather(own_tiles, "rep", axis=0, tiled=True)]
        numbers = lax.all_gather(numbers, "rep", axis=0)
    rows = (numbers[:, 0] - rep * n_blocks).reshape(-1)
    cols = numbers[:, 1]

    mine = candidate(features, node_order, section_owner, send_blocks, tile_len)
    landed = lax.all_to_all(mine, "dom", 0, 0, tiled=True)
    landed = landed.reshape(n_dom, -1, width)
    shard = landed.at[section_owner].get(mode="promise_in_bounds")

    if small:
        pieces, places = gather_small(shard)
        half = n_dom * sections
        pieces = pieces + [lax.ppermute(piece, "rep", swap) for piece in pieces]
        places = places + [half + place for place in places]
        source = cols % n_dom
        other = (cols // n_dom != rep).astype(jnp.int32)
        across = (source ^ me) & 3
        shift = (source // 4 - me // 4) & 3
        slots = ((other * 4 + across) * 4 + shift) * sections + section_of
    else:
        whole = lax.all_gather(shard, ("rep", "dom"), axis=0)
        whole = whole.transpose(1, 0, 2, 3).reshape(sections * n_send, tile_len, width)
        pieces, places = [whole], [0]
        slots = section_of * n_send + cols
    hidden = products(
        pieces, places, tile_list, rows, slots.reshape(-1), weight, sections * n_send, n_blocks
    )
    return hidden.reshape(n_blocks * tile_len, -1)


def solution(mesh):
    return jax.shard_map(
        body,
        mesh=mesh,
        in_specs=(
            P("dom", None),
            P("dom", None),
            P(),
            P(),
            P("dom", None, "rep"),
            P("dom", None, "rep"),
            P("dom", None, "rep", None, None),
            P(),
        ),
        out_specs=P(("dom", "rep"), None),
        check_vma=False,
    )
```

time: 355 us -> 149 us (0.42)
  waiting for transfers between devices: 213 us -> 36.4 us
  starting transfers between devices: 0.38 us -> 59.5 us
  local copies, waits for them, and re-layouts: 71.8 us -> 28.9 us
  other arithmetic: 37.2 us -> 2.2 us
  Pallas kernels: 0 us -> 18.9 us
  matrix products: 15.3 us -> 0 us
  between operations: 16.1 us -> 2.26 us
    psum x1 -> x0, waiting for transfers between devices: 172 us -> none  [spread(): return lax.psum(kept, axis)]
    ppermute x0 -> x25, starting transfers between devices: none -> 51.8 us  [the longest x12 25.8 us: body(): pieces = pieces + [lax.ppermute(piece, 'rep', swap) for piece in pieces]]
    gather x9 -> x3, local copies, waits for them, and re-layouts: 54.6 us -> 12.4 us  [the longest x1 11.2 us: candidate(): return features.at[rows].get(mode='promise_in_bounds')]
    all_gather x4 -> x0, waiting for transfers between devices: 26.1 us -> none  [body(): arrived = lax.all_gather(landed, 'rep', axis=0, tiled=True)]
    all_to_all x0 -> x1, waiting for transfers between devices: none -> 21.1 us  [body(): landed = lax.all_to_all(mine, 'dom', 0, 0, tiled=True)]
    scatter-add x4 -> x0, other arithmetic: 19.5 us -> none  [body(): total = total.at[tile_rows[0, s]].add(product)]
    pallas_call x0 -> x1, Pallas kernels: none -> 18.9 us  [products(): pl.pallas_call(functools.partial(kernel, tuple(places), len(tile_list)),...]
    dot_general x5 -> x0, matrix products: 15.3 us -> none  [the longest x4 11.7 us: body(): jnp.einsum('kij,kjf->kif', tiles[0, s], chosen, preferred_element_type=jn...]
  transfers between devices with their start and end apart: 6 -> 26, of which waited for: 6 -> 9; matrix products, arithmetic and copies ran while one was open for 7% -> 2% of each run, Pallas kernels for 0% -> 0%
where the time goes in v1:
time: 149 us; the launch traced here: 148 us
  starting transfers between devices  59.5 us (40%)
  waiting for transfers between devices  36.4 us (24%)
  local copies, waits for them, and re-layouts  28.9 us (19%)
  Pallas kernels  18.9 us (13%)
  between operations  2.26 us (2%)
  other arithmetic  2.2 us (1%)
    ppermute x12, starting transfers between devices, body(): pieces = pieces + [lax.ppermute(piece, 'rep', swap) for piece in pieces]  25.8 us
    all_to_all x1, waiting for transfers between devices, body(): landed = lax.all_to_all(mine, 'dom', 0, 0, tiled=True)  21.1 us
    pallas_call x1, Pallas kernels, products(): pl.pallas_call(functools.partial(kernel, tuple(places), len(tile_list)),...  18.9 us
    ppermute x11, starting transfers between devices, move(): return lax.ppermute(value, 'dom', pairs)  17.9 us
    unnamed x59, local copies, waits for them, and re-layouts  14.3 us
    ppermute x11, waiting for transfers between devices, move(): return lax.ppermute(value, 'dom', pairs)  12.4 us
    gather x1, local copies, waits for them, and re-layouts, candidate(): return features.at[rows].get(mode='promise_in_bounds')  11.2 us
    all_to_all x1, starting transfers between devices, body(): landed = lax.all_to_all(mine, 'dom', 0, 0, tiled=True)  7.69 us
  transfers between devices with their start and end apart: 26, of which 9 were waited for; matrix products, arithmetic and copies ran while one was open for 2% of the time, Pallas kernels for 0%

profile of v1, /device:TPU:1, one launch (start us, length us, event | category | flops | bytes accessed | tf_op | source)
XLA Modules:
  0.0 148.2 jit_solution(1329485211152221833)
XLA Ops:
  0.0 1.4 compare_reduce_fusion
  3.4 0.8 fusion.3
  4.2 0.6 gather_fusion
  4.8 0.0 copy-start.27
  4.8 11.2 %gather_fusion.1 = bf16[2048,256]{1,0:T(8,128)(2,1)} fusion(bf16[8192,256]{1,0:T(8,128)(2,1)} %param.8, s32[2048]{0:T(1024)S(1)} %broadcast_clamp_fusion), kind=kCustom, calls=%fused_computation.1 | custom fusion | bytes 2105344 | tf_op jit(solution)/shard_map/gather | solution.py:122
  16.0 7.7 %all-to-all-start = ((bf16[16,128,256]{2,1,0:T(8,128)(2,1)}), bf16[16,128,256]{2,1,0:T(8,128)(2,1)S(1)}, u32[]{:S(2)}, u32[]{:S(2)}) async-start(bf16[16,128,256]{2,1,0:T(8,128)(2,1)} %bitcast.7), calls=%async_computation | async-start | bytes 2097152 | tf_op jit(solution)/shard_map/all_to_all | solution.py:177
  23.7 1.0 collective-permute-start.24
  24.8 21.1 %all-to-all-done = bf16[16,128,256]{2,1,0:T(8,128)(2,1)S(1)} async-done(((bf16[16,128,256]{2,1,0:T(8,128)(2,1)}), bf16[16,128,256]{2,1,0:T(8,128)(2,1)S(1)}, u32[]{:S(2)}, u32[]{:S(2)}) %all-to-all-start) | async-done | bytes 1048608 | tf_op jit(solution)/shard_map/all_to_all | solution.py:177
  45.9 0.6 gather_fusion.2
  46.5 3.1 %collective-permute-start.1 = (bf16[4,128,256]{2,1,0:T(8,128)(2,1)S(1)}, bf16[4,128,256]{2,1,0:T(8,128)(2,1)S(1)}, u32[]{:S(2)}, u32[]{:S(2)}) collective-permute-start(bf16[4,128,256]{2,1,0:T(8,128)(2,1)S(1)} %gather_fusion.2), channel_id=1, source_target_pairs={{0,24},{2,26},{4,28},{6,30},{8,0},{10,2},{12,4},{14,6},{16,8},{18,... | collective-permute-start | bytes 786440 | tf_op jit(solution)/shard_map/ppermute | solution.py:134
  49.6 0.5 collective-permute-start.3
  50.1 1.9 %collective-permute-start.2 = (bf16[4,128,256]{2,1,0:T(8,128)(2,1)S(1)}, bf16[4,128,256]{2,1,0:T(8,128)(2,1)S(1)}, u32[]{:S(2)}, u32[]{:S(2)}) collective-permute-start(bf16[4,128,256]{2,1,0:T(8,128)(2,1)S(1)} %gather_fusion.2), channel_id=1, source_target_pairs={{0,16},{2,18},{4,20},{6,22},{8,24},{10,26},{12,28},{14,30},{16,0},... | collective-permute-start | bytes 786440 | tf_op jit(solution)/shard_map/ppermute | solution.py:134
  52.1 2.1 %collective-permute-done.1.refs_1_ = bf16[4,128,256]{2,1,0:T(8,128)(2,1)S(1)} collective-permute-done((bf16[4,128,256]{2,1,0:T(8,128)(2,1)S(1)}, bf16[4,128,256]{2,1,0:T(8,128)(2,1)S(1)}, u32[]{:S(2)}, u32[]{:S(2)}) %collective-permute-start.1) | collective-permute-done | bytes 262176 | tf_op jit(solution)/shard_map/ppermute | solution.py:134
  54.2 2.5 %collective-permute-start.5 = (bf16[8,128,256]{2,1,0:T(8,128)(2,1)S(1)}, bf16[8,128,256]{2,1,0:T(8,128)(2,1)S(1)}, u32[]{:S(2)}, u32[]{:S(2)}) collective-permute-start(bf16[8,128,256]{2,1,0:T(8,128)(2,1)S(1)} %constant_dynamic-update-slice_fusion.2), channel_id=1, source_target_pairs={{0,4},{2,6},{4,0},{6,2},{8,12},{10,14},{12,8},{14,10},{16,20},{18,... | collective-permute-start | bytes 1572872 | tf_op jit(solution)/shard_map/ppermute | solution.py:134
  56.7 7.1 %collective-permute-start = (s32[2,4,16]{2,1,0:T(4,128)S(1)}, s32[2,4,16]{2,1,0:T(4,128)S(1)}, u32[]{:S(2)}, u32[]{:S(2)}) collective-permute-start(s32[2,4,16]{2,1,0:T(4,128)S(1)} %constant_dynamic-update-slice_fusion), channel_id=1, source_target_pairs={{0,1},{1,0},{2,3},{3,2},{4,5},{5,4},{6,7},{7,6},{8,9},{9,8},{10,11... | collective-permute-start | bytes 1544 | tf_op jit(solution)/shard_map/ppermute | solution.py:169
  63.8 7.9 %collective-permute-done.2.refs_2_ = bf16[4,128,256]{2,1,0:T(8,128)(2,1)S(1)} collective-permute-done((bf16[4,128,256]{2,1,0:T(8,128)(2,1)S(1)}, bf16[4,128,256]{2,1,0:T(8,128)(2,1)S(1)}, u32[]{:S(2)}, u32[]{:S(2)}) %collective-permute-start.2) | collective-permute-done | bytes 262176 | tf_op jit(solution)/shard_map/ppermute | solution.py:134
  71.7 1.1 collective-permute-start.4
  72.8 0.0 collective-permute-done.3.refs_3_
  72.9 1.9 %collective-permute-start.9 = (bf16[8,128,256]{2,1,0:T(8,128)(2,1)S(1)}, bf16[8,128,256]{2,1,0:T(8,128)(2,1)}, u32[]{:S(2)}, u32[]{:S(2)}) collective-permute-start(bf16[8,128,256]{2,1,0:T(8,128)(2,1)S(1)} %constant_dynamic-update-slice_fusion.4), channel_id=1, source_target_pairs={{0,4},{2,6},{4,0},{6,2},{8,12},{10,14},{12,8},{14,10},{16,20},{18,... | collective-permute-start | bytes 1572872 | tf_op jit(solution)/shard_map/ppermute | solution.py:134
  74.8 1.2 collective-permute-start.8
  76.0 3.5 %collective-permute-start.12 = (bf16[4,128,256]{2,1,0:T(8,128)(2,1)S(1)}, bf16[4,128,256]{2,1,0:T(8,128)(2,1)S(1)}, u32[]{:S(2)}, u32[]{:S(2)}) collective-permute-start(bf16[4,128,256]{2,1,0:T(8,128)(2,1)S(1)} %gather_fusion.2), channel_id=1, source_target_pairs={{0,1},{1,0},{2,3},{3,2},{4,5},{5,4},{6,7},{7,6},{8,9},{9,8},{10,11... | collective-permute-start | bytes 786440 | tf_op jit(solution)/shard_map/ppermute | solution.py:184
  79.5 0.1 collective-permute-start.15
  79.6 1.1 collective-permute-done.12.refs_12_
  80.6 0.4 collective-permute-start.14
  81.0 0.4 collective-permute-start.13
  81.4 0.1 collective-permute-done.4.refs_4_
  81.5 1.7 %collective-permute-start.7 = (bf16[4,128,256]{2,1,0:T(8,128)(2,1)S(1)}, bf16[4,128,256]{2,1,0:T(8,128)(2,1)S(1)}, u32[]{:S(2)}, u32[]{:S(2)}) collective-permute-start(bf16[4,128,256]{2,1,0:T(8,128)(2,1)S(1)} %slice.33), channel_id=1, source_target_pairs={{0,2},{2,0},{4,6},{6,4},{8,10},{10,8},{12,14},{14,12},{16,18},{18,... | collective-permute-start | bytes 786440 | tf_op jit(solution)/shard_map/ppermute | solution.py:134
  83.2 0.6 collective-permute-done.9.refs_9_
  83.8 7.3 %collective-permute-start.17 = (bf16[8,128,256]{2,1,0:T(8,128)(2,1)S(1)}, bf16[8,128,256]{2,1,0:T(8,128)(2,1)}, u32[]{:S(2)}, u32[]{:S(2)}) collective-permute-start(bf16[8,128,256]{2,1,0:T(8,128)(2,1)S(1)} %collective-permute-done.5.refs_5_), channel_id=1, source_target_pairs={{0,1},{1,0},{2,3},{3,2},{4,5},{5,4},{6,7},{7,6},{8,9},{9,8},{10,11... | collective-permute-start | bytes 1572872 | tf_op jit(solution)/shard_map/ppermute | solution.py:184
  91.1 1.6 %collective-permute-done.8.refs_8_ = bf16[8,128,256]{2,1,0:T(8,128)(2,1)} collective-permute-done((bf16[8,128,256]{2,1,0:T(8,128)(2,1)S(1)}, bf16[8,128,256]{2,1,0:T(8,128)(2,1)}, u32[]{:S(2)}, u32[]{:S(2)}) %collective-permute-start.8) | collective-permute-done | bytes 524320 | tf_op jit(solution)/shard_map/ppermute | solution.py:134
  92.7 3.7 %collective-permute-start.6 = (bf16[4,128,256]{2,1,0:T(8,128)(2,1)S(1)}, bf16[4,128,256]{2,1,0:T(8,128)(2,1)}, u32[]{:S(2)}, u32[]{:S(2)}) collective-permute-start(bf16[4,128,256]{2,1,0:T(8,128)(2,1)S(1)} %slice.32), channel_id=1, source_target_pairs={{0,4},{2,6},{4,0},{6,2},{8,12},{10,14},{12,8},{14,10},{16,20},{18,... | collective-permute-start | bytes 786440 | tf_op jit(solution)/shard_map/ppermute | solution.py:134
  96.4 1.0 slice.35
  97.4 1.0 slice.34
  98.4 0.7 copy-done.12
  99.1 0.3 collective-permute-start.11
  99.4 0.7 copy-done.14
  100.1 0.0 collective-permute-start.10
  100.1 7.3 %collective-permute-start.19 = (bf16[4,128,256]{2,1,0:T(8,128)(2,1)S(1)}, bf16[4,128,256]{2,1,0:T(8,128)(2,1)S(1)}, u32[]{:S(2)}, u32[]{:S(2)}) collective-permute-start(bf16[4,128,256]{2,1,0:T(8,128)(2,1)S(1)} %collective-permute-done.7.refs_7_), channel_id=1, source_target_pairs={{0,1},{1,0},{2,3},{3,2},{4,5},{5,4},{6,7},{7,6},{8,9},{9,8},{10,11... | collective-permute-start | bytes 786440 | tf_op jit(solution)/shard_map/ppermute | solution.py:184
  107.5 0.7 copy-done.16
  108.2 0.8 collective-permute-start.18
  109.0 3.6 %collective-permute-start.16 = (bf16[8,128,256]{2,1,0:T(8,128)(2,1)S(1)}, bf16[8,128,256]{2,1,0:T(8,128)(2,1)}, u32[]{:S(2)}, u32[]{:S(2)}) collective-permute-start(bf16[8,128,256]{2,1,0:T(8,128)(2,1)S(1)} %collective-permute-done.4.refs_4_), channel_id=1, source_target_pairs={{0,1},{1,0},{2,3},{3,2},{4,5},{5,4},{6,7},{7,6},{8,9},{9,8},{10,11... | collective-permute-start | bytes 1572872 | tf_op jit(solution)/shard_map/ppermute | solution.py:184
  112.6 1.3 collective-permute-start.21
  113.9 0.7 copy-done.22
  114.6 0.7 collective-permute-start.20
  115.3 0.1 add_broadcast_in_dim_broadcast_in_dim.8
  115.4 0.1 collective-permute-start.23
  115.5 0.5 collective-permute-start.22
  116.0 0.1 squeeze.7
  116.0 0.1 sub.33.rows_ref
  116.2 1.4 collective-permute-done.23.refs_23_
  117.5 0.4 collective-permute-done.22.refs_22_
  117.9 0.9 copy-done.3
  118.9 0.9 copy-done.5
  119.8 0.9 copy-done.7
  120.8 0.9 copy-done.9
  121.7 0.9 copy-done.11
  122.7 0.9 copy-done.13
  123.6 0.9 copy-done.15
  124.6 0.9 copy-done.17
  125.5 0.9 copy-done.19
  126.5 0.9 copy-done.21
  127.4 0.9 copy-done.23
  128.4 0.9 copy-done.24
  129.3 18.9 %shard_map.82 = bf16[32,128,256]{2,1,0:T(8,128)(2,1)} custom-call(s32[128]{0:T(128)S(1)} %sub.33.rows_ref, s32[128]{0:T(128)S(1)} %multiply_add_fusion.cols_ref, bf16[4,128,256]{2,1,0:T(8,128)(2,1)S(1)} %gather_fusion.2, bf16[4,128,256]{2,1,0:T(8,128)(2,1)S(1)} %copy-done.3, bf16[4,128,256]{2,1,0:T(8,128)(2,1)S(1)} %copy-done.7, ...), custom_call_target="tpu_custom_call" | custom-call | flops 1073741824 | bytes 16777216 | tf_op jit(solution)/shard_map/pallas_call | solution.py:89
  (71 shorter events, 0.3 us)
Async XLA Ops:
  0.0 4.2 %copy-start = (s32[1,8192]{1,0:T(1,128)S(1)}, s32[1,8192]{1,0:T(1,128)}, u32[]{:S(2)}) copy-start(s32[1,8192]{1,0:T(1,128)} %param.9) | copy-start | bytes 98308
  4.8 20.0 %copy-start.27 = (s32[4]{0:T(128)S(1)}, s32[4]{0:T(128)}, u32[]{:S(2)}) copy-start(s32[4]{0:T(128)} %param.10) | copy-start | bytes 52
  16.0 7.7 %copy-start.1 = (bf16[1,4,16,128,128]{4,3,2,1,0:T(8,128)(2,1)S(1)}, bf16[1,4,16,128,128]{4,3,2,1,0:T(8,128)(2,1)}, u32[]{:S(2)}) copy-start(bf16[1,4,16,128,128]{4,3,2,1,0:T(8,128)(2,1)} %param.14) | copy-start | bytes 6291460
  16.0 40.7 %copy-start.25 = (s32[1,4,16]{2,1,0:T(4,128)S(1)}, s32[1,4,16]{2,1,0:T(4,128)}, u32[]{:S(2)}) copy-start(s32[1,4,16]{2,1,0:T(4,128)} %param.12) | copy-start | bytes 772
  16.0 40.7 %copy-start.26 = (s32[1,4,16]{2,1,0:T(4,128)S(1)}, s32[1,4,16]{2,1,0:T(4,128)}, u32[]{:S(2)}) copy-start(s32[1,4,16]{2,1,0:T(4,128)} %param.13) | copy-start | bytes 772
  16.0 29.9 %all-to-all-start = ((bf16[16,128,256]{2,1,0:T(8,128)(2,1)}), bf16[16,128,256]{2,1,0:T(8,128)(2,1)S(1)}, u32[]{:S(2)}, u32[]{:S(2)}) async-start(bf16[16,128,256]{2,1,0:T(8,128)(2,1)} %bitcast.7), calls=%async_computation | async-start | bytes 2097152 | tf_op jit(solution)/shard_map/all_to_all | solution.py:177
  23.7 52.2 %collective-permute-start.24 = (bf16[64,128,128]{2,1,0:T(8,128)(2,1)S(1)}, bf16[64,128,128]{2,1,0:T(8,128)(2,1)}, u32[]{:S(2)}, u32[]{:S(2)}) collective-permute-start(bf16[64,128,128]{2,1,0:T(8,128)(2,1)S(1)} %bitcast.13), channel_id=1, source_target_pairs={{0,1},{1,0},{2,3},{3,2},{4,5},{5,4},{6,7},{7,6},{8,9},{9,8},{10,11... | collective-permute-start | bytes 6291464 | tf_op jit(solution)/shard_map/ppermute | solution.py:168
  46.5 7.7 %collective-permute-start.1 = (bf16[4,128,256]{2,1,0:T(8,128)(2,1)S(1)}, bf16[4,128,256]{2,1,0:T(8,128)(2,1)S(1)}, u32[]{:S(2)}, u32[]{:S(2)}) collective-permute-start(bf16[4,128,256]{2,1,0:T(8,128)(2,1)S(1)} %gather_fusion.2), channel_id=1, source_target_pairs={{0,24},{2,26},{4,28},{6,30},{8,0},{10,2},{12,4},{14,6},{16,8},{18,... | collective-permute-start | bytes 786440 | tf_op jit(solution)/shard_map/ppermute | solution.py:134
  49.6 23.2 %collective-permute-start.3 = (bf16[4,128,256]{2,1,0:T(8,128)(2,1)S(1)}, bf16[4,128,256]{2,1,0:T(8,128)(2,1)S(1)}, u32[]{:S(2)}, u32[]{:S(2)}) collective-permute-start(bf16[4,128,256]{2,1,0:T(8,128)(2,1)S(1)} %gather_fusion.2), channel_id=1, source_target_pairs={{0,8},{2,10},{4,12},{6,14},{8,16},{10,18},{12,20},{14,22},{16,24},... | collective-permute-start | bytes 786440 | tf_op jit(solution)/shard_map/ppermute | solution.py:134
  50.1 21.6 %collective-permute-start.2 = (bf16[4,128,256]{2,1,0:T(8,128)(2,1)S(1)}, bf16[4,128,256]{2,1,0:T(8,128)(2,1)S(1)}, u32[]{:S(2)}, u32[]{:S(2)}) collective-permute-start(bf16[4,128,256]{2,1,0:T(8,128)(2,1)S(1)} %gather_fusion.2), channel_id=1, source_target_pairs={{0,16},{2,18},{4,20},{6,22},{8,24},{10,26},{12,28},{14,30},{16,0},... | collective-permute-start | bytes 786440 | tf_op jit(solution)/shard_map/ppermute | solution.py:134
  54.2 54.7 %copy-start.2 = (bf16[4,128,256]{2,1,0:T(8,128)(2,1)}, bf16[4,128,256]{2,1,0:T(8,128)(2,1)S(1)}, u32[]{:S(2)}) copy-start(bf16[4,128,256]{2,1,0:T(8,128)(2,1)S(1)} %collective-permute-done.1.refs_1_) | copy-start | bytes 786436
  54.2 25.2 %collective-permute-start.5 = (bf16[8,128,256]{2,1,0:T(8,128)(2,1)S(1)}, bf16[8,128,256]{2,1,0:T(8,128)(2,1)S(1)}, u32[]{:S(2)}, u32[]{:S(2)}) collective-permute-start(bf16[8,128,256]{2,1,0:T(8,128)(2,1)S(1)} %constant_dynamic-update-slice_fusion.2), channel_id=1, source_target_pairs={{0,4},{2,6},{4,0},{6,2},{8,12},{10,14},{12,8},{14,10},{16,20},{18,... | collective-permute-start | bytes 1572872 | tf_op jit(solution)/shard_map/ppermute | solution.py:134
  56.7 18.1 %collective-permute-start = (s32[2,4,16]{2,1,0:T(4,128)S(1)}, s32[2,4,16]{2,1,0:T(4,128)S(1)}, u32[]{:S(2)}, u32[]{:S(2)}) collective-permute-start(s32[2,4,16]{2,1,0:T(4,128)S(1)} %constant_dynamic-update-slice_fusion), channel_id=1, source_target_pairs={{0,1},{1,0},{2,3},{3,2},{4,5},{5,4},{6,7},{7,6},{8,9},{9,8},{10,11... | collective-permute-start | bytes 1544 | tf_op jit(solution)/shard_map/ppermute | solution.py:169
  71.7 40.9 %copy-start.6 = (bf16[4,128,256]{2,1,0:T(8,128)(2,1)}, bf16[4,128,256]{2,1,0:T(8,128)(2,1)S(1)}, u32[]{:S(2)}) copy-start(bf16[4,128,256]{2,1,0:T(8,128)(2,1)S(1)} %collective-permute-done.2.refs_2_) | copy-start | bytes 786436
  71.7 9.9 %collective-permute-start.4 = (bf16[8,128,256]{2,1,0:T(8,128)(2,1)S(1)}, bf16[8,128,256]{2,1,0:T(8,128)(2,1)S(1)}, u32[]{:S(2)}, u32[]{:S(2)}) collective-permute-start(bf16[8,128,256]{2,1,0:T(8,128)(2,1)S(1)} %constant_dynamic-update-slice_fusion.2), channel_id=1, source_target_pairs={{0,2},{2,0},{4,6},{6,4},{8,10},{10,8},{12,14},{14,12},{16,18},{18,... | collective-permute-start | bytes 1572872 | tf_op jit(solution)/shard_map/ppermute | solution.py:134
  72.8 36.1 %copy-start.4 = (bf16[4,128,256]{2,1,0:T(8,128)(2,1)}, bf16[4,128,256]{2,1,0:T(8,128)(2,1)S(1)}, u32[]{:S(2)}) copy-start(bf16[4,128,256]{2,1,0:T(8,128)(2,1)S(1)} %collective-permute-done.3.refs_3_) | copy-start | bytes 786436
  72.9 11.0 %collective-permute-start.9 = (bf16[8,128,256]{2,1,0:T(8,128)(2,1)S(1)}, bf16[8,128,256]{2,1,0:T(8,128)(2,1)}, u32[]{:S(2)}, u32[]{:S(2)}) collective-permute-start(bf16[8,128,256]{2,1,0:T(8,128)(2,1)S(1)} %constant_dynamic-update-slice_fusion.4), channel_id=1, source_target_pairs={{0,4},{2,6},{4,0},{6,2},{8,12},{10,14},{12,8},{14,10},{16,20},{18,... | collective-permute-start | bytes 1572872 | tf_op jit(solution)/shard_map/ppermute | solution.py:134
  74.8 18.0 %collective-permute-start.8 = (bf16[8,128,256]{2,1,0:T(8,128)(2,1)S(1)}, bf16[8,128,256]{2,1,0:T(8,128)(2,1)}, u32[]{:S(2)}, u32[]{:S(2)}) collective-permute-start(bf16[8,128,256]{2,1,0:T(8,128)(2,1)S(1)} %constant_dynamic-update-slice_fusion.4), channel_id=1, source_target_pairs={{0,2},{2,0},{4,6},{6,4},{8,10},{10,8},{12,14},{14,12},{16,18},{18,... | collective-permute-start | bytes 1572872 | tf_op jit(solution)/shard_map/ppermute | solution.py:134
  76.0 4.7 %collective-permute-start.12 = (bf16[4,128,256]{2,1,0:T(8,128)(2,1)S(1)}, bf16[4,128,256]{2,1,0:T(8,128)(2,1)S(1)}, u32[]{:S(2)}, u32[]{:S(2)}) collective-permute-start(bf16[4,128,256]{2,1,0:T(8,128)(2,1)S(1)} %gather_fusion.2), channel_id=1, source_target_pairs={{0,1},{1,0},{2,3},{3,2},{4,5},{5,4},{6,7},{7,6},{8,9},{9,8},{10,11... | collective-permute-start | bytes 786440 | tf_op jit(solution)/shard_map/ppermute | solution.py:184
  79.5 1.5 %collective-permute-start.15 = (bf16[4,128,256]{2,1,0:T(8,128)(2,1)S(1)}, bf16[4,128,256]{2,1,0:T(8,128)(2,1)S(1)}, u32[]{:S(2)}, u32[]{:S(2)}) collective-permute-start(bf16[4,128,256]{2,1,0:T(8,128)(2,1)S(1)} %collective-permute-done.3.refs_3_), channel_id=1, source_target_pairs={{0,1},{1,0},{2,3},{3,2},{4,5},{5,4},{6,7},{7,6},{8,9},{9,8},{10,11... | collective-permute-start | bytes 786440 | tf_op jit(solution)/shard_map/ppermute | solution.py:184
  80.6 31.9 %copy-start.8 = (bf16[4,128,256]{2,1,0:T(8,128)(2,1)}, bf16[4,128,256]{2,1,0:T(8,128)(2,1)S(1)}, u32[]{:S(2)}) copy-start(bf16[4,128,256]{2,1,0:T(8,128)(2,1)S(1)} %collective-permute-done.12.refs_12_) | copy-start | bytes 786436
  80.6 17.7 %collective-permute-start.14 = (bf16[4,128,256]{2,1,0:T(8,128)(2,1)S(1)}, bf16[4,128,256]{2,1,0:T(8,128)(2,1)S(1)}, u32[]{:S(2)}, u32[]{:S(2)}) collective-permute-start(bf16[4,128,256]{2,1,0:T(8,128)(2,1)S(1)} %collective-permute-done.2.refs_2_), channel_id=1, source_target_pairs={{0,1},{1,0},{2,3},{3,2},{4,5},{5,4},{6,7},{7,6},{8,9},{9,8},{10,11... | collective-permute-start | bytes 786440 | tf_op jit(solution)/shard_map/ppermute | solution.py:184
  81.0 32.8 %copy-start.10 = (bf16[4,128,256]{2,1,0:T(8,128)(2,1)}, bf16[4,128,256]{2,1,0:T(8,128)(2,1)S(1)}, u32[]{:S(2)}) copy-start(bf16[4,128,256]{2,1,0:T(8,128)(2,1)S(1)} %collective-permute-done.15.refs_15_) | copy-start | bytes 786436
  81.0 18.4 %collective-permute-start.13 = (bf16[4,128,256]{2,1,0:T(8,128)(2,1)S(1)}, bf16[4,128,256]{2,1,0:T(8,128)(2,1)S(1)}, u32[]{:S(2)}, u32[]{:S(2)}) collective-permute-start(bf16[4,128,256]{2,1,0:T(8,128)(2,1)S(1)} %collective-permute-done.1.refs_1_), channel_id=1, source_target_pairs={{0,1},{1,0},{2,3},{3,2},{4,5},{5,4},{6,7},{7,6},{8,9},{9,8},{10,11... | collective-permute-start | bytes 786440 | tf_op jit(solution)/shard_map/ppermute | solution.py:184
  81.5 18.6 %collective-permute-start.7 = (bf16[4,128,256]{2,1,0:T(8,128)(2,1)S(1)}, bf16[4,128,256]{2,1,0:T(8,128)(2,1)S(1)}, u32[]{:S(2)}, u32[]{:S(2)}) collective-permute-start(bf16[4,128,256]{2,1,0:T(8,128)(2,1)S(1)} %slice.33), channel_id=1, source_target_pairs={{0,2},{2,0},{4,6},{6,4},{8,10},{10,8},{12,14},{14,12},{16,18},{18,... | collective-permute-start | bytes 786440 | tf_op jit(solution)/shard_map/ppermute | solution.py:134
  83.8 31.5 %collective-permute-start.17 = (bf16[8,128,256]{2,1,0:T(8,128)(2,1)S(1)}, bf16[8,128,256]{2,1,0:T(8,128)(2,1)}, u32[]{:S(2)}, u32[]{:S(2)}) collective-permute-start(bf16[8,128,256]{2,1,0:T(8,128)(2,1)S(1)} %collective-permute-done.5.refs_5_), channel_id=1, source_target_pairs={{0,1},{1,0},{2,3},{3,2},{4,5},{5,4},{6,7},{7,6},{8,9},{9,8},{10,11... | collective-permute-start | bytes 1572872 | tf_op jit(solution)/shard_map/ppermute | solution.py:184
  92.7 15.4 %collective-permute-start.6 = (bf16[4,128,256]{2,1,0:T(8,128)(2,1)S(1)}, bf16[4,128,256]{2,1,0:T(8,128)(2,1)}, u32[]{:S(2)}, u32[]{:S(2)}) collective-permute-start(bf16[4,128,256]{2,1,0:T(8,128)(2,1)S(1)} %slice.32), channel_id=1, source_target_pairs={{0,4},{2,6},{4,0},{6,2},{8,12},{10,14},{12,8},{14,10},{16,20},{18,... | collective-permute-start | bytes 786440 | tf_op jit(solution)/shard_map/ppermute | solution.py:134
  98.4 0.7 copy-start.12
  99.1 9.8 %collective-permute-start.11 = (bf16[4,128,256]{2,1,0:T(8,128)(2,1)S(1)}, bf16[4,128,256]{2,1,0:T(8,128)(2,1)S(1)}, u32[]{:S(2)}, u32[]{:S(2)}) collective-permute-start(bf16[4,128,256]{2,1,0:T(8,128)(2,1)S(1)} %slice.35), channel_id=1, source_target_pairs={{0,2},{2,0},{4,6},{6,4},{8,10},{10,8},{12,14},{14,12},{16,18},{18,... | collective-permute-start | bytes 786440 | tf_op jit(solution)/shard_map/ppermute | solution.py:134
  99.4 0.7 copy-start.14
  100.1 12.5 %collective-permute-start.10 = (bf16[4,128,256]{2,1,0:T(8,128)(2,1)S(1)}, bf16[4,128,256]{2,1,0:T(8,128)(2,1)S(1)}, u32[]{:S(2)}, u32[]{:S(2)}) collective-permute-start(bf16[4,128,256]{2,1,0:T(8,128)(2,1)S(1)} %slice.34), channel_id=1, source_target_pairs={{0,4},{2,6},{4,0},{6,2},{8,12},{10,14},{12,8},{14,10},{16,20},{18,... | collective-permute-start | bytes 786440 | tf_op jit(solution)/shard_map/ppermute | solution.py:134
  100.1 13.7 %collective-permute-start.19 = (bf16[4,128,256]{2,1,0:T(8,128)(2,1)S(1)}, bf16[4,128,256]{2,1,0:T(8,128)(2,1)S(1)}, u32[]{:S(2)}, u32[]{:S(2)}) collective-permute-start(bf16[4,128,256]{2,1,0:T(8,128)(2,1)S(1)} %collective-permute-done.7.refs_7_), channel_id=1, source_target_pairs={{0,1},{1,0},{2,3},{3,2},{4,5},{5,4},{6,7},{7,6},{8,9},{9,8},{10,11... | collective-permute-start | bytes 786440 | tf_op jit(solution)/shard_map/ppermute | solution.py:184
  107.5 0.7 copy-start.16
  108.2 7.3 %collective-permute-start.18 = (bf16[4,128,256]{2,1,0:T(8,128)(2,1)}, bf16[4,128,256]{2,1,0:T(8,128)(2,1)}, u32[]{:S(2)}, u32[]{:S(2)}) collective-permute-start(bf16[4,128,256]{2,1,0:T(8,128)(2,1)} %collective-permute-done.6.refs_6_), channel_id=1, source_target_pairs={{0,1},{1,0},{2,3},{3,2},{4,5},{5,4},{6,7},{7,6},{8,9},{9,8},{10,11... | collective-permute-start | bytes 786440 | tf_op jit(solution)/shard_map/ppermute | solution.py:184
  108.9 4.9 %copy-start.18 = (bf16[4,128,256]{2,1,0:T(8,128)(2,1)}, bf16[4,128,256]{2,1,0:T(8,128)(2,1)S(1)}, u32[]{:S(2)}) copy-start(bf16[4,128,256]{2,1,0:T(8,128)(2,1)S(1)} %collective-permute-done.11.refs_11_) | copy-start | bytes 786436
  109.0 7.2 %collective-permute-start.16 = (bf16[8,128,256]{2,1,0:T(8,128)(2,1)S(1)}, bf16[8,128,256]{2,1,0:T(8,128)(2,1)}, u32[]{:S(2)}, u32[]{:S(2)}) collective-permute-start(bf16[8,128,256]{2,1,0:T(8,128)(2,1)S(1)} %collective-permute-done.4.refs_4_), channel_id=1, source_target_pairs={{0,1},{1,0},{2,3},{3,2},{4,5},{5,4},{6,7},{7,6},{8,9},{9,8},{10,11... | collective-permute-start | bytes 1572872 | tf_op jit(solution)/shard_map/ppermute | solution.py:184
  112.6 1.3 copy-start.20
  112.6 5.0 %collective-permute-start.21 = (bf16[8,128,256]{2,1,0:T(8,128)(2,1)}, bf16[8,128,256]{2,1,0:T(8,128)(2,1)}, u32[]{:S(2)}, u32[]{:S(2)}) collective-permute-start(bf16[8,128,256]{2,1,0:T(8,128)(2,1)} %collective-permute-done.9.refs_9_), channel_id=1, source_target_pairs={{0,1},{1,0},{2,3},{3,2},{4,5},{5,4},{6,7},{7,6},{8,9},{9,8},{10,11... | collective-permute-start | bytes 1572872 | tf_op jit(solution)/shard_map/ppermute | solution.py:184
  113.9 0.7 copy-start.22
  114.6 3.3 %collective-permute-start.20 = (bf16[8,128,256]{2,1,0:T(8,128)(2,1)}, bf16[8,128,256]{2,1,0:T(8,128)(2,1)}, u32[]{:S(2)}, u32[]{:S(2)}) collective-permute-start(bf16[8,128,256]{2,1,0:T(8,128)(2,1)} %collective-permute-done.8.refs_8_), channel_id=1, source_target_pairs={{0,1},{1,0},{2,3},{3,2},{4,5},{5,4},{6,7},{7,6},{8,9},{9,8},{10,11... | collective-permute-start | bytes 1572872 | tf_op jit(solution)/shard_map/ppermute | solution.py:184
  115.4 2.2 %collective-permute-start.23 = (bf16[4,128,256]{2,1,0:T(8,128)(2,1)}, bf16[4,128,256]{2,1,0:T(8,128)(2,1)}, u32[]{:S(2)}, u32[]{:S(2)}) collective-permute-start(bf16[4,128,256]{2,1,0:T(8,128)(2,1)} %copy-done.18), channel_id=1, source_target_pairs={{0,1},{1,0},{2,3},{3,2},{4,5},{5,4},{6,7},{7,6},{8,9},{9,8},{10,11... | collective-permute-start | bytes 786440 | tf_op jit(solution)/shard_map/ppermute | solution.py:184
  115.5 2.4 %collective-permute-start.22 = (bf16[4,128,256]{2,1,0:T(8,128)(2,1)}, bf16[4,128,256]{2,1,0:T(8,128)(2,1)}, u32[]{:S(2)}, u32[]{:S(2)}) collective-permute-start(bf16[4,128,256]{2,1,0:T(8,128)(2,1)} %copy-done.20), channel_id=1, source_target_pairs={{0,1},{1,0},{2,3},{3,2},{4,5},{5,4},{6,7},{7,6},{8,9},{9,8},{10,11... | collective-permute-start | bytes 786440 | tf_op jit(solution)/shard_map/ppermute | solution.py:184
  117.9 1.0 copy-start.3
  118.9 0.9 copy-start.5
  119.8 0.9 copy-start.7
  120.8 0.9 copy-start.9
  121.7 0.9 copy-start.11
  122.7 0.9 copy-start.13
  123.6 0.9 copy-start.15
  124.6 0.9 copy-start.17
  125.5 0.9 copy-start.19
  126.5 0.9 copy-start.21
  127.4 0.9 copy-start.23
  128.4 0.9 copy-start.24

commit v2 on v1

--- a/solution.py
+++ b/solution.py
@@ -84,7 +84,7 @@
     width = weight.shape[0]
     n_tiles = rows.shape[0]
     group = min(4, n_blocks)
-    any_spec = pl.BlockSpec(memory_space=pl.ANY)
+    any_spec = pl.BlockSpec(memory_space=pltpu.HBM)
     smem = pl.BlockSpec(memory_space=pltpu.SMEM)
     return pl.pallas_call(
         functools.partial(kernel, tuple(places), len(tile_list)),
@@ -110,44 +110,87 @@
     )(rows, cols, *pieces, *tile_list, weight)
 
 
-def candidate(features, node_order, section_owner, send_blocks, tile_len):
+def share_rows(node_order, section_owner, send_blocks, tile_len):
     me = lax.axis_index("dom")
-    section = jnp.argmax(section_owner == me)
-    share = send_blocks.shape[1] // lax.axis_size("rep")
+    sections, n_send = send_blocks.shape
+    mine = (section_owner == me).astype(jnp.int32)
+    section = jnp.sum(mine * jnp.arange(sections, dtype=jnp.int32))
+    share = n_send // lax.axis_size("rep")
     picks = lax.dynamic_slice(
         send_blocks, (section, lax.axis_index("rep") * share), (1, share)
     )[0]
     order = node_order[0].reshape(-1, tile_len)
-    rows = order.at[picks].get(mode="promise_in_bounds").reshape(-1)
-    return features.at[rows].get(mode="promise_in_bounds")
-
-
-def gather_small(shard):
-    sections = shard.shape[0]
-    ring = {
-        k: [(z * 4 + q, ((z - k) % 4) * 4 + q) for z in range(4) for q in range(4)]
-        for k in (1, 2, 3)
-    }
-    flip = {k: [(i, i ^ k) for i in range(16)] for k in (1, 2)}
-
-    def move(value, pairs):
-        return lax.ppermute(value, "dom", pairs)
-
-    shifted = [shard] + [move(shard, ring[k]) for k in (1, 2, 3)]
-    pieces = list(shifted)
-    places = [k * sections for k in range(4)]
-    for first in (0, 2):
-        pair = jnp.concatenate(shifted[first : first + 2])
-        by_x = move(pair, flip[1])
-        by_y = move(pair, flip[2])
-        pieces += [by_x, by_y, move(by_x[:sections], flip[2]), move(by_y[sections:], flip[1])]
-        places += [
-            (4 + first) * sections,
-            (8 + first) * sections,
-            (12 + first) * sections,
-            (13 + first) * sections,
-        ]
-    return pieces, places
+    return order.at[picks].get(mode="promise_in_bounds")
+
+
+def move(value, pairs):
+    return lax.ppermute(value, "dom", pairs)
+
+
+def flip(bits):
+    return [(i, i ^ bits) for i in range(16)]
+
+
+def quad_scatter(features, lines):
+    quad = lax.axis_index("dom") % 4
+    each = lines.shape[0] // 4
+    held = [None] * 4
+    for e in (3, 1, 2, 0):
+        own = lax.dynamic_slice_in_dim(lines, (quad ^ e) * each, each)
+        rows = features.at[own.reshape(-1)].get(mode="promise_in_bounds")
+        held[e] = rows.reshape(each, lines.shape[1], features.shape[1])
+        if e:
+            held[e] = move(held[e], flip(e))
+    return held
+
+
+def along_z(first, at, z, pair):
+    middle = [(i, i + 4) for i in range(4, 8)] + [(i, i - 4) for i in range(8, 12)]
+    outer = [(i, i - 4) for i in range(4, 8)] + [(i, i + 4) for i in range(8, 12)]
+    near = move(first, pair)
+    known = jnp.where(at == z, first, near)
+    across = move(known, middle)
+    beyond = move(across, outer)
+    inner = jnp.logical_or(z == 1, z == 2)
+    return known, jnp.where(inner, across, beyond)
+
+
+def quad_gather(own):
+    half = own.shape[0] // 2
+    by_x = move(own, flip(1))
+    by_y = move(own, flip(2))
+    return [own, by_x, by_y, move(by_x[:half], flip(2)), move(by_y[half:], flip(1))]
+
+
+def gather_small(features, lines, section_owner):
+    me = lax.axis_index("dom")
+    quad, z = me % 4, me // 4
+    held = quad_scatter(features, lines)
+    is_first, is_last = section_owner == 0, section_owner == 15
+    other = jnp.logical_not(jnp.logical_or(is_first, is_last))
+    rank = jnp.cumsum(other.astype(jnp.int32)) - 1
+    owners = [
+        jnp.sum(jnp.where(jnp.logical_and(other, rank == i), section_owner, 0)) for i in (0, 1)
+    ]
+    low = z < 2
+    slot = jnp.where(other, 2 + rank, jnp.where(is_first == low, 0, 1))
+
+    def of(source):
+        return lax.select_n(quad ^ source, *held)
+
+    end = jnp.where(low, 0, 3)
+    inward = [(i, i + 4) for i in range(4)] + [(i, i - 4) for i in range(12, 16)]
+    near, far = along_z(of(end), end, z, inward)
+    quarters = [near, far]
+    for owner in owners:
+        known, rest = along_z(of(owner % 4), owner // 4, z, flip(4))
+        quarters.append(jnp.where((owner // 8) == (z // 2), known, rest))
+    pieces, places = [], []
+    each = near.shape[0]
+    for i, quarter in enumerate(quarters):
+        pieces += quad_gather(quarter)
+        places += [(i * 4 + e) * each for e in range(4)] + [(i * 4 + 3) * each + each // 2]
+    return pieces, places, slot
 
 
 def body(features, node_order, section_owner, send_blocks, tile_rows, tile_cols, tiles, weight):
@@ -162,7 +205,6 @@
 
     own_tiles = tiles[0].reshape(-1, tile_len, tile_len)
     numbers = jnp.stack([tile_rows[0], tile_cols[0]])
-    section_of = jnp.broadcast_to(jnp.arange(sections)[:, None], tile_rows.shape[1:])
     if small:
         swap = [(0, 1), (1, 0)]
         tile_list = [own_tiles, lax.ppermute(own_tiles, "rep", swap)]
@@ -173,26 +215,25 @@
     rows = (numbers[:, 0] - rep * n_blocks).reshape(-1)
     cols = numbers[:, 1]
 
-    mine = candidate(features, node_order, section_owner, send_blocks, tile_len)
-    landed = lax.all_to_all(mine, "dom", 0, 0, tiled=True)
-    landed = landed.reshape(n_dom, -1, width)
-    shard = landed.at[section_owner].get(mode="promise_in_bounds")
-
+    lines = share_rows(node_order, section_owner, send_blocks, tile_len)
     if small:
-        pieces, places = gather_small(shard)
-        half = n_dom * sections
+        pieces, places, slot = gather_small(features, lines, section_owner)
+        half = sections * n_send // 2
         pieces = pieces + [lax.ppermute(piece, "rep", swap) for piece in pieces]
         places = places + [half + place for place in places]
-        source = cols % n_dom
+        block = cols % n_dom
+        across = (block // 4) ^ (me % 4)
         other = (cols // n_dom != rep).astype(jnp.int32)
-        across = (source ^ me) & 3
-        shift = (source // 4 - me // 4) & 3
-        slots = ((other * 4 + across) * 4 + shift) * sections + section_of
+        slots = ((other * sections + slot[:, None]) * 4 + across) * 4 + block % 4
     else:
+        mine = features.at[lines.reshape(-1)].get(mode="promise_in_bounds")
+        landed = lax.all_to_all(mine, "dom", 0, 0, tiled=True)
+        landed = landed.reshape(n_dom, -1, width)
+        shard = landed.at[section_owner].get(mode="promise_in_bounds")
         whole = lax.all_gather(shard, ("rep", "dom"), axis=0)
         whole = whole.transpose(1, 0, 2, 3).reshape(sections * n_send, tile_len, width)
         pieces, places = [whole], [0]
-        slots = section_of * n_send + cols
+        slots = jnp.arange(sections)[:, None] * n_send + cols
     hidden = products(
         pieces, places, tile_list, rows, slots.reshape(-1), weight, sections * n_send, n_blocks
     )

time: 149 us -> 167 us (1.12)
  local copies, waits for them, and re-layouts: 28.9 us -> 50 us
  starting transfers between devices: 59.5 us -> 49.8 us
  waiting for transfers between devices: 36.4 us -> 30.9 us
  between operations: 2.26 us -> 7.75 us
  other arithmetic: 2.2 us -> 7.31 us
    all_to_all x1 -> x0, waiting for transfers between devices: 21.1 us -> none  [body(): landed = lax.all_to_all(mine, 'dom', 0, 0, tiled=True)]
    ppermute x11 -> x28, waiting for transfers between devices: 12.4 us -> 27 us  [move(): return lax.ppermute(value, 'dom', pairs)]
    unnamed x59 -> x97, local copies, waits for them, and re-layouts: 14.3 us -> 28.6 us
    ppermute x12 -> x20, starting transfers between devices: 25.8 us -> 15.1 us  [body(): pieces = pieces + [lax.ppermute(piece, 'rep', swap) for piece in pieces]]
    ppermute x11 -> x28, starting transfers between devices: 17.9 us -> 28.2 us  [move(): return lax.ppermute(value, 'dom', pairs)]
    all_to_all x1 -> x0, starting transfers between devices: 7.69 us -> none  [body(): landed = lax.all_to_all(mine, 'dom', 0, 0, tiled=True)]
    gather x3 -> x5, local copies, waits for them, and re-layouts: 12.4 us -> 19.1 us  [the longest x4 18.6 us: quad_scatter(): rows = features.at[own.reshape(-1)].get(mode='promise_in_bounds')]
    select_n x3 -> x12, other arithmetic: 0.78 us -> 5.03 us  [the longest x2 2.06 us: gather_small(): quarters.append(jnp.where(owner // 8 == z // 2, known, rest))]
  transfers between devices with their start and end apart: 26 -> 50, of which waited for: 9 -> 19; matrix products, arithmetic and copies ran while one was open for 2% -> 12% of each run, Pallas kernels for 0% -> 0%
where the time goes in v2:
time: 167 us; the launch traced here: 165 us
  local copies, waits for them, and re-layouts  50 us (30%)
  starting transfers between devices  49.8 us (30%)
  waiting for transfers between devices  30.9 us (19%)
  Pallas kernels  19.7 us (12%)
  between operations  7.75 us (5%)
  other arithmetic  7.31 us (4%)
    unnamed x97, local copies, waits for them, and re-layouts  28.6 us
    ppermute x28, starting transfers between devices, move(): return lax.ppermute(value, 'dom', pairs)  28.2 us
    ppermute x28, waiting for transfers between devices, move(): return lax.ppermute(value, 'dom', pairs)  27 us
    pallas_call x1, Pallas kernels, products(): pl.pallas_call(functools.partial(kernel, tuple(places), len(tile_list)),...  19.7 us
    gather x4, local copies, waits for them, and re-layouts, quad_scatter(): rows = features.at[own.reshape(-1)].get(mode='promise_in_bounds')  18.6 us
    ppermute x20, starting transfers between devices, body(): pieces = pieces + [lax.ppermute(piece, 'rep', swap) for piece in pieces]  15.1 us
    ppermute x1, starting transfers between devices, body(): tile_list = [own_tiles, lax.ppermute(own_tiles, 'rep', swap)]  3.48 us
  transfers between devices with their start and end apart: 50, of which 19 were waited for; matrix products, arithmetic and copies ran while one was open for 12% of the time, Pallas kernels for 0%

profile of v2, /device:TPU:1, one launch (start us, length us, event | category | flops | bytes accessed | tf_op | source)
XLA Modules:
  0.0 165.4 jit_solution(10419966033753226354)
XLA Ops:
  0.8 1.4 fusion.10
  5.6 4.3 %gather_fusion.3 = bf16[512,256]{1,0:T(8,128)(2,1)S(1)} fusion(bf16[8192,256]{1,0:T(8,128)(2,1)} %param.8, s32[1024]{0:T(1024)S(1)} %get-tuple-element.19), kind=kCustom, calls=%fused_computation.3 | custom fusion | bytes 526336 | tf_op jit(solution)/shard_map/gather | solution.py:140
  9.9 2.1 %collective-permute-start.2 = (bf16[4,128,256]{2,1,0:T(8,128)(2,1)S(1)}, bf16[4,128,256]{2,1,0:T(8,128)(2,1)S(1)}, u32[]{:S(2)}, u32[]{:S(2)}) collective-permute-start(bf16[4,128,256]{2,1,0:T(8,128)(2,1)S(1)} %bitcast.41), channel_id=1, source_target_pairs={{0,4},{2,6},{4,0},{6,2},{8,12},{10,14},{12,8},{14,10},{16,20},{18,... | collective-permute-start | bytes 786440 | tf_op jit(solution)/shard_map/ppermute | solution.py:127
  12.0 4.9 %gather_fusion.4 = bf16[512,256]{1,0:T(8,128)(2,1)} fusion(bf16[8192,256]{1,0:T(8,128)(2,1)} %param.8, s32[1024]{0:T(1024)S(1)} %get-tuple-element.18), kind=kCustom, calls=%fused_computation.4 | custom fusion | bytes 526336 | tf_op jit(solution)/shard_map/gather | solution.py:140
  16.9 1.2 collective-permute-start.3
  18.2 5.1 %gather_fusion.2 = bf16[512,256]{1,0:T(8,128)(2,1)} fusion(bf16[8192,256]{1,0:T(8,128)(2,1)} %param.8, s32[1024]{0:T(1024)S(1)} %get-tuple-element.20), kind=kCustom, calls=%fused_computation.2 | custom fusion | bytes 526336 | tf_op jit(solution)/shard_map/gather | solution.py:140
  27.3 4.3 %gather_fusion.1 = bf16[512,256]{1,0:T(8,128)(2,1)S(1)} fusion(bf16[8192,256]{1,0:T(8,128)(2,1)} %param.8, s32[1024]{0:T(1024)S(1)} %get-tuple-element.21), kind=kCustom, calls=%fused_computation.1 | custom fusion | bytes 526336 | tf_op jit(solution)/shard_map/gather | solution.py:140
  33.0 1.1 select_select_fusion.1
  34.1 1.5 collective-permute-start.22
  37.1 3.3 %collective-permute-start.4 = (bf16[4,128,256]{2,1,0:T(8,128)(2,1)S(1)}, bf16[4,128,256]{2,1,0:T(8,128)(2,1)S(1)}, u32[]{:S(2)}, u32[]{:S(2)}) collective-permute-start(bf16[4,128,256]{2,1,0:T(8,128)(2,1)S(1)} %get-tuple-element.10), channel_id=1, source_target_pairs={{0,8},{2,10},{4,12},{6,14},{24,16},{26,18},{28,20},{30,22},{1,9},{... | collective-permute-start | bytes 786440 | tf_op jit(solution)/shard_map/ppermute | solution.py:127
  40.8 1.4 collective-permute-start.23
  42.2 4.2 %collective-permute-done.15 = bf16[4,128,256]{2,1,0:T(8,128)(2,1)S(1)} collective-permute-done((bf16[4,128,256]{2,1,0:T(8,128)(2,1)S(1)}, bf16[4,128,256]{2,1,0:T(8,128)(2,1)S(1)}, u32[]{:S(2)}, u32[]{:S(2)}) %collective-permute-start.15) | collective-permute-done | bytes 262176 | tf_op jit(solution)/shard_map/ppermute | solution.py:127
  46.4 1.4 collective-permute-start.16
  47.8 3.2 %collective-permute-done.4 = bf16[4,128,256]{2,1,0:T(8,128)(2,1)S(1)} collective-permute-done((bf16[4,128,256]{2,1,0:T(8,128)(2,1)S(1)}, bf16[4,128,256]{2,1,0:T(8,128)(2,1)S(1)}, u32[]{:S(2)}, u32[]{:S(2)}) %collective-permute-start.4) | collective-permute-done | bytes 262176 | tf_op jit(solution)/shard_map/ppermute | solution.py:127
  51.0 1.3 collective-permute-start.6
  52.3 1.2 collective-permute-start.5
  53.5 3.0 %collective-permute-start = (s32[2,4,16]{2,1,0:T(4,128)S(1)}, s32[2,4,16]{2,1,0:T(4,128)S(1)}, u32[]{:S(2)}, u32[]{:S(2)}) collective-permute-start(s32[2,4,16]{2,1,0:T(4,128)S(1)} %constant_dynamic-update-slice_fusion), channel_id=1, source_target_pairs={{0,1},{1,0},{2,3},{3,2},{4,5},{5,4},{6,7},{7,6},{8,9},{9,8},{10,11... | collective-permute-start | bytes 1544 | tf_op jit(solution)/shard_map/ppermute | solution.py:211
  58.7 1.3 collective-permute-start.24
  60.1 3.5 %collective-permute-start.49 = (bf16[64,128,128]{2,1,0:T(8,128)(2,1)S(1)}, bf16[64,128,128]{2,1,0:T(8,128)(2,1)}, u32[]{:S(2)}, u32[]{:S(2)}) collective-permute-start(bf16[64,128,128]{2,1,0:T(8,128)(2,1)S(1)} %bitcast.38), channel_id=1, source_target_pairs={{0,1},{1,0},{2,3},{3,2},{4,5},{5,4},{6,7},{7,6},{8,9},{9,8},{10,11... | collective-permute-start | bytes 6291464 | tf_op jit(solution)/shard_map/ppermute | solution.py:210
  64.3 1.2 collective-permute-start.7
  66.5 1.3 collective-permute-start.17
  67.9 1.6 collective-permute-done.7.refs_3_
  70.9 1.3 collective-permute-start.10
  72.2 1.1 collective-permute-start.32
  73.4 1.0 select_select_fusion.refs_15_
  75.6 4.8 %collective-permute-done.17 = bf16[4,128,256]{2,1,0:T(8,128)(2,1)} collective-permute-done((bf16[4,128,256]{2,1,0:T(8,128)(2,1)}, bf16[4,128,256]{2,1,0:T(8,128)(2,1)}, u32[]{:S(2)}, u32[]{:S(2)}) %collective-permute-start.17) | collective-permute-done | bytes 262176 | tf_op jit(solution)/shard_map/ppermute | solution.py:127
  80.4 0.9 collective-permute-start.44
  81.3 4.7 %collective-permute-done.10 = bf16[4,128,256]{2,1,0:T(8,128)(2,1)} collective-permute-done((bf16[4,128,256]{2,1,0:T(8,128)(2,1)}, bf16[4,128,256]{2,1,0:T(8,128)(2,1)}, u32[]{:S(2)}, u32[]{:S(2)}) %collective-permute-start.10) | collective-permute-done | bytes 262176 | tf_op jit(solution)/shard_map/ppermute | solution.py:127
  87.3 1.2 collective-permute-start.25
  88.5 1.1 select_select_fusion.2.refs_10_
  89.6 1.2 collective-permute-start.39
  91.1 1.0 broadcast_select_fusion.2.refs_5_
  92.1 1.3 collective-permute-done.26.refs_17_
  94.4 2.4 %collective-permute-start.34 = (bf16[4,128,256]{2,1,0:T(8,128)(2,1)S(1)}, bf16[4,128,256]{2,1,0:T(8,128)(2,1)S(1)}, u32[]{:S(2)}, u32[]{:S(2)}) collective-permute-start(bf16[4,128,256]{2,1,0:T(8,128)(2,1)S(1)} %broadcast_select_fusion.2.refs_5_), channel_id=1, source_target_pairs={{0,1},{1,0},{2,3},{3,2},{4,5},{5,4},{6,7},{7,6},{8,9},{9,8},{10,11... | collective-permute-start | bytes 786440 | tf_op jit(solution)/shard_map/ppermute | solution.py:222
  96.7 1.3 collective-permute-start.12
  98.0 1.2 collective-permute-done.19.refs_12_
  99.5 0.9 slice.59
  100.4 0.9 slice.58
  101.3 1.3 collective-permute-start.28
  102.9 2.2 %collective-permute-done.12.refs_7_ = bf16[4,128,256]{2,1,0:T(8,128)(2,1)S(1)} collective-permute-done((bf16[4,128,256]{2,1,0:T(8,128)(2,1)S(1)}, bf16[4,128,256]{2,1,0:T(8,128)(2,1)S(1)}, u32[]{:S(2)}, u32[]{:S(2)}) %collective-permute-start.12) | collective-permute-done | bytes 262176 | tf_op jit(solution)/shard_map/ppermute | solution.py:127
  106.8 1.5 collective-permute-done.28.refs_19_
  109.6 1.4 collective-permute-done.21.refs_14_
  111.0 4.5 %collective-permute-start.48 = (bf16[2,128,256]{2,1,0:T(8,128)(2,1)S(1)}, bf16[2,128,256]{2,1,0:T(8,128)(2,1)S(1)}, u32[]{:S(2)}, u32[]{:S(2)}) collective-permute-start(bf16[2,128,256]{2,1,0:T(8,128)(2,1)S(1)} %collective-permute-done.28.refs_19_), channel_id=1, source_target_pairs={{0,1},{1,0},{2,3},{3,2},{4,5},{5,4},{6,7},{7,6},{8,9},{9,8},{10,11... | collective-permute-start | bytes 393224 | tf_op jit(solution)/shard_map/ppermute | solution.py:222
  116.8 1.1 collective-permute-start.43
  125.5 1.0 collective-permute-done.40.refs_31_
  127.3 0.9 copy-done.3
  128.2 0.9 copy-done.5
  129.2 0.9 copy-done.7
  130.1 0.9 copy-done.9
  131.1 0.9 copy-done.11
  132.0 0.9 copy-done.13
  133.0 0.9 copy-done.15
  133.9 0.9 copy-done.17
  134.9 0.9 copy-done.19
  135.8 0.9 copy-done.20
  136.7 0.9 copy-done.22
  137.6 0.9 copy-done.24
  138.5 0.9 copy-done.26
  139.4 0.9 copy-done.28
  140.3 0.9 copy-done.30
  141.2 0.9 copy-done.32
  142.1 0.9 copy-done.34
  144.9 0.9 copy-done.40
  145.8 19.7 %shard_map.82 = bf16[32,128,256]{2,1,0:T(8,128)(2,1)} custom-call(s32[128]{0:T(128)S(1)} %sub.45.rows_ref, s32[128]{0:T(128)S(1)} %fusion.4.cols_ref, bf16[4,128,256]{2,1,0:T(8,128)(2,1)S(1)} %broadcast_select_fusion.3.refs_0_, bf16[4,128,256]{2,1,0:T(8,128)(2,1)S(1)} %copy-done.3, bf16[4,128,256]{2,1,0:T(8,128)(2,1)S(1)} %collective-permute-done.6.refs_2_, ...), custom_call_target="tpu_custom_call" | custom-call | flops 1073741824 | bytes 16777216 | tf_op jit(solution)/shard_map/pallas_call | solution.py:89
  (173 shorter events, 28.3 us)
Async XLA Ops:
  0.0 5.0 %copy-start = (s32[1,8192]{1,0:T(1,128)S(1)}, s32[1,8192]{1,0:T(1,128)}, u32[]{:S(2)}) copy-start(s32[1,8192]{1,0:T(1,128)} %param.9) | copy-start | bytes 98308
  9.9 21.7 %collective-permute-start.2 = (bf16[4,128,256]{2,1,0:T(8,128)(2,1)S(1)}, bf16[4,128,256]{2,1,0:T(8,128)(2,1)S(1)}, u32[]{:S(2)}, u32[]{:S(2)}) collective-permute-start(bf16[4,128,256]{2,1,0:T(8,128)(2,1)S(1)} %bitcast.41), channel_id=1, source_target_pairs={{0,4},{2,6},{4,0},{6,2},{8,12},{10,14},{12,8},{14,10},{16,20},{18,... | collective-permute-start | bytes 786440 | tf_op jit(solution)/shard_map/ppermute | solution.py:127
  16.9 14.6 %collective-permute-start.3 = (bf16[4,128,256]{2,1,0:T(8,128)(2,1)}, bf16[4,128,256]{2,1,0:T(8,128)(2,1)S(1)}, u32[]{:S(2)}, u32[]{:S(2)}) collective-permute-start(bf16[4,128,256]{2,1,0:T(8,128)(2,1)} %bitcast.18), channel_id=1, source_target_pairs={{0,6},{2,4},{4,2},{6,0},{8,14},{10,12},{12,10},{14,8},{16,22},{18,... | collective-permute-start | bytes 786440 | tf_op jit(solution)/shard_map/ppermute | solution.py:127
  18.1 34.2 %copy-start.46 = (s32[1,4,16]{2,1,0:T(4,128)S(1)}, s32[1,4,16]{2,1,0:T(4,128)}, u32[]{:S(2)}) copy-start(s32[1,4,16]{2,1,0:T(4,128)} %param.12) | copy-start | bytes 772
  18.1 35.4 %copy-start.47 = (s32[1,4,16]{2,1,0:T(4,128)S(1)}, s32[1,4,16]{2,1,0:T(4,128)}, u32[]{:S(2)}) copy-start(s32[1,4,16]{2,1,0:T(4,128)} %param.13) | copy-start | bytes 772
  18.1 41.9 %copy-start.1 = (bf16[1,4,16,128,128]{4,3,2,1,0:T(8,128)(2,1)S(1)}, bf16[1,4,16,128,128]{4,3,2,1,0:T(8,128)(2,1)}, u32[]{:S(2)}) copy-start(bf16[1,4,16,128,128]{4,3,2,1,0:T(8,128)(2,1)} %param.14) | copy-start | bytes 6291460
  23.2 8.4 %collective-permute-start.1 = (bf16[4,128,256]{2,1,0:T(8,128)(2,1)}, bf16[4,128,256]{2,1,0:T(8,128)(2,1)S(1)}, u32[]{:S(2)}, u32[]{:S(2)}) collective-permute-start(bf16[4,128,256]{2,1,0:T(8,128)(2,1)} %bitcast.12), channel_id=1, source_target_pairs={{0,2},{2,0},{4,6},{6,4},{8,10},{10,8},{12,14},{14,12},{16,18},{18,... | collective-permute-start | bytes 786440 | tf_op jit(solution)/shard_map/ppermute | solution.py:127
  34.1 6.6 %collective-permute-start.22 = (bf16[4,128,256]{2,1,0:T(8,128)(2,1)S(1)}, bf16[4,128,256]{2,1,0:T(8,128)(2,1)S(1)}, u32[]{:S(2)}, u32[]{:S(2)}) collective-permute-start(bf16[4,128,256]{2,1,0:T(8,128)(2,1)S(1)} %get-tuple-element.8), channel_id=1, source_target_pairs={{0,8},{2,10},{4,12},{6,14},{8,0},{10,2},{12,4},{14,6},{16,24},{18,... | collective-permute-start | bytes 786440 | tf_op jit(solution)/shard_map/ppermute | solution.py:127
  35.7 10.7 %collective-permute-start.15 = (bf16[4,128,256]{2,1,0:T(8,128)(2,1)S(1)}, bf16[4,128,256]{2,1,0:T(8,128)(2,1)S(1)}, u32[]{:S(2)}, u32[]{:S(2)}) collective-permute-start(bf16[4,128,256]{2,1,0:T(8,128)(2,1)S(1)} %get-tuple-element.9), channel_id=1, source_target_pairs={{0,8},{2,10},{4,12},{6,14},{8,0},{10,2},{12,4},{14,6},{16,24},{18,... | collective-permute-start | bytes 786440 | tf_op jit(solution)/shard_map/ppermute | solution.py:127
  37.1 13.9 %collective-permute-start.4 = (bf16[4,128,256]{2,1,0:T(8,128)(2,1)S(1)}, bf16[4,128,256]{2,1,0:T(8,128)(2,1)S(1)}, u32[]{:S(2)}, u32[]{:S(2)}) collective-permute-start(bf16[4,128,256]{2,1,0:T(8,128)(2,1)S(1)} %get-tuple-element.10), channel_id=1, source_target_pairs={{0,8},{2,10},{4,12},{6,14},{24,16},{26,18},{28,20},{30,22},{1,9},{... | collective-permute-start | bytes 786440 | tf_op jit(solution)/shard_map/ppermute | solution.py:127
  40.8 25.0 %copy-start.42 = (bf16[4,128,256]{2,1,0:T(8,128)(2,1)}, bf16[4,128,256]{2,1,0:T(8,128)(2,1)S(1)}, u32[]{:S(2)}) copy-start(bf16[4,128,256]{2,1,0:T(8,128)(2,1)S(1)} %broadcast_select_fusion) | copy-start | bytes 786436
  40.8 17.6 %collective-permute-start.23 = (bf16[4,128,256]{2,1,0:T(8,128)(2,1)S(1)}, bf16[4,128,256]{2,1,0:T(8,128)(2,1)}, u32[]{:S(2)}, u32[]{:S(2)}) collective-permute-start(bf16[4,128,256]{2,1,0:T(8,128)(2,1)S(1)} %broadcast_select_fusion), channel_id=1, source_target_pairs={{8,16},{10,18},{12,20},{14,22},{16,8},{18,10},{20,12},{22,14},{9,1... | collective-permute-start | bytes 786440 | tf_op jit(solution)/shard_map/ppermute | solution.py:127
  46.4 19.4 %copy-start.41 = (bf16[4,128,256]{2,1,0:T(8,128)(2,1)}, bf16[4,128,256]{2,1,0:T(8,128)(2,1)S(1)}, u32[]{:S(2)}) copy-start(bf16[4,128,256]{2,1,0:T(8,128)(2,1)S(1)} %broadcast_select_fusion.1) | copy-start | bytes 786436
  46.4 12.3 %collective-permute-start.16 = (bf16[4,128,256]{2,1,0:T(8,128)(2,1)S(1)}, bf16[4,128,256]{2,1,0:T(8,128)(2,1)}, u32[]{:S(2)}, u32[]{:S(2)}) collective-permute-start(bf16[4,128,256]{2,1,0:T(8,128)(2,1)S(1)} %broadcast_select_fusion.1), channel_id=1, source_target_pairs={{8,16},{10,18},{12,20},{14,22},{16,8},{18,10},{20,12},{22,14},{9,1... | collective-permute-start | bytes 786440 | tf_op jit(solution)/shard_map/ppermute | solution.py:127
  51.0 6.7 %collective-permute-start.6 = (bf16[4,128,256]{2,1,0:T(8,128)(2,1)S(1)}, bf16[4,128,256]{2,1,0:T(8,128)(2,1)S(1)}, u32[]{:S(2)}, u32[]{:S(2)}) collective-permute-start(bf16[4,128,256]{2,1,0:T(8,128)(2,1)S(1)} %broadcast_select_fusion.3.refs_0_), channel_id=1, source_target_pairs={{0,4},{2,6},{4,0},{6,2},{8,12},{10,14},{12,8},{14,10},{16,20},{18,... | collective-permute-start | bytes 786440 | tf_op jit(solution)/shard_map/ppermute | solution.py:127
  52.3 7.7 %collective-permute-start.5 = (bf16[4,128,256]{2,1,0:T(8,128)(2,1)S(1)}, bf16[4,128,256]{2,1,0:T(8,128)(2,1)S(1)}, u32[]{:S(2)}, u32[]{:S(2)}) collective-permute-start(bf16[4,128,256]{2,1,0:T(8,128)(2,1)S(1)} %broadcast_select_fusion.3.refs_0_), channel_id=1, source_target_pairs={{0,2},{2,0},{4,6},{6,4},{8,10},{10,8},{12,14},{14,12},{16,18},{18,... | collective-permute-start | bytes 786440 | tf_op jit(solution)/shard_map/ppermute | solution.py:127
  53.5 3.8 %collective-permute-start = (s32[2,4,16]{2,1,0:T(4,128)S(1)}, s32[2,4,16]{2,1,0:T(4,128)S(1)}, u32[]{:S(2)}, u32[]{:S(2)}) collective-permute-start(s32[2,4,16]{2,1,0:T(4,128)S(1)} %constant_dynamic-update-slice_fusion), channel_id=1, source_target_pairs={{0,1},{1,0},{2,3},{3,2},{4,5},{5,4},{6,7},{7,6},{8,9},{9,8},{10,11... | collective-permute-start | bytes 1544 | tf_op jit(solution)/shard_map/ppermute | solution.py:211
  57.4 6.2 %collective-permute-start.29 = (bf16[4,128,256]{2,1,0:T(8,128)(2,1)S(1)}, bf16[4,128,256]{2,1,0:T(8,128)(2,1)S(1)}, u32[]{:S(2)}, u32[]{:S(2)}) collective-permute-start(bf16[4,128,256]{2,1,0:T(8,128)(2,1)S(1)} %broadcast_select_fusion.3.refs_0_), channel_id=1, source_target_pairs={{0,1},{1,0},{2,3},{3,2},{4,5},{5,4},{6,7},{7,6},{8,9},{9,8},{10,11... | collective-permute-start | bytes 786440 | tf_op jit(solution)/shard_map/ppermute | solution.py:222
  57.7 8.1 %collective-permute-start.9 = (bf16[4,128,256]{2,1,0:T(8,128)(2,1)S(1)}, bf16[4,128,256]{2,1,0:T(8,128)(2,1)S(1)}, u32[]{:S(2)}, u32[]{:S(2)}) collective-permute-start(bf16[4,128,256]{2,1,0:T(8,128)(2,1)S(1)} %broadcast_select_fusion.3.refs_0_), channel_id=1, source_target_pairs={{8,16},{10,18},{12,20},{14,22},{16,8},{18,10},{20,12},{22,14},{9,1... | collective-permute-start | bytes 786440 | tf_op jit(solution)/shard_map/ppermute | solution.py:127
  58.4 7.1 %collective-permute-start.8 = (bf16[2,128,256]{2,1,0:T(8,128)(2,1)S(1)}, bf16[2,128,256]{2,1,0:T(8,128)(2,1)}, u32[]{:S(2)}, u32[]{:S(2)}) collective-permute-start(bf16[2,128,256]{2,1,0:T(8,128)(2,1)S(1)} %slice.53), channel_id=1, source_target_pairs={{0,2},{2,0},{4,6},{6,4},{8,10},{10,8},{12,14},{14,12},{16,18},{18,... | collective-permute-start | bytes 393224 | tf_op jit(solution)/shard_map/ppermute | solution.py:127
  58.7 13.5 %collective-permute-start.24 = (bf16[4,128,256]{2,1,0:T(8,128)(2,1)}, bf16[4,128,256]{2,1,0:T(8,128)(2,1)}, u32[]{:S(2)}, u32[]{:S(2)}) collective-permute-start(bf16[4,128,256]{2,1,0:T(8,128)(2,1)} %collective-permute-done.23), channel_id=1, source_target_pairs={{8,0},{10,2},{12,4},{14,6},{16,24},{18,26},{20,28},{22,30},{9,1},{... | collective-permute-start | bytes 786440 | tf_op jit(solution)/shard_map/ppermute | solution.py:127
  60.0 30.8 %copy-start.2 = (bf16[4,128,256]{2,1,0:T(8,128)(2,1)}, bf16[4,128,256]{2,1,0:T(8,128)(2,1)S(1)}, u32[]{:S(2)}) copy-start(bf16[4,128,256]{2,1,0:T(8,128)(2,1)S(1)} %collective-permute-done.5.refs_1_) | copy-start | bytes 786436
  60.1 67.2 %collective-permute-start.49 = (bf16[64,128,128]{2,1,0:T(8,128)(2,1)S(1)}, bf16[64,128,128]{2,1,0:T(8,128)(2,1)}, u32[]{:S(2)}, u32[]{:S(2)}) collective-permute-start(bf16[64,128,128]{2,1,0:T(8,128)(2,1)S(1)} %bitcast.38), channel_id=1, source_target_pairs={{0,1},{1,0},{2,3},{3,2},{4,5},{5,4},{6,7},{7,6},{8,9},{9,8},{10,11... | collective-permute-start | bytes 6291464 | tf_op jit(solution)/shard_map/ppermute | solution.py:210
  64.3 5.2 %collective-permute-start.7 = (bf16[2,128,256]{2,1,0:T(8,128)(2,1)S(1)}, bf16[2,128,256]{2,1,0:T(8,128)(2,1)}, u32[]{:S(2)}, u32[]{:S(2)}) collective-permute-start(bf16[2,128,256]{2,1,0:T(8,128)(2,1)S(1)} %slice.52), channel_id=1, source_target_pairs={{0,4},{2,6},{4,0},{6,2},{8,12},{10,14},{12,8},{14,10},{16,20},{18,... | collective-permute-start | bytes 393224 | tf_op jit(solution)/shard_map/ppermute | solution.py:127
  65.5 4.8 %collective-permute-start.33 = (bf16[2,128,256]{2,1,0:T(8,128)(2,1)}, bf16[2,128,256]{2,1,0:T(8,128)(2,1)S(1)}, u32[]{:S(2)}, u32[]{:S(2)}) collective-permute-start(bf16[2,128,256]{2,1,0:T(8,128)(2,1)} %collective-permute-done.8.refs_4_), channel_id=1, source_target_pairs={{0,1},{1,0},{2,3},{3,2},{4,5},{5,4},{6,7},{7,6},{8,9},{9,8},{10,11... | collective-permute-start | bytes 393224 | tf_op jit(solution)/shard_map/ppermute | solution.py:222
  66.5 13.9 %collective-permute-start.17 = (bf16[4,128,256]{2,1,0:T(8,128)(2,1)}, bf16[4,128,256]{2,1,0:T(8,128)(2,1)}, u32[]{:S(2)}, u32[]{:S(2)}) collective-permute-start(bf16[4,128,256]{2,1,0:T(8,128)(2,1)} %collective-permute-done.16), channel_id=1, source_target_pairs={{8,0},{10,2},{12,4},{14,6},{16,24},{18,26},{20,28},{22,30},{9,1},{... | collective-permute-start | bytes 786440 | tf_op jit(solution)/shard_map/ppermute | solution.py:127
  69.5 17.1 %collective-permute-start.31 = (bf16[4,128,256]{2,1,0:T(8,128)(2,1)S(1)}, bf16[4,128,256]{2,1,0:T(8,128)(2,1)S(1)}, u32[]{:S(2)}, u32[]{:S(2)}) collective-permute-start(bf16[4,128,256]{2,1,0:T(8,128)(2,1)S(1)} %collective-permute-done.6.refs_2_), channel_id=1, source_target_pairs={{0,1},{1,0},{2,3},{3,2},{4,5},{5,4},{6,7},{7,6},{8,9},{9,8},{10,11... | collective-permute-start | bytes 786440 | tf_op jit(solution)/shard_map/ppermute | solution.py:222
  70.9 15.1 %collective-permute-start.10 = (bf16[4,128,256]{2,1,0:T(8,128)(2,1)}, bf16[4,128,256]{2,1,0:T(8,128)(2,1)}, u32[]{:S(2)}, u32[]{:S(2)}) collective-permute-start(bf16[4,128,256]{2,1,0:T(8,128)(2,1)} %copy-done.43), channel_id=1, source_target_pairs={{8,0},{10,2},{12,4},{14,6},{16,24},{18,26},{20,28},{22,30},{9,1},{... | collective-permute-start | bytes 786440 | tf_op jit(solution)/shard_map/ppermute | solution.py:127
  72.2 2.3 %collective-permute-start.32 = (bf16[2,128,256]{2,1,0:T(8,128)(2,1)}, bf16[2,128,256]{2,1,0:T(8,128)(2,1)S(1)}, u32[]{:S(2)}, u32[]{:S(2)}) collective-permute-start(bf16[2,128,256]{2,1,0:T(8,128)(2,1)} %collective-permute-done.7.refs_3_), channel_id=1, source_target_pairs={{0,1},{1,0},{2,3},{3,2},{4,5},{5,4},{6,7},{7,6},{8,9},{9,8},{10,11... | collective-permute-start | bytes 393224 | tf_op jit(solution)/shard_map/ppermute | solution.py:222
  75.2 14.4 %collective-permute-start.30 = (bf16[4,128,256]{2,1,0:T(8,128)(2,1)S(1)}, bf16[4,128,256]{2,1,0:T(8,128)(2,1)}, u32[]{:S(2)}, u32[]{:S(2)}) collective-permute-start(bf16[4,128,256]{2,1,0:T(8,128)(2,1)S(1)} %collective-permute-done.5.refs_1_), channel_id=1, source_target_pairs={{0,1},{1,0},{2,3},{3,2},{4,5},{5,4},{6,7},{7,6},{8,9},{9,8},{10,11... | collective-permute-start | bytes 786440 | tf_op jit(solution)/shard_map/ppermute | solution.py:222
  80.4 10.4 %collective-permute-start.44 = (bf16[4,128,256]{2,1,0:T(8,128)(2,1)S(1)}, bf16[4,128,256]{2,1,0:T(8,128)(2,1)}, u32[]{:S(2)}, u32[]{:S(2)}) collective-permute-start(bf16[4,128,256]{2,1,0:T(8,128)(2,1)S(1)} %select_select_fusion.refs_15_), channel_id=1, source_target_pairs={{0,1},{1,0},{2,3},{3,2},{4,5},{5,4},{6,7},{7,6},{8,9},{9,8},{10,11... | collective-permute-start | bytes 786440 | tf_op jit(solution)/shard_map/ppermute | solution.py:222
  86.0 7.3 %collective-permute-start.26 = (bf16[4,128,256]{2,1,0:T(8,128)(2,1)S(1)}, bf16[4,128,256]{2,1,0:T(8,128)(2,1)}, u32[]{:S(2)}, u32[]{:S(2)}) collective-permute-start(bf16[4,128,256]{2,1,0:T(8,128)(2,1)S(1)} %select_select_fusion.refs_15_), channel_id=1, source_target_pairs={{0,4},{2,6},{4,0},{6,2},{8,12},{10,14},{12,8},{14,10},{16,20},{18,... | collective-permute-start | bytes 786440 | tf_op jit(solution)/shard_map/ppermute | solution.py:127
  87.3 7.1 %collective-permute-start.25 = (bf16[4,128,256]{2,1,0:T(8,128)(2,1)S(1)}, bf16[4,128,256]{2,1,0:T(8,128)(2,1)}, u32[]{:S(2)}, u32[]{:S(2)}) collective-permute-start(bf16[4,128,256]{2,1,0:T(8,128)(2,1)S(1)} %select_select_fusion.refs_15_), channel_id=1, source_target_pairs={{0,2},{2,0},{4,6},{6,4},{8,10},{10,8},{12,14},{14,12},{16,18},{18,... | collective-permute-start | bytes 786440 | tf_op jit(solution)/shard_map/ppermute | solution.py:127
  89.6 7.1 %collective-permute-start.39 = (bf16[4,128,256]{2,1,0:T(8,128)(2,1)S(1)}, bf16[4,128,256]{2,1,0:T(8,128)(2,1)S(1)}, u32[]{:S(2)}, u32[]{:S(2)}) collective-permute-start(bf16[4,128,256]{2,1,0:T(8,128)(2,1)S(1)} %select_select_fusion.2.refs_10_), channel_id=1, source_target_pairs={{0,1},{1,0},{2,3},{3,2},{4,5},{5,4},{6,7},{7,6},{8,9},{9,8},{10,11... | collective-permute-start | bytes 786440 | tf_op jit(solution)/shard_map/ppermute | solution.py:222
  90.8 8.4 %collective-permute-start.19 = (bf16[4,128,256]{2,1,0:T(8,128)(2,1)S(1)}, bf16[4,128,256]{2,1,0:T(8,128)(2,1)S(1)}, u32[]{:S(2)}, u32[]{:S(2)}) collective-permute-start(bf16[4,128,256]{2,1,0:T(8,128)(2,1)S(1)} %select_select_fusion.2.refs_10_), channel_id=1, source_target_pairs={{0,4},{2,6},{4,0},{6,2},{8,12},{10,14},{12,8},{14,10},{16,20},{18,... | collective-permute-start | bytes 786440 | tf_op jit(solution)/shard_map/ppermute | solution.py:127
  93.3 8.0 %collective-permute-start.18 = (bf16[4,128,256]{2,1,0:T(8,128)(2,1)S(1)}, bf16[4,128,256]{2,1,0:T(8,128)(2,1)S(1)}, u32[]{:S(2)}, u32[]{:S(2)}) collective-permute-start(bf16[4,128,256]{2,1,0:T(8,128)(2,1)S(1)} %select_select_fusion.2.refs_10_), channel_id=1, source_target_pairs={{0,2},{2,0},{4,6},{6,4},{8,10},{10,8},{12,14},{14,12},{16,18},{18,... | collective-permute-start | bytes 786440 | tf_op jit(solution)/shard_map/ppermute | solution.py:127
  94.4 8.2 %collective-permute-start.34 = (bf16[4,128,256]{2,1,0:T(8,128)(2,1)S(1)}, bf16[4,128,256]{2,1,0:T(8,128)(2,1)S(1)}, u32[]{:S(2)}, u32[]{:S(2)}) collective-permute-start(bf16[4,128,256]{2,1,0:T(8,128)(2,1)S(1)} %broadcast_select_fusion.2.refs_5_), channel_id=1, source_target_pairs={{0,1},{1,0},{2,3},{3,2},{4,5},{5,4},{6,7},{7,6},{8,9},{9,8},{10,11... | collective-permute-start | bytes 786440 | tf_op jit(solution)/shard_map/ppermute | solution.py:222
  96.7 11.5 %copy-start.16 = (bf16[4,128,256]{2,1,0:T(8,128)(2,1)}, bf16[4,128,256]{2,1,0:T(8,128)(2,1)S(1)}, u32[]{:S(2)}) copy-start(bf16[4,128,256]{2,1,0:T(8,128)(2,1)S(1)} %collective-permute-done.39.refs_30_) | copy-start | bytes 786436
  96.7 8.4 %collective-permute-start.12 = (bf16[4,128,256]{2,1,0:T(8,128)(2,1)S(1)}, bf16[4,128,256]{2,1,0:T(8,128)(2,1)S(1)}, u32[]{:S(2)}, u32[]{:S(2)}) collective-permute-start(bf16[4,128,256]{2,1,0:T(8,128)(2,1)S(1)} %broadcast_select_fusion.2.refs_5_), channel_id=1, source_target_pairs={{0,4},{2,6},{4,0},{6,2},{8,12},{10,14},{12,8},{14,10},{16,20},{18,... | collective-permute-start | bytes 786440 | tf_op jit(solution)/shard_map/ppermute | solution.py:127
  99.2 6.7 %copy-start.4 = (bf16[4,128,256]{2,1,0:T(8,128)(2,1)}, bf16[4,128,256]{2,1,0:T(8,128)(2,1)S(1)}, u32[]{:S(2)}) copy-start(bf16[4,128,256]{2,1,0:T(8,128)(2,1)S(1)} %collective-permute-done.19.refs_12_) | copy-start | bytes 786436
  99.2 6.7 %collective-permute-start.11 = (bf16[4,128,256]{2,1,0:T(8,128)(2,1)S(1)}, bf16[4,128,256]{2,1,0:T(8,128)(2,1)S(1)}, u32[]{:S(2)}, u32[]{:S(2)}) collective-permute-start(bf16[4,128,256]{2,1,0:T(8,128)(2,1)S(1)} %broadcast_select_fusion.2.refs_5_), channel_id=1, source_target_pairs={{0,2},{2,0},{4,6},{6,4},{8,10},{10,8},{12,14},{14,12},{16,18},{18,... | collective-permute-start | bytes 786440 | tf_op jit(solution)/shard_map/ppermute | solution.py:127
  101.3 5.4 %copy-start.6 = (bf16[4,128,256]{2,1,0:T(8,128)(2,1)}, bf16[4,128,256]{2,1,0:T(8,128)(2,1)S(1)}, u32[]{:S(2)}) copy-start(bf16[4,128,256]{2,1,0:T(8,128)(2,1)S(1)} %collective-permute-done.18.refs_11_) | copy-start | bytes 786436
  101.3 6.9 %collective-permute-start.28 = (bf16[2,128,256]{2,1,0:T(8,128)(2,1)S(1)}, bf16[2,128,256]{2,1,0:T(8,128)(2,1)S(1)}, u32[]{:S(2)}, u32[]{:S(2)}) collective-permute-start(bf16[2,128,256]{2,1,0:T(8,128)(2,1)S(1)} %slice.59), channel_id=1, source_target_pairs={{0,2},{2,0},{4,6},{6,4},{8,10},{10,8},{12,14},{14,12},{16,18},{18,... | collective-permute-start | bytes 393224 | tf_op jit(solution)/shard_map/ppermute | solution.py:127
  102.6 6.4 %copy-start.18 = (bf16[4,128,256]{2,1,0:T(8,128)(2,1)}, bf16[4,128,256]{2,1,0:T(8,128)(2,1)S(1)}, u32[]{:S(2)}) copy-start(bf16[4,128,256]{2,1,0:T(8,128)(2,1)S(1)} %collective-permute-done.34.refs_25_) | copy-start | bytes 786436
  102.6 6.4 %collective-permute-start.27 = (bf16[2,128,256]{2,1,0:T(8,128)(2,1)S(1)}, bf16[2,128,256]{2,1,0:T(8,128)(2,1)S(1)}, u32[]{:S(2)}, u32[]{:S(2)}) collective-permute-start(bf16[2,128,256]{2,1,0:T(8,128)(2,1)S(1)} %slice.58), channel_id=1, source_target_pairs={{0,4},{2,6},{4,0},{6,2},{8,12},{10,14},{12,8},{14,10},{16,20},{18,... | collective-permute-start | bytes 393224 | tf_op jit(solution)/shard_map/ppermute | solution.py:127
  105.1 1.6 copy-start.8
  105.1 5.9 %collective-permute-start.21 = (bf16[2,128,256]{2,1,0:T(8,128)(2,1)S(1)}, bf16[2,128,256]{2,1,0:T(8,128)(2,1)S(1)}, u32[]{:S(2)}, u32[]{:S(2)}) collective-permute-start(bf16[2,128,256]{2,1,0:T(8,128)(2,1)S(1)} %slice.57), channel_id=1, source_target_pairs={{0,2},{2,0},{4,6},{6,4},{8,10},{10,8},{12,14},{14,12},{16,18},{18,... | collective-permute-start | bytes 393224 | tf_op jit(solution)/shard_map/ppermute | solution.py:127
  105.9 10.3 %collective-permute-start.20 = (bf16[2,128,256]{2,1,0:T(8,128)(2,1)S(1)}, bf16[2,128,256]{2,1,0:T(8,128)(2,1)S(1)}, u32[]{:S(2)}, u32[]{:S(2)}) collective-permute-start(bf16[2,128,256]{2,1,0:T(8,128)(2,1)S(1)} %slice.56), channel_id=1, source_target_pairs={{0,4},{2,6},{4,0},{6,2},{8,12},{10,14},{12,8},{14,10},{16,20},{18,... | collective-permute-start | bytes 393224 | tf_op jit(solution)/shard_map/ppermute | solution.py:127
  108.2 8.6 %collective-permute-start.14 = (bf16[2,128,256]{2,1,0:T(8,128)(2,1)S(1)}, bf16[2,128,256]{2,1,0:T(8,128)(2,1)}, u32[]{:S(2)}, u32[]{:S(2)}) collective-permute-start(bf16[2,128,256]{2,1,0:T(8,128)(2,1)S(1)} %slice.55), channel_id=1, source_target_pairs={{0,2},{2,0},{4,6},{6,4},{8,10},{10,8},{12,14},{14,12},{16,18},{18,... | collective-permute-start | bytes 393224 | tf_op jit(solution)/shard_map/ppermute | solution.py:127
  109.0 9.6 %collective-permute-start.13 = (bf16[2,128,256]{2,1,0:T(8,128)(2,1)S(1)}, bf16[2,128,256]{2,1,0:T(8,128)(2,1)}, u32[]{:S(2)}, u32[]{:S(2)}) collective-permute-start(bf16[2,128,256]{2,1,0:T(8,128)(2,1)S(1)} %slice.54), channel_id=1, source_target_pairs={{0,4},{2,6},{4,0},{6,2},{8,12},{10,14},{12,8},{14,10},{16,20},{18,... | collective-permute-start | bytes 393224 | tf_op jit(solution)/shard_map/ppermute | solution.py:127
  111.0 8.2 %collective-permute-start.48 = (bf16[2,128,256]{2,1,0:T(8,128)(2,1)S(1)}, bf16[2,128,256]{2,1,0:T(8,128)(2,1)S(1)}, u32[]{:S(2)}, u32[]{:S(2)}) collective-permute-start(bf16[2,128,256]{2,1,0:T(8,128)(2,1)S(1)} %collective-permute-done.28.refs_19_), channel_id=1, source_target_pairs={{0,1},{1,0},{2,3},{3,2},{4,5},{5,4},{6,7},{7,6},{8,9},{9,8},{10,11... | collective-permute-start | bytes 393224 | tf_op jit(solution)/shard_map/ppermute | solution.py:222
  116.2 4.3 %collective-permute-start.47 = (bf16[2,128,256]{2,1,0:T(8,128)(2,1)S(1)}, bf16[2,128,256]{2,1,0:T(8,128)(2,1)S(1)}, u32[]{:S(2)}, u32[]{:S(2)}) collective-permute-start(bf16[2,128,256]{2,1,0:T(8,128)(2,1)S(1)} %collective-permute-done.27.refs_18_), channel_id=1, source_target_pairs={{0,1},{1,0},{2,3},{3,2},{4,5},{5,4},{6,7},{7,6},{8,9},{9,8},{10,11... | collective-permute-start | bytes 393224 | tf_op jit(solution)/shard_map/ppermute | solution.py:222
  116.8 4.3 %collective-permute-start.43 = (bf16[2,128,256]{2,1,0:T(8,128)(2,1)S(1)}, bf16[2,128,256]{2,1,0:T(8,128)(2,1)S(1)}, u32[]{:S(2)}, u32[]{:S(2)}) collective-permute-start(bf16[2,128,256]{2,1,0:T(8,128)(2,1)S(1)} %collective-permute-done.21.refs_14_), channel_id=1, source_target_pairs={{0,1},{1,0},{2,3},{3,2},{4,5},{5,4},{6,7},{7,6},{8,9},{9,8},{10,11... | collective-permute-start | bytes 393224 | tf_op jit(solution)/shard_map/ppermute | solution.py:222
  118.6 3.6 %collective-permute-start.42 = (bf16[2,128,256]{2,1,0:T(8,128)(2,1)S(1)}, bf16[2,128,256]{2,1,0:T(8,128)(2,1)S(1)}, u32[]{:S(2)}, u32[]{:S(2)}) collective-permute-start(bf16[2,128,256]{2,1,0:T(8,128)(2,1)S(1)} %collective-permute-done.20.refs_13_), channel_id=1, source_target_pairs={{0,1},{1,0},{2,3},{3,2},{4,5},{5,4},{6,7},{7,6},{8,9},{9,8},{10,11... | collective-permute-start | bytes 393224 | tf_op jit(solution)/shard_map/ppermute | solution.py:222
  119.9 4.8 %collective-permute-start.46 = (bf16[4,128,256]{2,1,0:T(8,128)(2,1)}, bf16[4,128,256]{2,1,0:T(8,128)(2,1)}, u32[]{:S(2)}, u32[]{:S(2)}) collective-permute-start(bf16[4,128,256]{2,1,0:T(8,128)(2,1)} %collective-permute-done.26.refs_17_), channel_id=1, source_target_pairs={{0,1},{1,0},{2,3},{3,2},{4,5},{5,4},{6,7},{7,6},{8,9},{9,8},{10,11... | collective-permute-start | bytes 786440 | tf_op jit(solution)/shard_map/ppermute | solution.py:222
  121.1 4.0 %collective-permute-start.45 = (bf16[4,128,256]{2,1,0:T(8,128)(2,1)}, bf16[4,128,256]{2,1,0:T(8,128)(2,1)}, u32[]{:S(2)}, u32[]{:S(2)}) collective-permute-start(bf16[4,128,256]{2,1,0:T(8,128)(2,1)} %collective-permute-done.25.refs_16_), channel_id=1, source_target_pairs={{0,1},{1,0},{2,3},{3,2},{4,5},{5,4},{6,7},{7,6},{8,9},{9,8},{10,11... | collective-permute-start | bytes 786440 | tf_op jit(solution)/shard_map/ppermute | solution.py:222
  121.8 1.8 %collective-permute-start.38 = (bf16[2,128,256]{2,1,0:T(8,128)(2,1)}, bf16[2,128,256]{2,1,0:T(8,128)(2,1)}, u32[]{:S(2)}, u32[]{:S(2)}) collective-permute-start(bf16[2,128,256]{2,1,0:T(8,128)(2,1)} %collective-permute-done.14.refs_9_), channel_id=1, source_target_pairs={{0,1},{1,0},{2,3},{3,2},{4,5},{5,4},{6,7},{7,6},{8,9},{9,8},{10,11... | collective-permute-start | bytes 393224 | tf_op jit(solution)/shard_map/ppermute | solution.py:222
  122.9 1.7 %collective-permute-start.37 = (bf16[2,128,256]{2,1,0:T(8,128)(2,1)}, bf16[2,128,256]{2,1,0:T(8,128)(2,1)}, u32[]{:S(2)}, u32[]{:S(2)}) collective-permute-start(bf16[2,128,256]{2,1,0:T(8,128)(2,1)} %collective-permute-done.13.refs_8_), channel_id=1, source_target_pairs={{0,1},{1,0},{2,3},{3,2},{4,5},{5,4},{6,7},{7,6},{8,9},{9,8},{10,11... | collective-permute-start | bytes 393224 | tf_op jit(solution)/shard_map/ppermute | solution.py:222
  123.6 1.9 %collective-permute-start.41 = (bf16[4,128,256]{2,1,0:T(8,128)(2,1)}, bf16[4,128,256]{2,1,0:T(8,128)(2,1)}, u32[]{:S(2)}, u32[]{:S(2)}) collective-permute-start(bf16[4,128,256]{2,1,0:T(8,128)(2,1)} %copy-done.4), channel_id=1, source_target_pairs={{0,1},{1,0},{2,3},{3,2},{4,5},{5,4},{6,7},{7,6},{8,9},{9,8},{10,11... | collective-permute-start | bytes 786440 | tf_op jit(solution)/shard_map/ppermute | solution.py:222
  124.6 1.9 %collective-permute-start.40 = (bf16[4,128,256]{2,1,0:T(8,128)(2,1)}, bf16[4,128,256]{2,1,0:T(8,128)(2,1)}, u32[]{:S(2)}, u32[]{:S(2)}) collective-permute-start(bf16[4,128,256]{2,1,0:T(8,128)(2,1)} %copy-done.6), channel_id=1, source_target_pairs={{0,1},{1,0},{2,3},{3,2},{4,5},{5,4},{6,7},{7,6},{8,9},{9,8},{10,11... | collective-permute-start | bytes 786440 | tf_op jit(solution)/shard_map/ppermute | solution.py:222
  124.8 2.1 %collective-permute-start.36 = (bf16[4,128,256]{2,1,0:T(8,128)(2,1)}, bf16[4,128,256]{2,1,0:T(8,128)(2,1)}, u32[]{:S(2)}, u32[]{:S(2)}) collective-permute-start(bf16[4,128,256]{2,1,0:T(8,128)(2,1)} %copy-done.8), channel_id=1, source_target_pairs={{0,1},{1,0},{2,3},{3,2},{4,5},{5,4},{6,7},{7,6},{8,9},{9,8},{10,11... | collective-permute-start | bytes 786440 | tf_op jit(solution)/shard_map/ppermute | solution.py:222
  125.1 2.1 %collective-permute-start.35 = (bf16[4,128,256]{2,1,0:T(8,128)(2,1)}, bf16[4,128,256]{2,1,0:T(8,128)(2,1)}, u32[]{:S(2)}, u32[]{:S(2)}) collective-permute-start(bf16[4,128,256]{2,1,0:T(8,128)(2,1)} %copy-done.10), channel_id=1, source_target_pairs={{0,1},{1,0},{2,3},{3,2},{4,5},{5,4},{6,7},{7,6},{8,9},{9,8},{10,11... | collective-permute-start | bytes 786440 | tf_op jit(solution)/shard_map/ppermute | solution.py:222
  127.2 1.0 copy-start.3
  128.2 0.9 copy-start.5
  (34 other events, 27.5 us)

commit v3 on v2

--- a/solution.py
+++ b/solution.py
@@ -103,7 +103,7 @@
             pltpu.SemaphoreType.DMA((len(tile_list),)),
             pltpu.SemaphoreType.DMA((2,)),
         ],
-        compiler_params=pltpu.CompilerParams(vmem_limit_bytes=40 * 1024 * 1024),
+        compiler_params=pltpu.CompilerParams(vmem_limit_bytes=60 * 1024 * 1024),
         cost_estimate=pl.CostEstimate(
             flops=2 * n_tiles * tile_len * tile_len * width, bytes_accessed=16 << 20, transcendentals=0
         ),
@@ -131,17 +131,32 @@
     return [(i, i ^ bits) for i in range(16)]
 
 
+def cross(value, turn):
+    pairs = []
+    for i in range(16):
+        for core in (0, 1):
+            pairs.append((2 * i + core, 2 * (i ^ (1 if core == turn else 2)) + core))
+    return lax.ppermute(value, ("dom", "rep"), pairs)
+
+
+def place_of(across, core):
+    return jnp.where(core == 0, across, (across & 1) * 2 + across // 2)
+
+
 def quad_scatter(features, lines):
-    quad = lax.axis_index("dom") % 4
+    quad, rep = lax.axis_index("dom") % 4, lax.axis_index("rep")
+    first, second = 1 + rep, 2 - rep
     each = lines.shape[0] // 4
-    held = [None] * 4
-    for e in (3, 1, 2, 0):
-        own = lax.dynamic_slice_in_dim(lines, (quad ^ e) * each, each)
-        rows = features.at[own.reshape(-1)].get(mode="promise_in_bounds")
-        held[e] = rows.reshape(each, lines.shape[1], features.shape[1])
-        if e:
-            held[e] = move(held[e], flip(e))
-    return held
+
+    def rows(*across):
+        own = [lax.dynamic_slice_in_dim(lines, (quad ^ e) * each, each) for e in across]
+        taken = features.at[jnp.concatenate(own).reshape(-1)].get(mode="promise_in_bounds")
+        return taken.reshape(2 * each, lines.shape[1], features.shape[1])
+
+    by_first = cross(rows(3, first), 0)
+    kept = rows(second, 0)
+    by_second = cross(jnp.concatenate([kept[:each], by_first[:each]]), 1)
+    return kept[each:], by_first[each:], by_second[:each], by_second[each:]
 
 
 def along_z(first, at, z, pair):
@@ -156,10 +171,8 @@
 
 
 def quad_gather(own):
-    half = own.shape[0] // 2
-    by_x = move(own, flip(1))
-    by_y = move(own, flip(2))
-    return [own, by_x, by_y, move(by_x[:half], flip(2)), move(by_y[half:], flip(1))]
+    pair = jnp.concatenate([own, cross(own, 0)])
+    return [pair, cross(pair, 1)]
 
 
 def gather_small(features, lines, section_owner):
@@ -176,20 +189,19 @@
     slot = jnp.where(other, 2 + rank, jnp.where(is_first == low, 0, 1))
 
     def of(source):
-        return lax.select_n(quad ^ source, *held)
+        return lax.select_n(place_of(quad ^ source, lax.axis_index("rep")), *held)
 
     end = jnp.where(low, 0, 3)
     inward = [(i, i + 4) for i in range(4)] + [(i, i - 4) for i in range(12, 16)]
-    near, far = along_z(of(end), end, z, inward)
-    quarters = [near, far]
+    quarters = list(along_z(of(end), end, z, inward))
     for owner in owners:
         known, rest = along_z(of(owner % 4), owner // 4, z, flip(4))
         quarters.append(jnp.where((owner // 8) == (z // 2), known, rest))
     pieces, places = [], []
-    each = near.shape[0]
+    each = quarters[0].shape[0]
     for i, quarter in enumerate(quarters):
         pieces += quad_gather(quarter)
-        places += [(i * 4 + e) * each for e in range(4)] + [(i * 4 + 3) * each + each // 2]
+        places += [i * 4 * each, (i * 4 + 2) * each]
     return pieces, places, slot
 
 
@@ -222,8 +234,9 @@
         pieces = pieces + [lax.ppermute(piece, "rep", swap) for piece in pieces]
         places = places + [half + place for place in places]
         block = cols % n_dom
-        across = (block // 4) ^ (me % 4)
-        other = (cols // n_dom != rep).astype(jnp.int32)
+        holder = cols // n_dom
+        across = place_of((block // 4) ^ (me % 4), holder)
+        other = (holder != rep).astype(jnp.int32)
         slots = ((other * sections + slot[:, None]) * 4 + across) * 4 + block % 4
     else:
         mine = features.at[lines.reshape(-1)].get(mode="promise_in_bounds")

time: 167 us -> 130 us (0.78)
  local copies, waits for them, and re-layouts: 50 us -> 16.2 us
  starting transfers between devices: 49.8 us -> 42.3 us
  waiting for transfers between devices: 30.9 us -> 34.1 us
    unnamed x97 -> x33, local copies, waits for them, and re-layouts: 28.6 us -> 1.03 us
    ppermute x0 -> x10, waiting for transfers between devices: none -> 20.5 us  [cross(): return lax.ppermute(value, ('dom', 'rep'), pairs)]
    ppermute x28 -> x9, starting transfers between devices: 28.2 us -> 12.2 us  [move(): return lax.ppermute(value, 'dom', pairs)]
    ppermute x28 -> x9, waiting for transfers between devices: 27 us -> 13.5 us  [move(): return lax.ppermute(value, 'dom', pairs)]
    ppermute x0 -> x10, starting transfers between devices: none -> 11 us  [cross(): return lax.ppermute(value, ('dom', 'rep'), pairs)]
    gather x4 -> x2, local copies, waits for them, and re-layouts: 18.6 us -> 13.7 us  [rows(): features.at[jnp.concatenate(own).reshape(-1)].get(mode='promise_in_bounds')]
    ppermute x20 -> x8, waiting for transfers between devices: 3.15 us -> 0.15 us  [body(): pieces = pieces + [lax.ppermute(piece, 'rep', swap) for piece in pieces]]
    ppermute x20 -> x8, starting transfers between devices: 15.1 us -> 12.4 us  [body(): pieces = pieces + [lax.ppermute(piece, 'rep', swap) for piece in pieces]]
  transfers between devices with their start and end apart: 50 -> 29, of which waited for: 19 -> 12; matrix products, arithmetic and copies ran while one was open for 12% -> 9% of each run, Pallas kernels for 0% -> 0%
where the time goes in v3:
time: 130 us; the launch traced here: 129 us
  starting transfers between devices  42.3 us (33%)
  waiting for transfers between devices  34.1 us (26%)
  Pallas kernels  21.1 us (16%)
  local copies, waits for them, and re-layouts  16.2 us (12%)
  other arithmetic  8.05 us (6%)
  between operations  7.47 us (6%)
    pallas_call x1, Pallas kernels, products(): pl.pallas_call(functools.partial(kernel, tuple(places), len(tile_list)),...  21.1 us
    ppermute x10, waiting for transfers between devices, cross(): return lax.ppermute(value, ('dom', 'rep'), pairs)  20.5 us
    gather x2, local copies, waits for them, and re-layouts, rows(): features.at[jnp.concatenate(own).reshape(-1)].get(mode='promise_in_bounds')  13.7 us
    ppermute x9, waiting for transfers between devices, move(): return lax.ppermute(value, 'dom', pairs)  13.5 us
    ppermute x8, starting transfers between devices, body(): pieces = pieces + [lax.ppermute(piece, 'rep', swap) for piece in pieces]  12.4 us
    ppermute x9, starting transfers between devices, move(): return lax.ppermute(value, 'dom', pairs)  12.2 us
    ppermute x10, starting transfers between devices, cross(): return lax.ppermute(value, ('dom', 'rep'), pairs)  11 us
    ppermute x1, starting transfers between devices, body(): numbers = jnp.stack([numbers, lax.ppermute(numbers, 'rep', swap)])  4.09 us
  transfers between devices with their start and end apart: 29, of which 12 were waited for; matrix products, arithmetic and copies ran while one was open for 9% of the time, Pallas kernels for 0%

profile of v3, /device:TPU:1, one launch (start us, length us, event | category | flops | bytes accessed | tf_op | source)
XLA Modules:
  0.0 129.3 jit_solution(9582546993448132960)
XLA Ops:
  0.0 0.7 convert_bitcast_fusion
  0.7 0.2 reduce-window.9
  0.8 1.4 %fusion.11 = (s32[]{:T(128)}, s32[]{:T(128)}, s32[]{:T(128)}, s32[4]{0:T(128)S(1)}) fusion(s32[4]{0:T(128)} %param.10, s32[4,1]{0,1:T(1,128)S(1)} %reduce-window.9, s32[]{:T(128)S(6)} %axis_index.17, pred[]{:T(512)S(6)} %lt.79), kind=kLoop, calls=%fused_computation.67 | loop fusion | flops 77 | bytes 65 | tf_op jit(solution)/shard_map/reduce_sum | solution.py:186
  4.1 0.8 fusion.9
  4.9 0.6 gather_fusion
  5.6 7.3 %gather_fusion.2 = bf16[1024,256]{1,0:T(8,128)(2,1)} fusion(bf16[8192,256]{1,0:T(8,128)(2,1)} %param.8, s32[1024]{0:T(1024)S(1)} %get-tuple-element.20), kind=kCustom, calls=%fused_computation.2 | custom fusion | bytes 1052672 | tf_op jit(solution)/shard_map/gather | solution.py:153
  12.9 2.1 %collective-permute-start.1 = (bf16[8,128,256]{2,1,0:T(8,128)(2,1)}, bf16[8,128,256]{2,1,0:T(8,128)(2,1)S(1)}, u32[]{:S(2)}, u32[]{:S(2)}) collective-permute-start(bf16[8,128,256]{2,1,0:T(8,128)(2,1)} %bitcast.12), channel_id=1, source_target_pairs={{0,2},{1,5},{2,0},{3,7},{4,6},{5,1},{6,4},{7,3},{8,10},{9,13},{10,... | collective-permute-start | bytes 1572872 | tf_op jit(solution)/shard_map/ppermute | solution.py:139
  15.0 6.3 %gather_fusion.1 = bf16[1024,256]{1,0:T(8,128)(2,1)S(1)} fusion(bf16[8192,256]{1,0:T(8,128)(2,1)} %param.8, s32[1024]{0:T(1024)S(1)} %get-tuple-element.21), kind=kCustom, calls=%fused_computation.1 | custom fusion | bytes 1052672 | tf_op jit(solution)/shard_map/gather | solution.py:153
  21.3 0.0 copy-start.14
  21.4 0.7 collective-permute-done.1
  22.2 1.5 %collective-permute-start.2 = (bf16[8,128,256]{2,1,0:T(8,128)(2,1)S(1)}, bf16[8,128,256]{2,1,0:T(8,128)(2,1)}, u32[]{:S(2)}, u32[]{:S(2)}) collective-permute-start(bf16[8,128,256]{2,1,0:T(8,128)(2,1)S(1)} %pad_maximum_fusion), channel_id=1, source_target_pairs={{0,4},{1,3},{2,6},{3,1},{4,0},{5,7},{6,2},{7,5},{8,12},{9,11},{10,... | collective-permute-start | bytes 1572872 | tf_op jit(solution)/shard_map/ppermute | solution.py:139
  25.5 0.0 copy-start.15
  27.5 3.2 %collective-permute-done.2 = bf16[8,128,256]{2,1,0:T(8,128)(2,1)} collective-permute-done((bf16[8,128,256]{2,1,0:T(8,128)(2,1)S(1)}, bf16[8,128,256]{2,1,0:T(8,128)(2,1)}, u32[]{:S(2)}, u32[]{:S(2)}) %collective-permute-start.2) | collective-permute-done | bytes 524320 | tf_op jit(solution)/shard_map/ppermute | solution.py:139
  30.7 1.2 select_select_fusion.1
  31.9 1.6 %collective-permute-start.15 = (bf16[4,128,256]{2,1,0:T(8,128)(2,1)S(1)}, bf16[4,128,256]{2,1,0:T(8,128)(2,1)S(1)}, u32[]{:S(2)}, u32[]{:S(2)}) collective-permute-start(bf16[4,128,256]{2,1,0:T(8,128)(2,1)S(1)} %get-tuple-element.8), channel_id=1, source_target_pairs={{0,8},{2,10},{4,12},{6,14},{8,0},{10,2},{12,4},{14,6},{16,24},{18,... | collective-permute-start | bytes 786440 | tf_op jit(solution)/shard_map/ppermute | solution.py:127
  33.4 2.6 %collective-permute-start.3 = (bf16[4,128,256]{2,1,0:T(8,128)(2,1)S(1)}, bf16[4,128,256]{2,1,0:T(8,128)(2,1)}, u32[]{:S(2)}, u32[]{:S(2)}) collective-permute-start(bf16[4,128,256]{2,1,0:T(8,128)(2,1)S(1)} %get-tuple-element.10), channel_id=1, source_target_pairs={{0,8},{2,10},{4,12},{6,14},{24,16},{26,18},{28,20},{30,22},{1,9},{... | collective-permute-start | bytes 786440 | tf_op jit(solution)/shard_map/ppermute | solution.py:127
  36.1 2.7 %collective-permute-start.28 = (bf16[64,128,128]{2,1,0:T(8,128)(2,1)S(1)}, bf16[64,128,128]{2,1,0:T(8,128)(2,1)}, u32[]{:S(2)}, u32[]{:S(2)}) collective-permute-start(bf16[64,128,128]{2,1,0:T(8,128)(2,1)S(1)} %bitcast.34), channel_id=1, source_target_pairs={{0,1},{1,0},{2,3},{3,2},{4,5},{5,4},{6,7},{7,6},{8,9},{9,8},{10,11... | collective-permute-start | bytes 6291464 | tf_op jit(solution)/shard_map/ppermute | solution.py:222
  40.0 0.1 collective-permute-start.10
  40.2 1.4 %collective-permute-start.16 = (bf16[4,128,256]{2,1,0:T(8,128)(2,1)S(1)}, bf16[4,128,256]{2,1,0:T(8,128)(2,1)}, u32[]{:S(2)}, u32[]{:S(2)}) collective-permute-start(bf16[4,128,256]{2,1,0:T(8,128)(2,1)S(1)} %broadcast_select_fusion), channel_id=1, source_target_pairs={{8,16},{10,18},{12,20},{14,22},{16,8},{18,10},{20,12},{22,14},{9,1... | collective-permute-start | bytes 786440 | tf_op jit(solution)/shard_map/ppermute | solution.py:127
  41.5 0.8 collective-permute-done.3
  42.3 1.4 %collective-permute-start.6 = (bf16[4,128,256]{2,1,0:T(8,128)(2,1)S(1)}, bf16[4,128,256]{2,1,0:T(8,128)(2,1)}, u32[]{:S(2)}, u32[]{:S(2)}) collective-permute-start(bf16[4,128,256]{2,1,0:T(8,128)(2,1)S(1)} %broadcast_select_fusion.3), channel_id=1, source_target_pairs={{8,16},{10,18},{12,20},{14,22},{16,8},{18,10},{20,12},{22,14},{9,1... | collective-permute-start | bytes 786440 | tf_op jit(solution)/shard_map/ppermute | solution.py:127
  43.7 1.2 collective-permute-start.4
  44.9 3.1 %collective-permute-done.10 = bf16[4,128,256]{2,1,0:T(8,128)(2,1)S(1)} collective-permute-done((bf16[4,128,256]{2,1,0:T(8,128)(2,1)S(1)}, bf16[4,128,256]{2,1,0:T(8,128)(2,1)S(1)}, u32[]{:S(2)}, u32[]{:S(2)}) %collective-permute-start.10) | collective-permute-done | bytes 262176 | tf_op jit(solution)/shard_map/ppermute | solution.py:127
  48.1 1.4 %collective-permute-start.11 = (bf16[4,128,256]{2,1,0:T(8,128)(2,1)S(1)}, bf16[4,128,256]{2,1,0:T(8,128)(2,1)}, u32[]{:S(2)}, u32[]{:S(2)}) collective-permute-start(bf16[4,128,256]{2,1,0:T(8,128)(2,1)S(1)} %broadcast_select_fusion.1), channel_id=1, source_target_pairs={{8,16},{10,18},{12,20},{14,22},{16,8},{18,10},{20,12},{22,14},{9,1... | collective-permute-start | bytes 786440 | tf_op jit(solution)/shard_map/ppermute | solution.py:127
  49.4 1.3 collective-permute-start.17
  50.8 0.0 collective-permute-done.6
  50.8 1.3 collective-permute-start.7
  52.1 1.0 pad_maximum_fusion.1.refs_0_
  53.2 4.2 %collective-permute-start.20 = (bf16[8,128,256]{2,1,0:T(8,128)(2,1)S(1)}, bf16[8,128,256]{2,1,0:T(8,128)(2,1)S(1)}, u32[]{:S(2)}, u32[]{:S(2)}) collective-permute-start(bf16[8,128,256]{2,1,0:T(8,128)(2,1)S(1)} %pad_maximum_fusion.1.refs_0_), channel_id=1, source_target_pairs={{0,1},{1,0},{2,3},{3,2},{4,5},{5,4},{6,7},{7,6},{8,9},{9,8},{10,11... | collective-permute-start | bytes 1572872 | tf_op jit(solution)/shard_map/ppermute | solution.py:234
  57.4 1.2 collective-permute-start.5
  58.6 0.8 collective-permute-done.17
  59.4 1.3 collective-permute-start.12
  60.7 1.0 select_select_fusion
  61.7 1.1 collective-permute-done.7
  62.7 1.1 collective-permute-start.18
  63.8 7.7 %collective-permute-done.12 = bf16[4,128,256]{2,1,0:T(8,128)(2,1)S(1)} collective-permute-done((bf16[4,128,256]{2,1,0:T(8,128)(2,1)}, bf16[4,128,256]{2,1,0:T(8,128)(2,1)S(1)}, u32[]{:S(2)}, u32[]{:S(2)}) %collective-permute-start.12) | collective-permute-done | bytes 262176 | tf_op jit(solution)/shard_map/ppermute | solution.py:127
  71.5 1.3 %collective-permute-start.8 = (bf16[4,128,256]{2,1,0:T(8,128)(2,1)S(1)}, bf16[4,128,256]{2,1,0:T(8,128)(2,1)S(1)}, u32[]{:S(2)}, u32[]{:S(2)}) collective-permute-start(bf16[4,128,256]{2,1,0:T(8,128)(2,1)S(1)} %broadcast_select_fusion.2), channel_id=1, source_target_pairs={{0,2},{1,5},{2,0},{3,7},{4,6},{5,1},{6,4},{7,3},{8,10},{9,13},{10,... | collective-permute-start | bytes 786440 | tf_op jit(solution)/shard_map/ppermute | solution.py:139
  72.9 0.2 collective-permute-start.13
  73.2 3.6 %collective-permute-done.8 = bf16[4,128,256]{2,1,0:T(8,128)(2,1)S(1)} collective-permute-done((bf16[4,128,256]{2,1,0:T(8,128)(2,1)S(1)}, bf16[4,128,256]{2,1,0:T(8,128)(2,1)S(1)}, u32[]{:S(2)}, u32[]{:S(2)}) %collective-permute-start.8) | collective-permute-done | bytes 262176 | tf_op jit(solution)/shard_map/ppermute | solution.py:139
  76.8 4.1 %collective-permute-start = (s32[2,4,16]{2,1,0:T(4,128)S(1)}, s32[2,4,16]{2,1,0:T(4,128)S(1)}, u32[]{:S(2)}, u32[]{:S(2)}) collective-permute-start(s32[2,4,16]{2,1,0:T(4,128)S(1)} %constant_dynamic-update-slice_fusion), channel_id=1, source_target_pairs={{0,1},{1,0},{2,3},{3,2},{4,5},{5,4},{6,7},{7,6},{8,9},{9,8},{10,11... | collective-permute-start | bytes 1544 | tf_op jit(solution)/shard_map/ppermute | solution.py:223
  80.9 2.7 %collective-permute-start.22 = (bf16[8,128,256]{2,1,0:T(8,128)(2,1)S(1)}, bf16[8,128,256]{2,1,0:T(8,128)(2,1)S(1)}, u32[]{:S(2)}, u32[]{:S(2)}) collective-permute-start(bf16[8,128,256]{2,1,0:T(8,128)(2,1)S(1)} %pad_maximum_fusion.2.refs_2_), channel_id=1, source_target_pairs={{0,1},{1,0},{2,3},{3,2},{4,5},{5,4},{6,7},{7,6},{8,9},{9,8},{10,11... | collective-permute-start | bytes 1572872 | tf_op jit(solution)/shard_map/ppermute | solution.py:234
  83.7 0.1 collective-permute-start.21
  83.7 0.9 pad_maximum_fusion.3.refs_4_
  84.7 0.9 collective-permute-start.9
  85.5 0.6 collective-permute-start.14
  86.1 0.9 collective-permute-start.19
  87.0 1.6 %collective-permute-start.24 = (bf16[8,128,256]{2,1,0:T(8,128)(2,1)}, bf16[8,128,256]{2,1,0:T(8,128)(2,1)S(1)}, u32[]{:S(2)}, u32[]{:S(2)}) collective-permute-start(bf16[8,128,256]{2,1,0:T(8,128)(2,1)} %pad_maximum_fusion.3.refs_4_), channel_id=1, source_target_pairs={{0,1},{1,0},{2,3},{3,2},{4,5},{5,4},{6,7},{7,6},{8,9},{9,8},{10,11... | collective-permute-start | bytes 1572872 | tf_op jit(solution)/shard_map/ppermute | solution.py:234
  88.6 0.1 collective-permute-start.26
  88.7 4.4 %collective-permute-done.9.refs_3_ = bf16[8,128,256]{2,1,0:T(8,128)(2,1)} collective-permute-done((bf16[8,128,256]{2,1,0:T(8,128)(2,1)S(1)}, bf16[8,128,256]{2,1,0:T(8,128)(2,1)}, u32[]{:S(2)}, u32[]{:S(2)}) %collective-permute-start.9) | collective-permute-done | bytes 524320 | tf_op jit(solution)/shard_map/ppermute | solution.py:139
  93.1 1.2 collective-permute-start.23
  94.3 4.4 %collective-permute-done.14.refs_5_ = bf16[8,128,256]{2,1,0:T(8,128)(2,1)} collective-permute-done((bf16[8,128,256]{2,1,0:T(8,128)(2,1)}, bf16[8,128,256]{2,1,0:T(8,128)(2,1)}, u32[]{:S(2)}, u32[]{:S(2)}) %collective-permute-start.14) | collective-permute-done | bytes 524320 | tf_op jit(solution)/shard_map/ppermute | solution.py:139
  98.7 1.2 collective-permute-start.25
  99.9 4.3 %collective-permute-done.19.refs_7_ = bf16[8,128,256]{2,1,0:T(8,128)(2,1)S(1)} collective-permute-done((bf16[8,128,256]{2,1,0:T(8,128)(2,1)S(1)}, bf16[8,128,256]{2,1,0:T(8,128)(2,1)S(1)}, u32[]{:S(2)}, u32[]{:S(2)}) %collective-permute-start.19) | collective-permute-done | bytes 524320 | tf_op jit(solution)/shard_map/ppermute | solution.py:139
  104.3 1.3 collective-permute-start.27
  105.5 0.1 add.134
  105.6 0.1 add.135
  105.7 0.1 squeeze.7
  105.8 0.6 sub.61.rows_ref
  106.4 0.6 fusion.4.cols_ref
  107.1 0.1 collective-permute-done.27.refs_15_
  107.2 0.6 copy-done.11
  107.9 0.1 copy-done.12
  108.0 0.2 copy-done.13
  108.2 21.1 %shard_map.82 = bf16[32,128,256]{2,1,0:T(8,128)(2,1)} custom-call(s32[128]{0:T(128)} %sub.61.rows_ref, s32[128]{0:T(128)} %fusion.4.cols_ref, bf16[8,128,256]{2,1,0:T(8,128)(2,1)} %copy-done.2, bf16[8,128,256]{2,1,0:T(8,128)(2,1)} %copy-done.7, bf16[8,128,256]{2,1,0:T(8,128)(2,1)} %copy-done.4, bf16[8,128,256]{2,1,0:T(8,128)(2,1)} %collective-permute-done.9.refs_3_, ...), custom_call_target="tpu_custom_call" | custom-call | flops 1073741824 | bytes 16777216 | tf_op jit(solution)/shard_map/pallas_call | solution.py:89
  (63 shorter events, 0.5 us)
Async XLA Ops:
  0.0 4.9 %copy-start = (s32[1,8192]{1,0:T(1,128)S(1)}, s32[1,8192]{1,0:T(1,128)}, u32[]{:S(2)}) copy-start(s32[1,8192]{1,0:T(1,128)} %param.9) | copy-start | bytes 98308
  12.9 9.1 %collective-permute-start.1 = (bf16[8,128,256]{2,1,0:T(8,128)(2,1)}, bf16[8,128,256]{2,1,0:T(8,128)(2,1)S(1)}, u32[]{:S(2)}, u32[]{:S(2)}) collective-permute-start(bf16[8,128,256]{2,1,0:T(8,128)(2,1)} %bitcast.12), channel_id=1, source_target_pairs={{0,2},{1,5},{2,0},{3,7},{4,6},{5,1},{6,4},{7,3},{8,10},{9,13},{10,... | collective-permute-start | bytes 1572872 | tf_op jit(solution)/shard_map/ppermute | solution.py:139
  15.0 21.1 %copy-start.1 = (bf16[1,4,16,128,128]{4,3,2,1,0:T(8,128)(2,1)S(1)}, bf16[1,4,16,128,128]{4,3,2,1,0:T(8,128)(2,1)}, u32[]{:S(2)}) copy-start(bf16[1,4,16,128,128]{4,3,2,1,0:T(8,128)(2,1)} %param.14) | copy-start | bytes 6291460
  21.3 29.5 %copy-start.14 = (s32[1,4,16]{2,1,0:T(4,128)S(1)}, s32[1,4,16]{2,1,0:T(4,128)}, u32[]{:S(2)}) copy-start(s32[1,4,16]{2,1,0:T(4,128)} %param.12) | copy-start | bytes 772
  22.1 8.6 %copy-start.5 = (bf16[8,128,256]{2,1,0:T(8,128)(2,1)}, bf16[8,128,256]{2,1,0:T(8,128)(2,1)S(1)}, u32[]{:S(2)}) copy-start(bf16[8,128,256]{2,1,0:T(8,128)(2,1)S(1)} %collective-permute-done.1) | copy-start | bytes 1572868
  22.2 8.5 %collective-permute-start.2 = (bf16[8,128,256]{2,1,0:T(8,128)(2,1)S(1)}, bf16[8,128,256]{2,1,0:T(8,128)(2,1)}, u32[]{:S(2)}, u32[]{:S(2)}) collective-permute-start(bf16[8,128,256]{2,1,0:T(8,128)(2,1)S(1)} %pad_maximum_fusion), channel_id=1, source_target_pairs={{0,4},{1,3},{2,6},{3,1},{4,0},{5,7},{6,2},{7,5},{8,12},{9,11},{10,... | collective-permute-start | bytes 1572872 | tf_op jit(solution)/shard_map/ppermute | solution.py:139
  25.5 47.6 %copy-start.15 = (s32[1,4,16]{2,1,0:T(4,128)S(1)}, s32[1,4,16]{2,1,0:T(4,128)}, u32[]{:S(2)}) copy-start(s32[1,4,16]{2,1,0:T(4,128)} %param.13) | copy-start | bytes 772
  31.9 8.3 %collective-permute-start.15 = (bf16[4,128,256]{2,1,0:T(8,128)(2,1)S(1)}, bf16[4,128,256]{2,1,0:T(8,128)(2,1)S(1)}, u32[]{:S(2)}, u32[]{:S(2)}) collective-permute-start(bf16[4,128,256]{2,1,0:T(8,128)(2,1)S(1)} %get-tuple-element.8), channel_id=1, source_target_pairs={{0,8},{2,10},{4,12},{6,14},{8,0},{10,2},{12,4},{14,6},{16,24},{18,... | collective-permute-start | bytes 786440 | tf_op jit(solution)/shard_map/ppermute | solution.py:127
  33.4 8.8 %collective-permute-start.3 = (bf16[4,128,256]{2,1,0:T(8,128)(2,1)S(1)}, bf16[4,128,256]{2,1,0:T(8,128)(2,1)}, u32[]{:S(2)}, u32[]{:S(2)}) collective-permute-start(bf16[4,128,256]{2,1,0:T(8,128)(2,1)S(1)} %get-tuple-element.10), channel_id=1, source_target_pairs={{0,8},{2,10},{4,12},{6,14},{24,16},{26,18},{28,20},{30,22},{1,9},{... | collective-permute-start | bytes 786440 | tf_op jit(solution)/shard_map/ppermute | solution.py:127
  36.1 50.1 %collective-permute-start.28 = (bf16[64,128,128]{2,1,0:T(8,128)(2,1)S(1)}, bf16[64,128,128]{2,1,0:T(8,128)(2,1)}, u32[]{:S(2)}, u32[]{:S(2)}) collective-permute-start(bf16[64,128,128]{2,1,0:T(8,128)(2,1)S(1)} %bitcast.34), channel_id=1, source_target_pairs={{0,1},{1,0},{2,3},{3,2},{4,5},{5,4},{6,7},{7,6},{8,9},{9,8},{10,11... | collective-permute-start | bytes 6291464 | tf_op jit(solution)/shard_map/ppermute | solution.py:222
  40.0 8.0 %collective-permute-start.10 = (bf16[4,128,256]{2,1,0:T(8,128)(2,1)S(1)}, bf16[4,128,256]{2,1,0:T(8,128)(2,1)S(1)}, u32[]{:S(2)}, u32[]{:S(2)}) collective-permute-start(bf16[4,128,256]{2,1,0:T(8,128)(2,1)S(1)} %get-tuple-element.9), channel_id=1, source_target_pairs={{0,8},{2,10},{4,12},{6,14},{8,0},{10,2},{12,4},{14,6},{16,24},{18,... | collective-permute-start | bytes 786440 | tf_op jit(solution)/shard_map/ppermute | solution.py:127
  40.2 9.3 %collective-permute-start.16 = (bf16[4,128,256]{2,1,0:T(8,128)(2,1)S(1)}, bf16[4,128,256]{2,1,0:T(8,128)(2,1)}, u32[]{:S(2)}, u32[]{:S(2)}) collective-permute-start(bf16[4,128,256]{2,1,0:T(8,128)(2,1)S(1)} %broadcast_select_fusion), channel_id=1, source_target_pairs={{8,16},{10,18},{12,20},{14,22},{16,8},{18,10},{20,12},{22,14},{9,1... | collective-permute-start | bytes 786440 | tf_op jit(solution)/shard_map/ppermute | solution.py:127
  42.3 8.5 %collective-permute-start.6 = (bf16[4,128,256]{2,1,0:T(8,128)(2,1)S(1)}, bf16[4,128,256]{2,1,0:T(8,128)(2,1)}, u32[]{:S(2)}, u32[]{:S(2)}) collective-permute-start(bf16[4,128,256]{2,1,0:T(8,128)(2,1)S(1)} %broadcast_select_fusion.3), channel_id=1, source_target_pairs={{8,16},{10,18},{12,20},{14,22},{16,8},{18,10},{20,12},{22,14},{9,1... | collective-permute-start | bytes 786440 | tf_op jit(solution)/shard_map/ppermute | solution.py:127
  43.7 8.5 %collective-permute-start.4 = (bf16[4,128,256]{2,1,0:T(8,128)(2,1)S(1)}, bf16[4,128,256]{2,1,0:T(8,128)(2,1)}, u32[]{:S(2)}, u32[]{:S(2)}) collective-permute-start(bf16[4,128,256]{2,1,0:T(8,128)(2,1)S(1)} %broadcast_select_fusion.3), channel_id=1, source_target_pairs={{0,2},{1,5},{2,0},{3,7},{4,6},{5,1},{6,4},{7,3},{8,10},{9,13},{10,... | collective-permute-start | bytes 786440 | tf_op jit(solution)/shard_map/ppermute | solution.py:139
  48.1 9.3 %collective-permute-start.11 = (bf16[4,128,256]{2,1,0:T(8,128)(2,1)S(1)}, bf16[4,128,256]{2,1,0:T(8,128)(2,1)}, u32[]{:S(2)}, u32[]{:S(2)}) collective-permute-start(bf16[4,128,256]{2,1,0:T(8,128)(2,1)S(1)} %broadcast_select_fusion.1), channel_id=1, source_target_pairs={{8,16},{10,18},{12,20},{14,22},{16,8},{18,10},{20,12},{22,14},{9,1... | collective-permute-start | bytes 786440 | tf_op jit(solution)/shard_map/ppermute | solution.py:127
  49.4 9.9 %collective-permute-start.17 = (bf16[4,128,256]{2,1,0:T(8,128)(2,1)}, bf16[4,128,256]{2,1,0:T(8,128)(2,1)}, u32[]{:S(2)}, u32[]{:S(2)}) collective-permute-start(bf16[4,128,256]{2,1,0:T(8,128)(2,1)} %collective-permute-done.16), channel_id=1, source_target_pairs={{8,0},{10,2},{12,4},{14,6},{16,24},{18,26},{20,28},{22,30},{9,1},{... | collective-permute-start | bytes 786440 | tf_op jit(solution)/shard_map/ppermute | solution.py:127
  50.8 11.9 %collective-permute-start.7 = (bf16[4,128,256]{2,1,0:T(8,128)(2,1)}, bf16[4,128,256]{2,1,0:T(8,128)(2,1)S(1)}, u32[]{:S(2)}, u32[]{:S(2)}) collective-permute-start(bf16[4,128,256]{2,1,0:T(8,128)(2,1)} %collective-permute-done.6), channel_id=1, source_target_pairs={{8,0},{10,2},{12,4},{14,6},{16,24},{18,26},{20,28},{22,30},{9,1},{... | collective-permute-start | bytes 786440 | tf_op jit(solution)/shard_map/ppermute | solution.py:127
  53.1 54.1 %copy-start.2 = (bf16[8,128,256]{2,1,0:T(8,128)(2,1)}, bf16[8,128,256]{2,1,0:T(8,128)(2,1)S(1)}, u32[]{:S(2)}) copy-start(bf16[8,128,256]{2,1,0:T(8,128)(2,1)S(1)} %pad_maximum_fusion.1.refs_0_) | copy-start | bytes 1572868
  53.2 32.4 %collective-permute-start.20 = (bf16[8,128,256]{2,1,0:T(8,128)(2,1)S(1)}, bf16[8,128,256]{2,1,0:T(8,128)(2,1)S(1)}, u32[]{:S(2)}, u32[]{:S(2)}) collective-permute-start(bf16[8,128,256]{2,1,0:T(8,128)(2,1)S(1)} %pad_maximum_fusion.1.refs_0_), channel_id=1, source_target_pairs={{0,1},{1,0},{2,3},{3,2},{4,5},{5,4},{6,7},{7,6},{8,9},{9,8},{10,11... | collective-permute-start | bytes 1572872 | tf_op jit(solution)/shard_map/ppermute | solution.py:234
  57.4 26.3 %collective-permute-start.5 = (bf16[8,128,256]{2,1,0:T(8,128)(2,1)S(1)}, bf16[8,128,256]{2,1,0:T(8,128)(2,1)S(1)}, u32[]{:S(2)}, u32[]{:S(2)}) collective-permute-start(bf16[8,128,256]{2,1,0:T(8,128)(2,1)S(1)} %pad_maximum_fusion.1.refs_0_), channel_id=1, source_target_pairs={{0,4},{1,3},{2,6},{3,1},{4,0},{5,7},{6,2},{7,5},{8,12},{9,11},{10,... | collective-permute-start | bytes 1572872 | tf_op jit(solution)/shard_map/ppermute | solution.py:139
  59.4 12.2 %collective-permute-start.12 = (bf16[4,128,256]{2,1,0:T(8,128)(2,1)}, bf16[4,128,256]{2,1,0:T(8,128)(2,1)S(1)}, u32[]{:S(2)}, u32[]{:S(2)}) collective-permute-start(bf16[4,128,256]{2,1,0:T(8,128)(2,1)} %collective-permute-done.11), channel_id=1, source_target_pairs={{8,0},{10,2},{12,4},{14,6},{16,24},{18,26},{20,28},{22,30},{9,1},{... | collective-permute-start | bytes 786440 | tf_op jit(solution)/shard_map/ppermute | solution.py:127
  62.7 10.2 %collective-permute-start.18 = (bf16[4,128,256]{2,1,0:T(8,128)(2,1)S(1)}, bf16[4,128,256]{2,1,0:T(8,128)(2,1)S(1)}, u32[]{:S(2)}, u32[]{:S(2)}) collective-permute-start(bf16[4,128,256]{2,1,0:T(8,128)(2,1)S(1)} %select_select_fusion), channel_id=1, source_target_pairs={{0,2},{1,5},{2,0},{3,7},{4,6},{5,1},{6,4},{7,3},{8,10},{9,13},{10,... | collective-permute-start | bytes 786440 | tf_op jit(solution)/shard_map/ppermute | solution.py:139
  71.5 5.2 %collective-permute-start.8 = (bf16[4,128,256]{2,1,0:T(8,128)(2,1)S(1)}, bf16[4,128,256]{2,1,0:T(8,128)(2,1)S(1)}, u32[]{:S(2)}, u32[]{:S(2)}) collective-permute-start(bf16[4,128,256]{2,1,0:T(8,128)(2,1)S(1)} %broadcast_select_fusion.2), channel_id=1, source_target_pairs={{0,2},{1,5},{2,0},{3,7},{4,6},{5,1},{6,4},{7,3},{8,10},{9,13},{10,... | collective-permute-start | bytes 786440 | tf_op jit(solution)/shard_map/ppermute | solution.py:139
  72.9 8.0 %collective-permute-start.13 = (bf16[4,128,256]{2,1,0:T(8,128)(2,1)S(1)}, bf16[4,128,256]{2,1,0:T(8,128)(2,1)S(1)}, u32[]{:S(2)}, u32[]{:S(2)}) collective-permute-start(bf16[4,128,256]{2,1,0:T(8,128)(2,1)S(1)} %select_select_fusion.2), channel_id=1, source_target_pairs={{0,2},{1,5},{2,0},{3,7},{4,6},{5,1},{6,4},{7,3},{8,10},{9,13},{10,... | collective-permute-start | bytes 786440 | tf_op jit(solution)/shard_map/ppermute | solution.py:139
  73.2 34.0 %copy-start.3 = (bf16[8,128,256]{2,1,0:T(8,128)(2,1)}, bf16[8,128,256]{2,1,0:T(8,128)(2,1)S(1)}, u32[]{:S(2)}) copy-start(bf16[8,128,256]{2,1,0:T(8,128)(2,1)S(1)} %pad_maximum_fusion.4.refs_6_) | copy-start | bytes 1572868
  76.8 7.9 %collective-permute-start = (s32[2,4,16]{2,1,0:T(4,128)S(1)}, s32[2,4,16]{2,1,0:T(4,128)S(1)}, u32[]{:S(2)}, u32[]{:S(2)}) collective-permute-start(s32[2,4,16]{2,1,0:T(4,128)S(1)} %constant_dynamic-update-slice_fusion), channel_id=1, source_target_pairs={{0,1},{1,0},{2,3},{3,2},{4,5},{5,4},{6,7},{7,6},{8,9},{9,8},{10,11... | collective-permute-start | bytes 1544 | tf_op jit(solution)/shard_map/ppermute | solution.py:223
  80.9 23.3 %copy-start.4 = (bf16[8,128,256]{2,1,0:T(8,128)(2,1)}, bf16[8,128,256]{2,1,0:T(8,128)(2,1)S(1)}, u32[]{:S(2)}) copy-start(bf16[8,128,256]{2,1,0:T(8,128)(2,1)S(1)} %pad_maximum_fusion.2.refs_2_) | copy-start | bytes 1572868
  80.9 7.7 %collective-permute-start.22 = (bf16[8,128,256]{2,1,0:T(8,128)(2,1)S(1)}, bf16[8,128,256]{2,1,0:T(8,128)(2,1)S(1)}, u32[]{:S(2)}, u32[]{:S(2)}) collective-permute-start(bf16[8,128,256]{2,1,0:T(8,128)(2,1)S(1)} %pad_maximum_fusion.2.refs_2_), channel_id=1, source_target_pairs={{0,1},{1,0},{2,3},{3,2},{4,5},{5,4},{6,7},{7,6},{8,9},{9,8},{10,11... | collective-permute-start | bytes 1572872 | tf_op jit(solution)/shard_map/ppermute | solution.py:234
  83.7 20.6 %copy-start.7 = (bf16[8,128,256]{2,1,0:T(8,128)(2,1)}, bf16[8,128,256]{2,1,0:T(8,128)(2,1)S(1)}, u32[]{:S(2)}) copy-start(bf16[8,128,256]{2,1,0:T(8,128)(2,1)S(1)} %collective-permute-done.5.refs_1_) | copy-start | bytes 1572868
  83.7 3.3 %collective-permute-start.21 = (bf16[8,128,256]{2,1,0:T(8,128)(2,1)S(1)}, bf16[8,128,256]{2,1,0:T(8,128)(2,1)S(1)}, u32[]{:S(2)}, u32[]{:S(2)}) collective-permute-start(bf16[8,128,256]{2,1,0:T(8,128)(2,1)S(1)} %collective-permute-done.5.refs_1_), channel_id=1, source_target_pairs={{0,1},{1,0},{2,3},{3,2},{4,5},{5,4},{6,7},{7,6},{8,9},{9,8},{10,11... | collective-permute-start | bytes 1572872 | tf_op jit(solution)/shard_map/ppermute | solution.py:234
  84.7 8.4 %collective-permute-start.9 = (bf16[8,128,256]{2,1,0:T(8,128)(2,1)S(1)}, bf16[8,128,256]{2,1,0:T(8,128)(2,1)}, u32[]{:S(2)}, u32[]{:S(2)}) collective-permute-start(bf16[8,128,256]{2,1,0:T(8,128)(2,1)S(1)} %pad_maximum_fusion.2.refs_2_), channel_id=1, source_target_pairs={{0,4},{1,3},{2,6},{3,1},{4,0},{5,7},{6,2},{7,5},{8,12},{9,11},{10,... | collective-permute-start | bytes 1572872 | tf_op jit(solution)/shard_map/ppermute | solution.py:139
  85.5 18.7 %copy-start.6 = (bf16[8,128,256]{2,1,0:T(8,128)(2,1)}, bf16[8,128,256]{2,1,0:T(8,128)(2,1)S(1)}, u32[]{:S(2)}) copy-start(bf16[8,128,256]{2,1,0:T(8,128)(2,1)S(1)} %collective-permute-done.20.refs_8_) | copy-start | bytes 1572868
  85.5 13.2 %collective-permute-start.14 = (bf16[8,128,256]{2,1,0:T(8,128)(2,1)}, bf16[8,128,256]{2,1,0:T(8,128)(2,1)}, u32[]{:S(2)}, u32[]{:S(2)}) collective-permute-start(bf16[8,128,256]{2,1,0:T(8,128)(2,1)} %pad_maximum_fusion.3.refs_4_), channel_id=1, source_target_pairs={{0,4},{1,3},{2,6},{3,1},{4,0},{5,7},{6,2},{7,5},{8,12},{9,11},{10,... | collective-permute-start | bytes 1572872 | tf_op jit(solution)/shard_map/ppermute | solution.py:139
  86.1 18.1 %collective-permute-start.19 = (bf16[8,128,256]{2,1,0:T(8,128)(2,1)S(1)}, bf16[8,128,256]{2,1,0:T(8,128)(2,1)S(1)}, u32[]{:S(2)}, u32[]{:S(2)}) collective-permute-start(bf16[8,128,256]{2,1,0:T(8,128)(2,1)S(1)} %pad_maximum_fusion.4.refs_6_), channel_id=1, source_target_pairs={{0,4},{1,3},{2,6},{3,1},{4,0},{5,7},{6,2},{7,5},{8,12},{9,11},{10,... | collective-permute-start | bytes 1572872 | tf_op jit(solution)/shard_map/ppermute | solution.py:139
  87.0 17.2 %copy-start.9 = (bf16[8,128,256]{2,1,0:T(8,128)(2,1)}, bf16[8,128,256]{2,1,0:T(8,128)(2,1)S(1)}, u32[]{:S(2)}) copy-start(bf16[8,128,256]{2,1,0:T(8,128)(2,1)S(1)} %collective-permute-done.21.refs_9_) | copy-start | bytes 1572868
  87.0 20.0 %collective-permute-start.24 = (bf16[8,128,256]{2,1,0:T(8,128)(2,1)}, bf16[8,128,256]{2,1,0:T(8,128)(2,1)S(1)}, u32[]{:S(2)}, u32[]{:S(2)}) collective-permute-start(bf16[8,128,256]{2,1,0:T(8,128)(2,1)} %pad_maximum_fusion.3.refs_4_), channel_id=1, source_target_pairs={{0,1},{1,0},{2,3},{3,2},{4,5},{5,4},{6,7},{7,6},{8,9},{9,8},{10,11... | collective-permute-start | bytes 1572872 | tf_op jit(solution)/shard_map/ppermute | solution.py:234
  88.6 15.6 %copy-start.8 = (bf16[8,128,256]{2,1,0:T(8,128)(2,1)}, bf16[8,128,256]{2,1,0:T(8,128)(2,1)S(1)}, u32[]{:S(2)}) copy-start(bf16[8,128,256]{2,1,0:T(8,128)(2,1)S(1)} %collective-permute-done.22.refs_10_) | copy-start | bytes 1572868
  88.6 18.4 %collective-permute-start.26 = (bf16[8,128,256]{2,1,0:T(8,128)(2,1)S(1)}, bf16[8,128,256]{2,1,0:T(8,128)(2,1)S(1)}, u32[]{:S(2)}, u32[]{:S(2)}) collective-permute-start(bf16[8,128,256]{2,1,0:T(8,128)(2,1)S(1)} %pad_maximum_fusion.4.refs_6_), channel_id=1, source_target_pairs={{0,1},{1,0},{2,3},{3,2},{4,5},{5,4},{6,7},{7,6},{8,9},{9,8},{10,11... | collective-permute-start | bytes 1572872 | tf_op jit(solution)/shard_map/ppermute | solution.py:234
  93.1 14.0 %collective-permute-start.23 = (bf16[8,128,256]{2,1,0:T(8,128)(2,1)}, bf16[8,128,256]{2,1,0:T(8,128)(2,1)S(1)}, u32[]{:S(2)}, u32[]{:S(2)}) collective-permute-start(bf16[8,128,256]{2,1,0:T(8,128)(2,1)} %collective-permute-done.9.refs_3_), channel_id=1, source_target_pairs={{0,1},{1,0},{2,3},{3,2},{4,5},{5,4},{6,7},{7,6},{8,9},{9,8},{10,11... | collective-permute-start | bytes 1572872 | tf_op jit(solution)/shard_map/ppermute | solution.py:234
  98.7 8.4 %collective-permute-start.25 = (bf16[8,128,256]{2,1,0:T(8,128)(2,1)}, bf16[8,128,256]{2,1,0:T(8,128)(2,1)}, u32[]{:S(2)}, u32[]{:S(2)}) collective-permute-start(bf16[8,128,256]{2,1,0:T(8,128)(2,1)} %collective-permute-done.14.refs_5_), channel_id=1, source_target_pairs={{0,1},{1,0},{2,3},{3,2},{4,5},{5,4},{6,7},{7,6},{8,9},{9,8},{10,11... | collective-permute-start | bytes 1572872 | tf_op jit(solution)/shard_map/ppermute | solution.py:234
  104.2 3.0 %copy-start.10 = (bf16[8,128,256]{2,1,0:T(8,128)(2,1)}, bf16[8,128,256]{2,1,0:T(8,128)(2,1)S(1)}, u32[]{:S(2)}) copy-start(bf16[8,128,256]{2,1,0:T(8,128)(2,1)S(1)} %collective-permute-done.19.refs_7_) | copy-start | bytes 1572868
  104.3 3.0 %collective-permute-start.27 = (bf16[8,128,256]{2,1,0:T(8,128)(2,1)S(1)}, bf16[8,128,256]{2,1,0:T(8,128)(2,1)}, u32[]{:S(2)}, u32[]{:S(2)}) collective-permute-start(bf16[8,128,256]{2,1,0:T(8,128)(2,1)S(1)} %collective-permute-done.19.refs_7_), channel_id=1, source_target_pairs={{0,1},{1,0},{2,3},{3,2},{4,5},{5,4},{6,7},{7,6},{8,9},{9,8},{10,11... | collective-permute-start | bytes 1572872 | tf_op jit(solution)/shard_map/ppermute | solution.py:234
  107.0 0.8 copy-start.11
  107.0 1.0 copy-start.12
  107.1 1.1 copy-start.13

commit v4 on v0

v4 whole, which is shorter than its diff:
```python
import functools

import jax
import jax.numpy as jnp
from jax import lax
from jax.experimental import pallas as pl
from jax.experimental.pallas import tpu as pltpu
from jax.sharding import PartitionSpec as P


UNROLL = 8


def load(n_first, pieces, places, sent, sem):
    return [
        pltpu.make_async_copy(piece, sent.at[pl.ds(place, piece.shape[0])], sem.at[n_first + i])
        for i, (piece, place) in enumerate(zip(pieces, places))
    ]


def put(lists, count, here, tile, row, place):
    lists[0, count] = tile
    lists[1, count] = row
    lists[2, count] = place
    return count + here.astype(jnp.int32)


def pad(lists, count, n_blocks):
    for i in range(UNROLL):
        put(lists, count + i, count >= 0, 0, n_blocks, 0)
    return (count + UNROLL - 1) // UNROLL


def run(lists, groups, tiles, sent, acc):
    def step(group, carry):
        at = [group * UNROLL + i for i in range(UNROLL)]
        done = [
            jnp.dot(
                tiles[lists[0, i]], sent[lists[2, i]], preferred_element_type=jnp.float32
            )
            for i in at
        ]
        for i, product in zip(at, done):
            acc[lists[1, i]] += product
        return carry

    lax.fori_loop(0, groups, step, 0)


def finish(acc, weight_ref, out_ref, stage, out_sem):
    steps, group, tile_len = stage.shape[:3]
    copies = []
    for i in range(steps):
        total = acc[pl.ds(i * group, group)].reshape(group * tile_len, acc.shape[2])
        mixed = jnp.dot(
            total.astype(jnp.bfloat16), weight_ref[...], preferred_element_type=jnp.float32
        )
        stage[i] = jnp.maximum(mixed, 0.0).astype(out_ref.dtype).reshape(stage.shape[1:])
        copies.append(
            pltpu.make_async_copy(stage.at[i], out_ref.at[pl.ds(i * group, group)], out_sem.at[i])
        )
        copies[-1].start()
    for copy in copies:
        copy.wait()


def whole_kernel(places, rows_ref, slots_ref, *refs):
    n = len(places)
    tile_ref, weight_ref, out_ref, sent, tiles, acc, stage, lists, sem, out_sem = refs[n:]
    n_tiles, n_blocks = rows_ref.shape[0], out_ref.shape[0]
    copies = load(0, refs[:n], places, sent, sem)
    copies.append(pltpu.make_async_copy(tile_ref, tiles, sem.at[n]))
    for copy in copies:
        copy.start()
    acc[...] = jnp.zeros_like(acc)

    def pick(t, count):
        row = rows_ref[t]
        here = jnp.logical_and(row >= 0, row < n_blocks)
        return put(lists, count, here, t, row, slots_ref[t])

    groups = pad(lists, lax.fori_loop(0, n_tiles, pick, jnp.int32(0)), n_blocks)
    for copy in copies:
        copy.wait()
    run(lists, groups, tiles, sent, acc)
    finish(acc, weight_ref, out_ref, stage, out_sem)


def tile_copies(n_first, tile_refs, section_ref, first_slot, tiles, sem):
    each = tiles.shape[0] // 4
    copies = []
    for i, ref in enumerate(tile_refs):
        for k in range(2):
            at = pl.ds(section_ref[first_slot + k] * each, each)
            copies.append(
                pltpu.make_async_copy(
                    ref.at[at], tiles.at[pl.ds((2 * i + k) * each, each)], sem.at[n_first + 2 * i + k]
                )
            )
    return copies


def first_kernel(places, rows_ref, slots_ref, section_ref, *refs):
    n = len(places)
    pieces, tile_refs = refs[:n], refs[n : n + 2]
    acc_ref, later_ref, sent, tiles, acc, lists, sem = refs[n + 2 :]
    n_blocks = acc_ref.shape[0]
    each = tiles.shape[0] // 4
    copies = load(0, pieces, places, sent, sem)
    copies += tile_copies(n, tile_refs, section_ref, 0, tiles, sem)
    for copy in copies:
        copy.start()
    acc[...] = jnp.zeros_like(acc)
    now, later = jnp.int32(0), jnp.int32(0)
    for part in range(2):
        for slot in range(4):
            first = part * 4 * each + section_ref[slot] * each
            place = (part * 2 + slot % 2) * each

            def pick(k, count):
                row = rows_ref[first + k]
                here = jnp.logical_and(row >= 0, row < n_blocks)
                target = lists if slot < 2 else later_ref
                return put(target, count, here, place + k, row, slots_ref[first + k])

            if slot < 2:
                now = lax.fori_loop(0, each, pick, now)
            else:
                later = lax.fori_loop(0, each, pick, later)
    later_ref[3, 0] = pad(later_ref, later, n_blocks)
    groups = pad(lists, now, n_blocks)
    for copy in copies:
        copy.wait()
    run(lists, groups, tiles, sent, acc)
    save = pltpu.make_async_copy(acc.at[pl.ds(0, n_blocks)], acc_ref, sem.at[0])
    save.start()
    save.wait()


def second_kernel(places, lists, section_ref, *refs):
    n = len(places)
    pieces, tile_refs = refs[:n], refs[n : n + 2]
    acc_ref, weight_ref, out_ref, sent, tiles, acc, stage, sem, out_sem = refs[n + 2 :]
    copies = [pltpu.make_async_copy(acc_ref, acc.at[pl.ds(0, out_ref.shape[0])], sem.at[n + 4])]
    copies += tile_copies(n, tile_refs, section_ref, 2, tiles, sem)
    copies += load(0, pieces, places, sent, sem)
    for copy in copies:
        copy.start()
    for copy in copies:
        copy.wait()
    run(lists, lists[3, 0], tiles, sent, acc)
    finish(acc, weight_ref, out_ref, stage, out_sem)


HBM = pl.BlockSpec(memory_space=pltpu.HBM)
SMEM = pl.BlockSpec(memory_space=pltpu.SMEM)
VMEM = pl.BlockSpec(memory_space=pltpu.VMEM)


def settings(n_products, tile_len, width, n_bytes):
    return {
        "compiler_params": pltpu.CompilerParams(vmem_limit_bytes=60 * 1024 * 1024),
        "cost_estimate": pl.CostEstimate(
            flops=2 * n_products * tile_len * tile_len * width,
            bytes_accessed=n_bytes,
            transcendentals=0,
        ),
    }


def out_stage(n_blocks, tile_len, width):
    group = min(4, n_blocks)
    return pltpu.VMEM((n_blocks // group, group, tile_len, width), jnp.bfloat16)


def products(pieces, places, tiles, rows, slots, weight, n_sent, n_blocks):
    n_tiles, tile_len = tiles.shape[:2]
    width = weight.shape[0]
    return pl.pallas_call(
        functools.partial(whole_kernel, tuple(places)),
        out_shape=jax.ShapeDtypeStruct((n_blocks, tile_len, weight.shape[1]), jnp.bfloat16),
        in_specs=[SMEM, SMEM] + [HBM] * (len(pieces) + 1) + [VMEM],
        out_specs=HBM,
        scratch_shapes=[
            pltpu.VMEM((n_sent, tile_len, width), jnp.bfloat16),
            pltpu.VMEM(tiles.shape, jnp.bfloat16),
            pltpu.VMEM((n_blocks + 1, tile_len, width), jnp.float32),
            out_stage(n_blocks, tile_len, weight.shape[1]),
            pltpu.SMEM((3, n_tiles + UNROLL), jnp.int32),
            pltpu.SemaphoreType.DMA((len(pieces) + 1,)),
            pltpu.SemaphoreType.DMA((n_blocks // min(4, n_blocks),)),
        ],
        **settings(n_tiles, tile_len, width, 16 << 20),
    )(rows, slots, *pieces, tiles, weight)


def products_in_two(pieces, places, tile_list, rows, slots, section_at, weight, n_blocks):
    n_tiles, tile_len = 2 * tile_list[0].shape[0], tile_list[0].shape[1]
    width = weight.shape[0]
    n_sent = 2 * sum(piece.shape[0] for piece in pieces[0][: len(pieces[0]) // 2])
    scratch = [
        pltpu.VMEM((n_sent, tile_len, width), jnp.bfloat16),
        pltpu.VMEM((n_tiles // 2, tile_len, tile_len), jnp.bfloat16),
        pltpu.VMEM((n_blocks + 1, tile_len, width), jnp.float32),
    ]
    lists = (4, n_tiles + UNROLL)
    first, second = pieces
    sums, later = pl.pallas_call(
        functools.partial(first_kernel, tuple(places[0])),
        out_shape=(
            jax.ShapeDtypeStruct((n_blocks, tile_len, width), jnp.float32),
            jax.ShapeDtypeStruct(lists, jnp.int32),
        ),
        in_specs=[SMEM] * 3 + [HBM] * (len(first) + 2),
        out_specs=(HBM, SMEM),
        scratch_shapes=scratch
        + [pltpu.SMEM(lists, jnp.int32), pltpu.SemaphoreType.DMA((len(first) + 4,))],
        **settings(n_tiles // 2, tile_len, width, 10 << 20),
    )(rows, slots, section_at, *first, *tile_list)
    return pl.pallas_call(
        functools.partial(second_kernel, tuple(places[1])),
        out_shape=jax.ShapeDtypeStruct((n_blocks, tile_len, weight.shape[1]), jnp.bfloat16),
        in_specs=[SMEM] * 2 + [HBM] * (len(second) + 3) + [VMEM],
        out_specs=HBM,
        scratch_shapes=scratch
        + [
            out_stage(n_blocks, tile_len, weight.shape[1]),
            pltpu.SemaphoreType.DMA((len(second) + 5,)),
            pltpu.SemaphoreType.DMA((n_blocks // min(4, n_blocks),)),
        ],
        **settings(n_tiles // 2, tile_len, width, 12 << 20),
    )(later, section_at, *second, *tile_list, sums, weight)


def lines_kernel(owner_ref, blocks_ref, order_ref, out_ref):
    me, rep = lax.axis_index("dom"), lax.axis_index("rep")
    sections, n_send = blocks_ref.shape
    section = jnp.int32(0)
    for s in range(sections):
        section = jnp.where(owner_ref[s] == me, s, section)
    each = n_send // 8
    for group, across in enumerate((3, 1 + rep, 2 - rep, 0)):
        base = rep * (n_send // 2) + ((me % 4) ^ across) * each
        for j in range(each):
            block = blocks_ref[section, base + j]
            out_ref[pl.ds(group * each + j, 1), :] = order_ref[pl.ds(block, 1), :]


def share_lines(node_order, section_owner, send_blocks, tile_len):
    return pl.pallas_call(
        lines_kernel,
        out_shape=jax.ShapeDtypeStruct((send_blocks.shape[1] // 2, tile_len), jnp.int32),
        in_specs=[SMEM, SMEM, VMEM],
        out_specs=VMEM,
    )(section_owner, send_blocks, node_order[0].reshape(-1, tile_len))


def share_rows(node_order, section_owner, send_blocks, tile_len):
    me = lax.axis_index("dom")
    sections, n_send = send_blocks.shape
    mine = (section_owner == me).astype(jnp.int32)
    section = jnp.sum(mine * jnp.arange(sections, dtype=jnp.int32))
    share = n_send // lax.axis_size("rep")
    picks = lax.dynamic_slice(
        send_blocks, (section, lax.axis_index("rep") * share), (1, share)
    )[0]
    order = node_order[0].reshape(-1, tile_len)
    return order.at[picks].get(mode="promise_in_bounds")


def move(value, pairs):
    return lax.ppermute(value, "dom", pairs)


def flip(bits):
    return [(i, i ^ bits) for i in range(16)]


def cross(value, turn):
    pairs = []
    for i in range(16):
        for core in (0, 1):
            pairs.append((2 * i + core, 2 * (i ^ (1 if core == turn else 2)) + core))
    return lax.ppermute(value, ("dom", "rep"), pairs)


def place_of(across, core):
    return jnp.where(core == 0, across, (across & 1) * 2 + across // 2)


def quad_scatter(features, lines):
    each = lines.shape[0] // 4

    def rows(first):
        taken = features.at[lines[first : first + 2 * each].reshape(-1)].get(
            mode="promise_in_bounds"
        )
        return taken.reshape(2 * each, lines.shape[1], features.shape[1])

    by_first = cross(rows(0), 0)
    kept = rows(2 * each)
    by_second = cross(jnp.concatenate([kept[:each], by_first[:each]]), 1)
    return kept[each:], by_first[each:], by_second[:each], by_second[each:]


INWARD = [(i, i + 4) for i in range(4)] + [(i, i - 4) for i in range(12, 16)]
MIDDLE = [(i, i + 4) for i in range(4, 8)] + [(i, i - 4) for i in range(8, 12)]
OUTWARD = [(i, i - 4) for i in range(4, 8)] + [(i, i + 4) for i in range(8, 12)]


def tie(value, after):
    return lax.optimization_barrier((value, after))[0]


def along_z(first, at, z, near):
    inner = jnp.logical_or(z == 1, z == 2)
    own = at == z
    known = jnp.where(own, first, near)
    across = move(known, MIDDLE)
    beyond = move(jnp.where(own, first, across), OUTWARD)
    same_half = (at // 2) == (z // 2)
    return jnp.where(inner, jnp.where(same_half, known, across), jnp.where(own, first, beyond))


def along_z_ends(first, z):
    outer = jnp.logical_or(z == 0, z == 3)
    came = move(first, INWARD)
    near = jnp.where(outer, first, came)
    across = move(came, MIDDLE)
    beyond = move(across, OUTWARD)
    return came, near, jnp.where(outer, beyond, across)


def quad_gather(own, after):
    came = cross(own if after is None else tie(own, after), 0)
    pair = jnp.concatenate([own, came])
    return came, [pair, cross(pair, 1)]


def gather_small(features, lines, section_owner):
    me = lax.axis_index("dom")
    quad, z = me % 4, me // 4
    held = quad_scatter(features, lines)
    is_first, is_last = section_owner == 0, section_owner == 15
    other = jnp.logical_not(jnp.logical_or(is_first, is_last))
    rank = jnp.cumsum(other.astype(jnp.int32)) - 1
    owners = [
        jnp.sum(jnp.where(jnp.logical_and(other, rank == i), section_owner, 0)) for i in (0, 1)
    ]
    low = z < 2
    slot = jnp.where(other, 2 + rank, jnp.where(is_first == low, 0, 1))

    def of(source):
        return lax.select_n(place_of(quad ^ source, lax.axis_index("rep")), *held)

    came, near, far = along_z_ends(of(jnp.where(low, 0, 3)), z)
    quarters = [near, far]
    for owner in owners:
        first = of(owner % 4)
        came = move(tie(first, came), INWARD)
        quarters.append(along_z(first, owner // 4, z, came))
    pieces, after = [], None
    for quarter in quarters:
        after, made = quad_gather(quarter, after)
        pieces += made
    return pieces, slot


def body(features, node_order, section_owner, send_blocks, tile_rows, tile_cols, tiles, weight):
    width = features.shape[1]
    tile_len = tiles.shape[3]
    blocks = features.shape[0] // tile_len
    n_dom, n_rep = lax.axis_size("dom"), lax.axis_size("rep")
    sections, n_send = send_blocks.shape
    me, rep = lax.axis_index("dom"), lax.axis_index("rep")
    n_blocks = blocks // n_rep
    small = n_dom == 16 and n_rep == 2 and n_send == n_dom * n_rep

    own_tiles = tiles[0].reshape(-1, tile_len, tile_len)
    numbers = jnp.stack([tile_rows[0], tile_cols[0]])
    if small:
        swap = [(0, 1), (1, 0)]

        def exchange(value):
            return lax.ppermute(value, "rep", swap)

        tile_list = [own_tiles, exchange(own_tiles)]
        numbers = jnp.stack([numbers, exchange(numbers)])
        rows = (numbers[:, 0] - rep * n_blocks).reshape(-1)
        cols = numbers[:, 1]
        lines = share_lines(node_order, section_owner, send_blocks, tile_len)
        pieces, slot = gather_small(features, lines, section_owner)
        quarter = n_dom // 4
        holder, block = cols // n_dom, cols % n_dom
        at = place_of((block // quarter) ^ (me % 4), holder) * quarter + block % quarter
        slots = ((holder != rep) * 2 + slot[:, None] % 2) * n_dom + at
        section_at = jnp.sum(
            jnp.where(slot[None, :] == jnp.arange(4)[:, None], jnp.arange(sections), 0), axis=1
        ).astype(jnp.int32)
        parts, places = [], []
        for first in (0, 4):
            own = pieces[first : first + 4]
            parts.append(own + [exchange(piece) for piece in own])
            places.append([i * 2 * quarter for i in range(8)])
        hidden = products_in_two(
            parts, places, tile_list, rows, slots.reshape(-1), section_at, weight, n_blocks
        )
    else:
        tile_list = lax.all_gather(own_tiles, "rep", axis=0, tiled=True)
        numbers = lax.all_gather(numbers, "rep", axis=0)
        rows = (numbers[:, 0] - rep * n_blocks).reshape(-1)
        lines = share_rows(node_order, section_owner, send_blocks, tile_len)
        mine = features.at[lines.reshape(-1)].get(mode="promise_in_bounds")
        landed = lax.all_to_all(mine, "dom", 0, 0, tiled=True)
        landed = landed.reshape(n_dom, -1, width)
        shard = landed.at[section_owner].get(mode="promise_in_bounds")
        whole = lax.all_gather(shard, ("rep", "dom"), axis=0)
        whole = whole.transpose(1, 0, 2, 3).reshape(sections * n_send, tile_len, width)
        slots = jnp.arange(sections)[:, None] * n_send + numbers[:, 1]
        hidden = products(
            [whole], [0], tile_list, rows, slots.reshape(-1), weight, sections * n_send, n_blocks
        )
    return hidden.reshape(n_blocks * tile_len, -1)


def solution(mesh):
    return jax.shard_map(
        body,
        mesh=mesh,
        in_specs=(
            P("dom", None),
            P("dom", None),
            P(),
            P(),
            P("dom", None, "rep"),
            P("dom", None, "rep"),
            P("dom", None, "rep", None, None),
            P(),
        ),
        out_specs=P(("dom", "rep"), None),
        check_vma=False,
    )
```

time: 355 us -> 123 us (0.35)
  waiting for transfers between devices: 213 us -> 23.4 us
  local copies, waits for them, and re-layouts: 71.8 us -> 16.5 us
  starting transfers between devices: 0.38 us -> 55.2 us
  other arithmetic: 37.2 us -> 4.61 us
  Pallas kernels: 0 us -> 17.2 us
  matrix products: 15.3 us -> 0 us
  between operations: 16.1 us -> 5.6 us
    psum x1 -> x0, waiting for transfers between devices: 172 us -> none  [spread(): return lax.psum(kept, axis)]
    ppermute x0 -> x29, starting transfers between devices: none -> 55.2 us  [the longest x10 27.1 us: exchange(): return lax.ppermute(value, 'rep', swap)]
    gather x9 -> x2, local copies, waits for them, and re-layouts: 54.6 us -> 13.7 us  [rows(): features.at[lines[first:first + 2 * each].reshape(-1)]]
    all_gather x4 -> x0, waiting for transfers between devices: 26.1 us -> none  [body(): arrived = lax.all_gather(landed, 'rep', axis=0, tiled=True)]
    ppermute x0 -> x29, waiting for transfers between devices: none -> 23.4 us  [the longest x10 11.9 us: cross(): return lax.ppermute(value, ('dom', 'rep'), pairs)]
    scatter-add x4 -> x0, other arithmetic: 19.5 us -> none  [body(): total = total.at[tile_rows[0, s]].add(product)]
    pallas_call x0 -> x3, Pallas kernels: none -> 17.2 us  [the longest x1 8.18 us: products_in_two(): pl.pallas_call(functools.partial(second_kernel, tuple(places[1])), out_sh...]
    dot_general x5 -> x0, matrix products: 15.3 us -> none  [the longest x4 11.7 us: body(): jnp.einsum('kij,kjf->kif', tiles[0, s], chosen, preferred_element_type=jn...]
  transfers between devices with their start and end apart: 6 -> 29, of which waited for: 6 -> 9; matrix products, arithmetic and copies ran while one was open for 7% -> 9% of each run, Pallas kernels for 0% -> 6%
where the time goes in v4:
time: 123 us; the launch traced here: 122 us
  starting transfers between devices  55.2 us (45%)
  waiting for transfers between devices  23.4 us (19%)
  Pallas kernels  17.2 us (14%)
  local copies, waits for them, and re-layouts  16.5 us (13%)
  between operations  5.6 us (5%)
  other arithmetic  4.61 us (4%)
    ppermute x10, starting transfers between devices, exchange(): return lax.ppermute(value, 'rep', swap)  27.1 us
    ppermute x9, starting transfers between devices, move(): return lax.ppermute(value, 'dom', pairs)  16.7 us
    gather x2, local copies, waits for them, and re-layouts, rows(): features.at[lines[first:first + 2 * each].reshape(-1)]  13.7 us
    ppermute x10, waiting for transfers between devices, cross(): return lax.ppermute(value, ('dom', 'rep'), pairs)  11.9 us
    ppermute x10, starting transfers between devices, cross(): return lax.ppermute(value, ('dom', 'rep'), pairs)  11.5 us
    ppermute x9, waiting for transfers between devices, move(): return lax.ppermute(value, 'dom', pairs)  11.4 us
    pallas_call x1, Pallas kernels, products_in_two(): pl.pallas_call(functools.partial(second_kernel, tuple(places[1])), out_sh...  8.18 us
    pallas_call x1, Pallas kernels, products_in_two(): pl.pallas_call(functools.partial(first_kernel, tuple(places[0])), out_sha...  7.65 us
  transfers between devices with their start and end apart: 29, of which 9 were waited for; matrix products, arithmetic and copies ran while one was open for 9% of the time, Pallas kernels for 6%

profile of v4, /device:TPU:1, one launch (start us, length us, event | category | flops | bytes accessed | tf_op | source)
XLA Modules:
  0.0 122.5 jit_solution(7134522237977724078)
XLA Ops:
  0.0 1.4 %shard_map.82 = s32[16,128]{1,0:T(8,128)} custom-call(s32[4]{0:T(128)} %owner_ref.1, s32[4,32]{1,0:T(4,128)} %blocks_ref.1, s32[64,128]{1,0:T(8,128)} %bitcast.34), custom_call_target="tpu_custom_call" | custom-call | tf_op jit(solution)/shard_map/pallas_call | solution.py:250
  1.4 0.7 fusion.15
  2.2 7.3 %gather_fusion.1 = bf16[1024,256]{1,0:T(8,128)(2,1)} fusion(bf16[8192,256]{1,0:T(8,128)(2,1)} %param.8, s32[1024]{0:T(1024)S(1)} %get-tuple-element.34), kind=kCustom, calls=%fused_computation.1 | custom fusion | bytes 1052672 | tf_op jit(solution)/shard_map/gather | solution.py:295
  9.5 2.1 %collective-permute-start.1 = (bf16[8,128,256]{2,1,0:T(8,128)(2,1)}, bf16[8,128,256]{2,1,0:T(8,128)(2,1)S(1)}, u32[]{:S(2)}, u32[]{:S(2)}) collective-permute-start(bf16[8,128,256]{2,1,0:T(8,128)(2,1)} %bitcast.10), channel_id=1, source_target_pairs={{0,2},{1,5},{2,0},{3,7},{4,6},{5,1},{6,4},{7,3},{8,10},{9,13},{10,... | collective-permute-start | bytes 1572872 | tf_op jit(solution)/shard_map/ppermute | solution.py:284
  11.6 6.3 %gather_fusion = bf16[1024,256]{1,0:T(8,128)(2,1)S(1)} fusion(bf16[8192,256]{1,0:T(8,128)(2,1)} %param.8, s32[1024]{0:T(1024)S(1)} %get-tuple-element.35), kind=kCustom, calls=%fused_computation | custom fusion | bytes 1052672 | tf_op jit(solution)/shard_map/gather | solution.py:295
  18.0 0.7 collective-permute-done.1
  18.7 1.5 %collective-permute-start.2 = (bf16[8,128,256]{2,1,0:T(8,128)(2,1)S(1)}, bf16[8,128,256]{2,1,0:T(8,128)(2,1)}, u32[]{:S(2)}, u32[]{:S(2)}) collective-permute-start(bf16[8,128,256]{2,1,0:T(8,128)(2,1)S(1)} %pad_maximum_fusion), channel_id=1, source_target_pairs={{0,4},{1,3},{2,6},{3,1},{4,0},{5,7},{6,2},{7,5},{8,12},{9,11},{10,... | collective-permute-start | bytes 1572872 | tf_op jit(solution)/shard_map/ppermute | solution.py:284
  20.2 0.2 reduce-window.9
  20.4 0.7 fusion.11
  24.9 2.3 %collective-permute-done.2 = bf16[8,128,256]{2,1,0:T(8,128)(2,1)} collective-permute-done((bf16[8,128,256]{2,1,0:T(8,128)(2,1)S(1)}, bf16[8,128,256]{2,1,0:T(8,128)(2,1)}, u32[]{:S(2)}, u32[]{:S(2)}) %collective-permute-start.2) | collective-permute-done | bytes 524320 | tf_op jit(solution)/shard_map/ppermute | solution.py:284
  27.2 1.2 select_select_fusion.1
  28.4 3.4 %collective-permute-start.3 = (bf16[4,128,256]{2,1,0:T(8,128)(2,1)S(1)}, bf16[4,128,256]{2,1,0:T(8,128)(2,1)S(1)}, u32[]{:S(2)}, u32[]{:S(2)}) collective-permute-start(bf16[4,128,256]{2,1,0:T(8,128)(2,1)S(1)} %get-tuple-element.25), channel_id=1, source_target_pairs={{0,8},{2,10},{4,12},{6,14},{24,16},{26,18},{28,20},{30,22},{1,9},{... | collective-permute-start | bytes 786440 | tf_op jit(solution)/shard_map/ppermute | solution.py:272
  31.9 3.3 %collective-permute-done.3 = bf16[4,128,256]{2,1,0:T(8,128)(2,1)S(1)} collective-permute-done((bf16[4,128,256]{2,1,0:T(8,128)(2,1)S(1)}, bf16[4,128,256]{2,1,0:T(8,128)(2,1)S(1)}, u32[]{:S(2)}, u32[]{:S(2)}) %collective-permute-start.3) | collective-permute-done | bytes 262176 | tf_op jit(solution)/shard_map/ppermute | solution.py:272
  35.2 3.8 %collective-permute-start.15 = (bf16[4,128,256]{2,1,0:T(8,128)(2,1)S(1)}, bf16[4,128,256]{2,1,0:T(8,128)(2,1)S(1)}, u32[]{:S(2)}, u32[]{:S(2)}) collective-permute-start(bf16[4,128,256]{2,1,0:T(8,128)(2,1)S(1)} %get-tuple-element.14), channel_id=1, source_target_pairs={{0,8},{2,10},{4,12},{6,14},{24,16},{26,18},{28,20},{30,22},{1,9},{... | collective-permute-start | bytes 786440 | tf_op jit(solution)/shard_map/ppermute | solution.py:272
  39.0 3.9 %collective-permute-start.14 = (bf16[64,128,128]{2,1,0:T(8,128)(2,1)S(1)}, bf16[64,128,128]{2,1,0:T(8,128)(2,1)}, u32[]{:S(2)}, u32[]{:S(2)}) collective-permute-start(bf16[64,128,128]{2,1,0:T(8,128)(2,1)S(1)} %bitcast.31), channel_id=1, source_target_pairs={{0,1},{1,0},{2,3},{3,2},{4,5},{5,4},{6,7},{7,6},{8,9},{9,8},{10,11... | collective-permute-start | bytes 6291464 | tf_op jit(solution)/shard_map/ppermute | solution.py:385
  44.2 0.7 collective-permute-start.6
  44.9 0.0 collective-permute-done.15
  44.9 0.0 copy-start.15
  44.9 3.5 %collective-permute-start.20 = (bf16[4,128,256]{2,1,0:T(8,128)(2,1)S(1)}, bf16[4,128,256]{2,1,0:T(8,128)(2,1)S(1)}, u32[]{:S(2)}, u32[]{:S(2)}) collective-permute-start(bf16[4,128,256]{2,1,0:T(8,128)(2,1)S(1)} %get-tuple-element.16), channel_id=1, source_target_pairs={{0,8},{2,10},{4,12},{6,14},{24,16},{26,18},{28,20},{30,22},{1,9},{... | collective-permute-start | bytes 786440 | tf_op jit(solution)/shard_map/ppermute | solution.py:272
  48.5 0.7 collective-permute-start.16
  49.3 1.3 %collective-permute-start.4 = (bf16[4,128,256]{2,1,0:T(8,128)(2,1)S(1)}, bf16[4,128,256]{2,1,0:T(8,128)(2,1)S(1)}, u32[]{:S(2)}, u32[]{:S(2)}) collective-permute-start(bf16[4,128,256]{2,1,0:T(8,128)(2,1)S(1)} %broadcast_select_fusion.5), channel_id=1, source_target_pairs={{0,2},{1,5},{2,0},{3,7},{4,6},{5,1},{6,4},{7,3},{8,10},{9,13},{10,... | collective-permute-start | bytes 786440 | tf_op jit(solution)/shard_map/ppermute | solution.py:284
  50.6 1.3 %collective-permute-start.7 = (bf16[4,128,256]{2,1,0:T(8,128)(2,1)S(1)}, bf16[4,128,256]{2,1,0:T(8,128)(2,1)S(1)}, u32[]{:S(2)}, u32[]{:S(2)}) collective-permute-start(bf16[4,128,256]{2,1,0:T(8,128)(2,1)S(1)} %collective-permute-done.6), channel_id=1, source_target_pairs={{8,0},{10,2},{12,4},{14,6},{16,24},{18,26},{20,28},{22,30},{9,1},{... | collective-permute-start | bytes 786440 | tf_op jit(solution)/shard_map/ppermute | solution.py:272
  51.9 0.7 collective-permute-start.21
  52.6 0.0 collective-permute-done.16
  52.6 1.3 %collective-permute-start.17 = (bf16[4,128,256]{2,1,0:T(8,128)(2,1)S(1)}, bf16[4,128,256]{2,1,0:T(8,128)(2,1)S(1)}, u32[]{:S(2)}, u32[]{:S(2)}) collective-permute-start(bf16[4,128,256]{2,1,0:T(8,128)(2,1)S(1)} %broadcast_select_fusion.2), channel_id=1, source_target_pairs={{8,0},{10,2},{12,4},{14,6},{16,24},{18,26},{20,28},{22,30},{9,1},{... | collective-permute-start | bytes 786440 | tf_op jit(solution)/shard_map/ppermute | solution.py:272
  53.9 4.2 %collective-permute-done.7 = bf16[4,128,256]{2,1,0:T(8,128)(2,1)S(1)} collective-permute-done((bf16[4,128,256]{2,1,0:T(8,128)(2,1)S(1)}, bf16[4,128,256]{2,1,0:T(8,128)(2,1)S(1)}, u32[]{:S(2)}, u32[]{:S(2)}) %collective-permute-start.7) | collective-permute-done | bytes 262176 | tf_op jit(solution)/shard_map/ppermute | solution.py:272
  58.2 0.0 collective-permute-done.4
  58.2 1.3 %collective-permute-start.8 = (bf16[4,128,256]{2,1,0:T(8,128)(2,1)S(1)}, bf16[4,128,256]{2,1,0:T(8,128)(2,1)S(1)}, u32[]{:S(2)}, u32[]{:S(2)}) collective-permute-start(bf16[4,128,256]{2,1,0:T(8,128)(2,1)S(1)} %broadcast_select_fusion.4), channel_id=1, source_target_pairs={{0,2},{1,5},{2,0},{3,7},{4,6},{5,1},{6,4},{7,3},{8,10},{9,13},{10,... | collective-permute-start | bytes 786440 | tf_op jit(solution)/shard_map/ppermute | solution.py:284
  59.6 1.3 %collective-permute-start.22 = (bf16[4,128,256]{2,1,0:T(8,128)(2,1)S(1)}, bf16[4,128,256]{2,1,0:T(8,128)(2,1)S(1)}, u32[]{:S(2)}, u32[]{:S(2)}) collective-permute-start(bf16[4,128,256]{2,1,0:T(8,128)(2,1)S(1)} %broadcast_select_fusion), channel_id=1, source_target_pairs={{8,0},{10,2},{12,4},{14,6},{16,24},{18,26},{20,28},{22,30},{9,1},{... | collective-permute-start | bytes 786440 | tf_op jit(solution)/shard_map/ppermute | solution.py:272
  60.9 3.9 %collective-permute-done.17 = bf16[4,128,256]{2,1,0:T(8,128)(2,1)S(1)} collective-permute-done((bf16[4,128,256]{2,1,0:T(8,128)(2,1)S(1)}, bf16[4,128,256]{2,1,0:T(8,128)(2,1)S(1)}, u32[]{:S(2)}, u32[]{:S(2)}) %collective-permute-start.17) | collective-permute-done | bytes 262176 | tf_op jit(solution)/shard_map/ppermute | solution.py:272
  64.8 0.0 collective-permute-done.8
  64.8 1.3 %collective-permute-start.18 = (bf16[4,128,256]{2,1,0:T(8,128)(2,1)S(1)}, bf16[4,128,256]{2,1,0:T(8,128)(2,1)S(1)}, u32[]{:S(2)}, u32[]{:S(2)}) collective-permute-start(bf16[4,128,256]{2,1,0:T(8,128)(2,1)S(1)} %select_select_fusion.2), channel_id=1, source_target_pairs={{0,2},{1,5},{2,0},{3,7},{4,6},{5,1},{6,4},{7,3},{8,10},{9,13},{10,... | collective-permute-start | bytes 786440 | tf_op jit(solution)/shard_map/ppermute | solution.py:284
  66.2 0.0 copy-start.1
  66.2 1.3 %collective-permute-start.5 = (bf16[8,128,256]{2,1,0:T(8,128)(2,1)S(1)}, bf16[8,128,256]{2,1,0:T(8,128)(2,1)S(1)}, u32[]{:S(2)}, u32[]{:S(2)}) collective-permute-start(bf16[8,128,256]{2,1,0:T(8,128)(2,1)S(1)} %pad_maximum_fusion.1.refs_0_), channel_id=1, source_target_pairs={{0,4},{1,3},{2,6},{3,1},{4,0},{5,7},{6,2},{7,5},{8,12},{9,11},{10,... | collective-permute-start | bytes 1572872 | tf_op jit(solution)/shard_map/ppermute | solution.py:284
  67.5 5.4 %collective-permute-start.10 = (bf16[8,128,256]{2,1,0:T(8,128)(2,1)S(1)}, bf16[8,128,256]{2,1,0:T(8,128)(2,1)S(1)}, u32[]{:S(2)}, u32[]{:S(2)}) collective-permute-start(bf16[8,128,256]{2,1,0:T(8,128)(2,1)S(1)} %pad_maximum_fusion.1.refs_0_), channel_id=1, source_target_pairs={{0,1},{1,0},{2,3},{3,2},{4,5},{5,4},{6,7},{7,6},{8,9},{9,8},{10,11... | collective-permute-start | bytes 1572872 | tf_op jit(solution)/shard_map/ppermute | solution.py:385
  72.9 0.0 collective-permute-done.22
  72.9 0.1 collective-permute-start.23
  73.1 6.2 %collective-permute-start = (s32[2,4,16]{2,1,0:T(4,128)S(1)}, s32[2,4,16]{2,1,0:T(4,128)S(1)}, u32[]{:S(2)}, u32[]{:S(2)}) collective-permute-start(s32[2,4,16]{2,1,0:T(4,128)S(1)} %constant_dynamic-update-slice_fusion), channel_id=1, source_target_pairs={{0,1},{1,0},{2,3},{3,2},{4,5},{5,4},{6,7},{7,6},{8,9},{9,8},{10,11... | collective-permute-start | bytes 1544 | tf_op jit(solution)/shard_map/ppermute | solution.py:385
  79.4 0.3 collective-permute-start.9
  79.8 1.6 %collective-permute-done.23 = bf16[4,128,256]{2,1,0:T(8,128)(2,1)S(1)} collective-permute-done((bf16[4,128,256]{2,1,0:T(8,128)(2,1)S(1)}, bf16[4,128,256]{2,1,0:T(8,128)(2,1)S(1)}, u32[]{:S(2)}, u32[]{:S(2)}) %collective-permute-start.23) | collective-permute-done | bytes 262176 | tf_op jit(solution)/shard_map/ppermute | solution.py:284
  81.4 4.3 %collective-permute-start.11 = (bf16[8,128,256]{2,1,0:T(8,128)(2,1)S(1)}, bf16[8,128,256]{2,1,0:T(8,128)(2,1)S(1)}, u32[]{:S(2)}, u32[]{:S(2)}) collective-permute-start(bf16[8,128,256]{2,1,0:T(8,128)(2,1)S(1)} %collective-permute-done.5.refs_1_), channel_id=1, source_target_pairs={{0,1},{1,0},{2,3},{3,2},{4,5},{5,4},{6,7},{7,6},{8,9},{9,8},{10,11... | collective-permute-start | bytes 1572872 | tf_op jit(solution)/shard_map/ppermute | solution.py:385
  85.7 0.8 pad_maximum_fusion.4.refs_2_
  86.5 0.0 collective-permute-start.12
  86.6 2.2 %collective-permute-start.19 = (bf16[8,128,256]{2,1,0:T(8,128)(2,1)S(1)}, bf16[8,128,256]{2,1,0:T(8,128)(2,1)}, u32[]{:S(2)}, u32[]{:S(2)}) collective-permute-start(bf16[8,128,256]{2,1,0:T(8,128)(2,1)S(1)} %pad_maximum_fusion.3.refs_0_), channel_id=1, source_target_pairs={{0,4},{1,3},{2,6},{3,1},{4,0},{5,7},{6,2},{7,5},{8,12},{9,11},{10,... | collective-permute-start | bytes 1572872 | tf_op jit(solution)/shard_map/ppermute | solution.py:284
  88.8 0.1 collective-permute-start.24
  88.9 0.6 collective-permute-done.9.refs_3_
  89.5 2.6 %collective-permute-start.13 = (bf16[8,128,256]{2,1,0:T(8,128)(2,1)}, bf16[8,128,256]{2,1,0:T(8,128)(2,1)}, u32[]{:S(2)}, u32[]{:S(2)}) collective-permute-start(bf16[8,128,256]{2,1,0:T(8,128)(2,1)} %collective-permute-done.9.refs_3_), channel_id=1, source_target_pairs={{0,1},{1,0},{2,3},{3,2},{4,5},{5,4},{6,7},{7,6},{8,9},{9,8},{10,11... | collective-permute-start | bytes 1572872 | tf_op jit(solution)/shard_map/ppermute | solution.py:385
  92.1 0.1 collective-permute-start.25
  92.2 0.4 collective-permute-start.27
  92.7 3.1 %collective-permute-done.19.refs_1_ = bf16[8,128,256]{2,1,0:T(8,128)(2,1)} collective-permute-done((bf16[8,128,256]{2,1,0:T(8,128)(2,1)S(1)}, bf16[8,128,256]{2,1,0:T(8,128)(2,1)}, u32[]{:S(2)}, u32[]{:S(2)}) %collective-permute-start.19) | collective-permute-done | bytes 524320 | tf_op jit(solution)/shard_map/ppermute | solution.py:284
  95.8 2.0 %collective-permute-start.26 = (bf16[8,128,256]{2,1,0:T(8,128)(2,1)}, bf16[8,128,256]{2,1,0:T(8,128)(2,1)S(1)}, u32[]{:S(2)}, u32[]{:S(2)}) collective-permute-start(bf16[8,128,256]{2,1,0:T(8,128)(2,1)} %collective-permute-done.19.refs_1_), channel_id=1, source_target_pairs={{0,1},{1,0},{2,3},{3,2},{4,5},{5,4},{6,7},{7,6},{8,9},{9,8},{10,11... | collective-permute-start | bytes 1572872 | tf_op jit(solution)/shard_map/ppermute | solution.py:385
  97.8 3.5 %collective-permute-done.24.refs_3_ = bf16[8,128,256]{2,1,0:T(8,128)(2,1)S(1)} collective-permute-done((bf16[8,128,256]{2,1,0:T(8,128)(2,1)}, bf16[8,128,256]{2,1,0:T(8,128)(2,1)S(1)}, u32[]{:S(2)}, u32[]{:S(2)}) %collective-permute-start.24) | collective-permute-done | bytes 524320 | tf_op jit(solution)/shard_map/ppermute | solution.py:284
  101.3 2.1 %collective-permute-start.28 = (bf16[8,128,256]{2,1,0:T(8,128)(2,1)S(1)}, bf16[8,128,256]{2,1,0:T(8,128)(2,1)}, u32[]{:S(2)}, u32[]{:S(2)}) collective-permute-start(bf16[8,128,256]{2,1,0:T(8,128)(2,1)S(1)} %collective-permute-done.24.refs_3_), channel_id=1, source_target_pairs={{0,1},{1,0},{2,3},{3,2},{4,5},{5,4},{6,7},{7,6},{8,9},{9,8},{10,11... | collective-permute-start | bytes 1572872 | tf_op jit(solution)/shard_map/ppermute | solution.py:385
  103.4 0.1 add.110
  103.4 0.1 add.111
  103.5 0.7 select_reduce_fusion.section_ref
  104.2 0.6 sub.58.rows_ref
  104.8 0.1 squeeze.4
  104.9 0.6 fusion.5.slots_ref
  105.5 7.6 %shard_map.83 = (f32[32,128,256]{2,1,0:T(8,128)}, s32[4,136]{1,0:T(4,128)}) custom-call(s32[128]{0:T(128)} %sub.58.rows_ref, s32[128]{0:T(128)} %fusion.5.slots_ref, s32[4]{0:T(128)} %select_reduce_fusion.section_ref, bf16[8,128,256]{2,1,0:T(8,128)(2,1)} %copy-done.1, bf16[8,128,256]{2,1,0:T(8,128)(2,1)} %copy-done.4, bf16[8,128,256]{2,1,0:T(8,128)(2,1)} %copy-done.3, ...), custom_call_target="tpu_custom_call" | custom-call | flops 536870912 | bytes 10485760 | tf_op jit(solution)/shard_map/pallas_call | solution.py:208
  113.2 0.7 copy-done.9
  113.9 0.2 copy-done.10
  114.1 0.2 copy-done.11
  114.3 8.2 %shard_map.84 = bf16[32,128,256]{2,1,0:T(8,128)(2,1)} custom-call(s32[4,136]{1,0:T(4,128)} %get-tuple-element.13.lists, s32[4]{0:T(128)} %select_reduce_fusion.section_ref, bf16[8,128,256]{2,1,0:T(8,128)(2,1)} %copy-done.2, bf16[8,128,256]{2,1,0:T(8,128)(2,1)} %collective-permute-done.19.refs_1_, bf16[8,128,256]{2,1,0:T(8,128)(2,1)} %pad_maximum_fusion.4.refs_2_, ...), custom_call_target="tpu_custom_call" | custom-call | flops 536870912 | bytes 12582912 | tf_op jit(solution)/shard_map/pallas_call | solution.py:220
  (63 shorter events, 0.7 us)
Async XLA Ops:
  9.5 10.7 %copy-start.13 = (s32[4]{0:T(128)S(1)}, s32[4]{0:T(128)}, u32[]{:S(2)}) copy-start(s32[4]{0:T(128)} %owner_ref.1) | copy-start | bytes 52
  9.5 9.1 %collective-permute-start.1 = (bf16[8,128,256]{2,1,0:T(8,128)(2,1)}, bf16[8,128,256]{2,1,0:T(8,128)(2,1)S(1)}, u32[]{:S(2)}, u32[]{:S(2)}) collective-permute-start(bf16[8,128,256]{2,1,0:T(8,128)(2,1)} %bitcast.10), channel_id=1, source_target_pairs={{0,2},{1,5},{2,0},{3,7},{4,6},{5,1},{6,4},{7,3},{8,10},{9,13},{10,... | collective-permute-start | bytes 1572872 | tf_op jit(solution)/shard_map/ppermute | solution.py:284
  11.6 27.4 %copy-start = (bf16[1,4,16,128,128]{4,3,2,1,0:T(8,128)(2,1)S(1)}, bf16[1,4,16,128,128]{4,3,2,1,0:T(8,128)(2,1)}, u32[]{:S(2)}) copy-start(bf16[1,4,16,128,128]{4,3,2,1,0:T(8,128)(2,1)} %param.14) | copy-start | bytes 6291460
  11.6 32.6 %copy-start.14 = (s32[1,4,16]{2,1,0:T(4,128)S(1)}, s32[1,4,16]{2,1,0:T(4,128)}, u32[]{:S(2)}) copy-start(s32[1,4,16]{2,1,0:T(4,128)} %param.12) | copy-start | bytes 772
  18.6 8.6 %copy-start.12 = (bf16[8,128,256]{2,1,0:T(8,128)(2,1)}, bf16[8,128,256]{2,1,0:T(8,128)(2,1)S(1)}, u32[]{:S(2)}) copy-start(bf16[8,128,256]{2,1,0:T(8,128)(2,1)S(1)} %collective-permute-done.1) | copy-start | bytes 1572868
  18.7 8.5 %collective-permute-start.2 = (bf16[8,128,256]{2,1,0:T(8,128)(2,1)S(1)}, bf16[8,128,256]{2,1,0:T(8,128)(2,1)}, u32[]{:S(2)}, u32[]{:S(2)}) collective-permute-start(bf16[8,128,256]{2,1,0:T(8,128)(2,1)S(1)} %pad_maximum_fusion), channel_id=1, source_target_pairs={{0,4},{1,3},{2,6},{3,1},{4,0},{5,7},{6,2},{7,5},{8,12},{9,11},{10,... | collective-permute-start | bytes 1572872 | tf_op jit(solution)/shard_map/ppermute | solution.py:284
  28.4 6.7 %collective-permute-start.3 = (bf16[4,128,256]{2,1,0:T(8,128)(2,1)S(1)}, bf16[4,128,256]{2,1,0:T(8,128)(2,1)S(1)}, u32[]{:S(2)}, u32[]{:S(2)}) collective-permute-start(bf16[4,128,256]{2,1,0:T(8,128)(2,1)S(1)} %get-tuple-element.25), channel_id=1, source_target_pairs={{0,8},{2,10},{4,12},{6,14},{24,16},{26,18},{28,20},{30,22},{1,9},{... | collective-permute-start | bytes 786440 | tf_op jit(solution)/shard_map/ppermute | solution.py:272
  35.2 9.8 %collective-permute-start.15 = (bf16[4,128,256]{2,1,0:T(8,128)(2,1)S(1)}, bf16[4,128,256]{2,1,0:T(8,128)(2,1)S(1)}, u32[]{:S(2)}, u32[]{:S(2)}) collective-permute-start(bf16[4,128,256]{2,1,0:T(8,128)(2,1)S(1)} %get-tuple-element.14), channel_id=1, source_target_pairs={{0,8},{2,10},{4,12},{6,14},{24,16},{26,18},{28,20},{30,22},{1,9},{... | collective-permute-start | bytes 786440 | tf_op jit(solution)/shard_map/ppermute | solution.py:272
  39.0 49.8 %collective-permute-start.14 = (bf16[64,128,128]{2,1,0:T(8,128)(2,1)S(1)}, bf16[64,128,128]{2,1,0:T(8,128)(2,1)}, u32[]{:S(2)}, u32[]{:S(2)}) collective-permute-start(bf16[64,128,128]{2,1,0:T(8,128)(2,1)S(1)} %bitcast.31), channel_id=1, source_target_pairs={{0,1},{1,0},{2,3},{3,2},{4,5},{5,4},{6,7},{7,6},{8,9},{9,8},{10,11... | collective-permute-start | bytes 6291464 | tf_op jit(solution)/shard_map/ppermute | solution.py:385
  44.2 6.3 %collective-permute-start.6 = (bf16[4,128,256]{2,1,0:T(8,128)(2,1)S(1)}, bf16[4,128,256]{2,1,0:T(8,128)(2,1)S(1)}, u32[]{:S(2)}, u32[]{:S(2)}) collective-permute-start(bf16[4,128,256]{2,1,0:T(8,128)(2,1)S(1)} %collective-permute-done.3), channel_id=1, source_target_pairs={{8,16},{10,18},{12,20},{14,22},{16,8},{18,10},{20,12},{22,14},{9,1... | collective-permute-start | bytes 786440 | tf_op jit(solution)/shard_map/ppermute | solution.py:272
  44.9 28.1 %copy-start.15 = (s32[1,4,16]{2,1,0:T(4,128)S(1)}, s32[1,4,16]{2,1,0:T(4,128)}, u32[]{:S(2)}) copy-start(s32[1,4,16]{2,1,0:T(4,128)} %param.13) | copy-start | bytes 772
  44.9 6.9 %collective-permute-start.20 = (bf16[4,128,256]{2,1,0:T(8,128)(2,1)S(1)}, bf16[4,128,256]{2,1,0:T(8,128)(2,1)S(1)}, u32[]{:S(2)}, u32[]{:S(2)}) collective-permute-start(bf16[4,128,256]{2,1,0:T(8,128)(2,1)S(1)} %get-tuple-element.16), channel_id=1, source_target_pairs={{0,8},{2,10},{4,12},{6,14},{24,16},{26,18},{28,20},{30,22},{1,9},{... | collective-permute-start | bytes 786440 | tf_op jit(solution)/shard_map/ppermute | solution.py:272
  48.5 4.1 %collective-permute-start.16 = (bf16[4,128,256]{2,1,0:T(8,128)(2,1)S(1)}, bf16[4,128,256]{2,1,0:T(8,128)(2,1)S(1)}, u32[]{:S(2)}, u32[]{:S(2)}) collective-permute-start(bf16[4,128,256]{2,1,0:T(8,128)(2,1)S(1)} %broadcast_select_fusion.3), channel_id=1, source_target_pairs={{8,16},{10,18},{12,20},{14,22},{16,8},{18,10},{20,12},{22,14},{9,1... | collective-permute-start | bytes 786440 | tf_op jit(solution)/shard_map/ppermute | solution.py:272
  49.3 9.0 %collective-permute-start.4 = (bf16[4,128,256]{2,1,0:T(8,128)(2,1)S(1)}, bf16[4,128,256]{2,1,0:T(8,128)(2,1)S(1)}, u32[]{:S(2)}, u32[]{:S(2)}) collective-permute-start(bf16[4,128,256]{2,1,0:T(8,128)(2,1)S(1)} %broadcast_select_fusion.5), channel_id=1, source_target_pairs={{0,2},{1,5},{2,0},{3,7},{4,6},{5,1},{6,4},{7,3},{8,10},{9,13},{10,... | collective-permute-start | bytes 786440 | tf_op jit(solution)/shard_map/ppermute | solution.py:284
  50.6 7.6 %collective-permute-start.7 = (bf16[4,128,256]{2,1,0:T(8,128)(2,1)S(1)}, bf16[4,128,256]{2,1,0:T(8,128)(2,1)S(1)}, u32[]{:S(2)}, u32[]{:S(2)}) collective-permute-start(bf16[4,128,256]{2,1,0:T(8,128)(2,1)S(1)} %collective-permute-done.6), channel_id=1, source_target_pairs={{8,0},{10,2},{12,4},{14,6},{16,24},{18,26},{20,28},{22,30},{9,1},{... | collective-permute-start | bytes 786440 | tf_op jit(solution)/shard_map/ppermute | solution.py:272
  51.9 7.6 %collective-permute-start.21 = (bf16[4,128,256]{2,1,0:T(8,128)(2,1)S(1)}, bf16[4,128,256]{2,1,0:T(8,128)(2,1)S(1)}, u32[]{:S(2)}, u32[]{:S(2)}) collective-permute-start(bf16[4,128,256]{2,1,0:T(8,128)(2,1)S(1)} %broadcast_select_fusion.1), channel_id=1, source_target_pairs={{8,16},{10,18},{12,20},{14,22},{16,8},{18,10},{20,12},{22,14},{9,1... | collective-permute-start | bytes 786440 | tf_op jit(solution)/shard_map/ppermute | solution.py:272
  52.6 12.1 %collective-permute-start.17 = (bf16[4,128,256]{2,1,0:T(8,128)(2,1)S(1)}, bf16[4,128,256]{2,1,0:T(8,128)(2,1)S(1)}, u32[]{:S(2)}, u32[]{:S(2)}) collective-permute-start(bf16[4,128,256]{2,1,0:T(8,128)(2,1)S(1)} %broadcast_select_fusion.2), channel_id=1, source_target_pairs={{8,0},{10,2},{12,4},{14,6},{16,24},{18,26},{20,28},{22,30},{9,1},{... | collective-permute-start | bytes 786440 | tf_op jit(solution)/shard_map/ppermute | solution.py:272
  58.2 6.6 %collective-permute-start.8 = (bf16[4,128,256]{2,1,0:T(8,128)(2,1)S(1)}, bf16[4,128,256]{2,1,0:T(8,128)(2,1)S(1)}, u32[]{:S(2)}, u32[]{:S(2)}) collective-permute-start(bf16[4,128,256]{2,1,0:T(8,128)(2,1)S(1)} %broadcast_select_fusion.4), channel_id=1, source_target_pairs={{0,2},{1,5},{2,0},{3,7},{4,6},{5,1},{6,4},{7,3},{8,10},{9,13},{10,... | collective-permute-start | bytes 786440 | tf_op jit(solution)/shard_map/ppermute | solution.py:284
  59.6 13.3 %collective-permute-start.22 = (bf16[4,128,256]{2,1,0:T(8,128)(2,1)S(1)}, bf16[4,128,256]{2,1,0:T(8,128)(2,1)S(1)}, u32[]{:S(2)}, u32[]{:S(2)}) collective-permute-start(bf16[4,128,256]{2,1,0:T(8,128)(2,1)S(1)} %broadcast_select_fusion), channel_id=1, source_target_pairs={{8,0},{10,2},{12,4},{14,6},{16,24},{18,26},{20,28},{22,30},{9,1},{... | collective-permute-start | bytes 786440 | tf_op jit(solution)/shard_map/ppermute | solution.py:272
  64.8 8.1 %collective-permute-start.18 = (bf16[4,128,256]{2,1,0:T(8,128)(2,1)S(1)}, bf16[4,128,256]{2,1,0:T(8,128)(2,1)S(1)}, u32[]{:S(2)}, u32[]{:S(2)}) collective-permute-start(bf16[4,128,256]{2,1,0:T(8,128)(2,1)S(1)} %select_select_fusion.2), channel_id=1, source_target_pairs={{0,2},{1,5},{2,0},{3,7},{4,6},{5,1},{6,4},{7,3},{8,10},{9,13},{10,... | collective-permute-start | bytes 786440 | tf_op jit(solution)/shard_map/ppermute | solution.py:284
  66.2 39.3 %copy-start.1 = (bf16[8,128,256]{2,1,0:T(8,128)(2,1)}, bf16[8,128,256]{2,1,0:T(8,128)(2,1)S(1)}, u32[]{:S(2)}) copy-start(bf16[8,128,256]{2,1,0:T(8,128)(2,1)S(1)} %pad_maximum_fusion.1.refs_0_) | copy-start | bytes 1572868
  66.2 13.2 %collective-permute-start.5 = (bf16[8,128,256]{2,1,0:T(8,128)(2,1)S(1)}, bf16[8,128,256]{2,1,0:T(8,128)(2,1)S(1)}, u32[]{:S(2)}, u32[]{:S(2)}) collective-permute-start(bf16[8,128,256]{2,1,0:T(8,128)(2,1)S(1)} %pad_maximum_fusion.1.refs_0_), channel_id=1, source_target_pairs={{0,4},{1,3},{2,6},{3,1},{4,0},{5,7},{6,2},{7,5},{8,12},{9,11},{10,... | collective-permute-start | bytes 1572872 | tf_op jit(solution)/shard_map/ppermute | solution.py:284
  67.5 19.1 %collective-permute-start.10 = (bf16[8,128,256]{2,1,0:T(8,128)(2,1)S(1)}, bf16[8,128,256]{2,1,0:T(8,128)(2,1)S(1)}, u32[]{:S(2)}, u32[]{:S(2)}) collective-permute-start(bf16[8,128,256]{2,1,0:T(8,128)(2,1)S(1)} %pad_maximum_fusion.1.refs_0_), channel_id=1, source_target_pairs={{0,1},{1,0},{2,3},{3,2},{4,5},{5,4},{6,7},{7,6},{8,9},{9,8},{10,11... | collective-permute-start | bytes 1572872 | tf_op jit(solution)/shard_map/ppermute | solution.py:385
  72.9 8.5 %collective-permute-start.23 = (bf16[4,128,256]{2,1,0:T(8,128)(2,1)S(1)}, bf16[4,128,256]{2,1,0:T(8,128)(2,1)S(1)}, u32[]{:S(2)}, u32[]{:S(2)}) collective-permute-start(bf16[4,128,256]{2,1,0:T(8,128)(2,1)S(1)} %select_select_fusion), channel_id=1, source_target_pairs={{0,2},{1,5},{2,0},{3,7},{4,6},{5,1},{6,4},{7,3},{8,10},{9,13},{10,... | collective-permute-start | bytes 786440 | tf_op jit(solution)/shard_map/ppermute | solution.py:284
  73.1 13.5 %collective-permute-start = (s32[2,4,16]{2,1,0:T(4,128)S(1)}, s32[2,4,16]{2,1,0:T(4,128)S(1)}, u32[]{:S(2)}, u32[]{:S(2)}) collective-permute-start(s32[2,4,16]{2,1,0:T(4,128)S(1)} %constant_dynamic-update-slice_fusion), channel_id=1, source_target_pairs={{0,1},{1,0},{2,3},{3,2},{4,5},{5,4},{6,7},{7,6},{8,9},{9,8},{10,11... | collective-permute-start | bytes 1544 | tf_op jit(solution)/shard_map/ppermute | solution.py:385
  79.3 16.4 %copy-start.3 = (bf16[8,128,256]{2,1,0:T(8,128)(2,1)}, bf16[8,128,256]{2,1,0:T(8,128)(2,1)S(1)}, u32[]{:S(2)}) copy-start(bf16[8,128,256]{2,1,0:T(8,128)(2,1)S(1)} %pad_maximum_fusion.2.refs_2_) | copy-start | bytes 1572868
  79.4 33.7 %copy-start.2 = (bf16[8,128,256]{2,1,0:T(8,128)(2,1)}, bf16[8,128,256]{2,1,0:T(8,128)(2,1)S(1)}, u32[]{:S(2)}) copy-start(bf16[8,128,256]{2,1,0:T(8,128)(2,1)S(1)} %pad_maximum_fusion.3.refs_0_) | copy-start | bytes 1572868
  79.4 18.3 %copy-start.4 = (bf16[8,128,256]{2,1,0:T(8,128)(2,1)}, bf16[8,128,256]{2,1,0:T(8,128)(2,1)S(1)}, u32[]{:S(2)}) copy-start(bf16[8,128,256]{2,1,0:T(8,128)(2,1)S(1)} %collective-permute-done.5.refs_1_) | copy-start | bytes 1572868
  79.4 10.1 %collective-permute-start.9 = (bf16[8,128,256]{2,1,0:T(8,128)(2,1)S(1)}, bf16[8,128,256]{2,1,0:T(8,128)(2,1)}, u32[]{:S(2)}, u32[]{:S(2)}) collective-permute-start(bf16[8,128,256]{2,1,0:T(8,128)(2,1)S(1)} %pad_maximum_fusion.2.refs_2_), channel_id=1, source_target_pairs={{0,4},{1,3},{2,6},{3,1},{4,0},{5,7},{6,2},{7,5},{8,12},{9,11},{10,... | collective-permute-start | bytes 1572872 | tf_op jit(solution)/shard_map/ppermute | solution.py:284
  81.4 10.7 %collective-permute-start.11 = (bf16[8,128,256]{2,1,0:T(8,128)(2,1)S(1)}, bf16[8,128,256]{2,1,0:T(8,128)(2,1)S(1)}, u32[]{:S(2)}, u32[]{:S(2)}) collective-permute-start(bf16[8,128,256]{2,1,0:T(8,128)(2,1)S(1)} %collective-permute-done.5.refs_1_), channel_id=1, source_target_pairs={{0,1},{1,0},{2,3},{3,2},{4,5},{5,4},{6,7},{7,6},{8,9},{9,8},{10,11... | collective-permute-start | bytes 1572872 | tf_op jit(solution)/shard_map/ppermute | solution.py:385
  86.5 5.7 %collective-permute-start.12 = (bf16[8,128,256]{2,1,0:T(8,128)(2,1)S(1)}, bf16[8,128,256]{2,1,0:T(8,128)(2,1)S(1)}, u32[]{:S(2)}, u32[]{:S(2)}) collective-permute-start(bf16[8,128,256]{2,1,0:T(8,128)(2,1)S(1)} %pad_maximum_fusion.2.refs_2_), channel_id=1, source_target_pairs={{0,1},{1,0},{2,3},{3,2},{4,5},{5,4},{6,7},{7,6},{8,9},{9,8},{10,11... | collective-permute-start | bytes 1572872 | tf_op jit(solution)/shard_map/ppermute | solution.py:385
  86.5 14.7 %copy-start.5 = (bf16[8,128,256]{2,1,0:T(8,128)(2,1)}, bf16[8,128,256]{2,1,0:T(8,128)(2,1)S(1)}, u32[]{:S(2)}) copy-start(bf16[8,128,256]{2,1,0:T(8,128)(2,1)S(1)} %collective-permute-done.10.refs_4_) | copy-start | bytes 1572868
  86.6 9.2 %collective-permute-start.19 = (bf16[8,128,256]{2,1,0:T(8,128)(2,1)S(1)}, bf16[8,128,256]{2,1,0:T(8,128)(2,1)}, u32[]{:S(2)}, u32[]{:S(2)}) collective-permute-start(bf16[8,128,256]{2,1,0:T(8,128)(2,1)S(1)} %pad_maximum_fusion.3.refs_0_), channel_id=1, source_target_pairs={{0,4},{1,3},{2,6},{3,1},{4,0},{5,7},{6,2},{7,5},{8,12},{9,11},{10,... | collective-permute-start | bytes 1572872 | tf_op jit(solution)/shard_map/ppermute | solution.py:284
  88.8 12.5 %collective-permute-start.24 = (bf16[8,128,256]{2,1,0:T(8,128)(2,1)}, bf16[8,128,256]{2,1,0:T(8,128)(2,1)S(1)}, u32[]{:S(2)}, u32[]{:S(2)}) collective-permute-start(bf16[8,128,256]{2,1,0:T(8,128)(2,1)} %pad_maximum_fusion.4.refs_2_), channel_id=1, source_target_pairs={{0,4},{1,3},{2,6},{3,1},{4,0},{5,7},{6,2},{7,5},{8,12},{9,11},{10,... | collective-permute-start | bytes 1572872 | tf_op jit(solution)/shard_map/ppermute | solution.py:284
  89.5 15.9 %collective-permute-start.13 = (bf16[8,128,256]{2,1,0:T(8,128)(2,1)}, bf16[8,128,256]{2,1,0:T(8,128)(2,1)}, u32[]{:S(2)}, u32[]{:S(2)}) collective-permute-start(bf16[8,128,256]{2,1,0:T(8,128)(2,1)} %collective-permute-done.9.refs_3_), channel_id=1, source_target_pairs={{0,1},{1,0},{2,3},{3,2},{4,5},{5,4},{6,7},{7,6},{8,9},{9,8},{10,11... | collective-permute-start | bytes 1572872 | tf_op jit(solution)/shard_map/ppermute | solution.py:385
  92.1 9.1 %copy-start.6 = (bf16[8,128,256]{2,1,0:T(8,128)(2,1)}, bf16[8,128,256]{2,1,0:T(8,128)(2,1)S(1)}, u32[]{:S(2)}) copy-start(bf16[8,128,256]{2,1,0:T(8,128)(2,1)S(1)} %collective-permute-done.11.refs_5_) | copy-start | bytes 1572868
  92.1 21.0 %collective-permute-start.25 = (bf16[8,128,256]{2,1,0:T(8,128)(2,1)S(1)}, bf16[8,128,256]{2,1,0:T(8,128)(2,1)S(1)}, u32[]{:S(2)}, u32[]{:S(2)}) collective-permute-start(bf16[8,128,256]{2,1,0:T(8,128)(2,1)S(1)} %pad_maximum_fusion.3.refs_0_), channel_id=1, source_target_pairs={{0,1},{1,0},{2,3},{3,2},{4,5},{5,4},{6,7},{7,6},{8,9},{9,8},{10,11... | collective-permute-start | bytes 1572872 | tf_op jit(solution)/shard_map/ppermute | solution.py:385
  92.2 9.1 %copy-start.8 = (bf16[8,128,256]{2,1,0:T(8,128)(2,1)}, bf16[8,128,256]{2,1,0:T(8,128)(2,1)S(1)}, u32[]{:S(2)}) copy-start(bf16[8,128,256]{2,1,0:T(8,128)(2,1)S(1)} %collective-permute-done.12.refs_6_) | copy-start | bytes 1572868
  92.2 20.9 %collective-permute-start.27 = (bf16[8,128,256]{2,1,0:T(8,128)(2,1)}, bf16[8,128,256]{2,1,0:T(8,128)(2,1)S(1)}, u32[]{:S(2)}, u32[]{:S(2)}) collective-permute-start(bf16[8,128,256]{2,1,0:T(8,128)(2,1)} %pad_maximum_fusion.4.refs_2_), channel_id=1, source_target_pairs={{0,1},{1,0},{2,3},{3,2},{4,5},{5,4},{6,7},{7,6},{8,9},{9,8},{10,11... | collective-permute-start | bytes 1572872 | tf_op jit(solution)/shard_map/ppermute | solution.py:385
  95.8 17.4 %collective-permute-start.26 = (bf16[8,128,256]{2,1,0:T(8,128)(2,1)}, bf16[8,128,256]{2,1,0:T(8,128)(2,1)S(1)}, u32[]{:S(2)}, u32[]{:S(2)}) collective-permute-start(bf16[8,128,256]{2,1,0:T(8,128)(2,1)} %collective-permute-done.19.refs_1_), channel_id=1, source_target_pairs={{0,1},{1,0},{2,3},{3,2},{4,5},{5,4},{6,7},{7,6},{8,9},{9,8},{10,11... | collective-permute-start | bytes 1572872 | tf_op jit(solution)/shard_map/ppermute | solution.py:385
  101.3 11.8 %copy-start.7 = (bf16[8,128,256]{2,1,0:T(8,128)(2,1)}, bf16[8,128,256]{2,1,0:T(8,128)(2,1)S(1)}, u32[]{:S(2)}) copy-start(bf16[8,128,256]{2,1,0:T(8,128)(2,1)S(1)} %collective-permute-done.24.refs_3_) | copy-start | bytes 1572868
  101.3 11.9 %collective-permute-start.28 = (bf16[8,128,256]{2,1,0:T(8,128)(2,1)S(1)}, bf16[8,128,256]{2,1,0:T(8,128)(2,1)}, u32[]{:S(2)}, u32[]{:S(2)}) collective-permute-start(bf16[8,128,256]{2,1,0:T(8,128)(2,1)S(1)} %collective-permute-done.24.refs_3_), channel_id=1, source_target_pairs={{0,1},{1,0},{2,3},{3,2},{4,5},{5,4},{6,7},{7,6},{8,9},{9,8},{10,11... | collective-permute-start | bytes 1572872 | tf_op jit(solution)/shard_map/ppermute | solution.py:385
  113.1 0.8 copy-start.9
  113.2 1.0 copy-start.10
  113.2 1.1 copy-start.11

commit v5 on v4

v5 whole, which is shorter than its diff:
```python
import functools

import jax
import jax.numpy as jnp
from jax import lax
from jax.experimental import pallas as pl
from jax.experimental.pallas import tpu as pltpu
from jax.sharding import PartitionSpec as P


UNROLL = 8


def load(n_first, pieces, places, sent, sem):
    return [
        pltpu.make_async_copy(piece, sent.at[pl.ds(place, piece.shape[0])], sem.at[n_first + i])
        for i, (piece, place) in enumerate(zip(pieces, places))
    ]


def put(lists, count, here, tile, row, place):
    lists[0, count] = tile
    lists[1, count] = row
    lists[2, count] = place
    return count + here.astype(jnp.int32)


def pad(lists, first, count, n_blocks):
    for i in range(UNROLL):
        put(lists, first + count + i, count >= 0, 0, n_blocks, 0)
    return (count + UNROLL - 1) // UNROLL


def run(lists, first, groups, tiles, sent, acc):
    def step(group, carry):
        at = [first + group * UNROLL + i for i in range(UNROLL)]
        done = [
            jnp.dot(
                tiles[lists[0, i]], sent[lists[2, i]], preferred_element_type=jnp.float32
            )
            for i in at
        ]
        for i, product in zip(at, done):
            acc[lists[1, i]] += product
        return carry

    lax.fori_loop(0, groups, step, 0)


def finish(acc, weight_ref, out_ref, stage, out_sem):
    steps, group, tile_len = stage.shape[:3]
    copies = []
    for i in range(steps):
        total = acc[pl.ds(i * group, group)].reshape(group * tile_len, acc.shape[2])
        mixed = jnp.dot(
            total.astype(jnp.bfloat16), weight_ref[...], preferred_element_type=jnp.float32
        )
        stage[i] = jnp.maximum(mixed, 0.0).astype(out_ref.dtype).reshape(stage.shape[1:])
        copies.append(
            pltpu.make_async_copy(stage.at[i], out_ref.at[pl.ds(i * group, group)], out_sem.at[i])
        )
        copies[-1].start()
    for copy in copies:
        copy.wait()


def whole_kernel(places, rows_ref, slots_ref, *refs):
    n = len(places)
    tile_ref, weight_ref, out_ref, sent, tiles, acc, stage, lists, sem, out_sem = refs[n:]
    n_tiles, n_blocks = rows_ref.shape[0], out_ref.shape[0]
    copies = load(0, refs[:n], places, sent, sem)
    copies.append(pltpu.make_async_copy(tile_ref, tiles, sem.at[n]))
    for copy in copies:
        copy.start()
    acc[...] = jnp.zeros_like(acc)

    def pick(t, count):
        row = rows_ref[t]
        here = jnp.logical_and(row >= 0, row < n_blocks)
        return put(lists, count, here, t, row, slots_ref[t])

    groups = pad(lists, 0, lax.fori_loop(0, n_tiles, pick, jnp.int32(0)), n_blocks)
    for copy in copies:
        copy.wait()
    run(lists, 0, groups, tiles, sent, acc)
    finish(acc, weight_ref, out_ref, stage, out_sem)


def phased_kernel(places, lists, *refs):
    counts = [len(part) for part in places]
    n = sum(counts)
    pieces, tile_refs = refs[:n], refs[n : n + 2]
    weight_ref, out_ref, sent, tiles, acc, stage, sem, out_sem = refs[n + 2 :]
    each = tiles.shape[0] // 2
    copies = [
        pltpu.make_async_copy(ref, tiles.at[pl.ds(i * each, each)], sem.at[n + i])
        for i, ref in enumerate(tile_refs)
    ]
    copies += load(0, pieces[: counts[0]], places[0], sent, sem)
    later = load(counts[0], pieces[counts[0] :], places[1], sent, sem)
    for copy in copies + later:
        copy.start()
    acc[...] = jnp.zeros_like(acc)
    middle = lists.shape[1] // 2
    for copy in copies:
        copy.wait()
    run(lists, 0, lists[3, 0], tiles, sent, acc)
    for copy in later:
        copy.wait()
    run(lists, middle, lists[3, middle], tiles, sent, acc)
    finish(acc, weight_ref, out_ref, stage, out_sem)


def lists_kernel(n_blocks, owner_ref, own_ref, other_ref, lists):
    me, rep = lax.axis_index("dom"), lax.axis_index("rep")
    quad, z = me % 4, me // 4
    sections, each = own_ref.shape[1:]
    middle = lists.shape[1] // 2
    known, others, rank = jnp.int32(0), jnp.int32(0), jnp.int32(0)
    for s in range(sections):
        owner = owner_ref[s]
        is_end = jnp.logical_or(owner == 0, owner == 15)
        slot = jnp.where(is_end, ((owner == 0) != (z < 2)).astype(jnp.int32), rank)
        rank = rank + 1 - is_end.astype(jnp.int32)
        for part, ref in enumerate((own_ref, other_ref)):

            def pick(k, counts, ref=ref, part=part, s=s, slot=slot, owner=owner, is_end=is_end):
                row = ref[0, s, k] - rep * n_blocks
                here = jnp.logical_and(row >= 0, row < n_blocks)
                col = ref[1, s, k]
                holder, quarter, within = col // 16, (col % 16) // 4, col % 4
                base = jnp.where(holder == rep, 0, 32)
                at_end = place_of(quarter ^ quad, holder) + 4 * slot
                turn = place_of(quarter ^ (owner % 4), holder)
                chip = jnp.where(turn == 0, 3, jnp.where(turn == 3, 0, turn)) * 4 + within
                shift = (chip // 4 - z) & 3
                by = place_of((chip % 4) ^ quad, holder)
                at_other = jnp.where(
                    (shift & 1) == 1,
                    8 + by * 4 + (shift // 2) * 2,
                    jnp.where(shift == 0, 0, 24) + by * 2,
                )
                place = jnp.where(is_end, base + at_end * 4 + within, 64 + base + at_other + slot)
                tile = (part * sections + s) * each + k
                known, others = counts
                target = jnp.where(is_end, known, middle + others)
                put(lists, target, here, tile, row, place)
                now = here.astype(jnp.int32)
                return known + jnp.where(is_end, now, 0), others + jnp.where(is_end, 0, now)

            known, others = lax.fori_loop(0, each, pick, (known, others))
    lists[3, 0] = pad(lists, 0, known, n_blocks)
    lists[3, middle] = pad(lists, middle, others, n_blocks)


HBM = pl.BlockSpec(memory_space=pltpu.HBM)
SMEM = pl.BlockSpec(memory_space=pltpu.SMEM)
VMEM = pl.BlockSpec(memory_space=pltpu.VMEM)


def settings(n_products, tile_len, width, n_bytes):
    return {
        "compiler_params": pltpu.CompilerParams(vmem_limit_bytes=60 * 1024 * 1024),
        "cost_estimate": pl.CostEstimate(
            flops=2 * n_products * tile_len * tile_len * width,
            bytes_accessed=n_bytes,
            transcendentals=0,
        ),
    }


def out_stage(n_blocks, tile_len, width):
    group = min(4, n_blocks)
    return pltpu.VMEM((n_blocks // group, group, tile_len, width), jnp.bfloat16)


def products(pieces, places, tiles, rows, slots, weight, n_sent, n_blocks):
    n_tiles, tile_len = tiles.shape[:2]
    width = weight.shape[0]
    return pl.pallas_call(
        functools.partial(whole_kernel, tuple(places)),
        out_shape=jax.ShapeDtypeStruct((n_blocks, tile_len, weight.shape[1]), jnp.bfloat16),
        in_specs=[SMEM, SMEM] + [HBM] * (len(pieces) + 1) + [VMEM],
        out_specs=HBM,
        scratch_shapes=[
            pltpu.VMEM((n_sent, tile_len, width), jnp.bfloat16),
            pltpu.VMEM(tiles.shape, jnp.bfloat16),
            pltpu.VMEM((n_blocks + 1, tile_len, width), jnp.float32),
            out_stage(n_blocks, tile_len, weight.shape[1]),
            pltpu.SMEM((3, n_tiles + UNROLL), jnp.int32),
            pltpu.SemaphoreType.DMA((len(pieces) + 1,)),
            pltpu.SemaphoreType.DMA((n_blocks // min(4, n_blocks),)),
        ],
        **settings(n_tiles, tile_len, width, 16 << 20),
    )(rows, slots, *pieces, tiles, weight)


def products_in_phases(pieces, places, tile_list, lists, weight, n_blocks):
    n_tiles, tile_len = 2 * tile_list[0].shape[0], tile_list[0].shape[1]
    width = weight.shape[0]
    flat = pieces[0] + pieces[1]
    n_sent = sum(piece.shape[0] for piece in flat)
    return pl.pallas_call(
        functools.partial(phased_kernel, places),
        out_shape=jax.ShapeDtypeStruct((n_blocks, tile_len, weight.shape[1]), jnp.bfloat16),
        in_specs=[SMEM] + [HBM] * (len(flat) + 2) + [VMEM],
        out_specs=HBM,
        scratch_shapes=[
            pltpu.VMEM((n_sent, tile_len, width), jnp.bfloat16),
            pltpu.VMEM((n_tiles, tile_len, tile_len), jnp.bfloat16),
            pltpu.VMEM((n_blocks + 1, tile_len, width), jnp.float32),
            out_stage(n_blocks, tile_len, weight.shape[1]),
            pltpu.SemaphoreType.DMA((len(flat) + 2,)),
            pltpu.SemaphoreType.DMA((n_blocks // min(4, n_blocks),)),
        ],
        **settings(n_tiles, tile_len, width, 16 << 20),
    )(lists, *flat, *tile_list, weight)


def product_lists(section_owner, own, other, n_blocks):
    n_tiles = 2 * own.shape[1] * own.shape[2]
    return pl.pallas_call(
        functools.partial(lists_kernel, n_blocks),
        out_shape=jax.ShapeDtypeStruct((4, 2 * (n_tiles + UNROLL)), jnp.int32),
        in_specs=[SMEM] * 3,
        out_specs=SMEM,
    )(section_owner, own, other)


def lines_kernel(owner_ref, blocks_ref, order_ref, out_ref):
    me, rep = lax.axis_index("dom"), lax.axis_index("rep")
    sections, n_send = blocks_ref.shape
    section = jnp.int32(0)
    for s in range(sections):
        section = jnp.where(owner_ref[s] == me, s, section)
    each = n_send // 8
    for group, across in enumerate((3, 1 + rep, 2 - rep, 0)):
        base = rep * (n_send // 2) + ((me % 4) ^ across) * each
        for j in range(each):
            block = blocks_ref[section, base + j]
            out_ref[pl.ds(group * each + j, 1), :] = order_ref[pl.ds(block, 1), :]


def share_lines(node_order, section_owner, send_blocks, tile_len):
    return pl.pallas_call(
        lines_kernel,
        out_shape=jax.ShapeDtypeStruct((send_blocks.shape[1] // 2, tile_len), jnp.int32),
        in_specs=[SMEM, SMEM, VMEM],
        out_specs=VMEM,
    )(section_owner, send_blocks, node_order[0].reshape(-1, tile_len))


def share_rows(node_order, section_owner, send_blocks, tile_len):
    me = lax.axis_index("dom")
    sections, n_send = send_blocks.shape
    mine = (section_owner == me).astype(jnp.int32)
    section = jnp.sum(mine * jnp.arange(sections, dtype=jnp.int32))
    share = n_send // lax.axis_size("rep")
    picks = lax.dynamic_slice(
        send_blocks, (section, lax.axis_index("rep") * share), (1, share)
    )[0]
    order = node_order[0].reshape(-1, tile_len)
    return order.at[picks].get(mode="promise_in_bounds")


def move(value, pairs):
    return lax.ppermute(value, "dom", pairs)


def flip(bits):
    return [(i, i ^ bits) for i in range(16)]


def cross(value, turn):
    pairs = []
    for i in range(16):
        for core in (0, 1):
            pairs.append((2 * i + core, 2 * (i ^ (1 if core == turn else 2)) + core))
    return lax.ppermute(value, ("dom", "rep"), pairs)


def place_of(across, core):
    return jnp.where(core == 0, across, (across & 1) * 2 + across // 2)


def quad_scatter(rows):
    each = rows.shape[0] // 4
    by_first = cross(rows[: 2 * each], 0)
    by_second = cross(jnp.concatenate([rows[2 * each : 3 * each], by_first[:each]]), 1)
    return rows[3 * each :], by_first[each:], by_second[:each], by_second[each:]


INWARD = [(i, i + 4) for i in range(4)] + [(i, i - 4) for i in range(12, 16)]
MIDDLE = [(i, i + 4) for i in range(4, 8)] + [(i, i - 4) for i in range(8, 12)]
OUTWARD = [(i, i - 4) for i in range(4, 8)] + [(i, i + 4) for i in range(8, 12)]


def tie(value, after):
    return lax.optimization_barrier((value, after))[0]


def along_z_ends(first, z):
    outer = jnp.logical_or(z == 0, z == 3)
    came = move(first, INWARD)
    near = jnp.where(outer, first, came)
    across = move(came, MIDDLE)
    beyond = move(across, OUTWARD)
    return came, near, jnp.where(outer, beyond, across)


def quad_gather(own):
    pair = jnp.concatenate([own, cross(own, 0)])
    return [pair, cross(pair, 1)]


RING = {
    k: [(z * 4 + q, ((z - k) % 4) * 4 + q) for z in range(4) for q in range(4)] for k in (1, 2, 3)
}


def gather_ends(rows):
    me = lax.axis_index("dom")
    quad, z = me % 4, me // 4
    held = quad_scatter(rows)
    source = jnp.where(z < 2, 0, 3)
    quarter = lax.select_n(place_of(quad ^ source, lax.axis_index("rep")), *held)
    came, near, far = along_z_ends(quarter, z)
    return quad_gather(near) + quad_gather(far)


def gather_others(rows, section_owner):
    is_end = jnp.logical_or(section_owner == 0, section_owner == 15)
    rank = jnp.cumsum(1 - is_end.astype(jnp.int32)) - 1
    owners = jnp.stack(
        [jnp.sum(jnp.where(jnp.logical_or(is_end, rank != i), 0, section_owner)) for i in (0, 1)]
    )
    landed = lax.all_to_all(rows, "dom", 0, 0, tiled=True)
    shard = landed.at[owners].get(mode="promise_in_bounds")
    near = [move(shard, RING[1]), move(shard, RING[3])]
    far = move(tie(shard, near[0]), RING[2])
    return quad_gather(shard) + quad_gather(jnp.concatenate(near)) + quad_gather(far)


def body(features, node_order, section_owner, send_blocks, tile_rows, tile_cols, tiles, weight):
    width = features.shape[1]
    tile_len = tiles.shape[3]
    blocks = features.shape[0] // tile_len
    n_dom, n_rep = lax.axis_size("dom"), lax.axis_size("rep")
    sections, n_send = send_blocks.shape
    me, rep = lax.axis_index("dom"), lax.axis_index("rep")
    n_blocks = blocks // n_rep
    small = n_dom == 16 and n_rep == 2 and n_send == n_dom * n_rep

    own_tiles = tiles[0].reshape(-1, tile_len, tile_len)
    numbers = jnp.stack([tile_rows[0], tile_cols[0]])
    if small:
        swap = [(0, 1), (1, 0)]

        def exchange(value):
            return lax.ppermute(value, "rep", swap)

        tile_list = [own_tiles, exchange(own_tiles)]
        lists = product_lists(section_owner, numbers, exchange(numbers), n_blocks)
        lines = share_lines(node_order, section_owner, send_blocks, tile_len)
        mine = features.at[lines.reshape(-1)].get(mode="promise_in_bounds")
        mine = mine.reshape(-1, tile_len, width)
        own = [gather_ends(mine), gather_others(mine, section_owner)]
        parts = [part + [exchange(piece) for piece in part] for part in own]
        ends, place = [], 0
        for part in parts:
            ends.append([])
            for piece in part:
                ends[-1].append(place)
                place += piece.shape[0]
        hidden = products_in_phases(parts, ends, tile_list, lists, weight, n_blocks)
    else:
        tile_list = lax.all_gather(own_tiles, "rep", axis=0, tiled=True)
        numbers = lax.all_gather(numbers, "rep", axis=0)
        rows = (numbers[:, 0] - rep * n_blocks).reshape(-1)
        lines = share_rows(node_order, section_owner, send_blocks, tile_len)
        mine = features.at[lines.reshape(-1)].get(mode="promise_in_bounds")
        landed = lax.all_to_all(mine, "dom", 0, 0, tiled=True)
        landed = landed.reshape(n_dom, -1, width)
        shard = landed.at[section_owner].get(mode="promise_in_bounds")
        whole = lax.all_gather(shard, ("rep", "dom"), axis=0)
        whole = whole.transpose(1, 0, 2, 3).reshape(sections * n_send, tile_len, width)
        slots = jnp.arange(sections)[:, None] * n_send + numbers[:, 1]
        hidden = products(
            [whole], [0], tile_list, rows, slots.reshape(-1), weight, sections * n_send, n_blocks
        )
    return hidden.reshape(n_blocks * tile_len, -1)


def solution(mesh):
    return jax.shard_map(
        body,
        mesh=mesh,
        in_specs=(
            P("dom", None),
            P("dom", None),
            P(),
            P(),
            P("dom", None, "rep"),
            P("dom", None, "rep"),
            P("dom", None, "rep", None, None),
            P(),
        ),
        out_specs=P(("dom", "rep"), None),
        check_vma=False,
    )
```

time: 123 us -> 137 us (1.11)
  waiting for transfers between devices: 23.4 us -> 40.1 us
  starting transfers between devices: 55.2 us -> 49.9 us
  between operations: 5.6 us -> 0.45 us
  Pallas kernels: 17.2 us -> 19.6 us
  local copies, waits for them, and re-layouts: 16.5 us -> 18.9 us
  other arithmetic: 4.61 us -> 6.78 us
    ppermute x9 -> x6, waiting for transfers between devices: 11.4 us -> 22.9 us  [move(): return lax.ppermute(value, 'dom', pairs)]
    ppermute x10 -> x12, starting transfers between devices: 27.1 us -> 19.3 us  [exchange(): return lax.ppermute(value, 'rep', swap)]
    ppermute x9 -> x6, starting transfers between devices: 16.7 us -> 9.76 us  [move(): return lax.ppermute(value, 'dom', pairs)]
    all_to_all x0 -> x1, starting transfers between devices: none -> 5.84 us  [gather_others(): landed = lax.all_to_all(rows, 'dom', 0, 0, tiled=True)]
    ppermute x10 -> x12, waiting for transfers between devices: 11.9 us -> 16.4 us  [cross(): return lax.ppermute(value, ('dom', 'rep'), pairs)]
    ppermute x10 -> x12, starting transfers between devices: 11.5 us -> 15.1 us  [cross(): return lax.ppermute(value, ('dom', 'rep'), pairs)]
    pallas_call x2, Pallas kernels: 15.8 us -> 18.2 us  [the longest x1 9.26 us: product_lists(): pl.pallas_call(functools.partial(lists_kernel, n_blocks), out_shape=jax.S...]
    unnamed x33 -> x43, local copies, waits for them, and re-layouts: 1.16 us -> 2.95 us
  transfers between devices with their start and end apart: 29 -> 31, of which waited for: 9 -> 12; matrix products, arithmetic and copies ran while one was open for 9% -> 7% of each run, Pallas kernels for 6% -> 7%
where the time goes in v5:
time: 137 us; the launch traced here: 136 us
  starting transfers between devices  49.9 us (36%)
  waiting for transfers between devices  40.1 us (29%)
  Pallas kernels  19.6 us (14%)
  local copies, waits for them, and re-layouts  18.9 us (14%)
  other arithmetic  6.78 us (5%)
    ppermute x6, waiting for transfers between devices, move(): return lax.ppermute(value, 'dom', pairs)  22.9 us
    ppermute x12, starting transfers between devices, exchange(): return lax.ppermute(value, 'rep', swap)  19.3 us
    ppermute x12, waiting for transfers between devices, cross(): return lax.ppermute(value, ('dom', 'rep'), pairs)  16.4 us
    ppermute x12, starting transfers between devices, cross(): return lax.ppermute(value, ('dom', 'rep'), pairs)  15.1 us
    gather x1, local copies, waits for them, and re-layouts, body(): mine = features.at[lines.reshape(-1)].get(mode='promise_in_bounds')  11.2 us
    ppermute x6, starting transfers between devices, move(): return lax.ppermute(value, 'dom', pairs)  9.76 us
    pallas_call x1, Pallas kernels, product_lists(): pl.pallas_call(functools.partial(lists_kernel, n_blocks), out_shape=jax.S...  9.26 us
    pallas_call x1, Pallas kernels, products_in_phases(): pl.pallas_call(functools.partial(phased_kernel, places), out_shape=jax.Sh...  8.91 us
  transfers between devices with their start and end apart: 31, of which 12 were waited for; matrix products, arithmetic and copies ran while one was open for 7% of the time, Pallas kernels for 7%

profile of v5, /device:TPU:1, one launch (start us, length us, event | category | flops | bytes accessed | tf_op | source)
XLA Modules:
  0.0 135.8 jit_solution(1359016629191797651)
XLA Ops:
  0.0 1.4 %shard_map.83 = s32[16,128]{1,0:T(8,128)} custom-call(s32[4]{0:T(128)} %owner_ref.3, s32[4,32]{1,0:T(4,128)} %blocks_ref.1, s32[64,128]{1,0:T(8,128)} %bitcast.32), custom_call_target="tpu_custom_call" | custom-call | tf_op jit(solution)/shard_map/pallas_call | solution.py:245
  1.4 0.7 compare_select_fusion
  2.1 11.2 %gather_fusion = bf16[2048,256]{1,0:T(8,128)(2,1)} fusion(bf16[8192,256]{1,0:T(8,128)(2,1)} %param.8, s32[2048]{0:T(1024)S(1)} %broadcast_clamp_fusion), kind=kCustom, calls=%fused_computation | custom fusion | bytes 2105344 | tf_op jit(solution)/shard_map/gather | solution.py:365
  13.4 1.1 slice.45
  14.5 2.1 %collective-permute-start.1 = (bf16[8,128,256]{2,1,0:T(8,128)(2,1)S(1)}, bf16[8,128,256]{2,1,0:T(8,128)(2,1)S(1)}, u32[]{:S(2)}, u32[]{:S(2)}) collective-permute-start(bf16[8,128,256]{2,1,0:T(8,128)(2,1)S(1)} %bitcast.31), channel_id=1, source_target_pairs={{0,2},{1,5},{2,0},{3,7},{4,6},{5,1},{6,4},{7,3},{8,10},{9,13},{10,... | collective-permute-start | bytes 1572872 | tf_op jit(solution)/shard_map/ppermute | solution.py:279
  16.6 1.1 fusion.6
  17.7 5.8 %collective-permute-done.1 = bf16[8,128,256]{2,1,0:T(8,128)(2,1)S(1)} collective-permute-done((bf16[8,128,256]{2,1,0:T(8,128)(2,1)S(1)}, bf16[8,128,256]{2,1,0:T(8,128)(2,1)S(1)}, u32[]{:S(2)}, u32[]{:S(2)}) %collective-permute-start.1) | collective-permute-done | bytes 524320 | tf_op jit(solution)/shard_map/ppermute | solution.py:279
  23.5 0.8 copy-done.11
  24.3 0.9 pad_maximum_fusion
  25.1 1.4 %collective-permute-start.2 = (bf16[8,128,256]{2,1,0:T(8,128)(2,1)}, bf16[8,128,256]{2,1,0:T(8,128)(2,1)S(1)}, u32[]{:S(2)}, u32[]{:S(2)}) collective-permute-start(bf16[8,128,256]{2,1,0:T(8,128)(2,1)} %pad_maximum_fusion), channel_id=1, source_target_pairs={{0,4},{1,3},{2,6},{3,1},{4,0},{5,7},{6,2},{7,5},{8,12},{9,11},{10,... | collective-permute-start | bytes 1572872 | tf_op jit(solution)/shard_map/ppermute | solution.py:279
  26.6 5.8 %all-to-all-start = ((bf16[16,128,256]{2,1,0:T(8,128)(2,1)}), bf16[16,128,256]{2,1,0:T(8,128)(2,1)}, u32[]{:S(2)}, u32[]{:S(2)}) async-start(bf16[16,128,256]{2,1,0:T(8,128)(2,1)} %bitcast.6), calls=%async_computation | async-start | bytes 2097152 | tf_op jit(solution)/shard_map/all_to_all | solution.py:337
  32.5 1.2 collective-permute-done.2
  33.7 1.0 fusion
  34.7 3.4 %collective-permute-start.3 = (bf16[4,128,256]{2,1,0:T(8,128)(2,1)S(1)}, bf16[4,128,256]{2,1,0:T(8,128)(2,1)S(1)}, u32[]{:S(2)}, u32[]{:S(2)}) collective-permute-start(bf16[4,128,256]{2,1,0:T(8,128)(2,1)S(1)} %fusion), channel_id=1, source_target_pairs={{0,8},{2,10},{4,12},{6,14},{24,16},{26,18},{28,20},{30,22},{1,9},{... | collective-permute-start | bytes 786440 | tf_op jit(solution)/shard_map/ppermute | solution.py:267
  38.1 6.1 %collective-permute-start.29 = (bf16[64,128,128]{2,1,0:T(8,128)(2,1)S(1)}, bf16[64,128,128]{2,1,0:T(8,128)(2,1)}, u32[]{:S(2)}, u32[]{:S(2)}) collective-permute-start(bf16[64,128,128]{2,1,0:T(8,128)(2,1)S(1)} %bitcast.28), channel_id=1, source_target_pairs={{0,1},{1,0},{2,3},{3,2},{4,5},{5,4},{6,7},{7,6},{8,9},{9,8},{10,11... | collective-permute-start | bytes 6291464 | tf_op jit(solution)/shard_map/ppermute | solution.py:360
  44.2 0.2 reduce-window.9
  44.4 8.7 %collective-permute-done.3 = bf16[4,128,256]{2,1,0:T(8,128)(2,1)S(1)} collective-permute-done((bf16[4,128,256]{2,1,0:T(8,128)(2,1)S(1)}, bf16[4,128,256]{2,1,0:T(8,128)(2,1)S(1)}, u32[]{:S(2)}, u32[]{:S(2)}) %collective-permute-start.3) | collective-permute-done | bytes 262176 | tf_op jit(solution)/shard_map/ppermute | solution.py:267
  53.1 0.7 collective-permute-start.6
  53.8 0.7 fusion.4
  54.5 1.2 fusion.3
  55.7 0.0 collective-permute-done.6
  55.7 1.3 collective-permute-start.7
  57.1 1.3 collective-permute-start.4
  58.4 9.9 %collective-permute-done.7 = bf16[4,128,256]{2,1,0:T(8,128)(2,1)} collective-permute-done((bf16[4,128,256]{2,1,0:T(8,128)(2,1)S(1)}, bf16[4,128,256]{2,1,0:T(8,128)(2,1)}, u32[]{:S(2)}, u32[]{:S(2)}) %collective-permute-start.7) | collective-permute-done | bytes 262176 | tf_op jit(solution)/shard_map/ppermute | solution.py:267
  68.4 1.0 broadcast_select_fusion
  69.3 1.5 %collective-permute-start.8 = (bf16[4,128,256]{2,1,0:T(8,128)(2,1)S(1)}, bf16[4,128,256]{2,1,0:T(8,128)(2,1)}, u32[]{:S(2)}, u32[]{:S(2)}) collective-permute-start(bf16[4,128,256]{2,1,0:T(8,128)(2,1)S(1)} %broadcast_select_fusion), channel_id=1, source_target_pairs={{0,2},{1,5},{2,0},{3,7},{4,6},{5,1},{6,4},{7,3},{8,10},{9,13},{10,... | collective-permute-start | bytes 786440 | tf_op jit(solution)/shard_map/ppermute | solution.py:279
  71.0 4.7 %collective-permute-start.10 = (bf16[8,128,256]{2,1,0:T(8,128)(2,1)S(1)}, bf16[8,128,256]{2,1,0:T(8,128)(2,1)}, u32[]{:S(2)}, u32[]{:S(2)}) collective-permute-start(bf16[8,128,256]{2,1,0:T(8,128)(2,1)S(1)} %pad_maximum_fusion.1.refs_0_), channel_id=1, source_target_pairs={{0,1},{1,0},{2,3},{3,2},{4,5},{5,4},{6,7},{7,6},{8,9},{9,8},{10,11... | collective-permute-start | bytes 1572872 | tf_op jit(solution)/shard_map/ppermute | solution.py:360
  75.7 1.8 %gather_fusion.1 = bf16[2,128,256]{2,1,0:T(8,128)(2,1)S(1)} fusion(bf16[16,128,256]{2,1,0:T(8,128)(2,1)} %all-to-all-done, s32[1024]{0:T(1024)S(1)} %pad_clamp_fusion), kind=kCustom, calls=%fused_computation.1 | custom fusion | bytes 262152 | tf_op jit(solution)/shard_map/gather | solution.py:338
  77.5 0.1 collective-permute-start.17
  77.5 3.3 %collective-permute-start.16 = (bf16[2,128,256]{2,1,0:T(8,128)(2,1)S(1)}, bf16[2,128,256]{2,1,0:T(8,128)(2,1)S(1)}, u32[]{:S(2)}, u32[]{:S(2)}) collective-permute-start(bf16[2,128,256]{2,1,0:T(8,128)(2,1)S(1)} %gather_fusion.1), channel_id=1, source_target_pairs={{0,24},{2,26},{4,28},{6,30},{8,0},{10,2},{12,4},{14,6},{16,8},{18,... | collective-permute-start | bytes 393224 | tf_op jit(solution)/shard_map/ppermute | solution.py:267
  80.8 0.3 collective-permute-start.5
  81.2 1.0 pad_maximum_fusion.2.refs_2_
  82.2 2.2 %collective-permute-done.17 = bf16[2,128,256]{2,1,0:T(8,128)(2,1)S(1)} collective-permute-done((bf16[2,128,256]{2,1,0:T(8,128)(2,1)S(1)}, bf16[2,128,256]{2,1,0:T(8,128)(2,1)S(1)}, u32[]{:S(2)}, u32[]{:S(2)}) %collective-permute-start.17) | collective-permute-done | bytes 131104 | tf_op jit(solution)/shard_map/ppermute | solution.py:267
  84.3 1.4 %collective-permute-start.14 = (bf16[2,128,256]{2,1,0:T(8,128)(2,1)S(1)}, bf16[2,128,256]{2,1,0:T(8,128)(2,1)S(1)}, u32[]{:S(2)}, u32[]{:S(2)}) collective-permute-start(bf16[2,128,256]{2,1,0:T(8,128)(2,1)S(1)} %gather_fusion.1), channel_id=1, source_target_pairs={{0,2},{1,5},{2,0},{3,7},{4,6},{5,1},{6,4},{7,3},{8,10},{9,13},{10,... | collective-permute-start | bytes 393224 | tf_op jit(solution)/shard_map/ppermute | solution.py:279
  85.7 1.1 collective-permute-start.18
  86.8 0.7 constant_dynamic-update-slice_fusion.6
  87.5 2.4 %collective-permute-done.14 = bf16[2,128,256]{2,1,0:T(8,128)(2,1)S(1)} collective-permute-done((bf16[2,128,256]{2,1,0:T(8,128)(2,1)S(1)}, bf16[2,128,256]{2,1,0:T(8,128)(2,1)S(1)}, u32[]{:S(2)}, u32[]{:S(2)}) %collective-permute-start.14) | collective-permute-done | bytes 131104 | tf_op jit(solution)/shard_map/ppermute | solution.py:279
  89.9 1.1 collective-permute-start
  91.0 0.8 collective-permute-done.other_ref
  91.8 1.1 collective-permute-start.20
  92.9 0.6 collective-permute-start.23
  93.5 0.7 constant_dynamic-update-slice_fusion.5
  94.2 0.1 collective-permute-done.18
  94.3 1.6 %collective-permute-start.15 = (bf16[4,128,256]{2,1,0:T(8,128)(2,1)S(1)}, bf16[4,128,256]{2,1,0:T(8,128)(2,1)S(1)}, u32[]{:S(2)}, u32[]{:S(2)}) collective-permute-start(bf16[4,128,256]{2,1,0:T(8,128)(2,1)S(1)} %constant_dynamic-update-slice_fusion.2.refs_8_), channel_id=1, source_target_pairs={{0,4},{1,3},{2,6},{3,1},{4,0},{5,7},{6,2},{7,5},{8,12},{9,11},{10,... | collective-permute-start | bytes 786440 | tf_op jit(solution)/shard_map/ppermute | solution.py:279
  95.9 0.8 constant_dynamic-update-slice_fusion.4.refs_10_
  96.7 0.1 collective-permute-start.12
  96.8 1.6 %collective-permute-start.9 = (bf16[8,128,256]{2,1,0:T(8,128)(2,1)S(1)}, bf16[8,128,256]{2,1,0:T(8,128)(2,1)S(1)}, u32[]{:S(2)}, u32[]{:S(2)}) collective-permute-start(bf16[8,128,256]{2,1,0:T(8,128)(2,1)S(1)} %pad_maximum_fusion.2.refs_2_), channel_id=1, source_target_pairs={{0,4},{1,3},{2,6},{3,1},{4,0},{5,7},{6,2},{7,5},{8,12},{9,11},{10,... | collective-permute-start | bytes 1572872 | tf_op jit(solution)/shard_map/ppermute | solution.py:279
  98.4 2.1 %collective-permute-done.20 = bf16[2,128,256]{2,1,0:T(8,128)(2,1)S(1)} collective-permute-done((bf16[2,128,256]{2,1,0:T(8,128)(2,1)S(1)}, bf16[2,128,256]{2,1,0:T(8,128)(2,1)S(1)}, u32[]{:S(2)}, u32[]{:S(2)}) %collective-permute-start.20) | collective-permute-done | bytes 131104 | tf_op jit(solution)/shard_map/ppermute | solution.py:267
  100.5 0.7 collective-permute-start.19
  101.2 1.4 %collective-permute-start.21 = (bf16[2,128,256]{2,1,0:T(8,128)(2,1)S(1)}, bf16[2,128,256]{2,1,0:T(8,128)(2,1)S(1)}, u32[]{:S(2)}, u32[]{:S(2)}) collective-permute-start(bf16[2,128,256]{2,1,0:T(8,128)(2,1)S(1)} %collective-permute-done.20), channel_id=1, source_target_pairs={{0,2},{1,5},{2,0},{3,7},{4,6},{5,1},{6,4},{7,3},{8,10},{9,13},{10,... | collective-permute-start | bytes 393224 | tf_op jit(solution)/shard_map/ppermute | solution.py:279
  102.6 1.3 collective-permute-start.24
  103.8 2.9 %collective-permute-done.21 = bf16[2,128,256]{2,1,0:T(8,128)(2,1)S(1)} collective-permute-done((bf16[2,128,256]{2,1,0:T(8,128)(2,1)S(1)}, bf16[2,128,256]{2,1,0:T(8,128)(2,1)S(1)}, u32[]{:S(2)}, u32[]{:S(2)}) %collective-permute-start.21) | collective-permute-done | bytes 131104 | tf_op jit(solution)/shard_map/ppermute | solution.py:279
  106.8 2.8 %collective-permute-start.11 = (bf16[8,128,256]{2,1,0:T(8,128)(2,1)S(1)}, bf16[8,128,256]{2,1,0:T(8,128)(2,1)S(1)}, u32[]{:S(2)}, u32[]{:S(2)}) collective-permute-start(bf16[8,128,256]{2,1,0:T(8,128)(2,1)S(1)} %collective-permute-done.5.refs_1_), channel_id=1, source_target_pairs={{0,1},{1,0},{2,3},{3,2},{4,5},{5,4},{6,7},{7,6},{8,9},{9,8},{10,11... | collective-permute-start | bytes 1572872 | tf_op jit(solution)/shard_map/ppermute | solution.py:360
  109.6 0.1 collective-permute-start.25
  109.7 0.5 collective-permute-start.22
  110.2 0.4 collective-permute-start.13
  110.6 2.0 %collective-permute-done.19.refs_11_ = bf16[8,128,256]{2,1,0:T(8,128)(2,1)S(1)} collective-permute-done((bf16[8,128,256]{2,1,0:T(8,128)(2,1)}, bf16[8,128,256]{2,1,0:T(8,128)(2,1)S(1)}, u32[]{:S(2)}, u32[]{:S(2)}) %collective-permute-start.19) | collective-permute-done | bytes 524320 | tf_op jit(solution)/shard_map/ppermute | solution.py:279
  112.6 0.8 collective-permute-start.26
  113.5 0.1 collective-permute-start.27
  113.5 2.0 %collective-permute-done.22.refs_13_ = bf16[4,128,256]{2,1,0:T(8,128)(2,1)} collective-permute-done((bf16[4,128,256]{2,1,0:T(8,128)(2,1)S(1)}, bf16[4,128,256]{2,1,0:T(8,128)(2,1)}, u32[]{:S(2)}, u32[]{:S(2)}) %collective-permute-start.22) | collective-permute-done | bytes 262176 | tf_op jit(solution)/shard_map/ppermute | solution.py:279
  115.5 1.2 collective-permute-start.28
  116.7 9.3 %shard_map.82.lists = s32[4,272]{1,0:T(4,128)} custom-call(s32[4]{0:T(128)} %owner_ref.3, s32[2,4,16]{2,1,0:T(4,128)} %copy-done.14, s32[2,4,16]{2,1,0:T(4,128)} %copy-done.16), custom_call_target="tpu_custom_call" | custom-call | tf_op jit(solution)/shard_map/pallas_call | solution.py:222
  126.1 0.8 copy-done.10
  126.9 8.9 %shard_map.84 = bf16[32,128,256]{2,1,0:T(8,128)(2,1)} custom-call(s32[4,272]{1,0:T(4,128)} %shard_map.82.lists, bf16[8,128,256]{2,1,0:T(8,128)(2,1)} %copy-done, bf16[8,128,256]{2,1,0:T(8,128)(2,1)} %copy-done.5, bf16[8,128,256]{2,1,0:T(8,128)(2,1)} %copy-done.1, bf16[8,128,256]{2,1,0:T(8,128)(2,1)} %copy-done.7, ...), custom_call_target="tpu_custom_call" | custom-call | flops 1073741824 | bytes 16777216 | tf_op jit(solution)/shard_map/pallas_call | solution.py:203
  (67 shorter events, 0.3 us)
Async XLA Ops:
  14.5 9.0 %collective-permute-start.1 = (bf16[8,128,256]{2,1,0:T(8,128)(2,1)S(1)}, bf16[8,128,256]{2,1,0:T(8,128)(2,1)S(1)}, u32[]{:S(2)}, u32[]{:S(2)}) collective-permute-start(bf16[8,128,256]{2,1,0:T(8,128)(2,1)S(1)} %bitcast.31), channel_id=1, source_target_pairs={{0,2},{1,5},{2,0},{3,7},{4,6},{5,1},{6,4},{7,3},{8,10},{9,13},{10,... | collective-permute-start | bytes 1572872 | tf_op jit(solution)/shard_map/ppermute | solution.py:279
  23.5 0.8 copy-start.11
  24.3 13.9 %copy-start.2 = (bf16[1,4,16,128,128]{4,3,2,1,0:T(8,128)(2,1)S(1)}, bf16[1,4,16,128,128]{4,3,2,1,0:T(8,128)(2,1)}, u32[]{:S(2)}) copy-start(bf16[1,4,16,128,128]{4,3,2,1,0:T(8,128)(2,1)} %param.14) | copy-start | bytes 6291460
  24.3 20.0 %copy-start.15 = (s32[4]{0:T(128)S(1)}, s32[4]{0:T(128)}, u32[]{:S(2)}) copy-start(s32[4]{0:T(128)} %owner_ref.3) | copy-start | bytes 52
  24.3 32.8 %copy-start.17 = (s32[1,4,16]{2,1,0:T(4,128)S(1)}, s32[1,4,16]{2,1,0:T(4,128)}, u32[]{:S(2)}) copy-start(s32[1,4,16]{2,1,0:T(4,128)} %param.12) | copy-start | bytes 772
  25.1 8.5 %collective-permute-start.2 = (bf16[8,128,256]{2,1,0:T(8,128)(2,1)}, bf16[8,128,256]{2,1,0:T(8,128)(2,1)S(1)}, u32[]{:S(2)}, u32[]{:S(2)}) collective-permute-start(bf16[8,128,256]{2,1,0:T(8,128)(2,1)} %pad_maximum_fusion), channel_id=1, source_target_pairs={{0,4},{1,3},{2,6},{3,1},{4,0},{5,7},{6,2},{7,5},{8,12},{9,11},{10,... | collective-permute-start | bytes 1572872 | tf_op jit(solution)/shard_map/ppermute | solution.py:279
  26.6 44.3 %copy-start.18 = (s32[1,4,16]{2,1,0:T(4,128)S(1)}, s32[1,4,16]{2,1,0:T(4,128)}, u32[]{:S(2)}) copy-start(s32[1,4,16]{2,1,0:T(4,128)} %param.13) | copy-start | bytes 772
  26.6 49.1 %all-to-all-start = ((bf16[16,128,256]{2,1,0:T(8,128)(2,1)}), bf16[16,128,256]{2,1,0:T(8,128)(2,1)}, u32[]{:S(2)}, u32[]{:S(2)}) async-start(bf16[16,128,256]{2,1,0:T(8,128)(2,1)} %bitcast.6), calls=%async_computation | async-start | bytes 2097152 | tf_op jit(solution)/shard_map/all_to_all | solution.py:337
  34.7 18.5 %collective-permute-start.3 = (bf16[4,128,256]{2,1,0:T(8,128)(2,1)S(1)}, bf16[4,128,256]{2,1,0:T(8,128)(2,1)S(1)}, u32[]{:S(2)}, u32[]{:S(2)}) collective-permute-start(bf16[4,128,256]{2,1,0:T(8,128)(2,1)S(1)} %fusion), channel_id=1, source_target_pairs={{0,8},{2,10},{4,12},{6,14},{24,16},{26,18},{28,20},{30,22},{1,9},{... | collective-permute-start | bytes 786440 | tf_op jit(solution)/shard_map/ppermute | solution.py:267
  38.1 58.6 %collective-permute-start.29 = (bf16[64,128,128]{2,1,0:T(8,128)(2,1)S(1)}, bf16[64,128,128]{2,1,0:T(8,128)(2,1)}, u32[]{:S(2)}, u32[]{:S(2)}) collective-permute-start(bf16[64,128,128]{2,1,0:T(8,128)(2,1)S(1)} %bitcast.28), channel_id=1, source_target_pairs={{0,1},{1,0},{2,3},{3,2},{4,5},{5,4},{6,7},{7,6},{8,9},{9,8},{10,11... | collective-permute-start | bytes 6291464 | tf_op jit(solution)/shard_map/ppermute | solution.py:360
  53.1 2.6 %collective-permute-start.6 = (bf16[4,128,256]{2,1,0:T(8,128)(2,1)S(1)}, bf16[4,128,256]{2,1,0:T(8,128)(2,1)S(1)}, u32[]{:S(2)}, u32[]{:S(2)}) collective-permute-start(bf16[4,128,256]{2,1,0:T(8,128)(2,1)S(1)} %collective-permute-done.3), channel_id=1, source_target_pairs={{8,16},{10,18},{12,20},{14,22},{16,8},{18,10},{20,12},{22,14},{9,1... | collective-permute-start | bytes 786440 | tf_op jit(solution)/shard_map/ppermute | solution.py:267
  55.7 12.6 %collective-permute-start.7 = (bf16[4,128,256]{2,1,0:T(8,128)(2,1)S(1)}, bf16[4,128,256]{2,1,0:T(8,128)(2,1)}, u32[]{:S(2)}, u32[]{:S(2)}) collective-permute-start(bf16[4,128,256]{2,1,0:T(8,128)(2,1)S(1)} %collective-permute-done.6), channel_id=1, source_target_pairs={{8,0},{10,2},{12,4},{14,6},{16,24},{18,26},{20,28},{22,30},{9,1},{... | collective-permute-start | bytes 786440 | tf_op jit(solution)/shard_map/ppermute | solution.py:267
  57.1 13.8 %collective-permute-start.4 = (bf16[4,128,256]{2,1,0:T(8,128)(2,1)S(1)}, bf16[4,128,256]{2,1,0:T(8,128)(2,1)S(1)}, u32[]{:S(2)}, u32[]{:S(2)}) collective-permute-start(bf16[4,128,256]{2,1,0:T(8,128)(2,1)S(1)} %broadcast_select_fusion.1), channel_id=1, source_target_pairs={{0,2},{1,5},{2,0},{3,7},{4,6},{5,1},{6,4},{7,3},{8,10},{9,13},{10,... | collective-permute-start | bytes 786440 | tf_op jit(solution)/shard_map/ppermute | solution.py:279
  69.3 11.5 %collective-permute-start.8 = (bf16[4,128,256]{2,1,0:T(8,128)(2,1)S(1)}, bf16[4,128,256]{2,1,0:T(8,128)(2,1)}, u32[]{:S(2)}, u32[]{:S(2)}) collective-permute-start(bf16[4,128,256]{2,1,0:T(8,128)(2,1)S(1)} %broadcast_select_fusion), channel_id=1, source_target_pairs={{0,2},{1,5},{2,0},{3,7},{4,6},{5,1},{6,4},{7,3},{8,10},{9,13},{10,... | collective-permute-start | bytes 786440 | tf_op jit(solution)/shard_map/ppermute | solution.py:279
  70.9 25.8 %copy-start.14 = (s32[2,4,16]{2,1,0:T(4,128)}, s32[2,4,16]{2,1,0:T(4,128)S(1)}, u32[]{:S(2)}) copy-start(s32[2,4,16]{2,1,0:T(4,128)S(1)} %constant_dynamic-update-slice_fusion.own_ref) | copy-start | bytes 1540
  70.9 55.1 %copy-start = (bf16[8,128,256]{2,1,0:T(8,128)(2,1)}, bf16[8,128,256]{2,1,0:T(8,128)(2,1)S(1)}, u32[]{:S(2)}) copy-start(bf16[8,128,256]{2,1,0:T(8,128)(2,1)S(1)} %pad_maximum_fusion.1.refs_0_) | copy-start | bytes 1572868
  71.0 21.9 %collective-permute-start.10 = (bf16[8,128,256]{2,1,0:T(8,128)(2,1)S(1)}, bf16[8,128,256]{2,1,0:T(8,128)(2,1)}, u32[]{:S(2)}, u32[]{:S(2)}) collective-permute-start(bf16[8,128,256]{2,1,0:T(8,128)(2,1)S(1)} %pad_maximum_fusion.1.refs_0_), channel_id=1, source_target_pairs={{0,1},{1,0},{2,3},{3,2},{4,5},{5,4},{6,7},{7,6},{8,9},{9,8},{10,11... | collective-permute-start | bytes 1572872 | tf_op jit(solution)/shard_map/ppermute | solution.py:360
  77.5 6.9 %collective-permute-start.17 = (bf16[2,128,256]{2,1,0:T(8,128)(2,1)S(1)}, bf16[2,128,256]{2,1,0:T(8,128)(2,1)S(1)}, u32[]{:S(2)}, u32[]{:S(2)}) collective-permute-start(bf16[2,128,256]{2,1,0:T(8,128)(2,1)S(1)} %gather_fusion.1), channel_id=1, source_target_pairs={{0,8},{2,10},{4,12},{6,14},{8,16},{10,18},{12,20},{14,22},{16,24},... | collective-permute-start | bytes 393224 | tf_op jit(solution)/shard_map/ppermute | solution.py:267
  77.5 8.2 %collective-permute-start.16 = (bf16[2,128,256]{2,1,0:T(8,128)(2,1)S(1)}, bf16[2,128,256]{2,1,0:T(8,128)(2,1)S(1)}, u32[]{:S(2)}, u32[]{:S(2)}) collective-permute-start(bf16[2,128,256]{2,1,0:T(8,128)(2,1)S(1)} %gather_fusion.1), channel_id=1, source_target_pairs={{0,24},{2,26},{4,28},{6,30},{8,0},{10,2},{12,4},{14,6},{16,8},{18,... | collective-permute-start | bytes 393224 | tf_op jit(solution)/shard_map/ppermute | solution.py:267
  80.8 15.9 %collective-permute-start.5 = (bf16[8,128,256]{2,1,0:T(8,128)(2,1)S(1)}, bf16[8,128,256]{2,1,0:T(8,128)(2,1)S(1)}, u32[]{:S(2)}, u32[]{:S(2)}) collective-permute-start(bf16[8,128,256]{2,1,0:T(8,128)(2,1)S(1)} %pad_maximum_fusion.1.refs_0_), channel_id=1, source_target_pairs={{0,4},{1,3},{2,6},{3,1},{4,0},{5,7},{6,2},{7,5},{8,12},{9,11},{10,... | collective-permute-start | bytes 1572872 | tf_op jit(solution)/shard_map/ppermute | solution.py:279
  82.2 43.9 %copy-start.1 = (bf16[8,128,256]{2,1,0:T(8,128)(2,1)}, bf16[8,128,256]{2,1,0:T(8,128)(2,1)S(1)}, u32[]{:S(2)}) copy-start(bf16[8,128,256]{2,1,0:T(8,128)(2,1)S(1)} %pad_maximum_fusion.2.refs_2_) | copy-start | bytes 1572868
  84.3 5.6 %collective-permute-start.14 = (bf16[2,128,256]{2,1,0:T(8,128)(2,1)S(1)}, bf16[2,128,256]{2,1,0:T(8,128)(2,1)S(1)}, u32[]{:S(2)}, u32[]{:S(2)}) collective-permute-start(bf16[2,128,256]{2,1,0:T(8,128)(2,1)S(1)} %gather_fusion.1), channel_id=1, source_target_pairs={{0,2},{1,5},{2,0},{3,7},{4,6},{5,1},{6,4},{7,3},{8,10},{9,13},{10,... | collective-permute-start | bytes 393224 | tf_op jit(solution)/shard_map/ppermute | solution.py:279
  85.7 8.5 %collective-permute-start.18 = (bf16[4,128,256]{2,1,0:T(8,128)(2,1)S(1)}, bf16[4,128,256]{2,1,0:T(8,128)(2,1)S(1)}, u32[]{:S(2)}, u32[]{:S(2)}) collective-permute-start(bf16[4,128,256]{2,1,0:T(8,128)(2,1)S(1)} %pad_maximum_fusion.3), channel_id=1, source_target_pairs={{0,2},{1,5},{2,0},{3,7},{4,6},{5,1},{6,4},{7,3},{8,10},{9,13},{10,... | collective-permute-start | bytes 786440 | tf_op jit(solution)/shard_map/ppermute | solution.py:279
  89.9 1.9 %collective-permute-start = (s32[2,4,16]{2,1,0:T(4,128)S(1)}, s32[2,4,16]{2,1,0:T(4,128)S(1)}, u32[]{:S(2)}, u32[]{:S(2)}) collective-permute-start(s32[2,4,16]{2,1,0:T(4,128)S(1)} %constant_dynamic-update-slice_fusion.own_ref), channel_id=1, source_target_pairs={{0,1},{1,0},{2,3},{3,2},{4,5},{5,4},{6,7},{7,6},{8,9},{9,8},{10,11... | collective-permute-start | bytes 1544 | tf_op jit(solution)/shard_map/ppermute | solution.py:360
  91.0 19.2 %copy-start.3 = (bf16[4,128,256]{2,1,0:T(8,128)(2,1)}, bf16[4,128,256]{2,1,0:T(8,128)(2,1)S(1)}, u32[]{:S(2)}) copy-start(bf16[4,128,256]{2,1,0:T(8,128)(2,1)S(1)} %constant_dynamic-update-slice_fusion.2.refs_8_) | copy-start | bytes 786436
  91.8 24.9 %copy-start.16 = (s32[2,4,16]{2,1,0:T(4,128)}, s32[2,4,16]{2,1,0:T(4,128)S(1)}, u32[]{:S(2)}) copy-start(s32[2,4,16]{2,1,0:T(4,128)S(1)} %collective-permute-done.other_ref) | copy-start | bytes 1540
  91.8 8.7 %collective-permute-start.20 = (bf16[2,128,256]{2,1,0:T(8,128)(2,1)S(1)}, bf16[2,128,256]{2,1,0:T(8,128)(2,1)S(1)}, u32[]{:S(2)}, u32[]{:S(2)}) collective-permute-start(bf16[2,128,256]{2,1,0:T(8,128)(2,1)S(1)} %gather_fusion.1), channel_id=1, source_target_pairs={{0,16},{2,18},{4,20},{6,22},{8,24},{10,26},{12,28},{14,30},{16,0},... | collective-permute-start | bytes 393224 | tf_op jit(solution)/shard_map/ppermute | solution.py:267
  92.9 8.3 %collective-permute-start.23 = (bf16[4,128,256]{2,1,0:T(8,128)(2,1)S(1)}, bf16[4,128,256]{2,1,0:T(8,128)(2,1)S(1)}, u32[]{:S(2)}, u32[]{:S(2)}) collective-permute-start(bf16[4,128,256]{2,1,0:T(8,128)(2,1)S(1)} %constant_dynamic-update-slice_fusion.2.refs_8_), channel_id=1, source_target_pairs={{0,1},{1,0},{2,3},{3,2},{4,5},{5,4},{6,7},{7,6},{8,9},{9,8},{10,11... | collective-permute-start | bytes 786440 | tf_op jit(solution)/shard_map/ppermute | solution.py:360
  94.3 8.3 %collective-permute-start.15 = (bf16[4,128,256]{2,1,0:T(8,128)(2,1)S(1)}, bf16[4,128,256]{2,1,0:T(8,128)(2,1)S(1)}, u32[]{:S(2)}, u32[]{:S(2)}) collective-permute-start(bf16[4,128,256]{2,1,0:T(8,128)(2,1)S(1)} %constant_dynamic-update-slice_fusion.2.refs_8_), channel_id=1, source_target_pairs={{0,4},{1,3},{2,6},{3,1},{4,0},{5,7},{6,2},{7,5},{8,12},{9,11},{10,... | collective-permute-start | bytes 786440 | tf_op jit(solution)/shard_map/ppermute | solution.py:279
  96.7 18.8 %copy-start.5 = (bf16[8,128,256]{2,1,0:T(8,128)(2,1)}, bf16[8,128,256]{2,1,0:T(8,128)(2,1)S(1)}, u32[]{:S(2)}) copy-start(bf16[8,128,256]{2,1,0:T(8,128)(2,1)S(1)} %collective-permute-done.5.refs_1_) | copy-start | bytes 1572868
  96.7 13.0 %collective-permute-start.12 = (bf16[8,128,256]{2,1,0:T(8,128)(2,1)S(1)}, bf16[8,128,256]{2,1,0:T(8,128)(2,1)S(1)}, u32[]{:S(2)}, u32[]{:S(2)}) collective-permute-start(bf16[8,128,256]{2,1,0:T(8,128)(2,1)S(1)} %pad_maximum_fusion.2.refs_2_), channel_id=1, source_target_pairs={{0,1},{1,0},{2,3},{3,2},{4,5},{5,4},{6,7},{7,6},{8,9},{9,8},{10,11... | collective-permute-start | bytes 1572872 | tf_op jit(solution)/shard_map/ppermute | solution.py:360
  96.8 13.4 %collective-permute-start.9 = (bf16[8,128,256]{2,1,0:T(8,128)(2,1)S(1)}, bf16[8,128,256]{2,1,0:T(8,128)(2,1)S(1)}, u32[]{:S(2)}, u32[]{:S(2)}) collective-permute-start(bf16[8,128,256]{2,1,0:T(8,128)(2,1)S(1)} %pad_maximum_fusion.2.refs_2_), channel_id=1, source_target_pairs={{0,4},{1,3},{2,6},{3,1},{4,0},{5,7},{6,2},{7,5},{8,12},{9,11},{10,... | collective-permute-start | bytes 1572872 | tf_op jit(solution)/shard_map/ppermute | solution.py:279
  100.5 12.1 %collective-permute-start.19 = (bf16[8,128,256]{2,1,0:T(8,128)(2,1)}, bf16[8,128,256]{2,1,0:T(8,128)(2,1)S(1)}, u32[]{:S(2)}, u32[]{:S(2)}) collective-permute-start(bf16[8,128,256]{2,1,0:T(8,128)(2,1)} %constant_dynamic-update-slice_fusion.4.refs_10_), channel_id=1, source_target_pairs={{0,4},{1,3},{2,6},{3,1},{4,0},{5,7},{6,2},{7,5},{8,12},{9,11},{10,... | collective-permute-start | bytes 1572872 | tf_op jit(solution)/shard_map/ppermute | solution.py:279
  101.2 8.4 %copy-start.12 = (bf16[4,128,256]{2,1,0:T(8,128)(2,1)}, bf16[4,128,256]{2,1,0:T(8,128)(2,1)S(1)}, u32[]{:S(2)}) copy-start(bf16[4,128,256]{2,1,0:T(8,128)(2,1)S(1)} %collective-permute-done.23.refs_14_) | copy-start | bytes 786436
  101.2 5.6 %collective-permute-start.21 = (bf16[2,128,256]{2,1,0:T(8,128)(2,1)S(1)}, bf16[2,128,256]{2,1,0:T(8,128)(2,1)S(1)}, u32[]{:S(2)}, u32[]{:S(2)}) collective-permute-start(bf16[2,128,256]{2,1,0:T(8,128)(2,1)S(1)} %collective-permute-done.20), channel_id=1, source_target_pairs={{0,2},{1,5},{2,0},{3,7},{4,6},{5,1},{6,4},{7,3},{8,10},{9,13},{10,... | collective-permute-start | bytes 393224 | tf_op jit(solution)/shard_map/ppermute | solution.py:279
  102.6 13.0 %copy-start.13 = (bf16[4,128,256]{2,1,0:T(8,128)(2,1)}, bf16[4,128,256]{2,1,0:T(8,128)(2,1)S(1)}, u32[]{:S(2)}) copy-start(bf16[4,128,256]{2,1,0:T(8,128)(2,1)S(1)} %collective-permute-done.15.refs_9_) | copy-start | bytes 786436
  102.6 7.0 %collective-permute-start.24 = (bf16[4,128,256]{2,1,0:T(8,128)(2,1)S(1)}, bf16[4,128,256]{2,1,0:T(8,128)(2,1)}, u32[]{:S(2)}, u32[]{:S(2)}) collective-permute-start(bf16[4,128,256]{2,1,0:T(8,128)(2,1)S(1)} %collective-permute-done.15.refs_9_), channel_id=1, source_target_pairs={{0,1},{1,0},{2,3},{3,2},{4,5},{5,4},{6,7},{7,6},{8,9},{9,8},{10,11... | collective-permute-start | bytes 786440 | tf_op jit(solution)/shard_map/ppermute | solution.py:360
  106.8 6.7 %collective-permute-start.11 = (bf16[8,128,256]{2,1,0:T(8,128)(2,1)S(1)}, bf16[8,128,256]{2,1,0:T(8,128)(2,1)S(1)}, u32[]{:S(2)}, u32[]{:S(2)}) collective-permute-start(bf16[8,128,256]{2,1,0:T(8,128)(2,1)S(1)} %collective-permute-done.5.refs_1_), channel_id=1, source_target_pairs={{0,1},{1,0},{2,3},{3,2},{4,5},{5,4},{6,7},{7,6},{8,9},{9,8},{10,11... | collective-permute-start | bytes 1572872 | tf_op jit(solution)/shard_map/ppermute | solution.py:360
  109.6 16.5 %copy-start.4 = (bf16[4,128,256]{2,1,0:T(8,128)(2,1)}, bf16[4,128,256]{2,1,0:T(8,128)(2,1)S(1)}, u32[]{:S(2)}) copy-start(bf16[4,128,256]{2,1,0:T(8,128)(2,1)S(1)} %constant_dynamic-update-slice_fusion.7.refs_12_) | copy-start | bytes 786436
  109.6 16.4 %collective-permute-start.25 = (bf16[8,128,256]{2,1,0:T(8,128)(2,1)}, bf16[8,128,256]{2,1,0:T(8,128)(2,1)S(1)}, u32[]{:S(2)}, u32[]{:S(2)}) collective-permute-start(bf16[8,128,256]{2,1,0:T(8,128)(2,1)} %constant_dynamic-update-slice_fusion.4.refs_10_), channel_id=1, source_target_pairs={{0,1},{1,0},{2,3},{3,2},{4,5},{5,4},{6,7},{7,6},{8,9},{9,8},{10,11... | collective-permute-start | bytes 1572872 | tf_op jit(solution)/shard_map/ppermute | solution.py:360
  109.7 5.8 %copy-start.6 = (bf16[8,128,256]{2,1,0:T(8,128)(2,1)}, bf16[8,128,256]{2,1,0:T(8,128)(2,1)S(1)}, u32[]{:S(2)}) copy-start(bf16[8,128,256]{2,1,0:T(8,128)(2,1)S(1)} %collective-permute-done.12.refs_6_) | copy-start | bytes 1572868
  109.7 5.8 %collective-permute-start.22 = (bf16[4,128,256]{2,1,0:T(8,128)(2,1)S(1)}, bf16[4,128,256]{2,1,0:T(8,128)(2,1)}, u32[]{:S(2)}, u32[]{:S(2)}) collective-permute-start(bf16[4,128,256]{2,1,0:T(8,128)(2,1)S(1)} %constant_dynamic-update-slice_fusion.7.refs_12_), channel_id=1, source_target_pairs={{0,4},{1,3},{2,6},{3,1},{4,0},{5,7},{6,2},{7,5},{8,12},{9,11},{10,... | collective-permute-start | bytes 786440 | tf_op jit(solution)/shard_map/ppermute | solution.py:279
  110.2 15.9 %copy-start.7 = (bf16[8,128,256]{2,1,0:T(8,128)(2,1)}, bf16[8,128,256]{2,1,0:T(8,128)(2,1)S(1)}, u32[]{:S(2)}) copy-start(bf16[8,128,256]{2,1,0:T(8,128)(2,1)S(1)} %collective-permute-done.9.refs_3_) | copy-start | bytes 1572868
  110.2 15.8 %collective-permute-start.13 = (bf16[8,128,256]{2,1,0:T(8,128)(2,1)S(1)}, bf16[8,128,256]{2,1,0:T(8,128)(2,1)}, u32[]{:S(2)}, u32[]{:S(2)}) collective-permute-start(bf16[8,128,256]{2,1,0:T(8,128)(2,1)S(1)} %collective-permute-done.9.refs_3_), channel_id=1, source_target_pairs={{0,1},{1,0},{2,3},{3,2},{4,5},{5,4},{6,7},{7,6},{8,9},{9,8},{10,11... | collective-permute-start | bytes 1572872 | tf_op jit(solution)/shard_map/ppermute | solution.py:360
  112.6 13.5 %copy-start.8 = (bf16[8,128,256]{2,1,0:T(8,128)(2,1)}, bf16[8,128,256]{2,1,0:T(8,128)(2,1)S(1)}, u32[]{:S(2)}) copy-start(bf16[8,128,256]{2,1,0:T(8,128)(2,1)S(1)} %collective-permute-done.19.refs_11_) | copy-start | bytes 1572868
  112.6 13.5 %collective-permute-start.26 = (bf16[8,128,256]{2,1,0:T(8,128)(2,1)S(1)}, bf16[8,128,256]{2,1,0:T(8,128)(2,1)}, u32[]{:S(2)}, u32[]{:S(2)}) collective-permute-start(bf16[8,128,256]{2,1,0:T(8,128)(2,1)S(1)} %collective-permute-done.19.refs_11_), channel_id=1, source_target_pairs={{0,1},{1,0},{2,3},{3,2},{4,5},{5,4},{6,7},{7,6},{8,9},{9,8},{10,11... | collective-permute-start | bytes 1572872 | tf_op jit(solution)/shard_map/ppermute | solution.py:360
  113.5 12.7 %copy-start.9 = (bf16[8,128,256]{2,1,0:T(8,128)(2,1)}, bf16[8,128,256]{2,1,0:T(8,128)(2,1)S(1)}, u32[]{:S(2)}) copy-start(bf16[8,128,256]{2,1,0:T(8,128)(2,1)S(1)} %collective-permute-done.11.refs_5_) | copy-start | bytes 1572868
  113.5 12.5 %collective-permute-start.27 = (bf16[4,128,256]{2,1,0:T(8,128)(2,1)S(1)}, bf16[4,128,256]{2,1,0:T(8,128)(2,1)}, u32[]{:S(2)}, u32[]{:S(2)}) collective-permute-start(bf16[4,128,256]{2,1,0:T(8,128)(2,1)S(1)} %constant_dynamic-update-slice_fusion.7.refs_12_), channel_id=1, source_target_pairs={{0,1},{1,0},{2,3},{3,2},{4,5},{5,4},{6,7},{7,6},{8,9},{9,8},{10,11... | collective-permute-start | bytes 786440 | tf_op jit(solution)/shard_map/ppermute | solution.py:360
  115.5 10.5 %collective-permute-start.28 = (bf16[4,128,256]{2,1,0:T(8,128)(2,1)}, bf16[4,128,256]{2,1,0:T(8,128)(2,1)}, u32[]{:S(2)}, u32[]{:S(2)}) collective-permute-start(bf16[4,128,256]{2,1,0:T(8,128)(2,1)} %collective-permute-done.22.refs_13_), channel_id=1, source_target_pairs={{0,1},{1,0},{2,3},{3,2},{4,5},{5,4},{6,7},{7,6},{8,9},{9,8},{10,11... | collective-permute-start | bytes 786440 | tf_op jit(solution)/shard_map/ppermute | solution.py:360
  126.0 0.8 copy-start.10

commit v6 on v5

--- a/solution.py
+++ b/solution.py
@@ -111,46 +111,40 @@
     finish(acc, weight_ref, out_ref, stage, out_sem)
 
 
-def lists_kernel(n_blocks, owner_ref, own_ref, other_ref, lists):
+def lists_kernel(n_blocks, own_ref, other_ref, lists):
     me, rep = lax.axis_index("dom"), lax.axis_index("rep")
-    quad, z = me % 4, me // 4
     sections, each = own_ref.shape[1:]
     middle = lists.shape[1] // 2
-    known, others, rank = jnp.int32(0), jnp.int32(0), jnp.int32(0)
+    early, late = jnp.int32(0), jnp.int32(0)
     for s in range(sections):
-        owner = owner_ref[s]
-        is_end = jnp.logical_or(owner == 0, owner == 15)
-        slot = jnp.where(is_end, ((owner == 0) != (z < 2)).astype(jnp.int32), rank)
-        rank = rank + 1 - is_end.astype(jnp.int32)
         for part, ref in enumerate((own_ref, other_ref)):
 
-            def pick(k, counts, ref=ref, part=part, s=s, slot=slot, owner=owner, is_end=is_end):
+            def pick(k, counts, ref=ref, part=part, s=s):
+                early, late = counts
                 row = ref[0, s, k] - rep * n_blocks
                 here = jnp.logical_and(row >= 0, row < n_blocks)
                 col = ref[1, s, k]
-                holder, quarter, within = col // 16, (col % 16) // 4, col % 4
-                base = jnp.where(holder == rep, 0, 32)
-                at_end = place_of(quarter ^ quad, holder) + 4 * slot
-                turn = place_of(quarter ^ (owner % 4), holder)
-                chip = jnp.where(turn == 0, 3, jnp.where(turn == 3, 0, turn)) * 4 + within
-                shift = (chip // 4 - z) & 3
-                by = place_of((chip % 4) ^ quad, holder)
-                at_other = jnp.where(
-                    (shift & 1) == 1,
-                    8 + by * 4 + (shift // 2) * 2,
-                    jnp.where(shift == 0, 0, 24) + by * 2,
+                holder, chip = col // 16, col % 16
+                other = (holder != rep).astype(jnp.int32)
+                shift = (chip // 4 - me // 4) & 3
+                at = place_of((chip ^ me) & 3, holder) * sections + s
+                at = jnp.where((shift & 1) == 1, 4 * sections + at + (at // 4 + shift // 2) * 4, at)
+                is_late = shift == 2
+                place = jnp.where(is_late, 96 + other * 16 + at, other * 48 + at)
+                put(
+                    lists,
+                    jnp.where(is_late, middle + late, early),
+                    here,
+                    (part * sections + s) * each + k,
+                    row,
+                    place,
                 )
-                place = jnp.where(is_end, base + at_end * 4 + within, 64 + base + at_other + slot)
-                tile = (part * sections + s) * each + k
-                known, others = counts
-                target = jnp.where(is_end, known, middle + others)
-                put(lists, target, here, tile, row, place)
                 now = here.astype(jnp.int32)
-                return known + jnp.where(is_end, now, 0), others + jnp.where(is_end, 0, now)
-
-            known, others = lax.fori_loop(0, each, pick, (known, others))
-    lists[3, 0] = pad(lists, 0, known, n_blocks)
-    lists[3, middle] = pad(lists, middle, others, n_blocks)
+                return early + jnp.where(is_late, 0, now), late + jnp.where(is_late, now, 0)
+
+            early, late = lax.fori_loop(0, each, pick, (early, late))
+    lists[3, 0] = pad(lists, 0, early, n_blocks)
+    lists[3, middle] = pad(lists, middle, late, n_blocks)
 
 
 HBM = pl.BlockSpec(memory_space=pltpu.HBM)
@@ -217,28 +211,26 @@
     )(lists, *flat, *tile_list, weight)
 
 
-def product_lists(section_owner, own, other, n_blocks):
+def product_lists(own, other, n_blocks):
     n_tiles = 2 * own.shape[1] * own.shape[2]
     return pl.pallas_call(
         functools.partial(lists_kernel, n_blocks),
         out_shape=jax.ShapeDtypeStruct((4, 2 * (n_tiles + UNROLL)), jnp.int32),
-        in_specs=[SMEM] * 3,
+        in_specs=[SMEM] * 2,
         out_specs=SMEM,
-    )(section_owner, own, other)
+    )(own, other)
 
 
 def lines_kernel(owner_ref, blocks_ref, order_ref, out_ref):
     me, rep = lax.axis_index("dom"), lax.axis_index("rep")
-    sections, n_send = blocks_ref.shape
+    sections = blocks_ref.shape[0]
     section = jnp.int32(0)
     for s in range(sections):
         section = jnp.where(owner_ref[s] == me, s, section)
-    each = n_send // 8
-    for group, across in enumerate((3, 1 + rep, 2 - rep, 0)):
-        base = rep * (n_send // 2) + ((me % 4) ^ across) * each
-        for j in range(each):
-            block = blocks_ref[section, base + j]
-            out_ref[pl.ds(group * each + j, 1), :] = order_ref[pl.ds(block, 1), :]
+    share = out_ref.shape[0]
+    for j in range(share):
+        block = blocks_ref[section, rep * share + j]
+        out_ref[pl.ds(j, 1), :] = order_ref[pl.ds(block, 1), :]
 
 
 def share_lines(node_order, section_owner, send_blocks, tile_len):
@@ -283,29 +275,8 @@
     return jnp.where(core == 0, across, (across & 1) * 2 + across // 2)
 
 
-def quad_scatter(rows):
-    each = rows.shape[0] // 4
-    by_first = cross(rows[: 2 * each], 0)
-    by_second = cross(jnp.concatenate([rows[2 * each : 3 * each], by_first[:each]]), 1)
-    return rows[3 * each :], by_first[each:], by_second[:each], by_second[each:]
-
-
-INWARD = [(i, i + 4) for i in range(4)] + [(i, i - 4) for i in range(12, 16)]
-MIDDLE = [(i, i + 4) for i in range(4, 8)] + [(i, i - 4) for i in range(8, 12)]
-OUTWARD = [(i, i - 4) for i in range(4, 8)] + [(i, i + 4) for i in range(8, 12)]
-
-
 def tie(value, after):
     return lax.optimization_barrier((value, after))[0]
-
-
-def along_z_ends(first, z):
-    outer = jnp.logical_or(z == 0, z == 3)
-    came = move(first, INWARD)
-    near = jnp.where(outer, first, came)
-    across = move(came, MIDDLE)
-    beyond = move(across, OUTWARD)
-    return came, near, jnp.where(outer, beyond, across)
 
 
 def quad_gather(own):
@@ -318,27 +289,14 @@
 }
 
 
-def gather_ends(rows):
-    me = lax.axis_index("dom")
-    quad, z = me % 4, me // 4
-    held = quad_scatter(rows)
-    source = jnp.where(z < 2, 0, 3)
-    quarter = lax.select_n(place_of(quad ^ source, lax.axis_index("rep")), *held)
-    came, near, far = along_z_ends(quarter, z)
-    return quad_gather(near) + quad_gather(far)
-
-
-def gather_others(rows, section_owner):
-    is_end = jnp.logical_or(section_owner == 0, section_owner == 15)
-    rank = jnp.cumsum(1 - is_end.astype(jnp.int32)) - 1
-    owners = jnp.stack(
-        [jnp.sum(jnp.where(jnp.logical_or(is_end, rank != i), 0, section_owner)) for i in (0, 1)]
-    )
+def gather_small(rows, section_owner, lists):
     landed = lax.all_to_all(rows, "dom", 0, 0, tiled=True)
-    shard = landed.at[owners].get(mode="promise_in_bounds")
+    shard = landed.at[section_owner].get(mode="promise_in_bounds")
+    shard, lists = lax.optimization_barrier((shard, lists))
     near = [move(shard, RING[1]), move(shard, RING[3])]
     far = move(tie(shard, near[0]), RING[2])
-    return quad_gather(shard) + quad_gather(jnp.concatenate(near)) + quad_gather(far)
+    early = quad_gather(shard) + quad_gather(jnp.concatenate(near))
+    return early, quad_gather(far), lists
 
 
 def body(features, node_order, section_owner, send_blocks, tile_rows, tile_cols, tiles, weight):
@@ -360,12 +318,12 @@
             return lax.ppermute(value, "rep", swap)
 
         tile_list = [own_tiles, exchange(own_tiles)]
-        lists = product_lists(section_owner, numbers, exchange(numbers), n_blocks)
+        lists = product_lists(numbers, exchange(numbers), n_blocks)
         lines = share_lines(node_order, section_owner, send_blocks, tile_len)
         mine = features.at[lines.reshape(-1)].get(mode="promise_in_bounds")
         mine = mine.reshape(-1, tile_len, width)
-        own = [gather_ends(mine), gather_others(mine, section_owner)]
-        parts = [part + [exchange(piece) for piece in part] for part in own]
+        early, late, lists = gather_small(mine, section_owner, lists)
+        parts = [part + [exchange(piece) for piece in part] for part in (early, late)]
         ends, place = [], 0
         for part in parts:
             ends.append([])

time: 137 us -> 116 us (0.85)
  starting transfers between devices: 49.9 us -> 26.8 us
  waiting for transfers between devices: 40.1 us -> 54.4 us
  other arithmetic: 6.78 us -> 0.77 us
  local copies, waits for them, and re-layouts: 18.9 us -> 15.4 us
  Pallas kernels: 19.6 us -> 17.1 us
    all_to_all x1, waiting for transfers between devices: 0.01 us -> 13.2 us  [gather_small(): landed = lax.all_to_all(rows, 'dom', 0, 0, tiled=True)]
    ppermute x12 -> x8, starting transfers between devices: 19.3 us -> 6.71 us  [exchange(): return lax.ppermute(value, 'rep', swap)]
    ppermute x6 -> x3, starting transfers between devices: 9.76 us -> 3.56 us  [move(): return lax.ppermute(value, 'dom', pairs)]
    ppermute x12 -> x6, starting transfers between devices: 15.1 us -> 8.93 us  [cross(): return lax.ppermute(value, ('dom', 'rep'), pairs)]
    select_n x4 -> x1, other arithmetic: 3.25 us -> 0.01 us  [gather_small(): shard = landed.at[section_owner].get(mode='promise_in_bounds')]
    pallas_call x1, Pallas kernels: 9.26 us -> 6.51 us  [product_lists(): pl.pallas_call(functools.partial(lists_kernel, n_blocks), out_shape=jax.S...]
    slice x3 -> x0, local copies, waits for them, and re-layouts: 2.16 us -> none  [the longest x1 1.08 us: quad_scatter(): by_first = cross(rows[:2 * each], 0)]
    concatenate x4 -> x1, other arithmetic: 1.93 us -> 0.05 us  [gather_small(): early = quad_gather(shard) + quad_gather(jnp.concatenate(near))]
  transfers between devices with their start and end apart: 31 -> 18, of which waited for: 12 -> 10; matrix products, arithmetic and copies ran while one was open for 7% -> 1% of each run, Pallas kernels for 7% -> 6%
where the time goes in v6:
time: 116 us; the launch traced here: 115 us
  waiting for transfers between devices  54.4 us (47%)
  starting transfers between devices  26.8 us (23%)
  Pallas kernels  17.1 us (15%)
  local copies, waits for them, and re-layouts  15.4 us (13%)
    ppermute x3, waiting for transfers between devices, move(): return lax.ppermute(value, 'dom', pairs)  23 us
    ppermute x6, waiting for transfers between devices, cross(): return lax.ppermute(value, ('dom', 'rep'), pairs)  16 us
    all_to_all x1, waiting for transfers between devices, gather_small(): landed = lax.all_to_all(rows, 'dom', 0, 0, tiled=True)  13.2 us
    gather x1, local copies, waits for them, and re-layouts, body(): mine = features.at[lines.reshape(-1)].get(mode='promise_in_bounds')  11.2 us
    pallas_call x1, Pallas kernels, products_in_phases(): pl.pallas_call(functools.partial(phased_kernel, places), out_shape=jax.Sh...  9.15 us
    ppermute x6, starting transfers between devices, cross(): return lax.ppermute(value, ('dom', 'rep'), pairs)  8.93 us
    all_to_all x1, starting transfers between devices, gather_small(): landed = lax.all_to_all(rows, 'dom', 0, 0, tiled=True)  7.55 us
    ppermute x8, starting transfers between devices, exchange(): return lax.ppermute(value, 'rep', swap)  6.71 us
  transfers between devices with their start and end apart: 18, of which 10 were waited for; matrix products, arithmetic and copies ran while one was open for 1% of the time, Pallas kernels for 6%

profile of v6, /device:TPU:1, one launch (start us, length us, event | category | flops | bytes accessed | tf_op | source)
XLA Modules:
  0.0 114.6 jit_solution(14742581724008435105)
XLA Ops:
  0.0 1.4 %shard_map.82 = s32[16,128]{1,0:T(8,128)} custom-call(s32[4]{0:T(128)} %owner_ref.1, s32[4,32]{1,0:T(4,128)} %blocks_ref.1, s32[64,128]{1,0:T(8,128)} %bitcast.8), custom_call_target="tpu_custom_call" | custom-call | tf_op jit(solution)/shard_map/pallas_call | solution.py:237
  1.4 0.7 compare_select_fusion
  2.1 0.0 copy-start.15
  2.1 11.2 %gather_fusion = bf16[2048,256]{1,0:T(8,128)(2,1)} fusion(bf16[8192,256]{1,0:T(8,128)(2,1)} %param.8, s32[2048]{0:T(1024)S(1)} %broadcast_clamp_fusion), kind=kCustom, calls=%fused_computation | custom fusion | bytes 2105344 | tf_op jit(solution)/shard_map/gather | solution.py:323
  13.4 7.6 %all-to-all-start = ((bf16[16,128,256]{2,1,0:T(8,128)(2,1)}), bf16[16,128,256]{2,1,0:T(8,128)(2,1)S(1)}, u32[]{:S(2)}, u32[]{:S(2)}) async-start(bf16[16,128,256]{2,1,0:T(8,128)(2,1)} %bitcast.3), calls=%async_computation | async-start | bytes 2097152 | tf_op jit(solution)/shard_map/all_to_all | solution.py:293
  21.0 0.0 copy-done.15
  21.0 0.0 copy-done.16
  21.0 0.0 copy-start.13
  21.0 1.0 collective-permute-start
  22.0 0.0 copy-done
  22.0 0.1 collective-permute-start.16
  22.1 0.0 copy-done.17
  22.1 0.7 collective-permute-done.other_ref
  22.9 0.0 copy-done.13
  22.9 0.6 copy-done.14
  23.4 6.5 %shard_map.83.lists = s32[4,272]{1,0:T(4,128)} custom-call(s32[2,4,16]{2,1,0:T(4,128)} %copy-done.13, s32[2,4,16]{2,1,0:T(4,128)} %copy-done.14), custom_call_target="tpu_custom_call" | custom-call | tf_op jit(solution)/shard_map/pallas_call | solution.py:216
  30.0 13.2 %all-to-all-done = bf16[16,128,256]{2,1,0:T(8,128)(2,1)S(1)} async-done(((bf16[16,128,256]{2,1,0:T(8,128)(2,1)}), bf16[16,128,256]{2,1,0:T(8,128)(2,1)S(1)}, u32[]{:S(2)}, u32[]{:S(2)}) %all-to-all-start) | async-done | bytes 1048608 | tf_op jit(solution)/shard_map/all_to_all | solution.py:293
  43.1 0.6 gather_fusion.1
  43.7 3.6 %collective-permute-start.4 = (bf16[4,128,256]{2,1,0:T(8,128)(2,1)S(1)}, bf16[4,128,256]{2,1,0:T(8,128)(2,1)S(1)}, u32[]{:S(2)}, u32[]{:S(2)}) collective-permute-start(bf16[4,128,256]{2,1,0:T(8,128)(2,1)S(1)} %gather_fusion.1), channel_id=1, source_target_pairs={{0,8},{2,10},{4,12},{6,14},{8,16},{10,18},{12,20},{14,22},{16,24},... | collective-permute-start | bytes 786440 | tf_op jit(solution)/shard_map/ppermute | solution.py:259
  47.3 0.0 collective-permute-start.3
  47.3 3.6 %collective-permute-done.4 = bf16[4,128,256]{2,1,0:T(8,128)(2,1)S(1)} collective-permute-done((bf16[4,128,256]{2,1,0:T(8,128)(2,1)S(1)}, bf16[4,128,256]{2,1,0:T(8,128)(2,1)S(1)}, u32[]{:S(2)}, u32[]{:S(2)}) %collective-permute-start.4) | collective-permute-done | bytes 262176 | tf_op jit(solution)/shard_map/ppermute | solution.py:259
  50.9 7.0 %collective-permute-done.3 = bf16[4,128,256]{2,1,0:T(8,128)(2,1)S(1)} collective-permute-done((bf16[4,128,256]{2,1,0:T(8,128)(2,1)S(1)}, bf16[4,128,256]{2,1,0:T(8,128)(2,1)S(1)}, u32[]{:S(2)}, u32[]{:S(2)}) %collective-permute-start.3) | collective-permute-done | bytes 262176 | tf_op jit(solution)/shard_map/ppermute | solution.py:259
  58.0 3.2 %collective-permute-start.5 = (bf16[8,128,256]{2,1,0:T(8,128)(2,1)S(1)}, bf16[8,128,256]{2,1,0:T(8,128)(2,1)S(1)}, u32[]{:S(2)}, u32[]{:S(2)}) collective-permute-start(bf16[8,128,256]{2,1,0:T(8,128)(2,1)S(1)} %pad_maximum_fusion), channel_id=1, source_target_pairs={{0,2},{1,5},{2,0},{3,7},{4,6},{5,1},{6,4},{7,3},{8,10},{9,13},{10,... | collective-permute-start | bytes 1572872 | tf_op jit(solution)/shard_map/ppermute | solution.py:271
  61.3 6.8 %collective-permute-done.5 = bf16[8,128,256]{2,1,0:T(8,128)(2,1)S(1)} collective-permute-done((bf16[8,128,256]{2,1,0:T(8,128)(2,1)S(1)}, bf16[8,128,256]{2,1,0:T(8,128)(2,1)S(1)}, u32[]{:S(2)}, u32[]{:S(2)}) %collective-permute-start.5) | collective-permute-done | bytes 524320 | tf_op jit(solution)/shard_map/ppermute | solution.py:271
  68.1 0.0 copy-start.1
  68.2 0.4 collective-permute-start.6
  68.5 0.0 collective-permute-start.11
  68.5 1.5 %collective-permute-start.1 = (bf16[4,128,256]{2,1,0:T(8,128)(2,1)S(1)}, bf16[4,128,256]{2,1,0:T(8,128)(2,1)S(1)}, u32[]{:S(2)}, u32[]{:S(2)}) collective-permute-start(bf16[4,128,256]{2,1,0:T(8,128)(2,1)S(1)} %gather_fusion.1), channel_id=1, source_target_pairs={{0,2},{1,5},{2,0},{3,7},{4,6},{5,1},{6,4},{7,3},{8,10},{9,13},{10,... | collective-permute-start | bytes 786440 | tf_op jit(solution)/shard_map/ppermute | solution.py:271
  70.0 12.3 %collective-permute-done.11 = bf16[4,128,256]{2,1,0:T(8,128)(2,1)S(1)} collective-permute-done((bf16[4,128,256]{2,1,0:T(8,128)(2,1)S(1)}, bf16[4,128,256]{2,1,0:T(8,128)(2,1)S(1)}, u32[]{:S(2)}, u32[]{:S(2)}) %collective-permute-start.11) | collective-permute-done | bytes 262176 | tf_op jit(solution)/shard_map/ppermute | solution.py:259
  82.3 2.1 %collective-permute-start.12 = (bf16[4,128,256]{2,1,0:T(8,128)(2,1)S(1)}, bf16[4,128,256]{2,1,0:T(8,128)(2,1)S(1)}, u32[]{:S(2)}, u32[]{:S(2)}) collective-permute-start(bf16[4,128,256]{2,1,0:T(8,128)(2,1)S(1)} %collective-permute-done.11), channel_id=1, source_target_pairs={{0,2},{1,5},{2,0},{3,7},{4,6},{5,1},{6,4},{7,3},{8,10},{9,13},{10,... | collective-permute-start | bytes 786440 | tf_op jit(solution)/shard_map/ppermute | solution.py:271
  84.4 0.0 collective-permute-done.1
  84.4 0.0 copy-start.2
  84.4 0.9 collective-permute-start.7
  85.3 0.4 collective-permute-start.2
  85.8 2.7 %collective-permute-done.12 = bf16[4,128,256]{2,1,0:T(8,128)(2,1)S(1)} collective-permute-done((bf16[4,128,256]{2,1,0:T(8,128)(2,1)S(1)}, bf16[4,128,256]{2,1,0:T(8,128)(2,1)S(1)}, u32[]{:S(2)}, u32[]{:S(2)}) %collective-permute-start.12) | collective-permute-done | bytes 262176 | tf_op jit(solution)/shard_map/ppermute | solution.py:271
  88.4 0.0 copy-start.3
  88.4 1.4 %collective-permute-start.13 = (bf16[8,128,256]{2,1,0:T(8,128)(2,1)S(1)}, bf16[8,128,256]{2,1,0:T(8,128)(2,1)S(1)}, u32[]{:S(2)}, u32[]{:S(2)}) collective-permute-start(bf16[8,128,256]{2,1,0:T(8,128)(2,1)S(1)} %constant_dynamic-update-slice_fusion.7.refs_8_), channel_id=1, source_target_pairs={{0,4},{1,3},{2,6},{3,1},{4,0},{5,7},{6,2},{7,5},{8,12},{9,11},{10,... | collective-permute-start | bytes 1572872 | tf_op jit(solution)/shard_map/ppermute | solution.py:271
  89.9 0.0 collective-permute-done.16.refs_13_
  89.9 3.8 %collective-permute-start.9 = (bf16[16,128,256]{2,1,0:T(8,128)(2,1)S(1)}, bf16[16,128,256]{2,1,0:T(8,128)(2,1)S(1)}, u32[]{:S(2)}, u32[]{:S(2)}) collective-permute-start(bf16[16,128,256]{2,1,0:T(8,128)(2,1)S(1)} %constant_dynamic-update-slice_fusion.4.refs_2_), channel_id=1, source_target_pairs={{0,1},{1,0},{2,3},{3,2},{4,5},{5,4},{6,7},{7,6},{8,9},{9,8},{10,11... | collective-permute-start | bytes 3145736 | tf_op jit(solution)/shard_map/ppermute | solution.py:318
  93.6 0.0 collective-permute-done.6.refs_3_
  93.6 0.1 collective-permute-start.10
  93.7 0.0 collective-permute-done.7.refs_4_
  93.7 0.4 collective-permute-start.14
  94.2 1.2 %collective-permute-done.2.refs_1_ = bf16[8,128,256]{2,1,0:T(8,128)(2,1)S(1)} collective-permute-done((bf16[8,128,256]{2,1,0:T(8,128)(2,1)S(1)}, bf16[8,128,256]{2,1,0:T(8,128)(2,1)S(1)}, u32[]{:S(2)}, u32[]{:S(2)}) %collective-permute-start.2) | collective-permute-done | bytes 524320 | tf_op jit(solution)/shard_map/ppermute | solution.py:271
  95.4 0.0 collective-permute-start.8
  95.4 5.3 %collective-permute-done.13.refs_9_ = bf16[8,128,256]{2,1,0:T(8,128)(2,1)S(1)} collective-permute-done((bf16[8,128,256]{2,1,0:T(8,128)(2,1)S(1)}, bf16[8,128,256]{2,1,0:T(8,128)(2,1)S(1)}, u32[]{:S(2)}, u32[]{:S(2)}) %collective-permute-start.13) | collective-permute-done | bytes 524320 | tf_op jit(solution)/shard_map/ppermute | solution.py:271
  100.7 0.4 collective-permute-start.15
  101.1 0.0 collective-permute-done.8.refs_5_
  101.1 0.0 collective-permute-done.14.refs_10_
  101.1 0.0 copy-start.10
  101.1 1.5 %collective-permute-done.15.refs_11_ = bf16[8,128,256]{2,1,0:T(8,128)(2,1)S(1)} collective-permute-done((bf16[8,128,256]{2,1,0:T(8,128)(2,1)S(1)}, bf16[8,128,256]{2,1,0:T(8,128)(2,1)S(1)}, u32[]{:S(2)}, u32[]{:S(2)}) %collective-permute-start.15) | collective-permute-done | bytes 524320 | tf_op jit(solution)/shard_map/ppermute | solution.py:318
  102.6 0.0 collective-permute-done.9.refs_6_
  102.6 0.0 copy-done.3
  102.6 0.0 copy-done.4
  102.6 0.0 copy-done.7
  102.6 0.0 copy-done.8
  102.7 0.0 copy-done.9
  102.7 0.0 copy-done.11
  102.7 0.7 copy-done.12
  103.4 0.0 collective-permute-done.10.refs_7_
  103.4 0.0 copy-done.1
  103.4 1.0 copy-done.5
  104.5 1.0 copy-done.6
  105.5 9.1 %shard_map.84 = bf16[32,128,256]{2,1,0:T(8,128)(2,1)} custom-call(s32[4,272]{1,0:T(4,128)} %shard_map.83.lists, bf16[8,128,256]{2,1,0:T(8,128)(2,1)} %copy-done.2, bf16[8,128,256]{2,1,0:T(8,128)(2,1)} %copy-done.8, bf16[16,128,256]{2,1,0:T(8,128)(2,1)} %copy-done.1, bf16[16,128,256]{2,1,0:T(8,128)(2,1)} %copy-done.4, bf16[8,128,256]{2,1,0:T(8,128)(2,1)} %copy-done.7, ...), custom_call_target="tpu_custom_call" | custom-call | flops 1073741824 | bytes 16777216 | tf_op jit(solution)/shard_map/pallas_call | solution.py:197
  (27 shorter events, 0.2 us)
Async XLA Ops:
  2.1 18.8 %copy-start.15 = (s32[1,4,16]{2,1,0:T(4,128)S(1)}, s32[1,4,16]{2,1,0:T(4,128)}, u32[]{:S(2)}) copy-start(s32[1,4,16]{2,1,0:T(4,128)} %param.12) | copy-start | bytes 772
  13.4 7.6 %copy-start.16 = (s32[1,4,16]{2,1,0:T(4,128)S(1)}, s32[1,4,16]{2,1,0:T(4,128)}, u32[]{:S(2)}) copy-start(s32[1,4,16]{2,1,0:T(4,128)} %param.13) | copy-start | bytes 772
  13.4 8.6 %copy-start = (bf16[1,4,16,128,128]{4,3,2,1,0:T(8,128)(2,1)S(1)}, bf16[1,4,16,128,128]{4,3,2,1,0:T(8,128)(2,1)}, u32[]{:S(2)}) copy-start(bf16[1,4,16,128,128]{4,3,2,1,0:T(8,128)(2,1)} %param.14) | copy-start | bytes 6291460
  13.4 8.7 %copy-start.17 = (s32[4]{0:T(128)S(1)}, s32[4]{0:T(128)}, u32[]{:S(2)}) copy-start(s32[4]{0:T(128)} %owner_ref.1) | copy-start | bytes 52
  13.4 29.8 %all-to-all-start = ((bf16[16,128,256]{2,1,0:T(8,128)(2,1)}), bf16[16,128,256]{2,1,0:T(8,128)(2,1)S(1)}, u32[]{:S(2)}, u32[]{:S(2)}) async-start(bf16[16,128,256]{2,1,0:T(8,128)(2,1)} %bitcast.3), calls=%async_computation | async-start | bytes 2097152 | tf_op jit(solution)/shard_map/all_to_all | solution.py:293
  21.0 1.9 %copy-start.13 = (s32[2,4,16]{2,1,0:T(4,128)}, s32[2,4,16]{2,1,0:T(4,128)S(1)}, u32[]{:S(2)}) copy-start(s32[2,4,16]{2,1,0:T(4,128)S(1)} %constant_dynamic-update-slice_fusion.own_ref) | copy-start | bytes 1540
  21.0 1.8 %collective-permute-start = (s32[2,4,16]{2,1,0:T(4,128)S(1)}, s32[2,4,16]{2,1,0:T(4,128)S(1)}, u32[]{:S(2)}, u32[]{:S(2)}) collective-permute-start(s32[2,4,16]{2,1,0:T(4,128)S(1)} %constant_dynamic-update-slice_fusion.own_ref), channel_id=1, source_target_pairs={{0,1},{1,0},{2,3},{3,2},{4,5},{5,4},{6,7},{7,6},{8,9},{9,8},{10,11... | collective-permute-start | bytes 1544 | tf_op jit(solution)/shard_map/ppermute | solution.py:318
  22.0 67.8 %collective-permute-start.16 = (bf16[64,128,128]{2,1,0:T(8,128)(2,1)S(1)}, bf16[64,128,128]{2,1,0:T(8,128)(2,1)}, u32[]{:S(2)}, u32[]{:S(2)}) collective-permute-start(bf16[64,128,128]{2,1,0:T(8,128)(2,1)S(1)} %bitcast.7), channel_id=1, source_target_pairs={{0,1},{1,0},{2,3},{3,2},{4,5},{5,4},{6,7},{7,6},{8,9},{9,8},{10,11... | collective-permute-start | bytes 6291464 | tf_op jit(solution)/shard_map/ppermute | solution.py:318
  22.9 0.6 copy-start.14
  43.7 7.2 %collective-permute-start.4 = (bf16[4,128,256]{2,1,0:T(8,128)(2,1)S(1)}, bf16[4,128,256]{2,1,0:T(8,128)(2,1)S(1)}, u32[]{:S(2)}, u32[]{:S(2)}) collective-permute-start(bf16[4,128,256]{2,1,0:T(8,128)(2,1)S(1)} %gather_fusion.1), channel_id=1, source_target_pairs={{0,8},{2,10},{4,12},{6,14},{8,16},{10,18},{12,20},{14,22},{16,24},... | collective-permute-start | bytes 786440 | tf_op jit(solution)/shard_map/ppermute | solution.py:259
  47.3 10.7 %collective-permute-start.3 = (bf16[4,128,256]{2,1,0:T(8,128)(2,1)S(1)}, bf16[4,128,256]{2,1,0:T(8,128)(2,1)S(1)}, u32[]{:S(2)}, u32[]{:S(2)}) collective-permute-start(bf16[4,128,256]{2,1,0:T(8,128)(2,1)S(1)} %gather_fusion.1), channel_id=1, source_target_pairs={{0,24},{2,26},{4,28},{6,30},{8,0},{10,2},{12,4},{14,6},{16,8},{18,... | collective-permute-start | bytes 786440 | tf_op jit(solution)/shard_map/ppermute | solution.py:259
  58.0 10.1 %collective-permute-start.5 = (bf16[8,128,256]{2,1,0:T(8,128)(2,1)S(1)}, bf16[8,128,256]{2,1,0:T(8,128)(2,1)S(1)}, u32[]{:S(2)}, u32[]{:S(2)}) collective-permute-start(bf16[8,128,256]{2,1,0:T(8,128)(2,1)S(1)} %pad_maximum_fusion), channel_id=1, source_target_pairs={{0,2},{1,5},{2,0},{3,7},{4,6},{5,1},{6,4},{7,3},{8,10},{9,13},{10,... | collective-permute-start | bytes 1572872 | tf_op jit(solution)/shard_map/ppermute | solution.py:271
  68.1 35.3 %copy-start.1 = (bf16[16,128,256]{2,1,0:T(8,128)(2,1)}, bf16[16,128,256]{2,1,0:T(8,128)(2,1)S(1)}, u32[]{:S(2)}) copy-start(bf16[16,128,256]{2,1,0:T(8,128)(2,1)S(1)} %constant_dynamic-update-slice_fusion.4.refs_2_) | copy-start | bytes 3145732
  68.2 25.5 %collective-permute-start.6 = (bf16[16,128,256]{2,1,0:T(8,128)(2,1)S(1)}, bf16[16,128,256]{2,1,0:T(8,128)(2,1)S(1)}, u32[]{:S(2)}, u32[]{:S(2)}) collective-permute-start(bf16[16,128,256]{2,1,0:T(8,128)(2,1)S(1)} %constant_dynamic-update-slice_fusion.4.refs_2_), channel_id=1, source_target_pairs={{0,4},{1,3},{2,6},{3,1},{4,0},{5,7},{6,2},{7,5},{8,12},{9,11},{10,... | collective-permute-start | bytes 3145736 | tf_op jit(solution)/shard_map/ppermute | solution.py:271
  68.5 13.8 %collective-permute-start.11 = (bf16[4,128,256]{2,1,0:T(8,128)(2,1)S(1)}, bf16[4,128,256]{2,1,0:T(8,128)(2,1)S(1)}, u32[]{:S(2)}, u32[]{:S(2)}) collective-permute-start(bf16[4,128,256]{2,1,0:T(8,128)(2,1)S(1)} %gather_fusion.1), channel_id=1, source_target_pairs={{0,16},{2,18},{4,20},{6,22},{8,24},{10,26},{12,28},{14,30},{16,0},... | collective-permute-start | bytes 786440 | tf_op jit(solution)/shard_map/ppermute | solution.py:259
  68.5 15.9 %collective-permute-start.1 = (bf16[4,128,256]{2,1,0:T(8,128)(2,1)S(1)}, bf16[4,128,256]{2,1,0:T(8,128)(2,1)S(1)}, u32[]{:S(2)}, u32[]{:S(2)}) collective-permute-start(bf16[4,128,256]{2,1,0:T(8,128)(2,1)S(1)} %gather_fusion.1), channel_id=1, source_target_pairs={{0,2},{1,5},{2,0},{3,7},{4,6},{5,1},{6,4},{7,3},{8,10},{9,13},{10,... | collective-permute-start | bytes 786440 | tf_op jit(solution)/shard_map/ppermute | solution.py:271
  82.3 6.1 %collective-permute-start.12 = (bf16[4,128,256]{2,1,0:T(8,128)(2,1)S(1)}, bf16[4,128,256]{2,1,0:T(8,128)(2,1)S(1)}, u32[]{:S(2)}, u32[]{:S(2)}) collective-permute-start(bf16[4,128,256]{2,1,0:T(8,128)(2,1)S(1)} %collective-permute-done.11), channel_id=1, source_target_pairs={{0,2},{1,5},{2,0},{3,7},{4,6},{5,1},{6,4},{7,3},{8,10},{9,13},{10,... | collective-permute-start | bytes 786440 | tf_op jit(solution)/shard_map/ppermute | solution.py:271
  84.4 19.0 %copy-start.2 = (bf16[8,128,256]{2,1,0:T(8,128)(2,1)}, bf16[8,128,256]{2,1,0:T(8,128)(2,1)S(1)}, u32[]{:S(2)}) copy-start(bf16[8,128,256]{2,1,0:T(8,128)(2,1)S(1)} %constant_dynamic-update-slice_fusion.2.refs_0_) | copy-start | bytes 1572868
  84.4 9.3 %collective-permute-start.7 = (bf16[8,128,256]{2,1,0:T(8,128)(2,1)S(1)}, bf16[8,128,256]{2,1,0:T(8,128)(2,1)S(1)}, u32[]{:S(2)}, u32[]{:S(2)}) collective-permute-start(bf16[8,128,256]{2,1,0:T(8,128)(2,1)S(1)} %constant_dynamic-update-slice_fusion.2.refs_0_), channel_id=1, source_target_pairs={{0,1},{1,0},{2,3},{3,2},{4,5},{5,4},{6,7},{7,6},{8,9},{9,8},{10,11... | collective-permute-start | bytes 1572872 | tf_op jit(solution)/shard_map/ppermute | solution.py:318
  85.3 10.0 %collective-permute-start.2 = (bf16[8,128,256]{2,1,0:T(8,128)(2,1)S(1)}, bf16[8,128,256]{2,1,0:T(8,128)(2,1)S(1)}, u32[]{:S(2)}, u32[]{:S(2)}) collective-permute-start(bf16[8,128,256]{2,1,0:T(8,128)(2,1)S(1)} %constant_dynamic-update-slice_fusion.2.refs_0_), channel_id=1, source_target_pairs={{0,4},{1,3},{2,6},{3,1},{4,0},{5,7},{6,2},{7,5},{8,12},{9,11},{10,... | collective-permute-start | bytes 1572872 | tf_op jit(solution)/shard_map/ppermute | solution.py:271
  88.4 14.2 %copy-start.3 = (bf16[8,128,256]{2,1,0:T(8,128)(2,1)}, bf16[8,128,256]{2,1,0:T(8,128)(2,1)S(1)}, u32[]{:S(2)}) copy-start(bf16[8,128,256]{2,1,0:T(8,128)(2,1)S(1)} %constant_dynamic-update-slice_fusion.7.refs_8_) | copy-start | bytes 1572868
  88.4 12.2 %collective-permute-start.13 = (bf16[8,128,256]{2,1,0:T(8,128)(2,1)S(1)}, bf16[8,128,256]{2,1,0:T(8,128)(2,1)S(1)}, u32[]{:S(2)}, u32[]{:S(2)}) collective-permute-start(bf16[8,128,256]{2,1,0:T(8,128)(2,1)S(1)} %constant_dynamic-update-slice_fusion.7.refs_8_), channel_id=1, source_target_pairs={{0,4},{1,3},{2,6},{3,1},{4,0},{5,7},{6,2},{7,5},{8,12},{9,11},{10,... | collective-permute-start | bytes 1572872 | tf_op jit(solution)/shard_map/ppermute | solution.py:271
  89.9 12.8 %collective-permute-start.9 = (bf16[16,128,256]{2,1,0:T(8,128)(2,1)S(1)}, bf16[16,128,256]{2,1,0:T(8,128)(2,1)S(1)}, u32[]{:S(2)}, u32[]{:S(2)}) collective-permute-start(bf16[16,128,256]{2,1,0:T(8,128)(2,1)S(1)} %constant_dynamic-update-slice_fusion.4.refs_2_), channel_id=1, source_target_pairs={{0,1},{1,0},{2,3},{3,2},{4,5},{5,4},{6,7},{7,6},{8,9},{9,8},{10,11... | collective-permute-start | bytes 3145736 | tf_op jit(solution)/shard_map/ppermute | solution.py:318
  93.6 9.0 %copy-start.4 = (bf16[16,128,256]{2,1,0:T(8,128)(2,1)}, bf16[16,128,256]{2,1,0:T(8,128)(2,1)S(1)}, u32[]{:S(2)}) copy-start(bf16[16,128,256]{2,1,0:T(8,128)(2,1)S(1)} %collective-permute-done.6.refs_3_) | copy-start | bytes 3145732
  93.6 9.8 %collective-permute-start.10 = (bf16[16,128,256]{2,1,0:T(8,128)(2,1)S(1)}, bf16[16,128,256]{2,1,0:T(8,128)(2,1)S(1)}, u32[]{:S(2)}, u32[]{:S(2)}) collective-permute-start(bf16[16,128,256]{2,1,0:T(8,128)(2,1)S(1)} %collective-permute-done.6.refs_3_), channel_id=1, source_target_pairs={{0,1},{1,0},{2,3},{3,2},{4,5},{5,4},{6,7},{7,6},{8,9},{9,8},{10,11... | collective-permute-start | bytes 3145736 | tf_op jit(solution)/shard_map/ppermute | solution.py:318
  93.7 8.9 %copy-start.7 = (bf16[8,128,256]{2,1,0:T(8,128)(2,1)}, bf16[8,128,256]{2,1,0:T(8,128)(2,1)S(1)}, u32[]{:S(2)}) copy-start(bf16[8,128,256]{2,1,0:T(8,128)(2,1)S(1)} %collective-permute-done.7.refs_4_) | copy-start | bytes 1572868
  93.7 7.4 %collective-permute-start.14 = (bf16[8,128,256]{2,1,0:T(8,128)(2,1)S(1)}, bf16[8,128,256]{2,1,0:T(8,128)(2,1)S(1)}, u32[]{:S(2)}, u32[]{:S(2)}) collective-permute-start(bf16[8,128,256]{2,1,0:T(8,128)(2,1)S(1)} %constant_dynamic-update-slice_fusion.7.refs_8_), channel_id=1, source_target_pairs={{0,1},{1,0},{2,3},{3,2},{4,5},{5,4},{6,7},{7,6},{8,9},{9,8},{10,11... | collective-permute-start | bytes 1572872 | tf_op jit(solution)/shard_map/ppermute | solution.py:318
  95.4 7.3 %copy-start.8 = (bf16[8,128,256]{2,1,0:T(8,128)(2,1)}, bf16[8,128,256]{2,1,0:T(8,128)(2,1)S(1)}, u32[]{:S(2)}) copy-start(bf16[8,128,256]{2,1,0:T(8,128)(2,1)S(1)} %collective-permute-done.2.refs_1_) | copy-start | bytes 1572868
  95.4 5.7 %collective-permute-start.8 = (bf16[8,128,256]{2,1,0:T(8,128)(2,1)S(1)}, bf16[8,128,256]{2,1,0:T(8,128)(2,1)S(1)}, u32[]{:S(2)}, u32[]{:S(2)}) collective-permute-start(bf16[8,128,256]{2,1,0:T(8,128)(2,1)S(1)} %collective-permute-done.2.refs_1_), channel_id=1, source_target_pairs={{0,1},{1,0},{2,3},{3,2},{4,5},{5,4},{6,7},{7,6},{8,9},{9,8},{10,11... | collective-permute-start | bytes 1572872 | tf_op jit(solution)/shard_map/ppermute | solution.py:318
  100.7 2.0 %copy-start.9 = (bf16[8,128,256]{2,1,0:T(8,128)(2,1)}, bf16[8,128,256]{2,1,0:T(8,128)(2,1)S(1)}, u32[]{:S(2)}) copy-start(bf16[8,128,256]{2,1,0:T(8,128)(2,1)S(1)} %collective-permute-done.13.refs_9_) | copy-start | bytes 1572868
  100.7 1.9 %collective-permute-start.15 = (bf16[8,128,256]{2,1,0:T(8,128)(2,1)S(1)}, bf16[8,128,256]{2,1,0:T(8,128)(2,1)S(1)}, u32[]{:S(2)}, u32[]{:S(2)}) collective-permute-start(bf16[8,128,256]{2,1,0:T(8,128)(2,1)S(1)} %collective-permute-done.13.refs_9_), channel_id=1, source_target_pairs={{0,1},{1,0},{2,3},{3,2},{4,5},{5,4},{6,7},{7,6},{8,9},{9,8},{10,11... | collective-permute-start | bytes 1572872 | tf_op jit(solution)/shard_map/ppermute | solution.py:318
  101.1 1.6 %copy-start.11 = (bf16[8,128,256]{2,1,0:T(8,128)(2,1)}, bf16[8,128,256]{2,1,0:T(8,128)(2,1)S(1)}, u32[]{:S(2)}) copy-start(bf16[8,128,256]{2,1,0:T(8,128)(2,1)S(1)} %collective-permute-done.8.refs_5_) | copy-start | bytes 1572868
  101.1 1.6 %copy-start.10 = (bf16[8,128,256]{2,1,0:T(8,128)(2,1)}, bf16[8,128,256]{2,1,0:T(8,128)(2,1)S(1)}, u32[]{:S(2)}) copy-start(bf16[8,128,256]{2,1,0:T(8,128)(2,1)S(1)} %collective-permute-done.14.refs_10_) | copy-start | bytes 1572868
  102.6 0.8 copy-start.12
  103.4 1.0 copy-start.5
  104.5 1.0 copy-start.6

commit v7 on v6

--- a/solution.py
+++ b/solution.py
@@ -221,25 +221,65 @@
     )(own, other)
 
 
-def lines_kernel(owner_ref, blocks_ref, order_ref, out_ref):
+CHUNKS = 8
+ROWS = 16
+
+
+def pick_kernel(owner_ref, blocks_ref, order_ref, features_ref, out_ref, *scratch):
+    lines, held, wide, line_sem, sem = scratch
     me, rep = lax.axis_index("dom"), lax.axis_index("rep")
-    sections = blocks_ref.shape[0]
     section = jnp.int32(0)
-    for s in range(sections):
+    for s in range(blocks_ref.shape[0]):
         section = jnp.where(owner_ref[s] == me, s, section)
-    share = out_ref.shape[0]
-    for j in range(share):
-        block = blocks_ref[section, rep * share + j]
-        out_ref[pl.ds(j, 1), :] = order_ref[pl.ds(block, 1), :]
-
-
-def share_lines(node_order, section_owner, send_blocks, tile_len):
+    share, tile_len = out_ref.shape[:2]
+    size = held.shape[0] // CHUNKS
+    copies = [
+        pltpu.make_async_copy(
+            order_ref.at[blocks_ref[section, rep * share + j]], lines.at[j], line_sem.at[j]
+        )
+        for j in range(share)
+    ]
+    chunks = [
+        pltpu.make_async_copy(
+            features_ref.at[pl.ds(i * size, size)], held.at[pl.ds(i * size, size)], sem.at[i]
+        )
+        for i in range(CHUNKS)
+    ]
+    for copy in copies + chunks:
+        copy.start()
+    for i, copy in enumerate(chunks):
+        copy.wait()
+        wide[pl.ds(i * size, size)] = held[pl.ds(i * size, size)].astype(jnp.float32)
+    for copy in copies:
+        copy.wait()
+
+    def one_block(j, carry):
+        for first in range(0, tile_len, ROWS):
+            rows = [wide[pl.ds(lines[j, 0, first + u], 1), :] for u in range(ROWS)]
+            rows = jnp.concatenate(rows, axis=0).astype(out_ref.dtype)
+            out_ref[j, pl.ds(first, ROWS), :] = rows
+        return carry
+
+    lax.fori_loop(0, share, one_block, 0)
+
+
+def pick_share(features, node_order, section_owner, send_blocks, tile_len):
+    rows, width = features.shape
+    share = send_blocks.shape[1] // 2
     return pl.pallas_call(
-        lines_kernel,
-        out_shape=jax.ShapeDtypeStruct((send_blocks.shape[1] // 2, tile_len), jnp.int32),
-        in_specs=[SMEM, SMEM, VMEM],
+        pick_kernel,
+        out_shape=jax.ShapeDtypeStruct((share, tile_len, width), features.dtype),
+        in_specs=[SMEM, SMEM, HBM, HBM],
         out_specs=VMEM,
-    )(section_owner, send_blocks, node_order[0].reshape(-1, tile_len))
+        scratch_shapes=[
+            pltpu.SMEM((share, 1, tile_len), jnp.int32),
+            pltpu.VMEM((rows, width), features.dtype),
+            pltpu.VMEM((rows, width), jnp.float32),
+            pltpu.SemaphoreType.DMA((share,)),
+            pltpu.SemaphoreType.DMA((CHUNKS,)),
+        ],
+        compiler_params=pltpu.CompilerParams(vmem_limit_bytes=60 * 1024 * 1024),
+    )(section_owner, send_blocks, node_order[0].reshape(-1, 1, tile_len), features)
 
 
 def share_rows(node_order, section_owner, send_blocks, tile_len):
@@ -280,8 +320,9 @@
 
 
 def quad_gather(own):
-    pair = jnp.concatenate([own, cross(own, 0)])
-    return [pair, cross(pair, 1)]
+    came = cross(own, 0)
+    pair = jnp.concatenate([own, came])
+    return came, [pair, cross(pair, 1)]
 
 
 RING = {
@@ -293,10 +334,13 @@
     landed = lax.all_to_all(rows, "dom", 0, 0, tiled=True)
     shard = landed.at[section_owner].get(mode="promise_in_bounds")
     shard, lists = lax.optimization_barrier((shard, lists))
-    near = [move(shard, RING[1]), move(shard, RING[3])]
-    far = move(tie(shard, near[0]), RING[2])
-    early = quad_gather(shard) + quad_gather(jnp.concatenate(near))
-    return early, quad_gather(far), lists
+    one = move(shard, RING[1])
+    near = jnp.concatenate([one, move(shard, RING[3])])
+    came, level = quad_gather(shard)
+    far = move(one, RING[1])
+    near_came, near_level = quad_gather(tie(near, came))
+    near_level[1] = cross(tie(near_level[0], (far, level[1])), 1)
+    return level + near_level, quad_gather(far)[1], lists
 
 
 def body(features, node_order, section_owner, send_blocks, tile_rows, tile_cols, tiles, weight):
@@ -319,9 +363,7 @@
 
         tile_list = [own_tiles, exchange(own_tiles)]
         lists = product_lists(numbers, exchange(numbers), n_blocks)
-        lines = share_lines(node_order, section_owner, send_blocks, tile_len)
-        mine = features.at[lines.reshape(-1)].get(mode="promise_in_bounds")
-        mine = mine.reshape(-1, tile_len, width)
+        mine = pick_share(features, node_order, section_owner, send_blocks, tile_len)
         early, late, lists = gather_small(mine, section_owner, lists)
         parts = [part + [exchange(piece) for piece in part] for part in (early, late)]
         ends, place = [], 0

time: 116 us -> 106 us (0.914)
  local copies, waits for them, and re-layouts: 15.4 us -> 3.7 us
  Pallas kernels: 17.1 us -> 24 us
  waiting for transfers between devices: 54.4 us -> 48.6 us
  starting transfers between devices: 26.8 us -> 28.5 us
    ppermute x3, waiting for transfers between devices: 23 us -> 6.58 us  [move(): return lax.ppermute(value, 'dom', pairs)]
    gather x1 -> x0, local copies, waits for them, and re-layouts: 11.2 us -> none  [body(): mine = features.at[lines.reshape(-1)].get(mode='promise_in_bounds')]
    ppermute x6, waiting for transfers between devices: 16 us -> 26.5 us  [cross(): return lax.ppermute(value, ('dom', 'rep'), pairs)]
    pallas_call x1, Pallas kernels: 1.41 us -> 8.3 us  [pick_share(): pl.pallas_call(pick_kernel, out_shape=jax.ShapeDtypeStruct((share, tile_l...]
    ppermute x8, starting transfers between devices: 6.71 us -> 8.54 us  [exchange(): return lax.ppermute(value, 'rep', swap)]
    unnamed x41 -> x40, local copies, waits for them, and re-layouts: 3.49 us -> 1.83 us
    ppermute x6, starting transfers between devices: 8.93 us -> 7.53 us  [cross(): return lax.ppermute(value, ('dom', 'rep'), pairs)]
    ppermute x3, starting transfers between devices: 3.56 us -> 4.83 us  [move(): return lax.ppermute(value, 'dom', pairs)]
  transfers between devices with their start and end apart: 18 -> 18, of which waited for: 10 -> 9; matrix products, arithmetic and copies ran while one was open for 1% -> 0% of each run, Pallas kernels for 6% -> 6%
where the time goes in v7:
time: 106 us; the launch traced here: 105 us
  waiting for transfers between devices  48.6 us (46%)
  starting transfers between devices  28.5 us (27%)
  Pallas kernels  24 us (23%)
  local copies, waits for them, and re-layouts  3.7 us (3%)
    ppermute x6, waiting for transfers between devices, cross(): return lax.ppermute(value, ('dom', 'rep'), pairs)  26.5 us
    all_to_all x1, waiting for transfers between devices, gather_small(): landed = lax.all_to_all(rows, 'dom', 0, 0, tiled=True)  13.2 us
    pallas_call x1, Pallas kernels, products_in_phases(): pl.pallas_call(functools.partial(phased_kernel, places), out_shape=jax.Sh...  9.16 us
    ppermute x8, starting transfers between devices, exchange(): return lax.ppermute(value, 'rep', swap)  8.54 us
    pallas_call x1, Pallas kernels, pick_share(): pl.pallas_call(pick_kernel, out_shape=jax.ShapeDtypeStruct((share, tile_l...  8.3 us
    all_to_all x1, starting transfers between devices, gather_small(): landed = lax.all_to_all(rows, 'dom', 0, 0, tiled=True)  7.61 us
    ppermute x6, starting transfers between devices, cross(): return lax.ppermute(value, ('dom', 'rep'), pairs)  7.53 us
    ppermute x3, waiting for transfers between devices, move(): return lax.ppermute(value, 'dom', pairs)  6.58 us
  transfers between devices with their start and end apart: 18, of which 9 were waited for; matrix products, arithmetic and copies ran while one was open for 0% of the time, Pallas kernels for 6%

profile of v7, /device:TPU:1, one launch (start us, length us, event | category | flops | bytes accessed | tf_op | source)
XLA Modules:
  0.0 105.2 jit_solution(11787489636568156810)
XLA Ops:
  0.0 8.3 %shard_map.82 = bf16[16,128,256]{2,1,0:T(8,128)(2,1)} custom-call(s32[4]{0:T(128)} %owner_ref.1, s32[4,32]{1,0:T(4,128)} %blocks_ref.1, s32[64,1,128]{2,1,0:T(1,128)} %bitcast.5, bf16[8192,256]{1,0:T(8,128)(2,1)} %features_ref.1), custom_call_target="tpu_custom_call" | custom-call | tf_op jit(solution)/shard_map/pallas_call | solution.py:269
  8.3 0.0 copy-start.16
  8.3 0.0 copy-start.17
  8.3 0.0 copy-start.1
  8.4 7.6 %all-to-all-start = ((bf16[16,128,256]{2,1,0:T(8,128)(2,1)}), bf16[16,128,256]{2,1,0:T(8,128)(2,1)}, u32[]{:S(2)}, u32[]{:S(2)}) async-start(bf16[16,128,256]{2,1,0:T(8,128)(2,1)} %shard_map.82), calls=%async_computation | async-start | bytes 2097152 | tf_op jit(solution)/shard_map/all_to_all | solution.py:334
  16.0 0.0 copy-done.15
  16.0 0.0 copy-done.16
  16.0 0.0 copy-start.13
  16.0 1.0 collective-permute-start
  17.0 0.0 copy-done.17
  17.1 0.8 collective-permute-done.other_ref
  17.9 0.0 copy-done.13
  17.9 0.6 copy-done.14
  18.5 6.5 %shard_map.83.lists = s32[4,272]{1,0:T(4,128)} custom-call(s32[2,4,16]{2,1,0:T(4,128)} %copy-done.13, s32[2,4,16]{2,1,0:T(4,128)} %copy-done.14), custom_call_target="tpu_custom_call" | custom-call | tf_op jit(solution)/shard_map/pallas_call | solution.py:216
  25.0 13.2 %all-to-all-done = bf16[16,128,256]{2,1,0:T(8,128)(2,1)} async-done(((bf16[16,128,256]{2,1,0:T(8,128)(2,1)}), bf16[16,128,256]{2,1,0:T(8,128)(2,1)}, u32[]{:S(2)}, u32[]{:S(2)}) %all-to-all-start) | async-done | bytes 1048608 | tf_op jit(solution)/shard_map/all_to_all | solution.py:334
  38.2 1.8 %gather_fusion = bf16[4,128,256]{2,1,0:T(8,128)(2,1)S(1)} fusion(bf16[16,128,256]{2,1,0:T(8,128)(2,1)} %all-to-all-done, s32[1024]{0:T(1024)S(1)} %pad_clamp_fusion), kind=kCustom, calls=%fused_computation | custom fusion | bytes 524304 | tf_op jit(solution)/shard_map/gather | solution.py:335
  40.0 3.6 %collective-permute-start.4 = (bf16[4,128,256]{2,1,0:T(8,128)(2,1)S(1)}, bf16[4,128,256]{2,1,0:T(8,128)(2,1)S(1)}, u32[]{:S(2)}, u32[]{:S(2)}) collective-permute-start(bf16[4,128,256]{2,1,0:T(8,128)(2,1)S(1)} %gather_fusion), channel_id=1, source_target_pairs={{0,8},{2,10},{4,12},{6,14},{8,16},{10,18},{12,20},{14,22},{16,24},... | collective-permute-start | bytes 786440 | tf_op jit(solution)/shard_map/ppermute | solution.py:299
  43.6 0.0 collective-permute-start.3
  43.6 2.1 %collective-permute-start.1 = (bf16[4,128,256]{2,1,0:T(8,128)(2,1)S(1)}, bf16[4,128,256]{2,1,0:T(8,128)(2,1)S(1)}, u32[]{:S(2)}, u32[]{:S(2)}) collective-permute-start(bf16[4,128,256]{2,1,0:T(8,128)(2,1)S(1)} %gather_fusion), channel_id=1, source_target_pairs={{0,2},{1,5},{2,0},{3,7},{4,6},{5,1},{6,4},{7,3},{8,10},{9,13},{10,... | collective-permute-start | bytes 786440 | tf_op jit(solution)/shard_map/ppermute | solution.py:311
  45.6 0.0 copy-done.1
  45.6 2.0 %collective-permute-start.16 = (bf16[64,128,128]{2,1,0:T(8,128)(2,1)S(1)}, bf16[64,128,128]{2,1,0:T(8,128)(2,1)S(1)}, u32[]{:S(2)}, u32[]{:S(2)}) collective-permute-start(bf16[64,128,128]{2,1,0:T(8,128)(2,1)S(1)} %bitcast.4), channel_id=1, source_target_pairs={{0,1},{1,0},{2,3},{3,2},{4,5},{5,4},{6,7},{7,6},{8,9},{9,8},{10,11... | collective-permute-start | bytes 6291464 | tf_op jit(solution)/shard_map/ppermute | solution.py:362
  47.7 0.0 collective-permute-done.4
  47.7 6.6 %collective-permute-done.3 = bf16[4,128,256]{2,1,0:T(8,128)(2,1)S(1)} collective-permute-done((bf16[4,128,256]{2,1,0:T(8,128)(2,1)S(1)}, bf16[4,128,256]{2,1,0:T(8,128)(2,1)S(1)}, u32[]{:S(2)}, u32[]{:S(2)}) %collective-permute-start.3) | collective-permute-done | bytes 262176 | tf_op jit(solution)/shard_map/ppermute | solution.py:299
  54.3 0.0 collective-permute-done.1
  54.3 3.2 %collective-permute-start.5 = (bf16[8,128,256]{2,1,0:T(8,128)(2,1)S(1)}, bf16[8,128,256]{2,1,0:T(8,128)(2,1)S(1)}, u32[]{:S(2)}, u32[]{:S(2)}) collective-permute-start(bf16[8,128,256]{2,1,0:T(8,128)(2,1)S(1)} %pad_maximum_fusion), channel_id=1, source_target_pairs={{0,2},{1,5},{2,0},{3,7},{4,6},{5,1},{6,4},{7,3},{8,10},{9,13},{10,... | collective-permute-start | bytes 1572872 | tf_op jit(solution)/shard_map/ppermute | solution.py:311
  57.6 0.0 copy-start.4
  57.6 0.4 collective-permute-start.2
  58.0 1.3 %collective-permute-start.6 = (bf16[4,128,256]{2,1,0:T(8,128)(2,1)S(1)}, bf16[4,128,256]{2,1,0:T(8,128)(2,1)S(1)}, u32[]{:S(2)}, u32[]{:S(2)}) collective-permute-start(bf16[4,128,256]{2,1,0:T(8,128)(2,1)S(1)} %collective-permute-done.3), channel_id=1, source_target_pairs={{0,24},{2,26},{4,28},{6,30},{8,0},{10,2},{12,4},{14,6},{16,8},{18,... | collective-permute-start | bytes 786440 | tf_op jit(solution)/shard_map/ppermute | solution.py:299
  59.3 8.8 %collective-permute-done.5 = bf16[8,128,256]{2,1,0:T(8,128)(2,1)S(1)} collective-permute-done((bf16[8,128,256]{2,1,0:T(8,128)(2,1)S(1)}, bf16[8,128,256]{2,1,0:T(8,128)(2,1)S(1)}, u32[]{:S(2)}, u32[]{:S(2)}) %collective-permute-start.5) | collective-permute-done | bytes 524320 | tf_op jit(solution)/shard_map/ppermute | solution.py:311
  68.1 0.0 copy-start
  68.1 0.0 collective-permute-done.6
  68.1 2.3 %collective-permute-done.2.refs_1_ = bf16[8,128,256]{2,1,0:T(8,128)(2,1)S(1)} collective-permute-done((bf16[8,128,256]{2,1,0:T(8,128)(2,1)S(1)}, bf16[8,128,256]{2,1,0:T(8,128)(2,1)S(1)}, u32[]{:S(2)}, u32[]{:S(2)}) %collective-permute-start.2) | collective-permute-done | bytes 524320 | tf_op jit(solution)/shard_map/ppermute | solution.py:311
  70.4 0.1 collective-permute-start.7
  70.5 0.0 collective-permute-start.12
  70.5 2.5 %collective-permute-start.8 = (bf16[8,128,256]{2,1,0:T(8,128)(2,1)S(1)}, bf16[8,128,256]{2,1,0:T(8,128)(2,1)S(1)}, u32[]{:S(2)}, u32[]{:S(2)}) collective-permute-start(bf16[8,128,256]{2,1,0:T(8,128)(2,1)S(1)} %constant_dynamic-update-slice_fusion.2.refs_0_), channel_id=1, source_target_pairs={{0,1},{1,0},{2,3},{3,2},{4,5},{5,4},{6,7},{7,6},{8,9},{9,8},{10,11... | collective-permute-start | bytes 1572872 | tf_op jit(solution)/shard_map/ppermute | solution.py:362
  73.1 5.5 %collective-permute-done.12 = bf16[4,128,256]{2,1,0:T(8,128)(2,1)S(1)} collective-permute-done((bf16[4,128,256]{2,1,0:T(8,128)(2,1)S(1)}, bf16[4,128,256]{2,1,0:T(8,128)(2,1)S(1)}, u32[]{:S(2)}, u32[]{:S(2)}) %collective-permute-start.12) | collective-permute-done | bytes 262176 | tf_op jit(solution)/shard_map/ppermute | solution.py:311
  78.5 0.0 copy-start.3
  78.5 1.7 %collective-permute-start.13 = (bf16[8,128,256]{2,1,0:T(8,128)(2,1)S(1)}, bf16[8,128,256]{2,1,0:T(8,128)(2,1)S(1)}, u32[]{:S(2)}, u32[]{:S(2)}) collective-permute-start(bf16[8,128,256]{2,1,0:T(8,128)(2,1)S(1)} %constant_dynamic-update-slice_fusion.6.refs_8_), channel_id=1, source_target_pairs={{0,4},{1,3},{2,6},{3,1},{4,0},{5,7},{6,2},{7,5},{8,12},{9,11},{10,... | collective-permute-start | bytes 1572872 | tf_op jit(solution)/shard_map/ppermute | solution.py:311
  80.3 1.6 %collective-permute-start.10 = (bf16[16,128,256]{2,1,0:T(8,128)(2,1)S(1)}, bf16[16,128,256]{2,1,0:T(8,128)(2,1)S(1)}, u32[]{:S(2)}, u32[]{:S(2)}) collective-permute-start(bf16[16,128,256]{2,1,0:T(8,128)(2,1)S(1)} %constant_dynamic-update-slice_fusion.4.refs_2_), channel_id=1, source_target_pairs={{0,1},{1,0},{2,3},{3,2},{4,5},{5,4},{6,7},{7,6},{8,9},{9,8},{10,11... | collective-permute-start | bytes 3145736 | tf_op jit(solution)/shard_map/ppermute | solution.py:362
  81.9 5.3 %collective-permute-done.7.refs_3_ = bf16[16,128,256]{2,1,0:T(8,128)(2,1)S(1)} collective-permute-done((bf16[16,128,256]{2,1,0:T(8,128)(2,1)S(1)}, bf16[16,128,256]{2,1,0:T(8,128)(2,1)S(1)}, u32[]{:S(2)}, u32[]{:S(2)}) %collective-permute-start.7) | collective-permute-done | bytes 1048608 | tf_op jit(solution)/shard_map/ppermute | solution.py:311
  87.2 0.5 collective-permute-start.11
  87.6 0.0 collective-permute-done.16.refs_13_
  87.6 0.1 collective-permute-start.14
  87.7 0.0 collective-permute-done.8.refs_4_
  87.7 0.4 collective-permute-start.9
  88.2 4.6 %collective-permute-done.13.refs_9_ = bf16[8,128,256]{2,1,0:T(8,128)(2,1)S(1)} collective-permute-done((bf16[8,128,256]{2,1,0:T(8,128)(2,1)S(1)}, bf16[8,128,256]{2,1,0:T(8,128)(2,1)S(1)}, u32[]{:S(2)}, u32[]{:S(2)}) %collective-permute-start.13) | collective-permute-done | bytes 524320 | tf_op jit(solution)/shard_map/ppermute | solution.py:311
  92.8 0.5 collective-permute-start.15
  93.3 0.0 collective-permute-done.9.refs_5_
  93.3 0.0 collective-permute-done.14.refs_10_
  93.3 0.0 copy-start.10
  93.3 1.5 %collective-permute-done.15.refs_11_ = bf16[8,128,256]{2,1,0:T(8,128)(2,1)S(1)} collective-permute-done((bf16[8,128,256]{2,1,0:T(8,128)(2,1)S(1)}, bf16[8,128,256]{2,1,0:T(8,128)(2,1)S(1)}, u32[]{:S(2)}, u32[]{:S(2)}) %collective-permute-start.15) | collective-permute-done | bytes 524320 | tf_op jit(solution)/shard_map/ppermute | solution.py:362
  94.8 0.0 collective-permute-done.10.refs_6_
  94.8 0.0 copy-done.4
  94.8 0.0 copy-done.7
  94.8 0.0 copy-done.5
  94.8 0.0 copy-done.2
  94.8 0.0 copy-done.8
  94.8 0.0 copy-done.9
  94.9 1.1 %copy-done.6 = bf16[16,128,256]{2,1,0:T(8,128)(2,1)} copy-done((bf16[16,128,256]{2,1,0:T(8,128)(2,1)}, bf16[16,128,256]{2,1,0:T(8,128)(2,1)S(1)}, u32[]{:S(2)}) %copy-start.6) | copy-done | bytes 1048600
  96.0 0.0 collective-permute-done.11.refs_7_
  96.0 0.0 copy-done.11
  96.0 0.0 copy-done.10
  96.0 0.0 copy-done.12
  96.0 9.2 %shard_map.84 = bf16[32,128,256]{2,1,0:T(8,128)(2,1)} custom-call(s32[4,272]{1,0:T(4,128)} %shard_map.83.lists, bf16[8,128,256]{2,1,0:T(8,128)(2,1)} %copy-done.4, bf16[8,128,256]{2,1,0:T(8,128)(2,1)} %copy-done.7, bf16[16,128,256]{2,1,0:T(8,128)(2,1)} %copy-done, bf16[16,128,256]{2,1,0:T(8,128)(2,1)} %copy-done.5, bf16[8,128,256]{2,1,0:T(8,128)(2,1)} %copy-done.8, ...), custom_call_target="tpu_custom_call" | custom-call | flops 1073741824 | bytes 16777216 | tf_op jit(solution)/shard_map/pallas_call | solution.py:197
  (23 shorter events, 0.2 us)
Async XLA Ops:
  0.0 16.0 %copy-start.15 = (s32[1,4,16]{2,1,0:T(4,128)S(1)}, s32[1,4,16]{2,1,0:T(4,128)}, u32[]{:S(2)}) copy-start(s32[1,4,16]{2,1,0:T(4,128)} %param.12) | copy-start | bytes 772
  8.3 7.7 %copy-start.16 = (s32[1,4,16]{2,1,0:T(4,128)S(1)}, s32[1,4,16]{2,1,0:T(4,128)}, u32[]{:S(2)}) copy-start(s32[1,4,16]{2,1,0:T(4,128)} %param.13) | copy-start | bytes 772
  8.3 8.7 %copy-start.17 = (s32[4]{0:T(128)S(1)}, s32[4]{0:T(128)}, u32[]{:S(2)}) copy-start(s32[4]{0:T(128)} %owner_ref.1) | copy-start | bytes 52
  8.3 37.3 %copy-start.1 = (bf16[1,4,16,128,128]{4,3,2,1,0:T(8,128)(2,1)S(1)}, bf16[1,4,16,128,128]{4,3,2,1,0:T(8,128)(2,1)}, u32[]{:S(2)}) copy-start(bf16[1,4,16,128,128]{4,3,2,1,0:T(8,128)(2,1)} %param.14) | copy-start | bytes 6291460
  8.4 29.9 %all-to-all-start = ((bf16[16,128,256]{2,1,0:T(8,128)(2,1)}), bf16[16,128,256]{2,1,0:T(8,128)(2,1)}, u32[]{:S(2)}, u32[]{:S(2)}) async-start(bf16[16,128,256]{2,1,0:T(8,128)(2,1)} %shard_map.82), calls=%async_computation | async-start | bytes 2097152 | tf_op jit(solution)/shard_map/all_to_all | solution.py:334
  16.0 1.9 %copy-start.13 = (s32[2,4,16]{2,1,0:T(4,128)}, s32[2,4,16]{2,1,0:T(4,128)S(1)}, u32[]{:S(2)}) copy-start(s32[2,4,16]{2,1,0:T(4,128)S(1)} %constant_dynamic-update-slice_fusion.own_ref) | copy-start | bytes 1540
  16.0 1.8 %collective-permute-start = (s32[2,4,16]{2,1,0:T(4,128)S(1)}, s32[2,4,16]{2,1,0:T(4,128)S(1)}, u32[]{:S(2)}, u32[]{:S(2)}) collective-permute-start(s32[2,4,16]{2,1,0:T(4,128)S(1)} %constant_dynamic-update-slice_fusion.own_ref), channel_id=1, source_target_pairs={{0,1},{1,0},{2,3},{3,2},{4,5},{5,4},{6,7},{7,6},{8,9},{9,8},{10,11... | collective-permute-start | bytes 1544 | tf_op jit(solution)/shard_map/ppermute | solution.py:362
  17.9 0.6 copy-start.14
  40.0 7.7 %collective-permute-start.4 = (bf16[4,128,256]{2,1,0:T(8,128)(2,1)S(1)}, bf16[4,128,256]{2,1,0:T(8,128)(2,1)S(1)}, u32[]{:S(2)}, u32[]{:S(2)}) collective-permute-start(bf16[4,128,256]{2,1,0:T(8,128)(2,1)S(1)} %gather_fusion), channel_id=1, source_target_pairs={{0,8},{2,10},{4,12},{6,14},{8,16},{10,18},{12,20},{14,22},{16,24},... | collective-permute-start | bytes 786440 | tf_op jit(solution)/shard_map/ppermute | solution.py:299
  43.6 10.7 %collective-permute-start.3 = (bf16[4,128,256]{2,1,0:T(8,128)(2,1)S(1)}, bf16[4,128,256]{2,1,0:T(8,128)(2,1)S(1)}, u32[]{:S(2)}, u32[]{:S(2)}) collective-permute-start(bf16[4,128,256]{2,1,0:T(8,128)(2,1)S(1)} %gather_fusion), channel_id=1, source_target_pairs={{0,24},{2,26},{4,28},{6,30},{8,0},{10,2},{12,4},{14,6},{16,8},{18,... | collective-permute-start | bytes 786440 | tf_op jit(solution)/shard_map/ppermute | solution.py:299
  43.6 10.7 %collective-permute-start.1 = (bf16[4,128,256]{2,1,0:T(8,128)(2,1)S(1)}, bf16[4,128,256]{2,1,0:T(8,128)(2,1)S(1)}, u32[]{:S(2)}, u32[]{:S(2)}) collective-permute-start(bf16[4,128,256]{2,1,0:T(8,128)(2,1)S(1)} %gather_fusion), channel_id=1, source_target_pairs={{0,2},{1,5},{2,0},{3,7},{4,6},{5,1},{6,4},{7,3},{8,10},{9,13},{10,... | collective-permute-start | bytes 786440 | tf_op jit(solution)/shard_map/ppermute | solution.py:311
  45.6 42.0 %collective-permute-start.16 = (bf16[64,128,128]{2,1,0:T(8,128)(2,1)S(1)}, bf16[64,128,128]{2,1,0:T(8,128)(2,1)S(1)}, u32[]{:S(2)}, u32[]{:S(2)}) collective-permute-start(bf16[64,128,128]{2,1,0:T(8,128)(2,1)S(1)} %bitcast.4), channel_id=1, source_target_pairs={{0,1},{1,0},{2,3},{3,2},{4,5},{5,4},{6,7},{7,6},{8,9},{9,8},{10,11... | collective-permute-start | bytes 6291464 | tf_op jit(solution)/shard_map/ppermute | solution.py:362
  54.3 13.7 %collective-permute-start.5 = (bf16[8,128,256]{2,1,0:T(8,128)(2,1)S(1)}, bf16[8,128,256]{2,1,0:T(8,128)(2,1)S(1)}, u32[]{:S(2)}, u32[]{:S(2)}) collective-permute-start(bf16[8,128,256]{2,1,0:T(8,128)(2,1)S(1)} %pad_maximum_fusion), channel_id=1, source_target_pairs={{0,2},{1,5},{2,0},{3,7},{4,6},{5,1},{6,4},{7,3},{8,10},{9,13},{10,... | collective-permute-start | bytes 1572872 | tf_op jit(solution)/shard_map/ppermute | solution.py:311
  57.6 37.2 %copy-start.4 = (bf16[8,128,256]{2,1,0:T(8,128)(2,1)}, bf16[8,128,256]{2,1,0:T(8,128)(2,1)S(1)}, u32[]{:S(2)}) copy-start(bf16[8,128,256]{2,1,0:T(8,128)(2,1)S(1)} %constant_dynamic-update-slice_fusion.2.refs_0_) | copy-start | bytes 1572868
  57.6 12.8 %collective-permute-start.2 = (bf16[8,128,256]{2,1,0:T(8,128)(2,1)S(1)}, bf16[8,128,256]{2,1,0:T(8,128)(2,1)S(1)}, u32[]{:S(2)}, u32[]{:S(2)}) collective-permute-start(bf16[8,128,256]{2,1,0:T(8,128)(2,1)S(1)} %constant_dynamic-update-slice_fusion.2.refs_0_), channel_id=1, source_target_pairs={{0,4},{1,3},{2,6},{3,1},{4,0},{5,7},{6,2},{7,5},{8,12},{9,11},{10,... | collective-permute-start | bytes 1572872 | tf_op jit(solution)/shard_map/ppermute | solution.py:311
  58.0 10.1 %collective-permute-start.6 = (bf16[4,128,256]{2,1,0:T(8,128)(2,1)S(1)}, bf16[4,128,256]{2,1,0:T(8,128)(2,1)S(1)}, u32[]{:S(2)}, u32[]{:S(2)}) collective-permute-start(bf16[4,128,256]{2,1,0:T(8,128)(2,1)S(1)} %collective-permute-done.3), channel_id=1, source_target_pairs={{0,24},{2,26},{4,28},{6,30},{8,0},{10,2},{12,4},{14,6},{16,8},{18,... | collective-permute-start | bytes 786440 | tf_op jit(solution)/shard_map/ppermute | solution.py:299
  68.1 27.9 %copy-start = (bf16[16,128,256]{2,1,0:T(8,128)(2,1)}, bf16[16,128,256]{2,1,0:T(8,128)(2,1)S(1)}, u32[]{:S(2)}) copy-start(bf16[16,128,256]{2,1,0:T(8,128)(2,1)S(1)} %constant_dynamic-update-slice_fusion.4.refs_2_) | copy-start | bytes 3145732
  70.4 24.4 %copy-start.7 = (bf16[8,128,256]{2,1,0:T(8,128)(2,1)}, bf16[8,128,256]{2,1,0:T(8,128)(2,1)S(1)}, u32[]{:S(2)}) copy-start(bf16[8,128,256]{2,1,0:T(8,128)(2,1)S(1)} %collective-permute-done.2.refs_1_) | copy-start | bytes 1572868
  70.4 16.8 %collective-permute-start.7 = (bf16[16,128,256]{2,1,0:T(8,128)(2,1)S(1)}, bf16[16,128,256]{2,1,0:T(8,128)(2,1)S(1)}, u32[]{:S(2)}, u32[]{:S(2)}) collective-permute-start(bf16[16,128,256]{2,1,0:T(8,128)(2,1)S(1)} %constant_dynamic-update-slice_fusion.4.refs_2_), channel_id=1, source_target_pairs={{0,4},{1,3},{2,6},{3,1},{4,0},{5,7},{6,2},{7,5},{8,12},{9,11},{10,... | collective-permute-start | bytes 3145736 | tf_op jit(solution)/shard_map/ppermute | solution.py:311
  70.5 8.0 %collective-permute-start.12 = (bf16[4,128,256]{2,1,0:T(8,128)(2,1)S(1)}, bf16[4,128,256]{2,1,0:T(8,128)(2,1)S(1)}, u32[]{:S(2)}, u32[]{:S(2)}) collective-permute-start(bf16[4,128,256]{2,1,0:T(8,128)(2,1)S(1)} %collective-permute-done.6), channel_id=1, source_target_pairs={{0,2},{1,5},{2,0},{3,7},{4,6},{5,1},{6,4},{7,3},{8,10},{9,13},{10,... | collective-permute-start | bytes 786440 | tf_op jit(solution)/shard_map/ppermute | solution.py:311
  70.5 17.2 %collective-permute-start.8 = (bf16[8,128,256]{2,1,0:T(8,128)(2,1)S(1)}, bf16[8,128,256]{2,1,0:T(8,128)(2,1)S(1)}, u32[]{:S(2)}, u32[]{:S(2)}) collective-permute-start(bf16[8,128,256]{2,1,0:T(8,128)(2,1)S(1)} %constant_dynamic-update-slice_fusion.2.refs_0_), channel_id=1, source_target_pairs={{0,1},{1,0},{2,3},{3,2},{4,5},{5,4},{6,7},{7,6},{8,9},{9,8},{10,11... | collective-permute-start | bytes 1572872 | tf_op jit(solution)/shard_map/ppermute | solution.py:362
  78.5 17.4 %copy-start.3 = (bf16[8,128,256]{2,1,0:T(8,128)(2,1)}, bf16[8,128,256]{2,1,0:T(8,128)(2,1)S(1)}, u32[]{:S(2)}) copy-start(bf16[8,128,256]{2,1,0:T(8,128)(2,1)S(1)} %constant_dynamic-update-slice_fusion.6.refs_8_) | copy-start | bytes 1572868
  78.5 14.3 %collective-permute-start.13 = (bf16[8,128,256]{2,1,0:T(8,128)(2,1)S(1)}, bf16[8,128,256]{2,1,0:T(8,128)(2,1)S(1)}, u32[]{:S(2)}, u32[]{:S(2)}) collective-permute-start(bf16[8,128,256]{2,1,0:T(8,128)(2,1)S(1)} %constant_dynamic-update-slice_fusion.6.refs_8_), channel_id=1, source_target_pairs={{0,4},{1,3},{2,6},{3,1},{4,0},{5,7},{6,2},{7,5},{8,12},{9,11},{10,... | collective-permute-start | bytes 1572872 | tf_op jit(solution)/shard_map/ppermute | solution.py:311
  80.3 14.5 %collective-permute-start.10 = (bf16[16,128,256]{2,1,0:T(8,128)(2,1)S(1)}, bf16[16,128,256]{2,1,0:T(8,128)(2,1)S(1)}, u32[]{:S(2)}, u32[]{:S(2)}) collective-permute-start(bf16[16,128,256]{2,1,0:T(8,128)(2,1)S(1)} %constant_dynamic-update-slice_fusion.4.refs_2_), channel_id=1, source_target_pairs={{0,1},{1,0},{2,3},{3,2},{4,5},{5,4},{6,7},{7,6},{8,9},{9,8},{10,11... | collective-permute-start | bytes 3145736 | tf_op jit(solution)/shard_map/ppermute | solution.py:362
  87.2 7.6 %copy-start.5 = (bf16[16,128,256]{2,1,0:T(8,128)(2,1)}, bf16[16,128,256]{2,1,0:T(8,128)(2,1)S(1)}, u32[]{:S(2)}) copy-start(bf16[16,128,256]{2,1,0:T(8,128)(2,1)S(1)} %collective-permute-done.7.refs_3_) | copy-start | bytes 3145732
  87.2 8.8 %collective-permute-start.11 = (bf16[16,128,256]{2,1,0:T(8,128)(2,1)S(1)}, bf16[16,128,256]{2,1,0:T(8,128)(2,1)}, u32[]{:S(2)}, u32[]{:S(2)}) collective-permute-start(bf16[16,128,256]{2,1,0:T(8,128)(2,1)S(1)} %collective-permute-done.7.refs_3_), channel_id=1, source_target_pairs={{0,1},{1,0},{2,3},{3,2},{4,5},{5,4},{6,7},{7,6},{8,9},{9,8},{10,11... | collective-permute-start | bytes 3145736 | tf_op jit(solution)/shard_map/ppermute | solution.py:362
  87.6 7.2 %copy-start.2 = (bf16[64,128,128]{2,1,0:T(8,128)(2,1)}, bf16[64,128,128]{2,1,0:T(8,128)(2,1)S(1)}, u32[]{:S(2)}) copy-start(bf16[64,128,128]{2,1,0:T(8,128)(2,1)S(1)} %collective-permute-done.16.refs_13_) | copy-start | bytes 6291460
  87.6 5.6 %collective-permute-start.14 = (bf16[8,128,256]{2,1,0:T(8,128)(2,1)S(1)}, bf16[8,128,256]{2,1,0:T(8,128)(2,1)S(1)}, u32[]{:S(2)}, u32[]{:S(2)}) collective-permute-start(bf16[8,128,256]{2,1,0:T(8,128)(2,1)S(1)} %constant_dynamic-update-slice_fusion.6.refs_8_), channel_id=1, source_target_pairs={{0,1},{1,0},{2,3},{3,2},{4,5},{5,4},{6,7},{7,6},{8,9},{9,8},{10,11... | collective-permute-start | bytes 1572872 | tf_op jit(solution)/shard_map/ppermute | solution.py:362
  87.7 7.1 %copy-start.8 = (bf16[8,128,256]{2,1,0:T(8,128)(2,1)}, bf16[8,128,256]{2,1,0:T(8,128)(2,1)S(1)}, u32[]{:S(2)}) copy-start(bf16[8,128,256]{2,1,0:T(8,128)(2,1)S(1)} %collective-permute-done.8.refs_4_) | copy-start | bytes 1572868
  87.7 5.5 %collective-permute-start.9 = (bf16[8,128,256]{2,1,0:T(8,128)(2,1)S(1)}, bf16[8,128,256]{2,1,0:T(8,128)(2,1)S(1)}, u32[]{:S(2)}, u32[]{:S(2)}) collective-permute-start(bf16[8,128,256]{2,1,0:T(8,128)(2,1)S(1)} %collective-permute-done.2.refs_1_), channel_id=1, source_target_pairs={{0,1},{1,0},{2,3},{3,2},{4,5},{5,4},{6,7},{7,6},{8,9},{9,8},{10,11... | collective-permute-start | bytes 1572872 | tf_op jit(solution)/shard_map/ppermute | solution.py:362
  92.8 2.0 %copy-start.9 = (bf16[8,128,256]{2,1,0:T(8,128)(2,1)}, bf16[8,128,256]{2,1,0:T(8,128)(2,1)S(1)}, u32[]{:S(2)}) copy-start(bf16[8,128,256]{2,1,0:T(8,128)(2,1)S(1)} %collective-permute-done.13.refs_9_) | copy-start | bytes 1572868
  92.8 2.0 %collective-permute-start.15 = (bf16[8,128,256]{2,1,0:T(8,128)(2,1)S(1)}, bf16[8,128,256]{2,1,0:T(8,128)(2,1)S(1)}, u32[]{:S(2)}, u32[]{:S(2)}) collective-permute-start(bf16[8,128,256]{2,1,0:T(8,128)(2,1)S(1)} %collective-permute-done.13.refs_9_), channel_id=1, source_target_pairs={{0,1},{1,0},{2,3},{3,2},{4,5},{5,4},{6,7},{7,6},{8,9},{9,8},{10,11... | collective-permute-start | bytes 1572872 | tf_op jit(solution)/shard_map/ppermute | solution.py:362
  93.3 2.7 %copy-start.11 = (bf16[8,128,256]{2,1,0:T(8,128)(2,1)}, bf16[8,128,256]{2,1,0:T(8,128)(2,1)S(1)}, u32[]{:S(2)}) copy-start(bf16[8,128,256]{2,1,0:T(8,128)(2,1)S(1)} %collective-permute-done.9.refs_5_) | copy-start | bytes 1572868
  93.3 2.7 %copy-start.10 = (bf16[8,128,256]{2,1,0:T(8,128)(2,1)}, bf16[8,128,256]{2,1,0:T(8,128)(2,1)S(1)}, u32[]{:S(2)}) copy-start(bf16[8,128,256]{2,1,0:T(8,128)(2,1)S(1)} %collective-permute-done.14.refs_10_) | copy-start | bytes 1572868
  94.8 1.2 %copy-start.12 = (bf16[8,128,256]{2,1,0:T(8,128)(2,1)}, bf16[8,128,256]{2,1,0:T(8,128)(2,1)S(1)}, u32[]{:S(2)}) copy-start(bf16[8,128,256]{2,1,0:T(8,128)(2,1)S(1)} %collective-permute-done.15.refs_11_) | copy-start | bytes 1572868
  94.9 1.1 %copy-start.6 = (bf16[16,128,256]{2,1,0:T(8,128)(2,1)}, bf16[16,128,256]{2,1,0:T(8,128)(2,1)S(1)}, u32[]{:S(2)}) copy-start(bf16[16,128,256]{2,1,0:T(8,128)(2,1)S(1)} %collective-permute-done.10.refs_6_) | copy-start | bytes 3145732

commit v8 on v7

--- a/solution.py
+++ b/solution.py
@@ -128,7 +128,11 @@
                 other = (holder != rep).astype(jnp.int32)
                 shift = (chip // 4 - me // 4) & 3
                 at = place_of((chip ^ me) & 3, holder) * sections + s
-                at = jnp.where((shift & 1) == 1, 4 * sections + at + (at // 4 + shift // 2) * 4, at)
+                turn, by_shift = at // 8, shift // 2
+                near = 16 + jnp.where(
+                    turn == 0, at + (at // 4) * 4 + by_shift * 4, 8 + at + by_shift * 8
+                )
+                at = jnp.where((shift & 1) == 1, near, at)
                 is_late = shift == 2
                 place = jnp.where(is_late, 96 + other * 16 + at, other * 48 + at)
                 put(
@@ -319,12 +323,6 @@
     return lax.optimization_barrier((value, after))[0]
 
 
-def quad_gather(own):
-    came = cross(own, 0)
-    pair = jnp.concatenate([own, came])
-    return came, [pair, cross(pair, 1)]
-
-
 RING = {
     k: [(z * 4 + q, ((z - k) % 4) * 4 + q) for z in range(4) for q in range(4)] for k in (1, 2, 3)
 }
@@ -334,13 +332,18 @@
     landed = lax.all_to_all(rows, "dom", 0, 0, tiled=True)
     shard = landed.at[section_owner].get(mode="promise_in_bounds")
     shard, lists = lax.optimization_barrier((shard, lists))
-    one = move(shard, RING[1])
-    near = jnp.concatenate([one, move(shard, RING[3])])
-    came, level = quad_gather(shard)
+    one, three = move(shard, RING[1]), move(shard, RING[3])
+    came, turned = cross(shard, 0), cross(shard, 1)
+    second = jnp.concatenate([turned, cross(came, 1)])
+    near = jnp.concatenate([one, three])
     far = move(one, RING[1])
-    near_came, near_level = quad_gather(tie(near, came))
-    near_level[1] = cross(tie(near_level[0], (far, level[1])), 1)
-    return level + near_level, quad_gather(far)[1], lists
+    one_second = move(second, RING[1])
+    near_came = cross(tie(near, (came, turned)), 0)
+    each = shard.shape[0]
+    three_second = cross(jnp.concatenate([three, near_came[each:]]), 1)
+    far_pair = jnp.concatenate([far, cross(far, 0)])
+    early = [shard, came, second, near, near_came, one_second, three_second]
+    return early, [far_pair, cross(tie(far_pair, (one_second, three_second)), 1)], lists
 
 
 def body(features, node_order, section_owner, send_blocks, tile_rows, tile_cols, tiles, weight):

time: 106 us -> 99.8 us (0.942)
  waiting for transfers between devices: 48.6 us -> 32.9 us
  starting transfers between devices: 28.5 us -> 39 us
  local copies, waits for them, and re-layouts: 3.7 us -> 1.38 us
    ppermute x6 -> x7, waiting for transfers between devices: 26.5 us -> 7.29 us  [cross(): return lax.ppermute(value, ('dom', 'rep'), pairs)]
    ppermute x3 -> x4, starting transfers between devices: 4.83 us -> 10.8 us  [move(): return lax.ppermute(value, 'dom', pairs)]
    ppermute x8 -> x11, starting transfers between devices: 8.54 us -> 14.3 us  [exchange(): return lax.ppermute(value, 'rep', swap)]
    ppermute x3 -> x4, waiting for transfers between devices: 6.58 us -> 9.81 us  [move(): return lax.ppermute(value, 'dom', pairs)]
    gather x1, local copies, waits for them, and re-layouts: 1.79 us -> 0.56 us  [gather_small(): shard = landed.at[section_owner].get(mode='promise_in_bounds')]
    ppermute x6 -> x7, starting transfers between devices: 7.53 us -> 6.32 us  [cross(): return lax.ppermute(value, ('dom', 'rep'), pairs)]
    unnamed x40 -> x50, local copies, waits for them, and re-layouts: 1.83 us -> 0.74 us
    ppermute x8 -> x11, waiting for transfers between devices: 2.34 us -> 3.34 us  [exchange(): return lax.ppermute(value, 'rep', swap)]
  transfers between devices with their start and end apart: 18 -> 23, of which waited for: 9 -> 9; matrix products, arithmetic and copies ran while one was open for 0% -> 1% of each run, Pallas kernels for 6% -> 7%
where the time goes in v8:
time: 99.8 us; the launch traced here: 98.5 us
  starting transfers between devices  39 us (39%)
  waiting for transfers between devices  32.9 us (33%)
  Pallas kernels  24.7 us (25%)
  local copies, waits for them, and re-layouts  1.38 us (1%)
    ppermute x11, starting transfers between devices, exchange(): return lax.ppermute(value, 'rep', swap)  14.3 us
    all_to_all x1, waiting for transfers between devices, gather_small(): landed = lax.all_to_all(rows, 'dom', 0, 0, tiled=True)  12.5 us
    ppermute x4, starting transfers between devices, move(): return lax.ppermute(value, 'dom', pairs)  10.8 us
    ppermute x4, waiting for transfers between devices, move(): return lax.ppermute(value, 'dom', pairs)  9.81 us
    pallas_call x1, Pallas kernels, products_in_phases(): pl.pallas_call(functools.partial(phased_kernel, places), out_shape=jax.Sh...  9.19 us
    pallas_call x1, Pallas kernels, pick_share(): pl.pallas_call(pick_kernel, out_shape=jax.ShapeDtypeStruct((share, tile_l...  8.3 us
    all_to_all x1, starting transfers between devices, gather_small(): landed = lax.all_to_all(rows, 'dom', 0, 0, tiled=True)  7.56 us
    ppermute x7, waiting for transfers between devices, cross(): return lax.ppermute(value, ('dom', 'rep'), pairs)  7.29 us
  transfers between devices with their start and end apart: 23, of which 9 were waited for; matrix products, arithmetic and copies ran while one was open for 1% of the time, Pallas kernels for 7%

profile of v8, /device:TPU:1, one launch (start us, length us, event | category | flops | bytes accessed | tf_op | source)
XLA Modules:
  0.0 98.5 jit_solution(3427115765345705813)
XLA Ops:
  0.0 8.3 %shard_map.82 = bf16[16,128,256]{2,1,0:T(8,128)(2,1)} custom-call(s32[4]{0:T(128)} %owner_ref.1, s32[4,32]{1,0:T(4,128)} %blocks_ref.1, s32[64,1,128]{2,1,0:T(1,128)} %bitcast.5, bf16[8192,256]{1,0:T(8,128)(2,1)} %features_ref.1), custom_call_target="tpu_custom_call" | custom-call | tf_op jit(solution)/shard_map/pallas_call | solution.py:273
  8.3 0.0 copy-start.21
  8.3 0.0 copy-start
  8.3 0.0 copy-start.22
  8.4 7.6 %all-to-all-start = ((bf16[16,128,256]{2,1,0:T(8,128)(2,1)}), bf16[16,128,256]{2,1,0:T(8,128)(2,1)S(1)}, u32[]{:S(2)}, u32[]{:S(2)}) async-start(bf16[16,128,256]{2,1,0:T(8,128)(2,1)} %shard_map.82), calls=%async_computation | async-start | bytes 2097152 | tf_op jit(solution)/shard_map/all_to_all | solution.py:332
  15.9 0.0 copy-done.20
  15.9 0.0 copy-done.21
  16.0 0.0 copy-start.18
  16.0 1.0 %collective-permute-start = (s32[2,4,16]{2,1,0:T(4,128)S(1)}, s32[2,4,16]{2,1,0:T(4,128)S(1)}, u32[]{:S(2)}, u32[]{:S(2)}) collective-permute-start(s32[2,4,16]{2,1,0:T(4,128)S(1)} %constant_dynamic-update-slice_fusion.own_ref), channel_id=1, source_target_pairs={{0,1},{1,0},{2,3},{3,2},{4,5},{5,4},{6,7},{7,6},{8,9},{9,8},{10,11... | collective-permute-start | bytes 1544 | tf_op jit(solution)/shard_map/ppermute | solution.py:365
  17.0 0.1 collective-permute-start.21
  17.1 0.7 collective-permute-done.other_ref
  17.8 0.6 copy-done.19
  18.4 7.2 %shard_map.83.lists = s32[4,272]{1,0:T(4,128)} custom-call(s32[2,4,16]{2,1,0:T(4,128)} %copy-done.18, s32[2,4,16]{2,1,0:T(4,128)} %copy-done.19), custom_call_target="tpu_custom_call" | custom-call | tf_op jit(solution)/shard_map/pallas_call | solution.py:220
  25.6 12.5 %all-to-all-done = bf16[16,128,256]{2,1,0:T(8,128)(2,1)S(1)} async-done(((bf16[16,128,256]{2,1,0:T(8,128)(2,1)}), bf16[16,128,256]{2,1,0:T(8,128)(2,1)S(1)}, u32[]{:S(2)}, u32[]{:S(2)}) %all-to-all-start) | async-done | bytes 1048608 | tf_op jit(solution)/shard_map/all_to_all | solution.py:332
  38.1 0.6 gather_fusion
  38.7 0.0 copy-start.5
  38.7 3.1 %collective-permute-start.4 = (bf16[4,128,256]{2,1,0:T(8,128)(2,1)S(1)}, bf16[4,128,256]{2,1,0:T(8,128)(2,1)S(1)}, u32[]{:S(2)}, u32[]{:S(2)}) collective-permute-start(bf16[4,128,256]{2,1,0:T(8,128)(2,1)S(1)} %gather_fusion), channel_id=1, source_target_pairs={{0,24},{2,26},{4,28},{6,30},{8,0},{10,2},{12,4},{14,6},{16,8},{18,... | collective-permute-start | bytes 786440 | tf_op jit(solution)/shard_map/ppermute | solution.py:303
  41.8 0.5 collective-permute-start.5
  42.3 0.3 collective-permute-start.2
  42.6 2.0 %collective-permute-start.1 = (bf16[4,128,256]{2,1,0:T(8,128)(2,1)S(1)}, bf16[4,128,256]{2,1,0:T(8,128)(2,1)S(1)}, u32[]{:S(2)}, u32[]{:S(2)}) collective-permute-start(bf16[4,128,256]{2,1,0:T(8,128)(2,1)S(1)} %gather_fusion), channel_id=1, source_target_pairs={{0,2},{1,5},{2,0},{3,7},{4,6},{5,1},{6,4},{7,3},{8,10},{9,13},{10,... | collective-permute-start | bytes 786440 | tf_op jit(solution)/shard_map/ppermute | solution.py:315
  44.5 1.9 %collective-permute-done.4 = bf16[4,128,256]{2,1,0:T(8,128)(2,1)S(1)} collective-permute-done((bf16[4,128,256]{2,1,0:T(8,128)(2,1)S(1)}, bf16[4,128,256]{2,1,0:T(8,128)(2,1)S(1)}, u32[]{:S(2)}, u32[]{:S(2)}) %collective-permute-start.4) | collective-permute-done | bytes 262176 | tf_op jit(solution)/shard_map/ppermute | solution.py:303
  46.4 7.9 %collective-permute-done.5 = bf16[4,128,256]{2,1,0:T(8,128)(2,1)S(1)} collective-permute-done((bf16[4,128,256]{2,1,0:T(8,128)(2,1)S(1)}, bf16[4,128,256]{2,1,0:T(8,128)(2,1)S(1)}, u32[]{:S(2)}, u32[]{:S(2)}) %collective-permute-start.5) | collective-permute-done | bytes 262176 | tf_op jit(solution)/shard_map/ppermute | solution.py:303
  54.4 0.0 copy-start.4
  54.4 0.0 collective-permute-done.2
  54.4 0.0 collective-permute-done.1.refs_1_
  54.4 0.1 collective-permute-start.6
  54.5 1.3 %collective-permute-start.3 = (bf16[4,128,256]{2,1,0:T(8,128)(2,1)S(1)}, bf16[4,128,256]{2,1,0:T(8,128)(2,1)S(1)}, u32[]{:S(2)}, u32[]{:S(2)}) collective-permute-start(bf16[4,128,256]{2,1,0:T(8,128)(2,1)S(1)} %collective-permute-done.1.refs_1_), channel_id=1, source_target_pairs={{0,4},{1,3},{2,6},{3,1},{4,0},{5,7},{6,2},{7,5},{8,12},{9,11},{10,... | collective-permute-start | bytes 786440 | tf_op jit(solution)/shard_map/ppermute | solution.py:315
  55.8 2.0 %collective-permute-start.16 = (bf16[4,128,256]{2,1,0:T(8,128)(2,1)S(1)}, bf16[4,128,256]{2,1,0:T(8,128)(2,1)S(1)}, u32[]{:S(2)}, u32[]{:S(2)}) collective-permute-start(bf16[4,128,256]{2,1,0:T(8,128)(2,1)S(1)} %collective-permute-done.4), channel_id=1, source_target_pairs={{0,24},{2,26},{4,28},{6,30},{8,0},{10,2},{12,4},{14,6},{16,8},{18,... | collective-permute-start | bytes 786440 | tf_op jit(solution)/shard_map/ppermute | solution.py:303
  57.8 2.0 %collective-permute-done.3 = bf16[4,128,256]{2,1,0:T(8,128)(2,1)S(1)} collective-permute-done((bf16[4,128,256]{2,1,0:T(8,128)(2,1)S(1)}, bf16[4,128,256]{2,1,0:T(8,128)(2,1)S(1)}, u32[]{:S(2)}, u32[]{:S(2)}) %collective-permute-start.3) | collective-permute-done | bytes 262176 | tf_op jit(solution)/shard_map/ppermute | solution.py:315
  59.8 0.0 copy-start.3
  59.8 5.2 %collective-permute-start.7 = (bf16[8,128,256]{2,1,0:T(8,128)(2,1)S(1)}, bf16[8,128,256]{2,1,0:T(8,128)(2,1)S(1)}, u32[]{:S(2)}, u32[]{:S(2)}) collective-permute-start(bf16[8,128,256]{2,1,0:T(8,128)(2,1)S(1)} %constant_dynamic-update-slice_fusion.2.refs_2_), channel_id=1, source_target_pairs={{0,24},{2,26},{4,28},{6,30},{8,0},{10,2},{12,4},{14,6},{16,8},{18,... | collective-permute-start | bytes 1572872 | tf_op jit(solution)/shard_map/ppermute | solution.py:303
  65.1 0.0 collective-permute-done.6.refs_4_
  65.1 1.1 %collective-permute-start.8 = (bf16[8,128,256]{2,1,0:T(8,128)(2,1)S(1)}, bf16[8,128,256]{2,1,0:T(8,128)(2,1)S(1)}, u32[]{:S(2)}, u32[]{:S(2)}) collective-permute-start(bf16[8,128,256]{2,1,0:T(8,128)(2,1)S(1)} %pad_maximum_fusion), channel_id=1, source_target_pairs={{0,4},{1,3},{2,6},{3,1},{4,0},{5,7},{6,2},{7,5},{8,12},{9,11},{10,... | collective-permute-start | bytes 1572872 | tf_op jit(solution)/shard_map/ppermute | solution.py:315
  66.2 0.0 collective-permute-done.16
  66.2 0.6 collective-permute-start.17
  66.8 3.5 %collective-permute-start.12 = (bf16[8,128,256]{2,1,0:T(8,128)(2,1)S(1)}, bf16[8,128,256]{2,1,0:T(8,128)(2,1)S(1)}, u32[]{:S(2)}, u32[]{:S(2)}) collective-permute-start(bf16[8,128,256]{2,1,0:T(8,128)(2,1)S(1)} %constant_dynamic-update-slice_fusion.4.refs_3_), channel_id=1, source_target_pairs={{0,1},{1,0},{2,3},{3,2},{4,5},{5,4},{6,7},{7,6},{8,9},{9,8},{10,11... | collective-permute-start | bytes 1572872 | tf_op jit(solution)/shard_map/ppermute | solution.py:365
  70.4 1.5 %collective-permute-done.17 = bf16[4,128,256]{2,1,0:T(8,128)(2,1)S(1)} collective-permute-done((bf16[4,128,256]{2,1,0:T(8,128)(2,1)S(1)}, bf16[4,128,256]{2,1,0:T(8,128)(2,1)S(1)}, u32[]{:S(2)}, u32[]{:S(2)}) %collective-permute-start.17) | collective-permute-done | bytes 262176 | tf_op jit(solution)/shard_map/ppermute | solution.py:315
  71.9 4.9 %collective-permute-start.11 = (bf16[8,128,256]{2,1,0:T(8,128)(2,1)S(1)}, bf16[8,128,256]{2,1,0:T(8,128)(2,1)S(1)}, u32[]{:S(2)}, u32[]{:S(2)}) collective-permute-start(bf16[8,128,256]{2,1,0:T(8,128)(2,1)S(1)} %constant_dynamic-update-slice_fusion.2.refs_2_), channel_id=1, source_target_pairs={{0,1},{1,0},{2,3},{3,2},{4,5},{5,4},{6,7},{7,6},{8,9},{9,8},{10,11... | collective-permute-start | bytes 1572872 | tf_op jit(solution)/shard_map/ppermute | solution.py:365
  76.8 0.0 copy-start.2
  76.8 0.0 collective-permute-done.7.refs_5_
  76.8 0.0 collective-permute-done.8.refs_6_
  76.8 1.1 %collective-permute-start.18 = (bf16[8,128,256]{2,1,0:T(8,128)(2,1)S(1)}, bf16[8,128,256]{2,1,0:T(8,128)(2,1)S(1)}, u32[]{:S(2)}, u32[]{:S(2)}) collective-permute-start(bf16[8,128,256]{2,1,0:T(8,128)(2,1)S(1)} %constant_dynamic-update-slice_fusion.6.refs_14_), channel_id=1, source_target_pairs={{0,4},{1,3},{2,6},{3,1},{4,0},{5,7},{6,2},{7,5},{8,12},{9,11},{10,... | collective-permute-start | bytes 1572872 | tf_op jit(solution)/shard_map/ppermute | solution.py:315
  77.9 1.1 %collective-permute-start.9 = (bf16[4,128,256]{2,1,0:T(8,128)(2,1)S(1)}, bf16[4,128,256]{2,1,0:T(8,128)(2,1)S(1)}, u32[]{:S(2)}, u32[]{:S(2)}) collective-permute-start(bf16[4,128,256]{2,1,0:T(8,128)(2,1)S(1)} %gather_fusion), channel_id=1, source_target_pairs={{0,1},{1,0},{2,3},{3,2},{4,5},{5,4},{6,7},{7,6},{8,9},{9,8},{10,11... | collective-permute-start | bytes 786440 | tf_op jit(solution)/shard_map/ppermute | solution.py:365
  79.0 0.0 collective-permute-done.21.refs_19_
  79.0 0.1 collective-permute-start.10
  79.1 1.1 %collective-permute-done.9.refs_7_ = bf16[4,128,256]{2,1,0:T(8,128)(2,1)S(1)} collective-permute-done((bf16[4,128,256]{2,1,0:T(8,128)(2,1)S(1)}, bf16[4,128,256]{2,1,0:T(8,128)(2,1)S(1)}, u32[]{:S(2)}, u32[]{:S(2)}) %collective-permute-start.9) | collective-permute-done | bytes 262176 | tf_op jit(solution)/shard_map/ppermute | solution.py:365
  80.2 0.4 collective-permute-start.19
  80.6 0.0 collective-permute-done.10.refs_8_
  80.6 0.4 collective-permute-start.13
  80.9 0.0 collective-permute-done.12.refs_10_
  81.0 0.1 collective-permute-start.14
  81.1 0.0 collective-permute-done.11.refs_9_
  81.1 0.4 collective-permute-start.15
  81.5 3.7 %collective-permute-done.18.refs_15_ = bf16[8,128,256]{2,1,0:T(8,128)(2,1)S(1)} collective-permute-done((bf16[8,128,256]{2,1,0:T(8,128)(2,1)S(1)}, bf16[8,128,256]{2,1,0:T(8,128)(2,1)S(1)}, u32[]{:S(2)}, u32[]{:S(2)}) %collective-permute-start.18) | collective-permute-done | bytes 524320 | tf_op jit(solution)/shard_map/ppermute | solution.py:315
  85.2 2.4 %collective-permute-start.20 = (bf16[8,128,256]{2,1,0:T(8,128)(2,1)S(1)}, bf16[8,128,256]{2,1,0:T(8,128)(2,1)}, u32[]{:S(2)}, u32[]{:S(2)}) collective-permute-start(bf16[8,128,256]{2,1,0:T(8,128)(2,1)S(1)} %collective-permute-done.18.refs_15_), channel_id=1, source_target_pairs={{0,1},{1,0},{2,3},{3,2},{4,5},{5,4},{6,7},{7,6},{8,9},{9,8},{10,11... | collective-permute-start | bytes 1572872 | tf_op jit(solution)/shard_map/ppermute | solution.py:365
  87.6 0.0 collective-permute-done.13.refs_11_
  87.6 0.0 collective-permute-done.19.refs_16_
  87.6 0.0 collective-permute-done.14.refs_12_
  87.6 0.0 copy-done.6
  87.6 0.0 copy-start.13
  87.6 0.0 collective-permute-done.15.refs_13_
  87.7 1.5 %collective-permute-done.20.refs_17_ = bf16[8,128,256]{2,1,0:T(8,128)(2,1)} collective-permute-done((bf16[8,128,256]{2,1,0:T(8,128)(2,1)S(1)}, bf16[8,128,256]{2,1,0:T(8,128)(2,1)}, u32[]{:S(2)}, u32[]{:S(2)}) %collective-permute-start.20) | collective-permute-done | bytes 524320 | tf_op jit(solution)/shard_map/ppermute | solution.py:365
  89.3 0.0 copy-done.1
  89.3 9.2 %shard_map.84 = bf16[32,128,256]{2,1,0:T(8,128)(2,1)} custom-call(s32[4,272]{1,0:T(4,128)} %shard_map.83.lists, bf16[4,128,256]{2,1,0:T(8,128)(2,1)} %copy-done.5, bf16[4,128,256]{2,1,0:T(8,128)(2,1)} %copy-done.15, bf16[8,128,256]{2,1,0:T(8,128)(2,1)} %copy-done.3, bf16[8,128,256]{2,1,0:T(8,128)(2,1)} %copy-done.4, bf16[8,128,256]{2,1,0:T(8,128)(2,1)} %copy-done.1, ...), custom_call_target="tpu_custom_call" | custom-call | flops 1073741824 | bytes 16777216 | tf_op jit(solution)/shard_map/pallas_call | solution.py:201
  (44 shorter events, 0.3 us)
Async XLA Ops:
  0.0 15.9 %copy-start.20 = (s32[1,4,16]{2,1,0:T(4,128)S(1)}, s32[1,4,16]{2,1,0:T(4,128)}, u32[]{:S(2)}) copy-start(s32[1,4,16]{2,1,0:T(4,128)} %param.12) | copy-start | bytes 772
  8.3 7.6 %copy-start.21 = (s32[1,4,16]{2,1,0:T(4,128)S(1)}, s32[1,4,16]{2,1,0:T(4,128)}, u32[]{:S(2)}) copy-start(s32[1,4,16]{2,1,0:T(4,128)} %param.13) | copy-start | bytes 772
  8.3 8.7 %copy-start = (bf16[1,4,16,128,128]{4,3,2,1,0:T(8,128)(2,1)S(1)}, bf16[1,4,16,128,128]{4,3,2,1,0:T(8,128)(2,1)}, u32[]{:S(2)}) copy-start(bf16[1,4,16,128,128]{4,3,2,1,0:T(8,128)(2,1)} %param.14) | copy-start | bytes 6291460
  8.3 8.7 %copy-start.22 = (s32[4]{0:T(128)S(1)}, s32[4]{0:T(128)}, u32[]{:S(2)}) copy-start(s32[4]{0:T(128)} %owner_ref.1) | copy-start | bytes 52
  8.4 29.8 %all-to-all-start = ((bf16[16,128,256]{2,1,0:T(8,128)(2,1)}), bf16[16,128,256]{2,1,0:T(8,128)(2,1)S(1)}, u32[]{:S(2)}, u32[]{:S(2)}) async-start(bf16[16,128,256]{2,1,0:T(8,128)(2,1)} %shard_map.82), calls=%async_computation | async-start | bytes 2097152 | tf_op jit(solution)/shard_map/all_to_all | solution.py:332
  16.0 1.9 %copy-start.18 = (s32[2,4,16]{2,1,0:T(4,128)}, s32[2,4,16]{2,1,0:T(4,128)S(1)}, u32[]{:S(2)}) copy-start(s32[2,4,16]{2,1,0:T(4,128)S(1)} %constant_dynamic-update-slice_fusion.own_ref) | copy-start | bytes 1540
  16.0 1.8 %collective-permute-start = (s32[2,4,16]{2,1,0:T(4,128)S(1)}, s32[2,4,16]{2,1,0:T(4,128)S(1)}, u32[]{:S(2)}, u32[]{:S(2)}) collective-permute-start(s32[2,4,16]{2,1,0:T(4,128)S(1)} %constant_dynamic-update-slice_fusion.own_ref), channel_id=1, source_target_pairs={{0,1},{1,0},{2,3},{3,2},{4,5},{5,4},{6,7},{7,6},{8,9},{9,8},{10,11... | collective-permute-start | bytes 1544 | tf_op jit(solution)/shard_map/ppermute | solution.py:365
  17.0 62.0 %collective-permute-start.21 = (bf16[64,128,128]{2,1,0:T(8,128)(2,1)S(1)}, bf16[64,128,128]{2,1,0:T(8,128)(2,1)}, u32[]{:S(2)}, u32[]{:S(2)}) collective-permute-start(bf16[64,128,128]{2,1,0:T(8,128)(2,1)S(1)} %bitcast.4), channel_id=1, source_target_pairs={{0,1},{1,0},{2,3},{3,2},{4,5},{5,4},{6,7},{7,6},{8,9},{9,8},{10,11... | collective-permute-start | bytes 6291464 | tf_op jit(solution)/shard_map/ppermute | solution.py:365
  17.8 0.6 copy-start.19
  38.7 39.2 %copy-start.5 = (bf16[4,128,256]{2,1,0:T(8,128)(2,1)}, bf16[4,128,256]{2,1,0:T(8,128)(2,1)S(1)}, u32[]{:S(2)}) copy-start(bf16[4,128,256]{2,1,0:T(8,128)(2,1)S(1)} %gather_fusion) | copy-start | bytes 786436
  38.7 7.7 %collective-permute-start.4 = (bf16[4,128,256]{2,1,0:T(8,128)(2,1)S(1)}, bf16[4,128,256]{2,1,0:T(8,128)(2,1)S(1)}, u32[]{:S(2)}, u32[]{:S(2)}) collective-permute-start(bf16[4,128,256]{2,1,0:T(8,128)(2,1)S(1)} %gather_fusion), channel_id=1, source_target_pairs={{0,24},{2,26},{4,28},{6,30},{8,0},{10,2},{12,4},{14,6},{16,8},{18,... | collective-permute-start | bytes 786440 | tf_op jit(solution)/shard_map/ppermute | solution.py:303
  41.8 12.6 %collective-permute-start.5 = (bf16[4,128,256]{2,1,0:T(8,128)(2,1)S(1)}, bf16[4,128,256]{2,1,0:T(8,128)(2,1)S(1)}, u32[]{:S(2)}, u32[]{:S(2)}) collective-permute-start(bf16[4,128,256]{2,1,0:T(8,128)(2,1)S(1)} %gather_fusion), channel_id=1, source_target_pairs={{0,8},{2,10},{4,12},{6,14},{8,16},{10,18},{12,20},{14,22},{16,24},... | collective-permute-start | bytes 786440 | tf_op jit(solution)/shard_map/ppermute | solution.py:303
  42.3 12.1 %collective-permute-start.2 = (bf16[4,128,256]{2,1,0:T(8,128)(2,1)S(1)}, bf16[4,128,256]{2,1,0:T(8,128)(2,1)S(1)}, u32[]{:S(2)}, u32[]{:S(2)}) collective-permute-start(bf16[4,128,256]{2,1,0:T(8,128)(2,1)S(1)} %gather_fusion), channel_id=1, source_target_pairs={{0,4},{1,3},{2,6},{3,1},{4,0},{5,7},{6,2},{7,5},{8,12},{9,11},{10,... | collective-permute-start | bytes 786440 | tf_op jit(solution)/shard_map/ppermute | solution.py:315
  42.6 11.8 %collective-permute-start.1 = (bf16[4,128,256]{2,1,0:T(8,128)(2,1)S(1)}, bf16[4,128,256]{2,1,0:T(8,128)(2,1)S(1)}, u32[]{:S(2)}, u32[]{:S(2)}) collective-permute-start(bf16[4,128,256]{2,1,0:T(8,128)(2,1)S(1)} %gather_fusion), channel_id=1, source_target_pairs={{0,2},{1,5},{2,0},{3,7},{4,6},{5,1},{6,4},{7,3},{8,10},{9,13},{10,... | collective-permute-start | bytes 786440 | tf_op jit(solution)/shard_map/ppermute | solution.py:315
  54.4 33.2 %copy-start.4 = (bf16[8,128,256]{2,1,0:T(8,128)(2,1)}, bf16[8,128,256]{2,1,0:T(8,128)(2,1)S(1)}, u32[]{:S(2)}) copy-start(bf16[8,128,256]{2,1,0:T(8,128)(2,1)S(1)} %constant_dynamic-update-slice_fusion.4.refs_3_) | copy-start | bytes 1572868
  54.4 33.2 %copy-start.15 = (bf16[4,128,256]{2,1,0:T(8,128)(2,1)}, bf16[4,128,256]{2,1,0:T(8,128)(2,1)S(1)}, u32[]{:S(2)}) copy-start(bf16[4,128,256]{2,1,0:T(8,128)(2,1)S(1)} %collective-permute-done.1.refs_1_) | copy-start | bytes 786436
  54.4 10.6 %collective-permute-start.6 = (bf16[8,128,256]{2,1,0:T(8,128)(2,1)S(1)}, bf16[8,128,256]{2,1,0:T(8,128)(2,1)S(1)}, u32[]{:S(2)}, u32[]{:S(2)}) collective-permute-start(bf16[8,128,256]{2,1,0:T(8,128)(2,1)S(1)} %constant_dynamic-update-slice_fusion.4.refs_3_), channel_id=1, source_target_pairs={{0,2},{1,5},{2,0},{3,7},{4,6},{5,1},{6,4},{7,3},{8,10},{9,13},{10,... | collective-permute-start | bytes 1572872 | tf_op jit(solution)/shard_map/ppermute | solution.py:315
  54.5 5.3 %collective-permute-start.3 = (bf16[4,128,256]{2,1,0:T(8,128)(2,1)S(1)}, bf16[4,128,256]{2,1,0:T(8,128)(2,1)S(1)}, u32[]{:S(2)}, u32[]{:S(2)}) collective-permute-start(bf16[4,128,256]{2,1,0:T(8,128)(2,1)S(1)} %collective-permute-done.1.refs_1_), channel_id=1, source_target_pairs={{0,4},{1,3},{2,6},{3,1},{4,0},{5,7},{6,2},{7,5},{8,12},{9,11},{10,... | collective-permute-start | bytes 786440 | tf_op jit(solution)/shard_map/ppermute | solution.py:315
  55.8 10.5 %collective-permute-start.16 = (bf16[4,128,256]{2,1,0:T(8,128)(2,1)S(1)}, bf16[4,128,256]{2,1,0:T(8,128)(2,1)S(1)}, u32[]{:S(2)}, u32[]{:S(2)}) collective-permute-start(bf16[4,128,256]{2,1,0:T(8,128)(2,1)S(1)} %collective-permute-done.4), channel_id=1, source_target_pairs={{0,24},{2,26},{4,28},{6,30},{8,0},{10,2},{12,4},{14,6},{16,8},{18,... | collective-permute-start | bytes 786440 | tf_op jit(solution)/shard_map/ppermute | solution.py:303
  59.8 29.4 %copy-start.3 = (bf16[8,128,256]{2,1,0:T(8,128)(2,1)}, bf16[8,128,256]{2,1,0:T(8,128)(2,1)S(1)}, u32[]{:S(2)}) copy-start(bf16[8,128,256]{2,1,0:T(8,128)(2,1)S(1)} %constant_dynamic-update-slice_fusion.2.refs_2_) | copy-start | bytes 1572868
  59.8 16.9 %collective-permute-start.7 = (bf16[8,128,256]{2,1,0:T(8,128)(2,1)S(1)}, bf16[8,128,256]{2,1,0:T(8,128)(2,1)S(1)}, u32[]{:S(2)}, u32[]{:S(2)}) collective-permute-start(bf16[8,128,256]{2,1,0:T(8,128)(2,1)S(1)} %constant_dynamic-update-slice_fusion.2.refs_2_), channel_id=1, source_target_pairs={{0,24},{2,26},{4,28},{6,30},{8,0},{10,2},{12,4},{14,6},{16,8},{18,... | collective-permute-start | bytes 1572872 | tf_op jit(solution)/shard_map/ppermute | solution.py:303
  65.1 24.2 %copy-start.1 = (bf16[8,128,256]{2,1,0:T(8,128)(2,1)}, bf16[8,128,256]{2,1,0:T(8,128)(2,1)S(1)}, u32[]{:S(2)}) copy-start(bf16[8,128,256]{2,1,0:T(8,128)(2,1)S(1)} %collective-permute-done.6.refs_4_) | copy-start | bytes 1572868
  65.1 11.7 %collective-permute-start.8 = (bf16[8,128,256]{2,1,0:T(8,128)(2,1)S(1)}, bf16[8,128,256]{2,1,0:T(8,128)(2,1)S(1)}, u32[]{:S(2)}, u32[]{:S(2)}) collective-permute-start(bf16[8,128,256]{2,1,0:T(8,128)(2,1)S(1)} %pad_maximum_fusion), channel_id=1, source_target_pairs={{0,4},{1,3},{2,6},{3,1},{4,0},{5,7},{6,2},{7,5},{8,12},{9,11},{10,... | collective-permute-start | bytes 1572872 | tf_op jit(solution)/shard_map/ppermute | solution.py:315
  66.2 5.6 %collective-permute-start.17 = (bf16[4,128,256]{2,1,0:T(8,128)(2,1)S(1)}, bf16[4,128,256]{2,1,0:T(8,128)(2,1)S(1)}, u32[]{:S(2)}, u32[]{:S(2)}) collective-permute-start(bf16[4,128,256]{2,1,0:T(8,128)(2,1)S(1)} %collective-permute-done.16), channel_id=1, source_target_pairs={{0,2},{1,5},{2,0},{3,7},{4,6},{5,1},{6,4},{7,3},{8,10},{9,13},{10,... | collective-permute-start | bytes 786440 | tf_op jit(solution)/shard_map/ppermute | solution.py:315
  66.8 14.1 %collective-permute-start.12 = (bf16[8,128,256]{2,1,0:T(8,128)(2,1)S(1)}, bf16[8,128,256]{2,1,0:T(8,128)(2,1)S(1)}, u32[]{:S(2)}, u32[]{:S(2)}) collective-permute-start(bf16[8,128,256]{2,1,0:T(8,128)(2,1)S(1)} %constant_dynamic-update-slice_fusion.4.refs_3_), channel_id=1, source_target_pairs={{0,1},{1,0},{2,3},{3,2},{4,5},{5,4},{6,7},{7,6},{8,9},{9,8},{10,11... | collective-permute-start | bytes 1572872 | tf_op jit(solution)/shard_map/ppermute | solution.py:365
  71.9 9.2 %collective-permute-start.11 = (bf16[8,128,256]{2,1,0:T(8,128)(2,1)S(1)}, bf16[8,128,256]{2,1,0:T(8,128)(2,1)S(1)}, u32[]{:S(2)}, u32[]{:S(2)}) collective-permute-start(bf16[8,128,256]{2,1,0:T(8,128)(2,1)S(1)} %constant_dynamic-update-slice_fusion.2.refs_2_), channel_id=1, source_target_pairs={{0,1},{1,0},{2,3},{3,2},{4,5},{5,4},{6,7},{7,6},{8,9},{9,8},{10,11... | collective-permute-start | bytes 1572872 | tf_op jit(solution)/shard_map/ppermute | solution.py:365
  76.8 12.5 %copy-start.2 = (bf16[8,128,256]{2,1,0:T(8,128)(2,1)}, bf16[8,128,256]{2,1,0:T(8,128)(2,1)S(1)}, u32[]{:S(2)}) copy-start(bf16[8,128,256]{2,1,0:T(8,128)(2,1)S(1)} %constant_dynamic-update-slice_fusion.6.refs_14_) | copy-start | bytes 1572868
  76.8 10.8 %copy-start.6 = (bf16[8,128,256]{2,1,0:T(8,128)(2,1)}, bf16[8,128,256]{2,1,0:T(8,128)(2,1)S(1)}, u32[]{:S(2)}) copy-start(bf16[8,128,256]{2,1,0:T(8,128)(2,1)S(1)} %collective-permute-done.7.refs_5_) | copy-start | bytes 1572868
  76.8 10.9 %copy-start.7 = (bf16[8,128,256]{2,1,0:T(8,128)(2,1)}, bf16[8,128,256]{2,1,0:T(8,128)(2,1)S(1)}, u32[]{:S(2)}) copy-start(bf16[8,128,256]{2,1,0:T(8,128)(2,1)S(1)} %collective-permute-done.8.refs_6_) | copy-start | bytes 1572868
  76.8 8.4 %collective-permute-start.18 = (bf16[8,128,256]{2,1,0:T(8,128)(2,1)S(1)}, bf16[8,128,256]{2,1,0:T(8,128)(2,1)S(1)}, u32[]{:S(2)}, u32[]{:S(2)}) collective-permute-start(bf16[8,128,256]{2,1,0:T(8,128)(2,1)S(1)} %constant_dynamic-update-slice_fusion.6.refs_14_), channel_id=1, source_target_pairs={{0,4},{1,3},{2,6},{3,1},{4,0},{5,7},{6,2},{7,5},{8,12},{9,11},{10,... | collective-permute-start | bytes 1572872 | tf_op jit(solution)/shard_map/ppermute | solution.py:315
  77.9 2.3 %collective-permute-start.9 = (bf16[4,128,256]{2,1,0:T(8,128)(2,1)S(1)}, bf16[4,128,256]{2,1,0:T(8,128)(2,1)S(1)}, u32[]{:S(2)}, u32[]{:S(2)}) collective-permute-start(bf16[4,128,256]{2,1,0:T(8,128)(2,1)S(1)} %gather_fusion), channel_id=1, source_target_pairs={{0,1},{1,0},{2,3},{3,2},{4,5},{5,4},{6,7},{7,6},{8,9},{9,8},{10,11... | collective-permute-start | bytes 786440 | tf_op jit(solution)/shard_map/ppermute | solution.py:365
  79.0 1.5 %collective-permute-start.10 = (bf16[4,128,256]{2,1,0:T(8,128)(2,1)S(1)}, bf16[4,128,256]{2,1,0:T(8,128)(2,1)S(1)}, u32[]{:S(2)}, u32[]{:S(2)}) collective-permute-start(bf16[4,128,256]{2,1,0:T(8,128)(2,1)S(1)} %collective-permute-done.1.refs_1_), channel_id=1, source_target_pairs={{0,1},{1,0},{2,3},{3,2},{4,5},{5,4},{6,7},{7,6},{8,9},{9,8},{10,11... | collective-permute-start | bytes 786440 | tf_op jit(solution)/shard_map/ppermute | solution.py:365
  80.2 7.5 %copy-start.16 = (bf16[4,128,256]{2,1,0:T(8,128)(2,1)}, bf16[4,128,256]{2,1,0:T(8,128)(2,1)S(1)}, u32[]{:S(2)}) copy-start(bf16[4,128,256]{2,1,0:T(8,128)(2,1)S(1)} %collective-permute-done.9.refs_7_) | copy-start | bytes 786436
  80.2 7.4 %collective-permute-start.19 = (bf16[8,128,256]{2,1,0:T(8,128)(2,1)S(1)}, bf16[8,128,256]{2,1,0:T(8,128)(2,1)S(1)}, u32[]{:S(2)}, u32[]{:S(2)}) collective-permute-start(bf16[8,128,256]{2,1,0:T(8,128)(2,1)S(1)} %constant_dynamic-update-slice_fusion.6.refs_14_), channel_id=1, source_target_pairs={{0,1},{1,0},{2,3},{3,2},{4,5},{5,4},{6,7},{7,6},{8,9},{9,8},{10,11... | collective-permute-start | bytes 1572872 | tf_op jit(solution)/shard_map/ppermute | solution.py:365
  80.6 7.1 %copy-start.17 = (bf16[4,128,256]{2,1,0:T(8,128)(2,1)}, bf16[4,128,256]{2,1,0:T(8,128)(2,1)S(1)}, u32[]{:S(2)}) copy-start(bf16[4,128,256]{2,1,0:T(8,128)(2,1)S(1)} %collective-permute-done.10.refs_8_) | copy-start | bytes 786436
  80.6 7.0 %collective-permute-start.13 = (bf16[8,128,256]{2,1,0:T(8,128)(2,1)S(1)}, bf16[8,128,256]{2,1,0:T(8,128)(2,1)S(1)}, u32[]{:S(2)}, u32[]{:S(2)}) collective-permute-start(bf16[8,128,256]{2,1,0:T(8,128)(2,1)S(1)} %collective-permute-done.6.refs_4_), channel_id=1, source_target_pairs={{0,1},{1,0},{2,3},{3,2},{4,5},{5,4},{6,7},{7,6},{8,9},{9,8},{10,11... | collective-permute-start | bytes 1572872 | tf_op jit(solution)/shard_map/ppermute | solution.py:365
  80.9 6.8 %copy-start.8 = (bf16[8,128,256]{2,1,0:T(8,128)(2,1)}, bf16[8,128,256]{2,1,0:T(8,128)(2,1)S(1)}, u32[]{:S(2)}) copy-start(bf16[8,128,256]{2,1,0:T(8,128)(2,1)S(1)} %collective-permute-done.12.refs_10_) | copy-start | bytes 1572868
  81.0 6.7 %collective-permute-start.14 = (bf16[8,128,256]{2,1,0:T(8,128)(2,1)S(1)}, bf16[8,128,256]{2,1,0:T(8,128)(2,1)S(1)}, u32[]{:S(2)}, u32[]{:S(2)}) collective-permute-start(bf16[8,128,256]{2,1,0:T(8,128)(2,1)S(1)} %collective-permute-done.7.refs_5_), channel_id=1, source_target_pairs={{0,1},{1,0},{2,3},{3,2},{4,5},{5,4},{6,7},{7,6},{8,9},{9,8},{10,11... | collective-permute-start | bytes 1572872 | tf_op jit(solution)/shard_map/ppermute | solution.py:365
  81.1 6.6 %copy-start.9 = (bf16[8,128,256]{2,1,0:T(8,128)(2,1)}, bf16[8,128,256]{2,1,0:T(8,128)(2,1)S(1)}, u32[]{:S(2)}) copy-start(bf16[8,128,256]{2,1,0:T(8,128)(2,1)S(1)} %collective-permute-done.11.refs_9_) | copy-start | bytes 1572868
  81.1 6.6 %collective-permute-start.15 = (bf16[8,128,256]{2,1,0:T(8,128)(2,1)S(1)}, bf16[8,128,256]{2,1,0:T(8,128)(2,1)S(1)}, u32[]{:S(2)}, u32[]{:S(2)}) collective-permute-start(bf16[8,128,256]{2,1,0:T(8,128)(2,1)S(1)} %collective-permute-done.8.refs_6_), channel_id=1, source_target_pairs={{0,1},{1,0},{2,3},{3,2},{4,5},{5,4},{6,7},{7,6},{8,9},{9,8},{10,11... | collective-permute-start | bytes 1572872 | tf_op jit(solution)/shard_map/ppermute | solution.py:365
  85.2 2.5 %copy-start.10 = (bf16[8,128,256]{2,1,0:T(8,128)(2,1)}, bf16[8,128,256]{2,1,0:T(8,128)(2,1)S(1)}, u32[]{:S(2)}) copy-start(bf16[8,128,256]{2,1,0:T(8,128)(2,1)S(1)} %collective-permute-done.18.refs_15_) | copy-start | bytes 1572868
  85.2 4.0 %collective-permute-start.20 = (bf16[8,128,256]{2,1,0:T(8,128)(2,1)S(1)}, bf16[8,128,256]{2,1,0:T(8,128)(2,1)}, u32[]{:S(2)}, u32[]{:S(2)}) collective-permute-start(bf16[8,128,256]{2,1,0:T(8,128)(2,1)S(1)} %collective-permute-done.18.refs_15_), channel_id=1, source_target_pairs={{0,1},{1,0},{2,3},{3,2},{4,5},{5,4},{6,7},{7,6},{8,9},{9,8},{10,11... | collective-permute-start | bytes 1572872 | tf_op jit(solution)/shard_map/ppermute | solution.py:365
  87.6 1.7 %copy-start.12 = (bf16[8,128,256]{2,1,0:T(8,128)(2,1)}, bf16[8,128,256]{2,1,0:T(8,128)(2,1)S(1)}, u32[]{:S(2)}) copy-start(bf16[8,128,256]{2,1,0:T(8,128)(2,1)S(1)} %collective-permute-done.13.refs_11_) | copy-start | bytes 1572868
  87.6 1.7 %copy-start.11 = (bf16[8,128,256]{2,1,0:T(8,128)(2,1)}, bf16[8,128,256]{2,1,0:T(8,128)(2,1)S(1)}, u32[]{:S(2)}) copy-start(bf16[8,128,256]{2,1,0:T(8,128)(2,1)S(1)} %collective-permute-done.19.refs_16_) | copy-start | bytes 1572868
  87.6 1.6 %copy-start.13 = (bf16[8,128,256]{2,1,0:T(8,128)(2,1)}, bf16[8,128,256]{2,1,0:T(8,128)(2,1)S(1)}, u32[]{:S(2)}) copy-start(bf16[8,128,256]{2,1,0:T(8,128)(2,1)S(1)} %collective-permute-done.14.refs_12_) | copy-start | bytes 1572868
  87.7 1.6 %copy-start.14 = (bf16[8,128,256]{2,1,0:T(8,128)(2,1)}, bf16[8,128,256]{2,1,0:T(8,128)(2,1)S(1)}, u32[]{:S(2)}) copy-start(bf16[8,128,256]{2,1,0:T(8,128)(2,1)S(1)} %collective-permute-done.15.refs_13_) | copy-start | bytes 1572868

commit v9 on v8

--- a/solution.py
+++ b/solution.py
@@ -87,68 +87,68 @@
 
 
 def phased_kernel(places, lists, *refs):
-    counts = [len(part) for part in places]
-    n = sum(counts)
+    n = sum(len(part) for part in places)
     pieces, tile_refs = refs[:n], refs[n : n + 2]
     weight_ref, out_ref, sent, tiles, acc, stage, sem, out_sem = refs[n + 2 :]
     each = tiles.shape[0] // 2
-    copies = [
+    copies, at = [], 0
+    for part in places:
+        copies.append(load(at, pieces[at : at + len(part)], part, sent, sem))
+        at += len(part)
+    copies[0] += [
         pltpu.make_async_copy(ref, tiles.at[pl.ds(i * each, each)], sem.at[n + i])
         for i, ref in enumerate(tile_refs)
     ]
-    copies += load(0, pieces[: counts[0]], places[0], sent, sem)
-    later = load(counts[0], pieces[counts[0] :], places[1], sent, sem)
-    for copy in copies + later:
+    for copy in copies[0]:
         copy.start()
     acc[...] = jnp.zeros_like(acc)
-    middle = lists.shape[1] // 2
-    for copy in copies:
-        copy.wait()
-    run(lists, 0, lists[3, 0], tiles, sent, acc)
-    for copy in later:
-        copy.wait()
-    run(lists, middle, lists[3, middle], tiles, sent, acc)
+    for part in copies[1:]:
+        for copy in part:
+            copy.start()
+    span = lists.shape[1] // len(places)
+    for i, part in enumerate(copies):
+        for copy in part:
+            copy.wait()
+        run(lists, i * span, lists[3, i * span], tiles, sent, acc)
     finish(acc, weight_ref, out_ref, stage, out_sem)
 
 
 def lists_kernel(n_blocks, own_ref, other_ref, lists):
     me, rep = lax.axis_index("dom"), lax.axis_index("rep")
     sections, each = own_ref.shape[1:]
-    middle = lists.shape[1] // 2
-    early, late = jnp.int32(0), jnp.int32(0)
+    span = lists.shape[1] // 3
+    counts = (jnp.int32(0),) * 3
     for s in range(sections):
         for part, ref in enumerate((own_ref, other_ref)):
 
             def pick(k, counts, ref=ref, part=part, s=s):
-                early, late = counts
                 row = ref[0, s, k] - rep * n_blocks
                 here = jnp.logical_and(row >= 0, row < n_blocks)
                 col = ref[1, s, k]
                 holder, chip = col // 16, col % 16
                 other = (holder != rep).astype(jnp.int32)
                 shift = (chip // 4 - me // 4) & 3
-                at = place_of((chip ^ me) & 3, holder) * sections + s
-                turn, by_shift = at // 8, shift // 2
-                near = 16 + jnp.where(
-                    turn == 0, at + (at // 4) * 4 + by_shift * 4, 8 + at + by_shift * 8
+                turn = place_of((chip ^ me) & 3, holder)
+                at = turn * sections + s
+                by_shift = shift // 2
+                near = jnp.where(
+                    turn < 2, at + (turn + by_shift) * 4, 8 + at + by_shift * 8
                 )
-                at = jnp.where((shift & 1) == 1, near, at)
-                is_late = shift == 2
-                place = jnp.where(is_late, 96 + other * 16 + at, other * 48 + at)
-                put(
-                    lists,
-                    jnp.where(is_late, middle + late, early),
-                    here,
-                    (part * sections + s) * each + k,
-                    row,
-                    place,
+                place = jnp.where(shift == 0, other * 16 + at, 96 + other * 16 + at)
+                place = jnp.where((shift & 1) == 1, 32 + other * 32 + near, place)
+                phase = jnp.where((shift & 1) == 1, 1, shift)
+                target = jnp.where(
+                    phase == 0,
+                    counts[0],
+                    jnp.where(phase == 1, span + counts[1], 2 * span + counts[2]),
                 )
+                put(lists, target, here, (part * sections + s) * each + k, row, place)
                 now = here.astype(jnp.int32)
-                return early + jnp.where(is_late, 0, now), late + jnp.where(is_late, now, 0)
-
-            early, late = lax.fori_loop(0, each, pick, (early, late))
-    lists[3, 0] = pad(lists, 0, early, n_blocks)
-    lists[3, middle] = pad(lists, middle, late, n_blocks)
+                return tuple(c + jnp.where(phase == i, now, 0) for i, c in enumerate(counts))
+
+            counts = lax.fori_loop(0, each, pick, counts)
+    for i, count in enumerate(counts):
+        lists[3, i * span] = pad(lists, i * span, count, n_blocks)
 
 
 HBM = pl.BlockSpec(memory_space=pltpu.HBM)
@@ -196,7 +196,7 @@
 def products_in_phases(pieces, places, tile_list, lists, weight, n_blocks):
     n_tiles, tile_len = 2 * tile_list[0].shape[0], tile_list[0].shape[1]
     width = weight.shape[0]
-    flat = pieces[0] + pieces[1]
+    flat = [piece for part in pieces for piece in part]
     n_sent = sum(piece.shape[0] for piece in flat)
     return pl.pallas_call(
         functools.partial(phased_kernel, places),
@@ -219,7 +219,7 @@
     n_tiles = 2 * own.shape[1] * own.shape[2]
     return pl.pallas_call(
         functools.partial(lists_kernel, n_blocks),
-        out_shape=jax.ShapeDtypeStruct((4, 2 * (n_tiles + UNROLL)), jnp.int32),
+        out_shape=jax.ShapeDtypeStruct((4, 3 * (n_tiles + UNROLL)), jnp.int32),
         in_specs=[SMEM] * 2,
         out_specs=SMEM,
     )(own, other)
@@ -342,8 +342,12 @@
     each = shard.shape[0]
     three_second = cross(jnp.concatenate([three, near_came[each:]]), 1)
     far_pair = jnp.concatenate([far, cross(far, 0)])
-    early = [shard, came, second, near, near_came, one_second, three_second]
-    return early, [far_pair, cross(tie(far_pair, (one_second, three_second)), 1)], lists
+    return (
+        [shard, came, second],
+        [near, near_came, one_second, three_second],
+        [far_pair, cross(tie(far_pair, (one_second, three_second)), 1)],
+        lists,
+    )
 
 
 def body(features, node_order, section_owner, send_blocks, tile_rows, tile_cols, tiles, weight):
@@ -367,8 +371,8 @@
         tile_list = [own_tiles, exchange(own_tiles)]
         lists = product_lists(numbers, exchange(numbers), n_blocks)
         mine = pick_share(features, node_order, section_owner, send_blocks, tile_len)
-        early, late, lists = gather_small(mine, section_owner, lists)
-        parts = [part + [exchange(piece) for piece in part] for part in (early, late)]
+        *own, lists = gather_small(mine, section_owner, lists)
+        parts = [part + [exchange(piece) for piece in part] for part in own]
         ends, place = [], 0
         for part in parts:
             ends.append([])

time: 99.8 us -> 99.1 us (level)
  no operation moved by 1% of the time
where the time goes in v9:
time: 99.1 us; the launch traced here: 98.2 us
  starting transfers between devices  39 us (39%)
  waiting for transfers between devices  33.3 us (34%)
  Pallas kernels  24 us (24%)
  local copies, waits for them, and re-layouts  1.38 us (1%)
    ppermute x11, starting transfers between devices, exchange(): return lax.ppermute(value, 'rep', swap)  14.3 us
    all_to_all x1, waiting for transfers between devices, gather_small(): landed = lax.all_to_all(rows, 'dom', 0, 0, tiled=True)  12.9 us
    ppermute x4, starting transfers between devices, move(): return lax.ppermute(value, 'dom', pairs)  10.8 us
    ppermute x4, waiting for transfers between devices, move(): return lax.ppermute(value, 'dom', pairs)  9.81 us
    pallas_call x1, Pallas kernels, products_in_phases(): pl.pallas_call(functools.partial(phased_kernel, places), out_shape=jax.Sh...  8.89 us
    pallas_call x1, Pallas kernels, pick_share(): pl.pallas_call(pick_kernel, out_shape=jax.ShapeDtypeStruct((share, tile_l...  8.3 us
    all_to_all x1, starting transfers between devices, gather_small(): landed = lax.all_to_all(rows, 'dom', 0, 0, tiled=True)  7.56 us
    ppermute x7, waiting for transfers between devices, cross(): return lax.ppermute(value, ('dom', 'rep'), pairs)  7.29 us
  transfers between devices with their start and end apart: 23, of which 9 were waited for; matrix products, arithmetic and copies ran while one was open for 1% of the time, Pallas kernels for 7%

profile of v9, /device:TPU:1, one launch (start us, length us, event | category | flops | bytes accessed | tf_op | source)
XLA Modules:
  0.0 98.2 jit_solution(4365424150930531417)
XLA Ops:
  0.0 8.3 %shard_map.82 = bf16[16,128,256]{2,1,0:T(8,128)(2,1)} custom-call(s32[4]{0:T(128)} %owner_ref.1, s32[4,32]{1,0:T(4,128)} %blocks_ref.1, s32[64,1,128]{2,1,0:T(1,128)} %bitcast.5, bf16[8192,256]{1,0:T(8,128)(2,1)} %features_ref.1), custom_call_target="tpu_custom_call" | custom-call | tf_op jit(solution)/shard_map/pallas_call | solution.py:273
  8.3 0.0 copy-start.21
  8.3 0.0 copy-start
  8.3 0.0 copy-start.22
  8.4 7.6 %all-to-all-start = ((bf16[16,128,256]{2,1,0:T(8,128)(2,1)}), bf16[16,128,256]{2,1,0:T(8,128)(2,1)S(1)}, u32[]{:S(2)}, u32[]{:S(2)}) async-start(bf16[16,128,256]{2,1,0:T(8,128)(2,1)} %shard_map.82), calls=%async_computation | async-start | bytes 2097152 | tf_op jit(solution)/shard_map/all_to_all | solution.py:332
  15.9 0.0 copy-done.20
  15.9 0.0 copy-done.21
  16.0 0.0 copy-start.18
  16.0 1.0 %collective-permute-start = (s32[2,4,16]{2,1,0:T(4,128)S(1)}, s32[2,4,16]{2,1,0:T(4,128)S(1)}, u32[]{:S(2)}, u32[]{:S(2)}) collective-permute-start(s32[2,4,16]{2,1,0:T(4,128)S(1)} %constant_dynamic-update-slice_fusion.own_ref), channel_id=1, source_target_pairs={{0,1},{1,0},{2,3},{3,2},{4,5},{5,4},{6,7},{7,6},{8,9},{9,8},{10,11... | collective-permute-start | bytes 1544 | tf_op jit(solution)/shard_map/ppermute | solution.py:369
  17.0 0.0 copy-done
  17.0 0.1 collective-permute-start.21
  17.1 0.0 copy-done.22
  17.1 0.7 collective-permute-done.other_ref
  17.8 0.0 copy-done.18
  17.8 0.6 copy-done.19
  18.4 6.8 %shard_map.83.lists = s32[4,408]{1,0:T(4,128)} custom-call(s32[2,4,16]{2,1,0:T(4,128)} %copy-done.18, s32[2,4,16]{2,1,0:T(4,128)} %copy-done.19), custom_call_target="tpu_custom_call" | custom-call | tf_op jit(solution)/shard_map/pallas_call | solution.py:220
  25.2 12.9 %all-to-all-done = bf16[16,128,256]{2,1,0:T(8,128)(2,1)S(1)} async-done(((bf16[16,128,256]{2,1,0:T(8,128)(2,1)}), bf16[16,128,256]{2,1,0:T(8,128)(2,1)S(1)}, u32[]{:S(2)}, u32[]{:S(2)}) %all-to-all-start) | async-done | bytes 1048608 | tf_op jit(solution)/shard_map/all_to_all | solution.py:332
  38.1 0.6 gather_fusion
  38.7 3.1 %collective-permute-start.7 = (bf16[4,128,256]{2,1,0:T(8,128)(2,1)S(1)}, bf16[4,128,256]{2,1,0:T(8,128)(2,1)S(1)}, u32[]{:S(2)}, u32[]{:S(2)}) collective-permute-start(bf16[4,128,256]{2,1,0:T(8,128)(2,1)S(1)} %gather_fusion), channel_id=1, source_target_pairs={{0,24},{2,26},{4,28},{6,30},{8,0},{10,2},{12,4},{14,6},{16,8},{18,... | collective-permute-start | bytes 786440 | tf_op jit(solution)/shard_map/ppermute | solution.py:303
  41.8 0.5 collective-permute-start.8
  42.3 0.3 collective-permute-start.2
  42.6 2.0 %collective-permute-start.1 = (bf16[4,128,256]{2,1,0:T(8,128)(2,1)S(1)}, bf16[4,128,256]{2,1,0:T(8,128)(2,1)S(1)}, u32[]{:S(2)}, u32[]{:S(2)}) collective-permute-start(bf16[4,128,256]{2,1,0:T(8,128)(2,1)S(1)} %gather_fusion), channel_id=1, source_target_pairs={{0,2},{1,5},{2,0},{3,7},{4,6},{5,1},{6,4},{7,3},{8,10},{9,13},{10,... | collective-permute-start | bytes 786440 | tf_op jit(solution)/shard_map/ppermute | solution.py:315
  44.5 1.9 %collective-permute-done.7 = bf16[4,128,256]{2,1,0:T(8,128)(2,1)S(1)} collective-permute-done((bf16[4,128,256]{2,1,0:T(8,128)(2,1)S(1)}, bf16[4,128,256]{2,1,0:T(8,128)(2,1)S(1)}, u32[]{:S(2)}, u32[]{:S(2)}) %collective-permute-start.7) | collective-permute-done | bytes 262176 | tf_op jit(solution)/shard_map/ppermute | solution.py:303
  46.4 7.9 %collective-permute-done.8 = bf16[4,128,256]{2,1,0:T(8,128)(2,1)S(1)} collective-permute-done((bf16[4,128,256]{2,1,0:T(8,128)(2,1)S(1)}, bf16[4,128,256]{2,1,0:T(8,128)(2,1)S(1)}, u32[]{:S(2)}, u32[]{:S(2)}) %collective-permute-start.8) | collective-permute-done | bytes 262176 | tf_op jit(solution)/shard_map/ppermute | solution.py:303
  54.4 0.0 collective-permute-done.2
  54.4 0.0 collective-permute-done.1.refs_1_
  54.4 0.0 copy-start.15
  54.4 0.1 collective-permute-start.9
  54.5 1.3 %collective-permute-start.3 = (bf16[4,128,256]{2,1,0:T(8,128)(2,1)S(1)}, bf16[4,128,256]{2,1,0:T(8,128)(2,1)S(1)}, u32[]{:S(2)}, u32[]{:S(2)}) collective-permute-start(bf16[4,128,256]{2,1,0:T(8,128)(2,1)S(1)} %collective-permute-done.1.refs_1_), channel_id=1, source_target_pairs={{0,4},{1,3},{2,6},{3,1},{4,0},{5,7},{6,2},{7,5},{8,12},{9,11},{10,... | collective-permute-start | bytes 786440 | tf_op jit(solution)/shard_map/ppermute | solution.py:315
  55.8 2.0 %collective-permute-start.16 = (bf16[4,128,256]{2,1,0:T(8,128)(2,1)S(1)}, bf16[4,128,256]{2,1,0:T(8,128)(2,1)S(1)}, u32[]{:S(2)}, u32[]{:S(2)}) collective-permute-start(bf16[4,128,256]{2,1,0:T(8,128)(2,1)S(1)} %collective-permute-done.7), channel_id=1, source_target_pairs={{0,24},{2,26},{4,28},{6,30},{8,0},{10,2},{12,4},{14,6},{16,8},{18,... | collective-permute-start | bytes 786440 | tf_op jit(solution)/shard_map/ppermute | solution.py:303
  57.8 2.0 %collective-permute-done.3 = bf16[4,128,256]{2,1,0:T(8,128)(2,1)S(1)} collective-permute-done((bf16[4,128,256]{2,1,0:T(8,128)(2,1)S(1)}, bf16[4,128,256]{2,1,0:T(8,128)(2,1)S(1)}, u32[]{:S(2)}, u32[]{:S(2)}) %collective-permute-start.3) | collective-permute-done | bytes 262176 | tf_op jit(solution)/shard_map/ppermute | solution.py:315
  59.8 5.2 %collective-permute-start.10 = (bf16[8,128,256]{2,1,0:T(8,128)(2,1)S(1)}, bf16[8,128,256]{2,1,0:T(8,128)(2,1)S(1)}, u32[]{:S(2)}, u32[]{:S(2)}) collective-permute-start(bf16[8,128,256]{2,1,0:T(8,128)(2,1)S(1)} %constant_dynamic-update-slice_fusion.2.refs_2_), channel_id=1, source_target_pairs={{0,24},{2,26},{4,28},{6,30},{8,0},{10,2},{12,4},{14,6},{16,8},{18,... | collective-permute-start | bytes 1572872 | tf_op jit(solution)/shard_map/ppermute | solution.py:303
  65.1 0.0 collective-permute-done.9.refs_7_
  65.1 1.1 %collective-permute-start.11 = (bf16[8,128,256]{2,1,0:T(8,128)(2,1)S(1)}, bf16[8,128,256]{2,1,0:T(8,128)(2,1)S(1)}, u32[]{:S(2)}, u32[]{:S(2)}) collective-permute-start(bf16[8,128,256]{2,1,0:T(8,128)(2,1)S(1)} %pad_maximum_fusion), channel_id=1, source_target_pairs={{0,4},{1,3},{2,6},{3,1},{4,0},{5,7},{6,2},{7,5},{8,12},{9,11},{10,... | collective-permute-start | bytes 1572872 | tf_op jit(solution)/shard_map/ppermute | solution.py:315
  66.2 0.0 collective-permute-done.16
  66.2 0.6 collective-permute-start.17
  66.8 3.5 %collective-permute-start.12 = (bf16[8,128,256]{2,1,0:T(8,128)(2,1)S(1)}, bf16[8,128,256]{2,1,0:T(8,128)(2,1)S(1)}, u32[]{:S(2)}, u32[]{:S(2)}) collective-permute-start(bf16[8,128,256]{2,1,0:T(8,128)(2,1)S(1)} %constant_dynamic-update-slice_fusion.4.refs_6_), channel_id=1, source_target_pairs={{0,1},{1,0},{2,3},{3,2},{4,5},{5,4},{6,7},{7,6},{8,9},{9,8},{10,11... | collective-permute-start | bytes 1572872 | tf_op jit(solution)/shard_map/ppermute | solution.py:369
  70.4 1.5 %collective-permute-done.17 = bf16[4,128,256]{2,1,0:T(8,128)(2,1)S(1)} collective-permute-done((bf16[4,128,256]{2,1,0:T(8,128)(2,1)S(1)}, bf16[4,128,256]{2,1,0:T(8,128)(2,1)S(1)}, u32[]{:S(2)}, u32[]{:S(2)}) %collective-permute-start.17) | collective-permute-done | bytes 262176 | tf_op jit(solution)/shard_map/ppermute | solution.py:315
  71.9 4.9 %collective-permute-start.6 = (bf16[8,128,256]{2,1,0:T(8,128)(2,1)S(1)}, bf16[8,128,256]{2,1,0:T(8,128)(2,1)S(1)}, u32[]{:S(2)}, u32[]{:S(2)}) collective-permute-start(bf16[8,128,256]{2,1,0:T(8,128)(2,1)S(1)} %constant_dynamic-update-slice_fusion.2.refs_2_), channel_id=1, source_target_pairs={{0,1},{1,0},{2,3},{3,2},{4,5},{5,4},{6,7},{7,6},{8,9},{9,8},{10,11... | collective-permute-start | bytes 1572872 | tf_op jit(solution)/shard_map/ppermute | solution.py:369
  76.8 0.0 collective-permute-done.10.refs_8_
  76.8 0.0 collective-permute-done.11.refs_9_
  76.8 1.1 %collective-permute-start.18 = (bf16[8,128,256]{2,1,0:T(8,128)(2,1)S(1)}, bf16[8,128,256]{2,1,0:T(8,128)(2,1)S(1)}, u32[]{:S(2)}, u32[]{:S(2)}) collective-permute-start(bf16[8,128,256]{2,1,0:T(8,128)(2,1)S(1)} %constant_dynamic-update-slice_fusion.6.refs_14_), channel_id=1, source_target_pairs={{0,4},{1,3},{2,6},{3,1},{4,0},{5,7},{6,2},{7,5},{8,12},{9,11},{10,... | collective-permute-start | bytes 1572872 | tf_op jit(solution)/shard_map/ppermute | solution.py:315
  77.9 1.1 %collective-permute-start.4 = (bf16[4,128,256]{2,1,0:T(8,128)(2,1)S(1)}, bf16[4,128,256]{2,1,0:T(8,128)(2,1)S(1)}, u32[]{:S(2)}, u32[]{:S(2)}) collective-permute-start(bf16[4,128,256]{2,1,0:T(8,128)(2,1)S(1)} %gather_fusion), channel_id=1, source_target_pairs={{0,1},{1,0},{2,3},{3,2},{4,5},{5,4},{6,7},{7,6},{8,9},{9,8},{10,11... | collective-permute-start | bytes 786440 | tf_op jit(solution)/shard_map/ppermute | solution.py:369
  79.0 0.0 collective-permute-done.21.refs_19_
  79.0 0.1 collective-permute-start.5
  79.1 1.1 %collective-permute-done.4.refs_3_ = bf16[4,128,256]{2,1,0:T(8,128)(2,1)S(1)} collective-permute-done((bf16[4,128,256]{2,1,0:T(8,128)(2,1)S(1)}, bf16[4,128,256]{2,1,0:T(8,128)(2,1)S(1)}, u32[]{:S(2)}, u32[]{:S(2)}) %collective-permute-start.4) | collective-permute-done | bytes 262176 | tf_op jit(solution)/shard_map/ppermute | solution.py:369
  80.2 0.4 collective-permute-start.19
  80.6 0.0 collective-permute-done.5.refs_4_
  80.6 0.4 collective-permute-start.13
  80.9 0.0 collective-permute-done.12.refs_10_
  81.0 0.1 collective-permute-start.14
  81.1 0.0 collective-permute-done.6.refs_5_
  81.1 0.4 collective-permute-start.15
  81.5 3.7 %collective-permute-done.18.refs_15_ = bf16[8,128,256]{2,1,0:T(8,128)(2,1)S(1)} collective-permute-done((bf16[8,128,256]{2,1,0:T(8,128)(2,1)S(1)}, bf16[8,128,256]{2,1,0:T(8,128)(2,1)S(1)}, u32[]{:S(2)}, u32[]{:S(2)}) %collective-permute-start.18) | collective-permute-done | bytes 524320 | tf_op jit(solution)/shard_map/ppermute | solution.py:315
  85.2 2.4 %collective-permute-start.20 = (bf16[8,128,256]{2,1,0:T(8,128)(2,1)S(1)}, bf16[8,128,256]{2,1,0:T(8,128)(2,1)}, u32[]{:S(2)}, u32[]{:S(2)}) collective-permute-start(bf16[8,128,256]{2,1,0:T(8,128)(2,1)S(1)} %collective-permute-done.18.refs_15_), channel_id=1, source_target_pairs={{0,1},{1,0},{2,3},{3,2},{4,5},{5,4},{6,7},{7,6},{8,9},{9,8},{10,11... | collective-permute-start | bytes 1572872 | tf_op jit(solution)/shard_map/ppermute | solution.py:369
  87.6 0.0 collective-permute-done.13.refs_11_
  87.6 0.0 collective-permute-done.19.refs_16_
  87.6 0.0 copy-done.4
  87.6 0.0 copy-start.11
  87.6 0.0 collective-permute-done.14.refs_12_
  87.6 0.0 collective-permute-done.15.refs_13_
  87.7 1.5 %collective-permute-done.20.refs_17_ = bf16[8,128,256]{2,1,0:T(8,128)(2,1)} collective-permute-done((bf16[8,128,256]{2,1,0:T(8,128)(2,1)S(1)}, bf16[8,128,256]{2,1,0:T(8,128)(2,1)}, u32[]{:S(2)}, u32[]{:S(2)}) %collective-permute-start.20) | collective-permute-done | bytes 524320 | tf_op jit(solution)/shard_map/ppermute | solution.py:369
  89.3 0.0 copy-done.2
  89.3 8.9 %shard_map.84 = bf16[32,128,256]{2,1,0:T(8,128)(2,1)} custom-call(s32[4,408]{1,0:T(4,128)} %shard_map.83.lists, bf16[4,128,256]{2,1,0:T(8,128)(2,1)} %copy-done.5, bf16[4,128,256]{2,1,0:T(8,128)(2,1)} %copy-done.15, bf16[8,128,256]{2,1,0:T(8,128)(2,1)} %copy-done.3, bf16[4,128,256]{2,1,0:T(8,128)(2,1)} %copy-done.16, bf16[4,128,256]{2,1,0:T(8,128)(2,1)} %copy-done.17, ...), custom_call_target="tpu_custom_call" | custom-call | flops 1073741824 | bytes 16777216 | tf_op jit(solution)/shard_map/pallas_call | solution.py:201
  (44 shorter events, 0.3 us)
Async XLA Ops:
  0.0 15.9 %copy-start.20 = (s32[1,4,16]{2,1,0:T(4,128)S(1)}, s32[1,4,16]{2,1,0:T(4,128)}, u32[]{:S(2)}) copy-start(s32[1,4,16]{2,1,0:T(4,128)} %param.12) | copy-start | bytes 772
  8.3 7.6 %copy-start.21 = (s32[1,4,16]{2,1,0:T(4,128)S(1)}, s32[1,4,16]{2,1,0:T(4,128)}, u32[]{:S(2)}) copy-start(s32[1,4,16]{2,1,0:T(4,128)} %param.13) | copy-start | bytes 772
  8.3 8.7 %copy-start = (bf16[1,4,16,128,128]{4,3,2,1,0:T(8,128)(2,1)S(1)}, bf16[1,4,16,128,128]{4,3,2,1,0:T(8,128)(2,1)}, u32[]{:S(2)}) copy-start(bf16[1,4,16,128,128]{4,3,2,1,0:T(8,128)(2,1)} %param.14) | copy-start | bytes 6291460
  8.3 8.7 %copy-start.22 = (s32[4]{0:T(128)S(1)}, s32[4]{0:T(128)}, u32[]{:S(2)}) copy-start(s32[4]{0:T(128)} %owner_ref.1) | copy-start | bytes 52
  8.4 29.8 %all-to-all-start = ((bf16[16,128,256]{2,1,0:T(8,128)(2,1)}), bf16[16,128,256]{2,1,0:T(8,128)(2,1)S(1)}, u32[]{:S(2)}, u32[]{:S(2)}) async-start(bf16[16,128,256]{2,1,0:T(8,128)(2,1)} %shard_map.82), calls=%async_computation | async-start | bytes 2097152 | tf_op jit(solution)/shard_map/all_to_all | solution.py:332
  16.0 1.9 %copy-start.18 = (s32[2,4,16]{2,1,0:T(4,128)}, s32[2,4,16]{2,1,0:T(4,128)S(1)}, u32[]{:S(2)}) copy-start(s32[2,4,16]{2,1,0:T(4,128)S(1)} %constant_dynamic-update-slice_fusion.own_ref) | copy-start | bytes 1540
  16.0 1.8 %collective-permute-start = (s32[2,4,16]{2,1,0:T(4,128)S(1)}, s32[2,4,16]{2,1,0:T(4,128)S(1)}, u32[]{:S(2)}, u32[]{:S(2)}) collective-permute-start(s32[2,4,16]{2,1,0:T(4,128)S(1)} %constant_dynamic-update-slice_fusion.own_ref), channel_id=1, source_target_pairs={{0,1},{1,0},{2,3},{3,2},{4,5},{5,4},{6,7},{7,6},{8,9},{9,8},{10,11... | collective-permute-start | bytes 1544 | tf_op jit(solution)/shard_map/ppermute | solution.py:369
  17.0 62.0 %collective-permute-start.21 = (bf16[64,128,128]{2,1,0:T(8,128)(2,1)S(1)}, bf16[64,128,128]{2,1,0:T(8,128)(2,1)}, u32[]{:S(2)}, u32[]{:S(2)}) collective-permute-start(bf16[64,128,128]{2,1,0:T(8,128)(2,1)S(1)} %bitcast.4), channel_id=1, source_target_pairs={{0,1},{1,0},{2,3},{3,2},{4,5},{5,4},{6,7},{7,6},{8,9},{9,8},{10,11... | collective-permute-start | bytes 6291464 | tf_op jit(solution)/shard_map/ppermute | solution.py:369
  17.8 0.6 copy-start.19
  38.7 39.2 %copy-start.5 = (bf16[4,128,256]{2,1,0:T(8,128)(2,1)}, bf16[4,128,256]{2,1,0:T(8,128)(2,1)S(1)}, u32[]{:S(2)}) copy-start(bf16[4,128,256]{2,1,0:T(8,128)(2,1)S(1)} %gather_fusion) | copy-start | bytes 786436
  38.7 7.7 %collective-permute-start.7 = (bf16[4,128,256]{2,1,0:T(8,128)(2,1)S(1)}, bf16[4,128,256]{2,1,0:T(8,128)(2,1)S(1)}, u32[]{:S(2)}, u32[]{:S(2)}) collective-permute-start(bf16[4,128,256]{2,1,0:T(8,128)(2,1)S(1)} %gather_fusion), channel_id=1, source_target_pairs={{0,24},{2,26},{4,28},{6,30},{8,0},{10,2},{12,4},{14,6},{16,8},{18,... | collective-permute-start | bytes 786440 | tf_op jit(solution)/shard_map/ppermute | solution.py:303
  41.8 12.6 %collective-permute-start.8 = (bf16[4,128,256]{2,1,0:T(8,128)(2,1)S(1)}, bf16[4,128,256]{2,1,0:T(8,128)(2,1)S(1)}, u32[]{:S(2)}, u32[]{:S(2)}) collective-permute-start(bf16[4,128,256]{2,1,0:T(8,128)(2,1)S(1)} %gather_fusion), channel_id=1, source_target_pairs={{0,8},{2,10},{4,12},{6,14},{8,16},{10,18},{12,20},{14,22},{16,24},... | collective-permute-start | bytes 786440 | tf_op jit(solution)/shard_map/ppermute | solution.py:303
  42.3 12.1 %collective-permute-start.2 = (bf16[4,128,256]{2,1,0:T(8,128)(2,1)S(1)}, bf16[4,128,256]{2,1,0:T(8,128)(2,1)S(1)}, u32[]{:S(2)}, u32[]{:S(2)}) collective-permute-start(bf16[4,128,256]{2,1,0:T(8,128)(2,1)S(1)} %gather_fusion), channel_id=1, source_target_pairs={{0,4},{1,3},{2,6},{3,1},{4,0},{5,7},{6,2},{7,5},{8,12},{9,11},{10,... | collective-permute-start | bytes 786440 | tf_op jit(solution)/shard_map/ppermute | solution.py:315
  42.6 11.8 %collective-permute-start.1 = (bf16[4,128,256]{2,1,0:T(8,128)(2,1)S(1)}, bf16[4,128,256]{2,1,0:T(8,128)(2,1)S(1)}, u32[]{:S(2)}, u32[]{:S(2)}) collective-permute-start(bf16[4,128,256]{2,1,0:T(8,128)(2,1)S(1)} %gather_fusion), channel_id=1, source_target_pairs={{0,2},{1,5},{2,0},{3,7},{4,6},{5,1},{6,4},{7,3},{8,10},{9,13},{10,... | collective-permute-start | bytes 786440 | tf_op jit(solution)/shard_map/ppermute | solution.py:315
  54.4 33.2 %copy-start.4 = (bf16[8,128,256]{2,1,0:T(8,128)(2,1)}, bf16[8,128,256]{2,1,0:T(8,128)(2,1)S(1)}, u32[]{:S(2)}) copy-start(bf16[8,128,256]{2,1,0:T(8,128)(2,1)S(1)} %constant_dynamic-update-slice_fusion.4.refs_6_) | copy-start | bytes 1572868
  54.4 33.2 %copy-start.15 = (bf16[4,128,256]{2,1,0:T(8,128)(2,1)}, bf16[4,128,256]{2,1,0:T(8,128)(2,1)S(1)}, u32[]{:S(2)}) copy-start(bf16[4,128,256]{2,1,0:T(8,128)(2,1)S(1)} %collective-permute-done.1.refs_1_) | copy-start | bytes 786436
  54.4 10.6 %collective-permute-start.9 = (bf16[8,128,256]{2,1,0:T(8,128)(2,1)S(1)}, bf16[8,128,256]{2,1,0:T(8,128)(2,1)S(1)}, u32[]{:S(2)}, u32[]{:S(2)}) collective-permute-start(bf16[8,128,256]{2,1,0:T(8,128)(2,1)S(1)} %constant_dynamic-update-slice_fusion.4.refs_6_), channel_id=1, source_target_pairs={{0,2},{1,5},{2,0},{3,7},{4,6},{5,1},{6,4},{7,3},{8,10},{9,13},{10,... | collective-permute-start | bytes 1572872 | tf_op jit(solution)/shard_map/ppermute | solution.py:315
  54.5 5.3 %collective-permute-start.3 = (bf16[4,128,256]{2,1,0:T(8,128)(2,1)S(1)}, bf16[4,128,256]{2,1,0:T(8,128)(2,1)S(1)}, u32[]{:S(2)}, u32[]{:S(2)}) collective-permute-start(bf16[4,128,256]{2,1,0:T(8,128)(2,1)S(1)} %collective-permute-done.1.refs_1_), channel_id=1, source_target_pairs={{0,4},{1,3},{2,6},{3,1},{4,0},{5,7},{6,2},{7,5},{8,12},{9,11},{10,... | collective-permute-start | bytes 786440 | tf_op jit(solution)/shard_map/ppermute | solution.py:315
  55.8 10.5 %collective-permute-start.16 = (bf16[4,128,256]{2,1,0:T(8,128)(2,1)S(1)}, bf16[4,128,256]{2,1,0:T(8,128)(2,1)S(1)}, u32[]{:S(2)}, u32[]{:S(2)}) collective-permute-start(bf16[4,128,256]{2,1,0:T(8,128)(2,1)S(1)} %collective-permute-done.7), channel_id=1, source_target_pairs={{0,24},{2,26},{4,28},{6,30},{8,0},{10,2},{12,4},{14,6},{16,8},{18,... | collective-permute-start | bytes 786440 | tf_op jit(solution)/shard_map/ppermute | solution.py:303
  59.8 29.4 %copy-start.3 = (bf16[8,128,256]{2,1,0:T(8,128)(2,1)}, bf16[8,128,256]{2,1,0:T(8,128)(2,1)S(1)}, u32[]{:S(2)}) copy-start(bf16[8,128,256]{2,1,0:T(8,128)(2,1)S(1)} %constant_dynamic-update-slice_fusion.2.refs_2_) | copy-start | bytes 1572868
  59.8 16.9 %collective-permute-start.10 = (bf16[8,128,256]{2,1,0:T(8,128)(2,1)S(1)}, bf16[8,128,256]{2,1,0:T(8,128)(2,1)S(1)}, u32[]{:S(2)}, u32[]{:S(2)}) collective-permute-start(bf16[8,128,256]{2,1,0:T(8,128)(2,1)S(1)} %constant_dynamic-update-slice_fusion.2.refs_2_), channel_id=1, source_target_pairs={{0,24},{2,26},{4,28},{6,30},{8,0},{10,2},{12,4},{14,6},{16,8},{18,... | collective-permute-start | bytes 1572872 | tf_op jit(solution)/shard_map/ppermute | solution.py:303
  65.1 24.2 %copy-start.1 = (bf16[8,128,256]{2,1,0:T(8,128)(2,1)}, bf16[8,128,256]{2,1,0:T(8,128)(2,1)S(1)}, u32[]{:S(2)}) copy-start(bf16[8,128,256]{2,1,0:T(8,128)(2,1)S(1)} %collective-permute-done.9.refs_7_) | copy-start | bytes 1572868
  65.1 11.7 %collective-permute-start.11 = (bf16[8,128,256]{2,1,0:T(8,128)(2,1)S(1)}, bf16[8,128,256]{2,1,0:T(8,128)(2,1)S(1)}, u32[]{:S(2)}, u32[]{:S(2)}) collective-permute-start(bf16[8,128,256]{2,1,0:T(8,128)(2,1)S(1)} %pad_maximum_fusion), channel_id=1, source_target_pairs={{0,4},{1,3},{2,6},{3,1},{4,0},{5,7},{6,2},{7,5},{8,12},{9,11},{10,... | collective-permute-start | bytes 1572872 | tf_op jit(solution)/shard_map/ppermute | solution.py:315
  66.2 5.6 %collective-permute-start.17 = (bf16[4,128,256]{2,1,0:T(8,128)(2,1)S(1)}, bf16[4,128,256]{2,1,0:T(8,128)(2,1)S(1)}, u32[]{:S(2)}, u32[]{:S(2)}) collective-permute-start(bf16[4,128,256]{2,1,0:T(8,128)(2,1)S(1)} %collective-permute-done.16), channel_id=1, source_target_pairs={{0,2},{1,5},{2,0},{3,7},{4,6},{5,1},{6,4},{7,3},{8,10},{9,13},{10,... | collective-permute-start | bytes 786440 | tf_op jit(solution)/shard_map/ppermute | solution.py:315
  66.8 14.1 %collective-permute-start.12 = (bf16[8,128,256]{2,1,0:T(8,128)(2,1)S(1)}, bf16[8,128,256]{2,1,0:T(8,128)(2,1)S(1)}, u32[]{:S(2)}, u32[]{:S(2)}) collective-permute-start(bf16[8,128,256]{2,1,0:T(8,128)(2,1)S(1)} %constant_dynamic-update-slice_fusion.4.refs_6_), channel_id=1, source_target_pairs={{0,1},{1,0},{2,3},{3,2},{4,5},{5,4},{6,7},{7,6},{8,9},{9,8},{10,11... | collective-permute-start | bytes 1572872 | tf_op jit(solution)/shard_map/ppermute | solution.py:369
  71.9 9.2 %collective-permute-start.6 = (bf16[8,128,256]{2,1,0:T(8,128)(2,1)S(1)}, bf16[8,128,256]{2,1,0:T(8,128)(2,1)S(1)}, u32[]{:S(2)}, u32[]{:S(2)}) collective-permute-start(bf16[8,128,256]{2,1,0:T(8,128)(2,1)S(1)} %constant_dynamic-update-slice_fusion.2.refs_2_), channel_id=1, source_target_pairs={{0,1},{1,0},{2,3},{3,2},{4,5},{5,4},{6,7},{7,6},{8,9},{9,8},{10,11... | collective-permute-start | bytes 1572872 | tf_op jit(solution)/shard_map/ppermute | solution.py:369
  76.8 12.5 %copy-start.2 = (bf16[8,128,256]{2,1,0:T(8,128)(2,1)}, bf16[8,128,256]{2,1,0:T(8,128)(2,1)S(1)}, u32[]{:S(2)}) copy-start(bf16[8,128,256]{2,1,0:T(8,128)(2,1)S(1)} %constant_dynamic-update-slice_fusion.6.refs_14_) | copy-start | bytes 1572868
  76.8 10.8 %copy-start.6 = (bf16[8,128,256]{2,1,0:T(8,128)(2,1)}, bf16[8,128,256]{2,1,0:T(8,128)(2,1)S(1)}, u32[]{:S(2)}) copy-start(bf16[8,128,256]{2,1,0:T(8,128)(2,1)S(1)} %collective-permute-done.10.refs_8_) | copy-start | bytes 1572868
  76.8 10.9 %copy-start.7 = (bf16[8,128,256]{2,1,0:T(8,128)(2,1)}, bf16[8,128,256]{2,1,0:T(8,128)(2,1)S(1)}, u32[]{:S(2)}) copy-start(bf16[8,128,256]{2,1,0:T(8,128)(2,1)S(1)} %collective-permute-done.11.refs_9_) | copy-start | bytes 1572868
  76.8 8.4 %collective-permute-start.18 = (bf16[8,128,256]{2,1,0:T(8,128)(2,1)S(1)}, bf16[8,128,256]{2,1,0:T(8,128)(2,1)S(1)}, u32[]{:S(2)}, u32[]{:S(2)}) collective-permute-start(bf16[8,128,256]{2,1,0:T(8,128)(2,1)S(1)} %constant_dynamic-update-slice_fusion.6.refs_14_), channel_id=1, source_target_pairs={{0,4},{1,3},{2,6},{3,1},{4,0},{5,7},{6,2},{7,5},{8,12},{9,11},{10,... | collective-permute-start | bytes 1572872 | tf_op jit(solution)/shard_map/ppermute | solution.py:315
  77.9 2.3 %collective-permute-start.4 = (bf16[4,128,256]{2,1,0:T(8,128)(2,1)S(1)}, bf16[4,128,256]{2,1,0:T(8,128)(2,1)S(1)}, u32[]{:S(2)}, u32[]{:S(2)}) collective-permute-start(bf16[4,128,256]{2,1,0:T(8,128)(2,1)S(1)} %gather_fusion), channel_id=1, source_target_pairs={{0,1},{1,0},{2,3},{3,2},{4,5},{5,4},{6,7},{7,6},{8,9},{9,8},{10,11... | collective-permute-start | bytes 786440 | tf_op jit(solution)/shard_map/ppermute | solution.py:369
  79.0 1.5 %collective-permute-start.5 = (bf16[4,128,256]{2,1,0:T(8,128)(2,1)S(1)}, bf16[4,128,256]{2,1,0:T(8,128)(2,1)S(1)}, u32[]{:S(2)}, u32[]{:S(2)}) collective-permute-start(bf16[4,128,256]{2,1,0:T(8,128)(2,1)S(1)} %collective-permute-done.1.refs_1_), channel_id=1, source_target_pairs={{0,1},{1,0},{2,3},{3,2},{4,5},{5,4},{6,7},{7,6},{8,9},{9,8},{10,11... | collective-permute-start | bytes 786440 | tf_op jit(solution)/shard_map/ppermute | solution.py:369
  80.2 7.5 %copy-start.16 = (bf16[4,128,256]{2,1,0:T(8,128)(2,1)}, bf16[4,128,256]{2,1,0:T(8,128)(2,1)S(1)}, u32[]{:S(2)}) copy-start(bf16[4,128,256]{2,1,0:T(8,128)(2,1)S(1)} %collective-permute-done.4.refs_3_) | copy-start | bytes 786436
  80.2 7.4 %collective-permute-start.19 = (bf16[8,128,256]{2,1,0:T(8,128)(2,1)S(1)}, bf16[8,128,256]{2,1,0:T(8,128)(2,1)S(1)}, u32[]{:S(2)}, u32[]{:S(2)}) collective-permute-start(bf16[8,128,256]{2,1,0:T(8,128)(2,1)S(1)} %constant_dynamic-update-slice_fusion.6.refs_14_), channel_id=1, source_target_pairs={{0,1},{1,0},{2,3},{3,2},{4,5},{5,4},{6,7},{7,6},{8,9},{9,8},{10,11... | collective-permute-start | bytes 1572872 | tf_op jit(solution)/shard_map/ppermute | solution.py:369
  80.6 7.1 %copy-start.17 = (bf16[4,128,256]{2,1,0:T(8,128)(2,1)}, bf16[4,128,256]{2,1,0:T(8,128)(2,1)S(1)}, u32[]{:S(2)}) copy-start(bf16[4,128,256]{2,1,0:T(8,128)(2,1)S(1)} %collective-permute-done.5.refs_4_) | copy-start | bytes 786436
  80.6 7.0 %collective-permute-start.13 = (bf16[8,128,256]{2,1,0:T(8,128)(2,1)S(1)}, bf16[8,128,256]{2,1,0:T(8,128)(2,1)S(1)}, u32[]{:S(2)}, u32[]{:S(2)}) collective-permute-start(bf16[8,128,256]{2,1,0:T(8,128)(2,1)S(1)} %collective-permute-done.9.refs_7_), channel_id=1, source_target_pairs={{0,1},{1,0},{2,3},{3,2},{4,5},{5,4},{6,7},{7,6},{8,9},{9,8},{10,11... | collective-permute-start | bytes 1572872 | tf_op jit(solution)/shard_map/ppermute | solution.py:369
  80.9 6.8 %copy-start.8 = (bf16[8,128,256]{2,1,0:T(8,128)(2,1)}, bf16[8,128,256]{2,1,0:T(8,128)(2,1)S(1)}, u32[]{:S(2)}) copy-start(bf16[8,128,256]{2,1,0:T(8,128)(2,1)S(1)} %collective-permute-done.12.refs_10_) | copy-start | bytes 1572868
  81.0 6.7 %collective-permute-start.14 = (bf16[8,128,256]{2,1,0:T(8,128)(2,1)S(1)}, bf16[8,128,256]{2,1,0:T(8,128)(2,1)S(1)}, u32[]{:S(2)}, u32[]{:S(2)}) collective-permute-start(bf16[8,128,256]{2,1,0:T(8,128)(2,1)S(1)} %collective-permute-done.10.refs_8_), channel_id=1, source_target_pairs={{0,1},{1,0},{2,3},{3,2},{4,5},{5,4},{6,7},{7,6},{8,9},{9,8},{10,11... | collective-permute-start | bytes 1572872 | tf_op jit(solution)/shard_map/ppermute | solution.py:369
  81.1 6.6 %copy-start.9 = (bf16[8,128,256]{2,1,0:T(8,128)(2,1)}, bf16[8,128,256]{2,1,0:T(8,128)(2,1)S(1)}, u32[]{:S(2)}) copy-start(bf16[8,128,256]{2,1,0:T(8,128)(2,1)S(1)} %collective-permute-done.6.refs_5_) | copy-start | bytes 1572868
  81.1 6.6 %collective-permute-start.15 = (bf16[8,128,256]{2,1,0:T(8,128)(2,1)S(1)}, bf16[8,128,256]{2,1,0:T(8,128)(2,1)S(1)}, u32[]{:S(2)}, u32[]{:S(2)}) collective-permute-start(bf16[8,128,256]{2,1,0:T(8,128)(2,1)S(1)} %collective-permute-done.11.refs_9_), channel_id=1, source_target_pairs={{0,1},{1,0},{2,3},{3,2},{4,5},{5,4},{6,7},{7,6},{8,9},{9,8},{10,11... | collective-permute-start | bytes 1572872 | tf_op jit(solution)/shard_map/ppermute | solution.py:369
  85.2 2.5 %copy-start.10 = (bf16[8,128,256]{2,1,0:T(8,128)(2,1)}, bf16[8,128,256]{2,1,0:T(8,128)(2,1)S(1)}, u32[]{:S(2)}) copy-start(bf16[8,128,256]{2,1,0:T(8,128)(2,1)S(1)} %collective-permute-done.18.refs_15_) | copy-start | bytes 1572868
  85.2 4.0 %collective-permute-start.20 = (bf16[8,128,256]{2,1,0:T(8,128)(2,1)S(1)}, bf16[8,128,256]{2,1,0:T(8,128)(2,1)}, u32[]{:S(2)}, u32[]{:S(2)}) collective-permute-start(bf16[8,128,256]{2,1,0:T(8,128)(2,1)S(1)} %collective-permute-done.18.refs_15_), channel_id=1, source_target_pairs={{0,1},{1,0},{2,3},{3,2},{4,5},{5,4},{6,7},{7,6},{8,9},{9,8},{10,11... | collective-permute-start | bytes 1572872 | tf_op jit(solution)/shard_map/ppermute | solution.py:369
  87.6 1.7 %copy-start.12 = (bf16[8,128,256]{2,1,0:T(8,128)(2,1)}, bf16[8,128,256]{2,1,0:T(8,128)(2,1)S(1)}, u32[]{:S(2)}) copy-start(bf16[8,128,256]{2,1,0:T(8,128)(2,1)S(1)} %collective-permute-done.13.refs_11_) | copy-start | bytes 1572868
  87.6 1.7 %copy-start.11 = (bf16[8,128,256]{2,1,0:T(8,128)(2,1)}, bf16[8,128,256]{2,1,0:T(8,128)(2,1)S(1)}, u32[]{:S(2)}) copy-start(bf16[8,128,256]{2,1,0:T(8,128)(2,1)S(1)} %collective-permute-done.19.refs_16_) | copy-start | bytes 1572868
  87.6 1.6 %copy-start.13 = (bf16[8,128,256]{2,1,0:T(8,128)(2,1)}, bf16[8,128,256]{2,1,0:T(8,128)(2,1)S(1)}, u32[]{:S(2)}) copy-start(bf16[8,128,256]{2,1,0:T(8,128)(2,1)S(1)} %collective-permute-done.14.refs_12_) | copy-start | bytes 1572868
  87.7 1.6 %copy-start.14 = (bf16[8,128,256]{2,1,0:T(8,128)(2,1)}, bf16[8,128,256]{2,1,0:T(8,128)(2,1)S(1)}, u32[]{:S(2)}) copy-start(bf16[8,128,256]{2,1,0:T(8,128)(2,1)S(1)} %collective-permute-done.15.refs_13_) | copy-start | bytes 1572868

commit v10 on v9

--- a/solution.py
+++ b/solution.py
@@ -335,16 +335,15 @@
     one, three = move(shard, RING[1]), move(shard, RING[3])
     came, turned = cross(shard, 0), cross(shard, 1)
     second = jnp.concatenate([turned, cross(came, 1)])
-    near = jnp.concatenate([one, three])
     far = move(one, RING[1])
     one_second = move(second, RING[1])
-    near_came = cross(tie(near, (came, turned)), 0)
-    each = shard.shape[0]
-    three_second = cross(jnp.concatenate([three, near_came[each:]]), 1)
+    near_one = cross(tie(one, (came, turned)), 0)
+    near_three = cross(tie(three, (came, turned)), 0)
+    three_second = cross(jnp.concatenate([three, near_three]), 1)
     far_pair = jnp.concatenate([far, cross(far, 0)])
     return (
         [shard, came, second],
-        [near, near_came, one_second, three_second],
+        [one, three, near_one, near_three, one_second, three_second],
         [far_pair, cross(tie(far_pair, (one_second, three_second)), 1)],
         lists,
     )

time: 99.1 us -> 97 us (0.979)
  starting transfers between devices: 39 us -> 31.4 us
  waiting for transfers between devices: 33.3 us -> 38.9 us
    ppermute x4, starting transfers between devices: 10.8 us -> 5.1 us  [move(): return lax.ppermute(value, 'dom', pairs)]
    ppermute x4, waiting for transfers between devices: 9.81 us -> 14.5 us  [move(): return lax.ppermute(value, 'dom', pairs)]
    all_to_all x1, waiting for transfers between devices: 12.9 us -> 10.1 us  [gather_small(): landed = lax.all_to_all(rows, 'dom', 0, 0, tiled=True)]
    ppermute x11 -> x13, waiting for transfers between devices: 3.34 us -> 5.49 us  [exchange(): return lax.ppermute(value, 'rep', swap)]
    ppermute x7 -> x8, waiting for transfers between devices: 7.29 us -> 8.72 us  [cross(): return lax.ppermute(value, ('dom', 'rep'), pairs)]
    ppermute x11 -> x13, starting transfers between devices: 14.3 us -> 13.2 us  [exchange(): return lax.ppermute(value, 'rep', swap)]
    ppermute x7 -> x8, starting transfers between devices: 6.32 us -> 5.39 us  [cross(): return lax.ppermute(value, ('dom', 'rep'), pairs)]
  transfers between devices with their start and end apart: 23 -> 26, of which waited for: 9 -> 14; matrix products, arithmetic and copies ran while one was open for 1% -> 1% of each run, Pallas kernels for 7% -> 7%
where the time goes in v10:
time: 97 us; the launch traced here: 96 us
  waiting for transfers between devices  38.9 us (40%)
  starting transfers between devices  31.4 us (32%)
  Pallas kernels  23.8 us (25%)
  local copies, waits for them, and re-layouts  1.58 us (2%)
    ppermute x4, waiting for transfers between devices, move(): return lax.ppermute(value, 'dom', pairs)  14.5 us
    ppermute x13, starting transfers between devices, exchange(): return lax.ppermute(value, 'rep', swap)  13.2 us
    all_to_all x1, waiting for transfers between devices, gather_small(): landed = lax.all_to_all(rows, 'dom', 0, 0, tiled=True)  10.1 us
    ppermute x8, waiting for transfers between devices, cross(): return lax.ppermute(value, ('dom', 'rep'), pairs)  8.72 us
    pallas_call x1, Pallas kernels, products_in_phases(): pl.pallas_call(functools.partial(phased_kernel, places), out_shape=jax.Sh...  8.7 us
    pallas_call x1, Pallas kernels, pick_share(): pl.pallas_call(pick_kernel, out_shape=jax.ShapeDtypeStruct((share, tile_l...  8.3 us
    all_to_all x1, starting transfers between devices, gather_small(): landed = lax.all_to_all(rows, 'dom', 0, 0, tiled=True)  7.69 us
    pallas_call x1, Pallas kernels, product_lists(): pl.pallas_call(functools.partial(lists_kernel, n_blocks), out_shape=jax.S...  6.8 us
  transfers between devices with their start and end apart: 26, of which 14 were waited for; matrix products, arithmetic and copies ran while one was open for 1% of the time, Pallas kernels for 7%

profile of v10, /device:TPU:1, one launch (start us, length us, event | category | flops | bytes accessed | tf_op | source)
XLA Modules:
  0.0 96.0 jit_solution(11459649509082433234)
XLA Ops:
  0.0 8.3 %shard_map.82 = bf16[16,128,256]{2,1,0:T(8,128)(2,1)} custom-call(s32[4]{0:T(128)} %owner_ref.1, s32[4,32]{1,0:T(4,128)} %blocks_ref.1, s32[64,1,128]{2,1,0:T(1,128)} %bitcast.5, bf16[8192,256]{1,0:T(8,128)(2,1)} %features_ref.1), custom_call_target="tpu_custom_call" | custom-call | tf_op jit(solution)/shard_map/pallas_call | solution.py:273
  8.3 0.0 copy-start
  8.3 0.0 copy-start.23
  8.3 0.0 copy-start.24
  8.4 7.7 %all-to-all-start = ((bf16[16,128,256]{2,1,0:T(8,128)(2,1)}), bf16[16,128,256]{2,1,0:T(8,128)(2,1)S(1)}, u32[]{:S(2)}, u32[]{:S(2)}) async-start(bf16[16,128,256]{2,1,0:T(8,128)(2,1)} %shard_map.82), calls=%async_computation | async-start | bytes 2097152 | tf_op jit(solution)/shard_map/all_to_all | solution.py:332
  16.1 1.0 %collective-permute-start.24 = (bf16[64,128,128]{2,1,0:T(8,128)(2,1)S(1)}, bf16[64,128,128]{2,1,0:T(8,128)(2,1)}, u32[]{:S(2)}, u32[]{:S(2)}) collective-permute-start(bf16[64,128,128]{2,1,0:T(8,128)(2,1)S(1)} %bitcast.4), channel_id=1, source_target_pairs={{0,1},{1,0},{2,3},{3,2},{4,5},{5,4},{6,7},{7,6},{8,9},{9,8},{10,11... | collective-permute-start | bytes 6291464 | tf_op jit(solution)/shard_map/ppermute | solution.py:368
  17.1 0.0 copy-done.22
  17.1 0.1 collective-permute-start
  17.2 3.5 %collective-permute-done.other_ref = s32[2,4,16]{2,1,0:T(4,128)S(1)} collective-permute-done((s32[2,4,16]{2,1,0:T(4,128)S(1)}, s32[2,4,16]{2,1,0:T(4,128)S(1)}, u32[]{:S(2)}, u32[]{:S(2)}) %collective-permute-start) | collective-permute-done | bytes 544 | tf_op jit(solution)/shard_map/ppermute | solution.py:368
  20.7 0.6 copy-done.21
  21.3 6.8 %shard_map.83.lists = s32[4,408]{1,0:T(4,128)} custom-call(s32[2,4,16]{2,1,0:T(4,128)} %copy-done.20, s32[2,4,16]{2,1,0:T(4,128)} %copy-done.21), custom_call_target="tpu_custom_call" | custom-call | tf_op jit(solution)/shard_map/pallas_call | solution.py:220
  28.1 10.1 %all-to-all-done = bf16[16,128,256]{2,1,0:T(8,128)(2,1)S(1)} async-done(((bf16[16,128,256]{2,1,0:T(8,128)(2,1)}), bf16[16,128,256]{2,1,0:T(8,128)(2,1)S(1)}, u32[]{:S(2)}, u32[]{:S(2)}) %all-to-all-start) | async-done | bytes 1048608 | tf_op jit(solution)/shard_map/all_to_all | solution.py:332
  38.2 0.6 gather_fusion
  38.8 2.2 %collective-permute-start.1 = (bf16[4,128,256]{2,1,0:T(8,128)(2,1)S(1)}, bf16[4,128,256]{2,1,0:T(8,128)(2,1)S(1)}, u32[]{:S(2)}, u32[]{:S(2)}) collective-permute-start(bf16[4,128,256]{2,1,0:T(8,128)(2,1)S(1)} %gather_fusion), channel_id=1, source_target_pairs={{0,2},{1,5},{2,0},{3,7},{4,6},{5,1},{6,4},{7,3},{8,10},{9,13},{10,... | collective-permute-start | bytes 786440 | tf_op jit(solution)/shard_map/ppermute | solution.py:315
  41.0 3.1 %collective-permute-start.8 = (bf16[4,128,256]{2,1,0:T(8,128)(2,1)S(1)}, bf16[4,128,256]{2,1,0:T(8,128)(2,1)S(1)}, u32[]{:S(2)}, u32[]{:S(2)}) collective-permute-start(bf16[4,128,256]{2,1,0:T(8,128)(2,1)S(1)} %gather_fusion), channel_id=1, source_target_pairs={{0,8},{2,10},{4,12},{6,14},{8,16},{10,18},{12,20},{14,22},{16,24},... | collective-permute-start | bytes 786440 | tf_op jit(solution)/shard_map/ppermute | solution.py:303
  44.1 0.3 collective-permute-start.2
  44.4 0.3 collective-permute-start.7
  44.7 0.1 collective-permute-done.1.refs_1_
  44.7 1.1 %collective-permute-start.3 = (bf16[4,128,256]{2,1,0:T(8,128)(2,1)S(1)}, bf16[4,128,256]{2,1,0:T(8,128)(2,1)S(1)}, u32[]{:S(2)}, u32[]{:S(2)}) collective-permute-start(bf16[4,128,256]{2,1,0:T(8,128)(2,1)S(1)} %collective-permute-done.1.refs_1_), channel_id=1, source_target_pairs={{0,4},{1,3},{2,6},{3,1},{4,0},{5,7},{6,2},{7,5},{8,12},{9,11},{10,... | collective-permute-start | bytes 786440 | tf_op jit(solution)/shard_map/ppermute | solution.py:315
  45.9 3.4 %collective-permute-done.8.refs_7_ = bf16[4,128,256]{2,1,0:T(8,128)(2,1)S(1)} collective-permute-done((bf16[4,128,256]{2,1,0:T(8,128)(2,1)S(1)}, bf16[4,128,256]{2,1,0:T(8,128)(2,1)S(1)}, u32[]{:S(2)}, u32[]{:S(2)}) %collective-permute-start.8) | collective-permute-done | bytes 262176 | tf_op jit(solution)/shard_map/ppermute | solution.py:303
  49.2 1.6 %collective-permute-done.2 = bf16[4,128,256]{2,1,0:T(8,128)(2,1)S(1)} collective-permute-done((bf16[4,128,256]{2,1,0:T(8,128)(2,1)S(1)}, bf16[4,128,256]{2,1,0:T(8,128)(2,1)S(1)}, u32[]{:S(2)}, u32[]{:S(2)}) %collective-permute-start.2) | collective-permute-done | bytes 262176 | tf_op jit(solution)/shard_map/ppermute | solution.py:315
  50.9 1.5 %collective-permute-start.10 = (bf16[4,128,256]{2,1,0:T(8,128)(2,1)S(1)}, bf16[4,128,256]{2,1,0:T(8,128)(2,1)S(1)}, u32[]{:S(2)}, u32[]{:S(2)}) collective-permute-start(bf16[4,128,256]{2,1,0:T(8,128)(2,1)S(1)} %collective-permute-done.8.refs_7_), channel_id=1, source_target_pairs={{0,2},{1,5},{2,0},{3,7},{4,6},{5,1},{6,4},{7,3},{8,10},{9,13},{10,... | collective-permute-start | bytes 786440 | tf_op jit(solution)/shard_map/ppermute | solution.py:315
  52.4 4.0 %collective-permute-done.7.refs_6_ = bf16[4,128,256]{2,1,0:T(8,128)(2,1)S(1)} collective-permute-done((bf16[4,128,256]{2,1,0:T(8,128)(2,1)S(1)}, bf16[4,128,256]{2,1,0:T(8,128)(2,1)S(1)}, u32[]{:S(2)}, u32[]{:S(2)}) %collective-permute-start.7) | collective-permute-done | bytes 262176 | tf_op jit(solution)/shard_map/ppermute | solution.py:303
  56.4 1.6 %collective-permute-start.19 = (bf16[4,128,256]{2,1,0:T(8,128)(2,1)S(1)}, bf16[4,128,256]{2,1,0:T(8,128)(2,1)S(1)}, u32[]{:S(2)}, u32[]{:S(2)}) collective-permute-start(bf16[4,128,256]{2,1,0:T(8,128)(2,1)S(1)} %collective-permute-done.7.refs_6_), channel_id=1, source_target_pairs={{0,24},{2,26},{4,28},{6,30},{8,0},{10,2},{12,4},{14,6},{16,8},{18,... | collective-permute-start | bytes 786440 | tf_op jit(solution)/shard_map/ppermute | solution.py:303
  58.0 0.0 collective-permute-done.3
  58.0 0.1 collective-permute-start.11
  58.1 0.4 collective-permute-done.10.refs_9_
  58.5 0.3 collective-permute-start.12
  58.9 4.4 %collective-permute-done.19 = bf16[4,128,256]{2,1,0:T(8,128)(2,1)S(1)} collective-permute-done((bf16[4,128,256]{2,1,0:T(8,128)(2,1)S(1)}, bf16[4,128,256]{2,1,0:T(8,128)(2,1)S(1)}, u32[]{:S(2)}, u32[]{:S(2)}) %collective-permute-start.19) | collective-permute-done | bytes 262176 | tf_op jit(solution)/shard_map/ppermute | solution.py:303
  63.2 0.0 collective-permute-start.20
  63.2 4.6 %collective-permute-start.4 = (bf16[4,128,256]{2,1,0:T(8,128)(2,1)S(1)}, bf16[4,128,256]{2,1,0:T(8,128)(2,1)S(1)}, u32[]{:S(2)}, u32[]{:S(2)}) collective-permute-start(bf16[4,128,256]{2,1,0:T(8,128)(2,1)S(1)} %gather_fusion), channel_id=1, source_target_pairs={{0,1},{1,0},{2,3},{3,2},{4,5},{5,4},{6,7},{7,6},{8,9},{9,8},{10,11... | collective-permute-start | bytes 786440 | tf_op jit(solution)/shard_map/ppermute | solution.py:368
  67.8 3.8 %collective-permute-done.20 = bf16[4,128,256]{2,1,0:T(8,128)(2,1)S(1)} collective-permute-done((bf16[4,128,256]{2,1,0:T(8,128)(2,1)S(1)}, bf16[4,128,256]{2,1,0:T(8,128)(2,1)S(1)}, u32[]{:S(2)}, u32[]{:S(2)}) %collective-permute-start.20) | collective-permute-done | bytes 262176 | tf_op jit(solution)/shard_map/ppermute | solution.py:315
  71.6 0.0 collective-permute-start.9
  71.7 2.8 %collective-permute-done.11.refs_10_ = bf16[8,128,256]{2,1,0:T(8,128)(2,1)S(1)} collective-permute-done((bf16[8,128,256]{2,1,0:T(8,128)(2,1)S(1)}, bf16[8,128,256]{2,1,0:T(8,128)(2,1)S(1)}, u32[]{:S(2)}, u32[]{:S(2)}) %collective-permute-start.11) | collective-permute-done | bytes 524320 | tf_op jit(solution)/shard_map/ppermute | solution.py:303
  74.5 1.8 %collective-permute-start.14 = (bf16[4,128,256]{2,1,0:T(8,128)(2,1)S(1)}, bf16[4,128,256]{2,1,0:T(8,128)(2,1)S(1)}, u32[]{:S(2)}, u32[]{:S(2)}) collective-permute-start(bf16[4,128,256]{2,1,0:T(8,128)(2,1)S(1)} %collective-permute-done.8.refs_7_), channel_id=1, source_target_pairs={{0,1},{1,0},{2,3},{3,2},{4,5},{5,4},{6,7},{7,6},{8,9},{9,8},{10,11... | collective-permute-start | bytes 786440 | tf_op jit(solution)/shard_map/ppermute | solution.py:368
  76.3 0.0 collective-permute-done.12.refs_11_
  76.3 0.0 collective-permute-start.21
  76.3 0.0 collective-permute-done.24.refs_23_
  76.3 0.2 collective-permute-start.13
  76.5 0.0 collective-permute-done.4.refs_3_
  76.5 0.4 collective-permute-start.5
  76.9 0.2 collective-permute-done.9.refs_8_
  77.2 3.4 %collective-permute-start.15 = (bf16[4,128,256]{2,1,0:T(8,128)(2,1)S(1)}, bf16[4,128,256]{2,1,0:T(8,128)(2,1)}, u32[]{:S(2)}, u32[]{:S(2)}) collective-permute-start(bf16[4,128,256]{2,1,0:T(8,128)(2,1)S(1)} %collective-permute-done.9.refs_8_), channel_id=1, source_target_pairs={{0,1},{1,0},{2,3},{3,2},{4,5},{5,4},{6,7},{7,6},{8,9},{9,8},{10,11... | collective-permute-start | bytes 786440 | tf_op jit(solution)/shard_map/ppermute | solution.py:368
  80.5 0.0 collective-permute-done.14.refs_13_
  80.5 0.1 collective-permute-start.16
  80.6 0.0 collective-permute-done.13.refs_12_
  80.6 0.4 collective-permute-start.6
  81.0 0.0 collective-permute-done.5.refs_4_
  81.0 0.1 collective-permute-start.22
  81.1 0.7 collective-permute-done.15.refs_14_
  81.8 0.4 collective-permute-start.17
  82.2 0.0 collective-permute-done.16.refs_15_
  82.2 0.4 collective-permute-start.18
  82.6 2.6 %collective-permute-done.21.refs_19_ = bf16[8,128,256]{2,1,0:T(8,128)(2,1)S(1)} collective-permute-done((bf16[8,128,256]{2,1,0:T(8,128)(2,1)S(1)}, bf16[8,128,256]{2,1,0:T(8,128)(2,1)S(1)}, u32[]{:S(2)}, u32[]{:S(2)}) %collective-permute-start.21) | collective-permute-done | bytes 524320 | tf_op jit(solution)/shard_map/ppermute | solution.py:315
  85.2 0.4 collective-permute-start.23
  85.6 0.0 collective-permute-done.6.refs_5_
  85.6 0.0 collective-permute-done.22.refs_20_
  85.6 0.0 collective-permute-done.17.refs_16_
  85.6 0.0 collective-permute-done.18.refs_17_
  85.7 0.0 copy-done.13
  85.7 0.0 copy-done.14
  85.7 0.3 copy-done.8
  86.0 1.3 %collective-permute-done.23.refs_21_ = bf16[8,128,256]{2,1,0:T(8,128)(2,1)} collective-permute-done((bf16[8,128,256]{2,1,0:T(8,128)(2,1)S(1)}, bf16[8,128,256]{2,1,0:T(8,128)(2,1)}, u32[]{:S(2)}, u32[]{:S(2)}) %collective-permute-start.23) | collective-permute-done | bytes 524320 | tf_op jit(solution)/shard_map/ppermute | solution.py:368
  87.3 8.7 %shard_map.84 = bf16[32,128,256]{2,1,0:T(8,128)(2,1)} custom-call(s32[4,408]{1,0:T(4,128)} %shard_map.83.lists, bf16[4,128,256]{2,1,0:T(8,128)(2,1)} %copy-done.3, bf16[4,128,256]{2,1,0:T(8,128)(2,1)} %copy-done.13, bf16[8,128,256]{2,1,0:T(8,128)(2,1)} %copy-done.2, bf16[4,128,256]{2,1,0:T(8,128)(2,1)} %copy-done.15, bf16[4,128,256]{2,1,0:T(8,128)(2,1)} %copy-done.19, ...), custom_call_target="tpu_custom_call" | custom-call | flops 1073741824 | bytes 16777216 | tf_op jit(solution)/shard_map/pallas_call | solution.py:201
  (51 shorter events, 0.2 us)
Async XLA Ops:
  0.0 17.1 %copy-start.22 = (s32[1,4,16]{2,1,0:T(4,128)S(1)}, s32[1,4,16]{2,1,0:T(4,128)}, u32[]{:S(2)}) copy-start(s32[1,4,16]{2,1,0:T(4,128)} %param.12) | copy-start | bytes 772
  8.3 7.7 %copy-start = (bf16[1,4,16,128,128]{4,3,2,1,0:T(8,128)(2,1)S(1)}, bf16[1,4,16,128,128]{4,3,2,1,0:T(8,128)(2,1)}, u32[]{:S(2)}) copy-start(bf16[1,4,16,128,128]{4,3,2,1,0:T(8,128)(2,1)} %param.14) | copy-start | bytes 6291460
  8.3 8.8 %copy-start.23 = (s32[1,4,16]{2,1,0:T(4,128)S(1)}, s32[1,4,16]{2,1,0:T(4,128)}, u32[]{:S(2)}) copy-start(s32[1,4,16]{2,1,0:T(4,128)} %param.13) | copy-start | bytes 772
  8.3 8.9 %copy-start.24 = (s32[4]{0:T(128)S(1)}, s32[4]{0:T(128)}, u32[]{:S(2)}) copy-start(s32[4]{0:T(128)} %owner_ref.1) | copy-start | bytes 52
  8.4 29.9 %all-to-all-start = ((bf16[16,128,256]{2,1,0:T(8,128)(2,1)}), bf16[16,128,256]{2,1,0:T(8,128)(2,1)S(1)}, u32[]{:S(2)}, u32[]{:S(2)}) async-start(bf16[16,128,256]{2,1,0:T(8,128)(2,1)} %shard_map.82), calls=%async_computation | async-start | bytes 2097152 | tf_op jit(solution)/shard_map/all_to_all | solution.py:332
  16.1 60.3 %collective-permute-start.24 = (bf16[64,128,128]{2,1,0:T(8,128)(2,1)S(1)}, bf16[64,128,128]{2,1,0:T(8,128)(2,1)}, u32[]{:S(2)}, u32[]{:S(2)}) collective-permute-start(bf16[64,128,128]{2,1,0:T(8,128)(2,1)S(1)} %bitcast.4), channel_id=1, source_target_pairs={{0,1},{1,0},{2,3},{3,2},{4,5},{5,4},{6,7},{7,6},{8,9},{9,8},{10,11... | collective-permute-start | bytes 6291464 | tf_op jit(solution)/shard_map/ppermute | solution.py:368
  17.1 3.6 %copy-start.20 = (s32[2,4,16]{2,1,0:T(4,128)}, s32[2,4,16]{2,1,0:T(4,128)S(1)}, u32[]{:S(2)}) copy-start(s32[2,4,16]{2,1,0:T(4,128)S(1)} %constant_dynamic-update-slice_fusion.own_ref) | copy-start | bytes 1540
  17.1 3.6 %collective-permute-start = (s32[2,4,16]{2,1,0:T(4,128)S(1)}, s32[2,4,16]{2,1,0:T(4,128)S(1)}, u32[]{:S(2)}, u32[]{:S(2)}) collective-permute-start(s32[2,4,16]{2,1,0:T(4,128)S(1)} %constant_dynamic-update-slice_fusion.own_ref), channel_id=1, source_target_pairs={{0,1},{1,0},{2,3},{3,2},{4,5},{5,4},{6,7},{7,6},{8,9},{9,8},{10,11... | collective-permute-start | bytes 1544 | tf_op jit(solution)/shard_map/ppermute | solution.py:368
  20.7 0.6 copy-start.21
  38.8 48.4 %copy-start.3 = (bf16[4,128,256]{2,1,0:T(8,128)(2,1)}, bf16[4,128,256]{2,1,0:T(8,128)(2,1)S(1)}, u32[]{:S(2)}) copy-start(bf16[4,128,256]{2,1,0:T(8,128)(2,1)S(1)} %gather_fusion) | copy-start | bytes 786436
  38.8 5.9 %collective-permute-start.1 = (bf16[4,128,256]{2,1,0:T(8,128)(2,1)S(1)}, bf16[4,128,256]{2,1,0:T(8,128)(2,1)S(1)}, u32[]{:S(2)}, u32[]{:S(2)}) collective-permute-start(bf16[4,128,256]{2,1,0:T(8,128)(2,1)S(1)} %gather_fusion), channel_id=1, source_target_pairs={{0,2},{1,5},{2,0},{3,7},{4,6},{5,1},{6,4},{7,3},{8,10},{9,13},{10,... | collective-permute-start | bytes 786440 | tf_op jit(solution)/shard_map/ppermute | solution.py:315
  41.0 8.3 %collective-permute-start.8 = (bf16[4,128,256]{2,1,0:T(8,128)(2,1)S(1)}, bf16[4,128,256]{2,1,0:T(8,128)(2,1)S(1)}, u32[]{:S(2)}, u32[]{:S(2)}) collective-permute-start(bf16[4,128,256]{2,1,0:T(8,128)(2,1)S(1)} %gather_fusion), channel_id=1, source_target_pairs={{0,8},{2,10},{4,12},{6,14},{8,16},{10,18},{12,20},{14,22},{16,24},... | collective-permute-start | bytes 786440 | tf_op jit(solution)/shard_map/ppermute | solution.py:303
  44.1 6.8 %collective-permute-start.2 = (bf16[4,128,256]{2,1,0:T(8,128)(2,1)S(1)}, bf16[4,128,256]{2,1,0:T(8,128)(2,1)S(1)}, u32[]{:S(2)}, u32[]{:S(2)}) collective-permute-start(bf16[4,128,256]{2,1,0:T(8,128)(2,1)S(1)} %gather_fusion), channel_id=1, source_target_pairs={{0,4},{1,3},{2,6},{3,1},{4,0},{5,7},{6,2},{7,5},{8,12},{9,11},{10,... | collective-permute-start | bytes 786440 | tf_op jit(solution)/shard_map/ppermute | solution.py:315
  44.4 12.0 %collective-permute-start.7 = (bf16[4,128,256]{2,1,0:T(8,128)(2,1)S(1)}, bf16[4,128,256]{2,1,0:T(8,128)(2,1)S(1)}, u32[]{:S(2)}, u32[]{:S(2)}) collective-permute-start(bf16[4,128,256]{2,1,0:T(8,128)(2,1)S(1)} %gather_fusion), channel_id=1, source_target_pairs={{0,24},{2,26},{4,28},{6,30},{8,0},{10,2},{12,4},{14,6},{16,8},{18,... | collective-permute-start | bytes 786440 | tf_op jit(solution)/shard_map/ppermute | solution.py:303
  44.7 40.9 %copy-start.13 = (bf16[4,128,256]{2,1,0:T(8,128)(2,1)}, bf16[4,128,256]{2,1,0:T(8,128)(2,1)S(1)}, u32[]{:S(2)}) copy-start(bf16[4,128,256]{2,1,0:T(8,128)(2,1)S(1)} %collective-permute-done.1.refs_1_) | copy-start | bytes 786436
  44.7 13.2 %collective-permute-start.3 = (bf16[4,128,256]{2,1,0:T(8,128)(2,1)S(1)}, bf16[4,128,256]{2,1,0:T(8,128)(2,1)S(1)}, u32[]{:S(2)}, u32[]{:S(2)}) collective-permute-start(bf16[4,128,256]{2,1,0:T(8,128)(2,1)S(1)} %collective-permute-done.1.refs_1_), channel_id=1, source_target_pairs={{0,4},{1,3},{2,6},{3,1},{4,0},{5,7},{6,2},{7,5},{8,12},{9,11},{10,... | collective-permute-start | bytes 786440 | tf_op jit(solution)/shard_map/ppermute | solution.py:315
  49.2 38.0 %copy-start.4 = (bf16[4,128,256]{2,1,0:T(8,128)(2,1)}, bf16[4,128,256]{2,1,0:T(8,128)(2,1)S(1)}, u32[]{:S(2)}) copy-start(bf16[4,128,256]{2,1,0:T(8,128)(2,1)S(1)} %collective-permute-done.8.refs_7_) | copy-start | bytes 786436
  50.9 7.6 %collective-permute-start.10 = (bf16[4,128,256]{2,1,0:T(8,128)(2,1)S(1)}, bf16[4,128,256]{2,1,0:T(8,128)(2,1)S(1)}, u32[]{:S(2)}, u32[]{:S(2)}) collective-permute-start(bf16[4,128,256]{2,1,0:T(8,128)(2,1)S(1)} %collective-permute-done.8.refs_7_), channel_id=1, source_target_pairs={{0,2},{1,5},{2,0},{3,7},{4,6},{5,1},{6,4},{7,3},{8,10},{9,13},{10,... | collective-permute-start | bytes 786440 | tf_op jit(solution)/shard_map/ppermute | solution.py:315
  56.3 29.3 %copy-start.14 = (bf16[4,128,256]{2,1,0:T(8,128)(2,1)}, bf16[4,128,256]{2,1,0:T(8,128)(2,1)S(1)}, u32[]{:S(2)}) copy-start(bf16[4,128,256]{2,1,0:T(8,128)(2,1)S(1)} %collective-permute-done.7.refs_6_) | copy-start | bytes 786436
  56.4 6.9 %collective-permute-start.19 = (bf16[4,128,256]{2,1,0:T(8,128)(2,1)S(1)}, bf16[4,128,256]{2,1,0:T(8,128)(2,1)S(1)}, u32[]{:S(2)}, u32[]{:S(2)}) collective-permute-start(bf16[4,128,256]{2,1,0:T(8,128)(2,1)S(1)} %collective-permute-done.7.refs_6_), channel_id=1, source_target_pairs={{0,24},{2,26},{4,28},{6,30},{8,0},{10,2},{12,4},{14,6},{16,8},{18,... | collective-permute-start | bytes 786440 | tf_op jit(solution)/shard_map/ppermute | solution.py:303
  58.0 29.2 %copy-start.2 = (bf16[8,128,256]{2,1,0:T(8,128)(2,1)}, bf16[8,128,256]{2,1,0:T(8,128)(2,1)S(1)}, u32[]{:S(2)}) copy-start(bf16[8,128,256]{2,1,0:T(8,128)(2,1)S(1)} %constant_dynamic-update-slice_fusion.2.refs_2_) | copy-start | bytes 1572868
  58.0 16.4 %collective-permute-start.11 = (bf16[8,128,256]{2,1,0:T(8,128)(2,1)S(1)}, bf16[8,128,256]{2,1,0:T(8,128)(2,1)S(1)}, u32[]{:S(2)}, u32[]{:S(2)}) collective-permute-start(bf16[8,128,256]{2,1,0:T(8,128)(2,1)S(1)} %constant_dynamic-update-slice_fusion.2.refs_2_), channel_id=1, source_target_pairs={{0,24},{2,26},{4,28},{6,30},{8,0},{10,2},{12,4},{14,6},{16,8},{18,... | collective-permute-start | bytes 1572872 | tf_op jit(solution)/shard_map/ppermute | solution.py:303
  58.5 28.8 %copy-start.5 = (bf16[4,128,256]{2,1,0:T(8,128)(2,1)}, bf16[4,128,256]{2,1,0:T(8,128)(2,1)S(1)}, u32[]{:S(2)}) copy-start(bf16[4,128,256]{2,1,0:T(8,128)(2,1)S(1)} %collective-permute-done.10.refs_9_) | copy-start | bytes 786436
  58.5 17.8 %collective-permute-start.12 = (bf16[8,128,256]{2,1,0:T(8,128)(2,1)S(1)}, bf16[8,128,256]{2,1,0:T(8,128)(2,1)S(1)}, u32[]{:S(2)}, u32[]{:S(2)}) collective-permute-start(bf16[8,128,256]{2,1,0:T(8,128)(2,1)S(1)} %pad_maximum_fusion), channel_id=1, source_target_pairs={{0,4},{1,3},{2,6},{3,1},{4,0},{5,7},{6,2},{7,5},{8,12},{9,11},{10,... | collective-permute-start | bytes 1572872 | tf_op jit(solution)/shard_map/ppermute | solution.py:315
  63.2 8.4 %collective-permute-start.20 = (bf16[4,128,256]{2,1,0:T(8,128)(2,1)S(1)}, bf16[4,128,256]{2,1,0:T(8,128)(2,1)S(1)}, u32[]{:S(2)}, u32[]{:S(2)}) collective-permute-start(bf16[4,128,256]{2,1,0:T(8,128)(2,1)S(1)} %collective-permute-done.19), channel_id=1, source_target_pairs={{0,2},{1,5},{2,0},{3,7},{4,6},{5,1},{6,4},{7,3},{8,10},{9,13},{10,... | collective-permute-start | bytes 786440 | tf_op jit(solution)/shard_map/ppermute | solution.py:315
  63.2 13.2 %collective-permute-start.4 = (bf16[4,128,256]{2,1,0:T(8,128)(2,1)S(1)}, bf16[4,128,256]{2,1,0:T(8,128)(2,1)S(1)}, u32[]{:S(2)}, u32[]{:S(2)}) collective-permute-start(bf16[4,128,256]{2,1,0:T(8,128)(2,1)S(1)} %gather_fusion), channel_id=1, source_target_pairs={{0,1},{1,0},{2,3},{3,2},{4,5},{5,4},{6,7},{7,6},{8,9},{9,8},{10,11... | collective-permute-start | bytes 786440 | tf_op jit(solution)/shard_map/ppermute | solution.py:368
  71.6 5.5 %collective-permute-start.9 = (bf16[4,128,256]{2,1,0:T(8,128)(2,1)S(1)}, bf16[4,128,256]{2,1,0:T(8,128)(2,1)S(1)}, u32[]{:S(2)}, u32[]{:S(2)}) collective-permute-start(bf16[4,128,256]{2,1,0:T(8,128)(2,1)S(1)} %collective-permute-done.7.refs_6_), channel_id=1, source_target_pairs={{0,2},{1,5},{2,0},{3,7},{4,6},{5,1},{6,4},{7,3},{8,10},{9,13},{10,... | collective-permute-start | bytes 786440 | tf_op jit(solution)/shard_map/ppermute | solution.py:315
  71.7 15.6 %copy-start.1 = (bf16[8,128,256]{2,1,0:T(8,128)(2,1)}, bf16[8,128,256]{2,1,0:T(8,128)(2,1)S(1)}, u32[]{:S(2)}) copy-start(bf16[8,128,256]{2,1,0:T(8,128)(2,1)S(1)} %constant_dynamic-update-slice_fusion.4.refs_18_) | copy-start | bytes 1572868
  74.5 11.1 %copy-start.6 = (bf16[8,128,256]{2,1,0:T(8,128)(2,1)}, bf16[8,128,256]{2,1,0:T(8,128)(2,1)S(1)}, u32[]{:S(2)}) copy-start(bf16[8,128,256]{2,1,0:T(8,128)(2,1)S(1)} %collective-permute-done.11.refs_10_) | copy-start | bytes 1572868
  74.5 6.0 %collective-permute-start.14 = (bf16[4,128,256]{2,1,0:T(8,128)(2,1)S(1)}, bf16[4,128,256]{2,1,0:T(8,128)(2,1)S(1)}, u32[]{:S(2)}, u32[]{:S(2)}) collective-permute-start(bf16[4,128,256]{2,1,0:T(8,128)(2,1)S(1)} %collective-permute-done.8.refs_7_), channel_id=1, source_target_pairs={{0,1},{1,0},{2,3},{3,2},{4,5},{5,4},{6,7},{7,6},{8,9},{9,8},{10,11... | collective-permute-start | bytes 786440 | tf_op jit(solution)/shard_map/ppermute | solution.py:368
  76.3 9.3 %copy-start.7 = (bf16[8,128,256]{2,1,0:T(8,128)(2,1)}, bf16[8,128,256]{2,1,0:T(8,128)(2,1)S(1)}, u32[]{:S(2)}) copy-start(bf16[8,128,256]{2,1,0:T(8,128)(2,1)S(1)} %collective-permute-done.12.refs_11_) | copy-start | bytes 1572868
  76.3 8.9 %collective-permute-start.21 = (bf16[8,128,256]{2,1,0:T(8,128)(2,1)S(1)}, bf16[8,128,256]{2,1,0:T(8,128)(2,1)S(1)}, u32[]{:S(2)}, u32[]{:S(2)}) collective-permute-start(bf16[8,128,256]{2,1,0:T(8,128)(2,1)S(1)} %constant_dynamic-update-slice_fusion.4.refs_18_), channel_id=1, source_target_pairs={{0,4},{1,3},{2,6},{3,1},{4,0},{5,7},{6,2},{7,5},{8,12},{9,11},{10,... | collective-permute-start | bytes 1572872 | tf_op jit(solution)/shard_map/ppermute | solution.py:315
  76.3 4.3 %collective-permute-start.13 = (bf16[4,128,256]{2,1,0:T(8,128)(2,1)S(1)}, bf16[4,128,256]{2,1,0:T(8,128)(2,1)S(1)}, u32[]{:S(2)}, u32[]{:S(2)}) collective-permute-start(bf16[4,128,256]{2,1,0:T(8,128)(2,1)S(1)} %collective-permute-done.7.refs_6_), channel_id=1, source_target_pairs={{0,1},{1,0},{2,3},{3,2},{4,5},{5,4},{6,7},{7,6},{8,9},{9,8},{10,11... | collective-permute-start | bytes 786440 | tf_op jit(solution)/shard_map/ppermute | solution.py:368
  76.5 9.2 %copy-start.15 = (bf16[4,128,256]{2,1,0:T(8,128)(2,1)}, bf16[4,128,256]{2,1,0:T(8,128)(2,1)S(1)}, u32[]{:S(2)}) copy-start(bf16[4,128,256]{2,1,0:T(8,128)(2,1)S(1)} %collective-permute-done.4.refs_3_) | copy-start | bytes 786436
  76.5 4.5 %collective-permute-start.5 = (bf16[4,128,256]{2,1,0:T(8,128)(2,1)S(1)}, bf16[4,128,256]{2,1,0:T(8,128)(2,1)S(1)}, u32[]{:S(2)}, u32[]{:S(2)}) collective-permute-start(bf16[4,128,256]{2,1,0:T(8,128)(2,1)S(1)} %collective-permute-done.1.refs_1_), channel_id=1, source_target_pairs={{0,1},{1,0},{2,3},{3,2},{4,5},{5,4},{6,7},{7,6},{8,9},{9,8},{10,11... | collective-permute-start | bytes 786440 | tf_op jit(solution)/shard_map/ppermute | solution.py:368
  77.1 8.5 %copy-start.16 = (bf16[4,128,256]{2,1,0:T(8,128)(2,1)}, bf16[4,128,256]{2,1,0:T(8,128)(2,1)S(1)}, u32[]{:S(2)}) copy-start(bf16[4,128,256]{2,1,0:T(8,128)(2,1)S(1)} %collective-permute-done.9.refs_8_) | copy-start | bytes 786436
  77.2 4.7 %collective-permute-start.15 = (bf16[4,128,256]{2,1,0:T(8,128)(2,1)S(1)}, bf16[4,128,256]{2,1,0:T(8,128)(2,1)}, u32[]{:S(2)}, u32[]{:S(2)}) collective-permute-start(bf16[4,128,256]{2,1,0:T(8,128)(2,1)S(1)} %collective-permute-done.9.refs_8_), channel_id=1, source_target_pairs={{0,1},{1,0},{2,3},{3,2},{4,5},{5,4},{6,7},{7,6},{8,9},{9,8},{10,11... | collective-permute-start | bytes 786440 | tf_op jit(solution)/shard_map/ppermute | solution.py:368
  80.5 5.2 %copy-start.17 = (bf16[4,128,256]{2,1,0:T(8,128)(2,1)}, bf16[4,128,256]{2,1,0:T(8,128)(2,1)S(1)}, u32[]{:S(2)}) copy-start(bf16[4,128,256]{2,1,0:T(8,128)(2,1)S(1)} %collective-permute-done.14.refs_13_) | copy-start | bytes 786436
  80.5 1.7 %collective-permute-start.16 = (bf16[4,128,256]{2,1,0:T(8,128)(2,1)S(1)}, bf16[4,128,256]{2,1,0:T(8,128)(2,1)}, u32[]{:S(2)}, u32[]{:S(2)}) collective-permute-start(bf16[4,128,256]{2,1,0:T(8,128)(2,1)S(1)} %collective-permute-done.10.refs_9_), channel_id=1, source_target_pairs={{0,1},{1,0},{2,3},{3,2},{4,5},{5,4},{6,7},{7,6},{8,9},{9,8},{10,11... | collective-permute-start | bytes 786440 | tf_op jit(solution)/shard_map/ppermute | solution.py:368
  80.6 5.1 %copy-start.18 = (bf16[4,128,256]{2,1,0:T(8,128)(2,1)}, bf16[4,128,256]{2,1,0:T(8,128)(2,1)S(1)}, u32[]{:S(2)}) copy-start(bf16[4,128,256]{2,1,0:T(8,128)(2,1)S(1)} %collective-permute-done.13.refs_12_) | copy-start | bytes 786436
  80.6 5.0 %collective-permute-start.6 = (bf16[8,128,256]{2,1,0:T(8,128)(2,1)S(1)}, bf16[8,128,256]{2,1,0:T(8,128)(2,1)S(1)}, u32[]{:S(2)}, u32[]{:S(2)}) collective-permute-start(bf16[8,128,256]{2,1,0:T(8,128)(2,1)S(1)} %constant_dynamic-update-slice_fusion.2.refs_2_), channel_id=1, source_target_pairs={{0,1},{1,0},{2,3},{3,2},{4,5},{5,4},{6,7},{7,6},{8,9},{9,8},{10,11... | collective-permute-start | bytes 1572872 | tf_op jit(solution)/shard_map/ppermute | solution.py:368
  81.0 4.7 %copy-start.19 = (bf16[4,128,256]{2,1,0:T(8,128)(2,1)}, bf16[4,128,256]{2,1,0:T(8,128)(2,1)S(1)}, u32[]{:S(2)}) copy-start(bf16[4,128,256]{2,1,0:T(8,128)(2,1)S(1)} %collective-permute-done.5.refs_4_) | copy-start | bytes 786436
  81.0 4.5 %collective-permute-start.22 = (bf16[8,128,256]{2,1,0:T(8,128)(2,1)S(1)}, bf16[8,128,256]{2,1,0:T(8,128)(2,1)S(1)}, u32[]{:S(2)}, u32[]{:S(2)}) collective-permute-start(bf16[8,128,256]{2,1,0:T(8,128)(2,1)S(1)} %constant_dynamic-update-slice_fusion.4.refs_18_), channel_id=1, source_target_pairs={{0,1},{1,0},{2,3},{3,2},{4,5},{5,4},{6,7},{7,6},{8,9},{9,8},{10,11... | collective-permute-start | bytes 1572872 | tf_op jit(solution)/shard_map/ppermute | solution.py:368
  81.8 3.8 %collective-permute-start.17 = (bf16[8,128,256]{2,1,0:T(8,128)(2,1)S(1)}, bf16[8,128,256]{2,1,0:T(8,128)(2,1)S(1)}, u32[]{:S(2)}, u32[]{:S(2)}) collective-permute-start(bf16[8,128,256]{2,1,0:T(8,128)(2,1)S(1)} %collective-permute-done.11.refs_10_), channel_id=1, source_target_pairs={{0,1},{1,0},{2,3},{3,2},{4,5},{5,4},{6,7},{7,6},{8,9},{9,8},{10,11... | collective-permute-start | bytes 1572872 | tf_op jit(solution)/shard_map/ppermute | solution.py:368
  82.2 3.5 %collective-permute-start.18 = (bf16[8,128,256]{2,1,0:T(8,128)(2,1)S(1)}, bf16[8,128,256]{2,1,0:T(8,128)(2,1)S(1)}, u32[]{:S(2)}, u32[]{:S(2)}) collective-permute-start(bf16[8,128,256]{2,1,0:T(8,128)(2,1)S(1)} %collective-permute-done.12.refs_11_), channel_id=1, source_target_pairs={{0,1},{1,0},{2,3},{3,2},{4,5},{5,4},{6,7},{7,6},{8,9},{9,8},{10,11... | collective-permute-start | bytes 1572872 | tf_op jit(solution)/shard_map/ppermute | solution.py:368
  85.2 0.8 copy-start.8
  85.2 2.1 %collective-permute-start.23 = (bf16[8,128,256]{2,1,0:T(8,128)(2,1)S(1)}, bf16[8,128,256]{2,1,0:T(8,128)(2,1)}, u32[]{:S(2)}, u32[]{:S(2)}) collective-permute-start(bf16[8,128,256]{2,1,0:T(8,128)(2,1)S(1)} %collective-permute-done.21.refs_19_), channel_id=1, source_target_pairs={{0,1},{1,0},{2,3},{3,2},{4,5},{5,4},{6,7},{7,6},{8,9},{9,8},{10,11... | collective-permute-start | bytes 1572872 | tf_op jit(solution)/shard_map/ppermute | solution.py:368
  85.6 1.7 %copy-start.9 = (bf16[8,128,256]{2,1,0:T(8,128)(2,1)}, bf16[8,128,256]{2,1,0:T(8,128)(2,1)S(1)}, u32[]{:S(2)}) copy-start(bf16[8,128,256]{2,1,0:T(8,128)(2,1)S(1)} %collective-permute-done.6.refs_5_) | copy-start | bytes 1572868
  85.6 1.7 %copy-start.10 = (bf16[8,128,256]{2,1,0:T(8,128)(2,1)}, bf16[8,128,256]{2,1,0:T(8,128)(2,1)S(1)}, u32[]{:S(2)}) copy-start(bf16[8,128,256]{2,1,0:T(8,128)(2,1)S(1)} %collective-permute-done.22.refs_20_) | copy-start | bytes 1572868
  85.6 1.7 %copy-start.11 = (bf16[8,128,256]{2,1,0:T(8,128)(2,1)}, bf16[8,128,256]{2,1,0:T(8,128)(2,1)S(1)}, u32[]{:S(2)}) copy-start(bf16[8,128,256]{2,1,0:T(8,128)(2,1)S(1)} %collective-permute-done.17.refs_16_) | copy-start | bytes 1572868
  86.0 1.3 %copy-start.12 = (bf16[8,128,256]{2,1,0:T(8,128)(2,1)}, bf16[8,128,256]{2,1,0:T(8,128)(2,1)S(1)}, u32[]{:S(2)}) copy-start(bf16[8,128,256]{2,1,0:T(8,128)(2,1)S(1)} %collective-permute-done.18.refs_17_) | copy-start | bytes 1572868

commit v11 on v10

--- a/solution.py
+++ b/solution.py
@@ -338,7 +338,7 @@
     far = move(one, RING[1])
     one_second = move(second, RING[1])
     near_one = cross(tie(one, (came, turned)), 0)
-    near_three = cross(tie(three, (came, turned)), 0)
+    near_three = cross(three, 0)
     three_second = cross(jnp.concatenate([three, near_three]), 1)
     far_pair = jnp.concatenate([far, cross(far, 0)])
     return (

time: 97 us -> 96.3 us (level)
  waiting for transfers between devices: 38.9 us -> 29.8 us
  starting transfers between devices: 31.4 us -> 39.4 us
    ppermute x4, waiting for transfers between devices: 14.5 us -> 9.08 us  [move(): return lax.ppermute(value, 'dom', pairs)]
    ppermute x8, waiting for transfers between devices: 8.72 us -> 3.92 us  [cross(): return lax.ppermute(value, ('dom', 'rep'), pairs)]
    ppermute x8, starting transfers between devices: 5.39 us -> 9.68 us  [cross(): return lax.ppermute(value, ('dom', 'rep'), pairs)]
    ppermute x4, starting transfers between devices: 5.1 us -> 7.14 us  [move(): return lax.ppermute(value, 'dom', pairs)]
    ppermute x13, starting transfers between devices: 13.2 us -> 14.9 us  [exchange(): return lax.ppermute(value, 'rep', swap)]
    ppermute x13, waiting for transfers between devices: 5.49 us -> 6.66 us  [exchange(): return lax.ppermute(value, 'rep', swap)]
  transfers between devices with their start and end apart: 26 -> 26, of which waited for: 14 -> 13; matrix products, arithmetic and copies ran while one was open for 1% -> 1% of each run, Pallas kernels for 7% -> 7%
where the time goes in v11:
time: 96.3 us; the launch traced here: 94.9 us
  starting transfers between devices  39.4 us (41%)
  waiting for transfers between devices  29.8 us (31%)
  Pallas kernels  23.5 us (24%)
  local copies, waits for them, and re-layouts  1.98 us (2%)
    ppermute x13, starting transfers between devices, exchange(): return lax.ppermute(value, 'rep', swap)  14.9 us
    all_to_all x1, waiting for transfers between devices, gather_small(): landed = lax.all_to_all(rows, 'dom', 0, 0, tiled=True)  10.1 us
    ppermute x8, starting transfers between devices, cross(): return lax.ppermute(value, ('dom', 'rep'), pairs)  9.68 us
    ppermute x4, waiting for transfers between devices, move(): return lax.ppermute(value, 'dom', pairs)  9.08 us
    pallas_call x1, Pallas kernels, products_in_phases(): pl.pallas_call(functools.partial(phased_kernel, places), out_shape=jax.Sh...  8.38 us
    pallas_call x1, Pallas kernels, pick_share(): pl.pallas_call(pick_kernel, out_shape=jax.ShapeDtypeStruct((share, tile_l...  8.3 us
    all_to_all x1, starting transfers between devices, gather_small(): landed = lax.all_to_all(rows, 'dom', 0, 0, tiled=True)  7.69 us
    ppermute x4, starting transfers between devices, move(): return lax.ppermute(value, 'dom', pairs)  7.14 us
  transfers between devices with their start and end apart: 26, of which 13 were waited for; matrix products, arithmetic and copies ran while one was open for 1% of the time, Pallas kernels for 7%

profile of v11, /device:TPU:1, one launch (start us, length us, event | category | flops | bytes accessed | tf_op | source)
XLA Modules:
  0.0 94.9 jit_solution(453743311882450195)
XLA Ops:
  0.0 8.3 %shard_map.82 = bf16[16,128,256]{2,1,0:T(8,128)(2,1)} custom-call(s32[4]{0:T(128)} %owner_ref.1, s32[4,32]{1,0:T(4,128)} %blocks_ref.1, s32[64,1,128]{2,1,0:T(1,128)} %bitcast.5, bf16[8192,256]{1,0:T(8,128)(2,1)} %features_ref.1), custom_call_target="tpu_custom_call" | custom-call | tf_op jit(solution)/shard_map/pallas_call | solution.py:273
  8.3 0.0 copy-start
  8.3 0.0 copy-start.23
  8.3 0.0 copy-start.24
  8.4 7.7 %all-to-all-start = ((bf16[16,128,256]{2,1,0:T(8,128)(2,1)}), bf16[16,128,256]{2,1,0:T(8,128)(2,1)S(1)}, u32[]{:S(2)}, u32[]{:S(2)}) async-start(bf16[16,128,256]{2,1,0:T(8,128)(2,1)} %shard_map.82), calls=%async_computation | async-start | bytes 2097152 | tf_op jit(solution)/shard_map/all_to_all | solution.py:332
  16.1 1.0 %collective-permute-start.24 = (bf16[64,128,128]{2,1,0:T(8,128)(2,1)S(1)}, bf16[64,128,128]{2,1,0:T(8,128)(2,1)}, u32[]{:S(2)}, u32[]{:S(2)}) collective-permute-start(bf16[64,128,128]{2,1,0:T(8,128)(2,1)S(1)} %bitcast.4), channel_id=1, source_target_pairs={{0,1},{1,0},{2,3},{3,2},{4,5},{5,4},{6,7},{7,6},{8,9},{9,8},{10,11... | collective-permute-start | bytes 6291464 | tf_op jit(solution)/shard_map/ppermute | solution.py:368
  17.1 0.0 copy-done.22
  17.1 0.0 copy-done.23
  17.1 0.1 collective-permute-start
  17.2 3.5 %collective-permute-done.other_ref = s32[2,4,16]{2,1,0:T(4,128)S(1)} collective-permute-done((s32[2,4,16]{2,1,0:T(4,128)S(1)}, s32[2,4,16]{2,1,0:T(4,128)S(1)}, u32[]{:S(2)}, u32[]{:S(2)}) %collective-permute-start) | collective-permute-done | bytes 544 | tf_op jit(solution)/shard_map/ppermute | solution.py:368
  20.7 0.6 copy-done.21
  21.3 6.8 %shard_map.83.lists = s32[4,408]{1,0:T(4,128)} custom-call(s32[2,4,16]{2,1,0:T(4,128)} %copy-done.20, s32[2,4,16]{2,1,0:T(4,128)} %copy-done.21), custom_call_target="tpu_custom_call" | custom-call | tf_op jit(solution)/shard_map/pallas_call | solution.py:220
  28.1 10.1 %all-to-all-done = bf16[16,128,256]{2,1,0:T(8,128)(2,1)S(1)} async-done(((bf16[16,128,256]{2,1,0:T(8,128)(2,1)}), bf16[16,128,256]{2,1,0:T(8,128)(2,1)S(1)}, u32[]{:S(2)}, u32[]{:S(2)}) %all-to-all-start) | async-done | bytes 1048608 | tf_op jit(solution)/shard_map/all_to_all | solution.py:332
  38.2 0.6 gather_fusion
  38.8 3.6 %collective-permute-start.8 = (bf16[4,128,256]{2,1,0:T(8,128)(2,1)S(1)}, bf16[4,128,256]{2,1,0:T(8,128)(2,1)S(1)}, u32[]{:S(2)}, u32[]{:S(2)}) collective-permute-start(bf16[4,128,256]{2,1,0:T(8,128)(2,1)S(1)} %gather_fusion), channel_id=1, source_target_pairs={{0,8},{2,10},{4,12},{6,14},{8,16},{10,18},{12,20},{14,22},{16,24},... | collective-permute-start | bytes 786440 | tf_op jit(solution)/shard_map/ppermute | solution.py:303
  42.4 1.7 %collective-permute-start.1 = (bf16[4,128,256]{2,1,0:T(8,128)(2,1)S(1)}, bf16[4,128,256]{2,1,0:T(8,128)(2,1)S(1)}, u32[]{:S(2)}, u32[]{:S(2)}) collective-permute-start(bf16[4,128,256]{2,1,0:T(8,128)(2,1)S(1)} %gather_fusion), channel_id=1, source_target_pairs={{0,2},{1,5},{2,0},{3,7},{4,6},{5,1},{6,4},{7,3},{8,10},{9,13},{10,... | collective-permute-start | bytes 786440 | tf_op jit(solution)/shard_map/ppermute | solution.py:315
  44.1 0.4 collective-permute-start.7
  44.5 0.3 collective-permute-start.2
  44.7 1.1 %collective-permute-done.8.refs_7_ = bf16[4,128,256]{2,1,0:T(8,128)(2,1)S(1)} collective-permute-done((bf16[4,128,256]{2,1,0:T(8,128)(2,1)S(1)}, bf16[4,128,256]{2,1,0:T(8,128)(2,1)S(1)}, u32[]{:S(2)}, u32[]{:S(2)}) %collective-permute-start.8) | collective-permute-done | bytes 262176 | tf_op jit(solution)/shard_map/ppermute | solution.py:303
  45.9 2.4 %collective-permute-start.10 = (bf16[4,128,256]{2,1,0:T(8,128)(2,1)S(1)}, bf16[4,128,256]{2,1,0:T(8,128)(2,1)S(1)}, u32[]{:S(2)}, u32[]{:S(2)}) collective-permute-start(bf16[4,128,256]{2,1,0:T(8,128)(2,1)S(1)} %collective-permute-done.8.refs_7_), channel_id=1, source_target_pairs={{0,2},{1,5},{2,0},{3,7},{4,6},{5,1},{6,4},{7,3},{8,10},{9,13},{10,... | collective-permute-start | bytes 786440 | tf_op jit(solution)/shard_map/ppermute | solution.py:315
  48.3 0.0 collective-permute-done.1.refs_1_
  48.3 0.2 collective-permute-start.3
  48.5 5.4 %collective-permute-done.7.refs_6_ = bf16[4,128,256]{2,1,0:T(8,128)(2,1)S(1)} collective-permute-done((bf16[4,128,256]{2,1,0:T(8,128)(2,1)S(1)}, bf16[4,128,256]{2,1,0:T(8,128)(2,1)S(1)}, u32[]{:S(2)}, u32[]{:S(2)}) %collective-permute-start.7) | collective-permute-done | bytes 262176 | tf_op jit(solution)/shard_map/ppermute | solution.py:303
  54.0 0.9 collective-permute-start.19
  54.8 0.0 collective-permute-done.2
  54.9 0.2 collective-permute-done.10.refs_9_
  55.1 0.2 collective-permute-start.12
  55.3 0.0 collective-permute-done.3
  55.3 2.3 %collective-permute-start.11 = (bf16[8,128,256]{2,1,0:T(8,128)(2,1)S(1)}, bf16[8,128,256]{2,1,0:T(8,128)(2,1)S(1)}, u32[]{:S(2)}, u32[]{:S(2)}) collective-permute-start(bf16[8,128,256]{2,1,0:T(8,128)(2,1)S(1)} %constant_dynamic-update-slice_fusion.2.refs_2_), channel_id=1, source_target_pairs={{0,24},{2,26},{4,28},{6,30},{8,0},{10,2},{12,4},{14,6},{16,8},{18,... | collective-permute-start | bytes 1572872 | tf_op jit(solution)/shard_map/ppermute | solution.py:303
  57.7 2.5 %collective-permute-done.19 = bf16[4,128,256]{2,1,0:T(8,128)(2,1)S(1)} collective-permute-done((bf16[4,128,256]{2,1,0:T(8,128)(2,1)S(1)}, bf16[4,128,256]{2,1,0:T(8,128)(2,1)S(1)}, u32[]{:S(2)}, u32[]{:S(2)}) %collective-permute-start.19) | collective-permute-done | bytes 262176 | tf_op jit(solution)/shard_map/ppermute | solution.py:303
  60.2 2.2 %collective-permute-start.20 = (bf16[4,128,256]{2,1,0:T(8,128)(2,1)S(1)}, bf16[4,128,256]{2,1,0:T(8,128)(2,1)S(1)}, u32[]{:S(2)}, u32[]{:S(2)}) collective-permute-start(bf16[4,128,256]{2,1,0:T(8,128)(2,1)S(1)} %collective-permute-done.19), channel_id=1, source_target_pairs={{0,2},{1,5},{2,0},{3,7},{4,6},{5,1},{6,4},{7,3},{8,10},{9,13},{10,... | collective-permute-start | bytes 786440 | tf_op jit(solution)/shard_map/ppermute | solution.py:315
  62.4 3.8 %collective-permute-start.4 = (bf16[4,128,256]{2,1,0:T(8,128)(2,1)S(1)}, bf16[4,128,256]{2,1,0:T(8,128)(2,1)S(1)}, u32[]{:S(2)}, u32[]{:S(2)}) collective-permute-start(bf16[4,128,256]{2,1,0:T(8,128)(2,1)S(1)} %gather_fusion), channel_id=1, source_target_pairs={{0,1},{1,0},{2,3},{3,2},{4,5},{5,4},{6,7},{7,6},{8,9},{9,8},{10,11... | collective-permute-start | bytes 786440 | tf_op jit(solution)/shard_map/ppermute | solution.py:368
  66.2 3.0 %collective-permute-done.20 = bf16[4,128,256]{2,1,0:T(8,128)(2,1)S(1)} collective-permute-done((bf16[4,128,256]{2,1,0:T(8,128)(2,1)S(1)}, bf16[4,128,256]{2,1,0:T(8,128)(2,1)S(1)}, u32[]{:S(2)}, u32[]{:S(2)}) %collective-permute-start.20) | collective-permute-done | bytes 262176 | tf_op jit(solution)/shard_map/ppermute | solution.py:315
  69.1 1.6 %collective-permute-start.9 = (bf16[4,128,256]{2,1,0:T(8,128)(2,1)S(1)}, bf16[4,128,256]{2,1,0:T(8,128)(2,1)S(1)}, u32[]{:S(2)}, u32[]{:S(2)}) collective-permute-start(bf16[4,128,256]{2,1,0:T(8,128)(2,1)S(1)} %collective-permute-done.7.refs_6_), channel_id=1, source_target_pairs={{0,2},{1,5},{2,0},{3,7},{4,6},{5,1},{6,4},{7,3},{8,10},{9,13},{10,... | collective-permute-start | bytes 786440 | tf_op jit(solution)/shard_map/ppermute | solution.py:315
  70.7 0.0 collective-permute-done.12.refs_11_
  70.7 0.0 copy-start.6
  70.7 1.9 %collective-permute-start.14 = (bf16[4,128,256]{2,1,0:T(8,128)(2,1)S(1)}, bf16[4,128,256]{2,1,0:T(8,128)(2,1)S(1)}, u32[]{:S(2)}, u32[]{:S(2)}) collective-permute-start(bf16[4,128,256]{2,1,0:T(8,128)(2,1)S(1)} %collective-permute-done.8.refs_7_), channel_id=1, source_target_pairs={{0,1},{1,0},{2,3},{3,2},{4,5},{5,4},{6,7},{7,6},{8,9},{9,8},{10,11... | collective-permute-start | bytes 786440 | tf_op jit(solution)/shard_map/ppermute | solution.py:368
  72.6 0.0 collective-permute-done.11.refs_10_
  72.7 1.1 %collective-permute-start.21 = (bf16[8,128,256]{2,1,0:T(8,128)(2,1)S(1)}, bf16[8,128,256]{2,1,0:T(8,128)(2,1)S(1)}, u32[]{:S(2)}, u32[]{:S(2)}) collective-permute-start(bf16[8,128,256]{2,1,0:T(8,128)(2,1)S(1)} %constant_dynamic-update-slice_fusion.4.refs_18_), channel_id=1, source_target_pairs={{0,4},{1,3},{2,6},{3,1},{4,0},{5,7},{6,2},{7,5},{8,12},{9,11},{10,... | collective-permute-start | bytes 1572872 | tf_op jit(solution)/shard_map/ppermute | solution.py:315
  73.8 0.0 collective-permute-done.24.refs_23_
  73.8 2.4 %collective-permute-start.13 = (bf16[4,128,256]{2,1,0:T(8,128)(2,1)S(1)}, bf16[4,128,256]{2,1,0:T(8,128)(2,1)S(1)}, u32[]{:S(2)}, u32[]{:S(2)}) collective-permute-start(bf16[4,128,256]{2,1,0:T(8,128)(2,1)S(1)} %collective-permute-done.7.refs_6_), channel_id=1, source_target_pairs={{0,1},{1,0},{2,3},{3,2},{4,5},{5,4},{6,7},{7,6},{8,9},{9,8},{10,11... | collective-permute-start | bytes 786440 | tf_op jit(solution)/shard_map/ppermute | solution.py:368
  76.2 0.0 collective-permute-done.4.refs_3_
  76.2 0.1 collective-permute-start.5
  76.2 0.0 collective-permute-done.14.refs_13_
  76.3 0.4 collective-permute-start.16
  76.7 0.0 collective-permute-done.9.refs_8_
  76.7 4.1 %collective-permute-start.15 = (bf16[4,128,256]{2,1,0:T(8,128)(2,1)S(1)}, bf16[4,128,256]{2,1,0:T(8,128)(2,1)}, u32[]{:S(2)}, u32[]{:S(2)}) collective-permute-start(bf16[4,128,256]{2,1,0:T(8,128)(2,1)S(1)} %collective-permute-done.9.refs_8_), channel_id=1, source_target_pairs={{0,1},{1,0},{2,3},{3,2},{4,5},{5,4},{6,7},{7,6},{8,9},{9,8},{10,11... | collective-permute-start | bytes 786440 | tf_op jit(solution)/shard_map/ppermute | solution.py:368
  80.8 0.0 collective-permute-done.13.refs_12_
  80.8 0.1 collective-permute-start.6
  80.9 0.0 collective-permute-done.5.refs_4_
  80.9 0.4 collective-permute-start.22
  81.3 0.0 collective-permute-done.16.refs_15_
  81.3 0.1 collective-permute-start.18
  81.4 0.7 collective-permute-done.15.refs_14_
  82.1 0.4 collective-permute-start.17
  82.5 0.7 collective-permute-done.21.refs_19_
  83.2 0.1 collective-permute-start.23
  83.3 0.0 collective-permute-done.6.refs_5_
  83.3 0.1 collective-permute-done.22.refs_20_
  83.5 0.7 collective-permute-done.18.refs_17_
  84.2 1.5 %collective-permute-done.17.refs_16_ = bf16[8,128,256]{2,1,0:T(8,128)(2,1)S(1)} collective-permute-done((bf16[8,128,256]{2,1,0:T(8,128)(2,1)S(1)}, bf16[8,128,256]{2,1,0:T(8,128)(2,1)S(1)}, u32[]{:S(2)}, u32[]{:S(2)}) %collective-permute-start.17) | collective-permute-done | bytes 524320 | tf_op jit(solution)/shard_map/ppermute | solution.py:368
  85.8 0.1 collective-permute-done.23.refs_21_
  85.9 0.7 copy-done.12
  86.6 8.4 %shard_map.84 = bf16[32,128,256]{2,1,0:T(8,128)(2,1)} custom-call(s32[4,408]{1,0:T(4,128)} %shard_map.83.lists, bf16[4,128,256]{2,1,0:T(8,128)(2,1)} %copy-done.3, bf16[4,128,256]{2,1,0:T(8,128)(2,1)} %copy-done.13, bf16[8,128,256]{2,1,0:T(8,128)(2,1)} %copy-done.1, bf16[4,128,256]{2,1,0:T(8,128)(2,1)} %copy-done.15, bf16[4,128,256]{2,1,0:T(8,128)(2,1)} %copy-done.19, ...), custom_call_target="tpu_custom_call" | custom-call | flops 1073741824 | bytes 16777216 | tf_op jit(solution)/shard_map/pallas_call | solution.py:201
  (51 shorter events, 0.2 us)
Async XLA Ops:
  0.0 17.1 %copy-start.22 = (s32[1,4,16]{2,1,0:T(4,128)S(1)}, s32[1,4,16]{2,1,0:T(4,128)}, u32[]{:S(2)}) copy-start(s32[1,4,16]{2,1,0:T(4,128)} %param.12) | copy-start | bytes 772
  8.3 7.7 %copy-start = (bf16[1,4,16,128,128]{4,3,2,1,0:T(8,128)(2,1)S(1)}, bf16[1,4,16,128,128]{4,3,2,1,0:T(8,128)(2,1)}, u32[]{:S(2)}) copy-start(bf16[1,4,16,128,128]{4,3,2,1,0:T(8,128)(2,1)} %param.14) | copy-start | bytes 6291460
  8.3 8.8 %copy-start.23 = (s32[1,4,16]{2,1,0:T(4,128)S(1)}, s32[1,4,16]{2,1,0:T(4,128)}, u32[]{:S(2)}) copy-start(s32[1,4,16]{2,1,0:T(4,128)} %param.13) | copy-start | bytes 772
  8.3 8.9 %copy-start.24 = (s32[4]{0:T(128)S(1)}, s32[4]{0:T(128)}, u32[]{:S(2)}) copy-start(s32[4]{0:T(128)} %owner_ref.1) | copy-start | bytes 52
  8.4 29.9 %all-to-all-start = ((bf16[16,128,256]{2,1,0:T(8,128)(2,1)}), bf16[16,128,256]{2,1,0:T(8,128)(2,1)S(1)}, u32[]{:S(2)}, u32[]{:S(2)}) async-start(bf16[16,128,256]{2,1,0:T(8,128)(2,1)} %shard_map.82), calls=%async_computation | async-start | bytes 2097152 | tf_op jit(solution)/shard_map/all_to_all | solution.py:332
  16.1 57.7 %collective-permute-start.24 = (bf16[64,128,128]{2,1,0:T(8,128)(2,1)S(1)}, bf16[64,128,128]{2,1,0:T(8,128)(2,1)}, u32[]{:S(2)}, u32[]{:S(2)}) collective-permute-start(bf16[64,128,128]{2,1,0:T(8,128)(2,1)S(1)} %bitcast.4), channel_id=1, source_target_pairs={{0,1},{1,0},{2,3},{3,2},{4,5},{5,4},{6,7},{7,6},{8,9},{9,8},{10,11... | collective-permute-start | bytes 6291464 | tf_op jit(solution)/shard_map/ppermute | solution.py:368
  17.1 3.6 %copy-start.20 = (s32[2,4,16]{2,1,0:T(4,128)}, s32[2,4,16]{2,1,0:T(4,128)S(1)}, u32[]{:S(2)}) copy-start(s32[2,4,16]{2,1,0:T(4,128)S(1)} %constant_dynamic-update-slice_fusion.own_ref) | copy-start | bytes 1540
  17.1 3.6 %collective-permute-start = (s32[2,4,16]{2,1,0:T(4,128)S(1)}, s32[2,4,16]{2,1,0:T(4,128)S(1)}, u32[]{:S(2)}, u32[]{:S(2)}) collective-permute-start(s32[2,4,16]{2,1,0:T(4,128)S(1)} %constant_dynamic-update-slice_fusion.own_ref), channel_id=1, source_target_pairs={{0,1},{1,0},{2,3},{3,2},{4,5},{5,4},{6,7},{7,6},{8,9},{9,8},{10,11... | collective-permute-start | bytes 1544 | tf_op jit(solution)/shard_map/ppermute | solution.py:368
  20.7 0.6 copy-start.21
  38.8 47.0 %copy-start.3 = (bf16[4,128,256]{2,1,0:T(8,128)(2,1)}, bf16[4,128,256]{2,1,0:T(8,128)(2,1)S(1)}, u32[]{:S(2)}) copy-start(bf16[4,128,256]{2,1,0:T(8,128)(2,1)S(1)} %gather_fusion) | copy-start | bytes 786436
  38.8 7.1 %collective-permute-start.8 = (bf16[4,128,256]{2,1,0:T(8,128)(2,1)S(1)}, bf16[4,128,256]{2,1,0:T(8,128)(2,1)S(1)}, u32[]{:S(2)}, u32[]{:S(2)}) collective-permute-start(bf16[4,128,256]{2,1,0:T(8,128)(2,1)S(1)} %gather_fusion), channel_id=1, source_target_pairs={{0,8},{2,10},{4,12},{6,14},{8,16},{10,18},{12,20},{14,22},{16,24},... | collective-permute-start | bytes 786440 | tf_op jit(solution)/shard_map/ppermute | solution.py:303
  42.4 5.9 %collective-permute-start.1 = (bf16[4,128,256]{2,1,0:T(8,128)(2,1)S(1)}, bf16[4,128,256]{2,1,0:T(8,128)(2,1)S(1)}, u32[]{:S(2)}, u32[]{:S(2)}) collective-permute-start(bf16[4,128,256]{2,1,0:T(8,128)(2,1)S(1)} %gather_fusion), channel_id=1, source_target_pairs={{0,2},{1,5},{2,0},{3,7},{4,6},{5,1},{6,4},{7,3},{8,10},{9,13},{10,... | collective-permute-start | bytes 786440 | tf_op jit(solution)/shard_map/ppermute | solution.py:315
  44.1 9.9 %collective-permute-start.7 = (bf16[4,128,256]{2,1,0:T(8,128)(2,1)S(1)}, bf16[4,128,256]{2,1,0:T(8,128)(2,1)S(1)}, u32[]{:S(2)}, u32[]{:S(2)}) collective-permute-start(bf16[4,128,256]{2,1,0:T(8,128)(2,1)S(1)} %gather_fusion), channel_id=1, source_target_pairs={{0,24},{2,26},{4,28},{6,30},{8,0},{10,2},{12,4},{14,6},{16,8},{18,... | collective-permute-start | bytes 786440 | tf_op jit(solution)/shard_map/ppermute | solution.py:303
  44.5 10.4 %collective-permute-start.2 = (bf16[4,128,256]{2,1,0:T(8,128)(2,1)S(1)}, bf16[4,128,256]{2,1,0:T(8,128)(2,1)S(1)}, u32[]{:S(2)}, u32[]{:S(2)}) collective-permute-start(bf16[4,128,256]{2,1,0:T(8,128)(2,1)S(1)} %gather_fusion), channel_id=1, source_target_pairs={{0,4},{1,3},{2,6},{3,1},{4,0},{5,7},{6,2},{7,5},{8,12},{9,11},{10,... | collective-permute-start | bytes 786440 | tf_op jit(solution)/shard_map/ppermute | solution.py:315
  45.9 40.0 %copy-start.4 = (bf16[4,128,256]{2,1,0:T(8,128)(2,1)}, bf16[4,128,256]{2,1,0:T(8,128)(2,1)S(1)}, u32[]{:S(2)}) copy-start(bf16[4,128,256]{2,1,0:T(8,128)(2,1)S(1)} %collective-permute-done.8.refs_7_) | copy-start | bytes 786436
  45.9 9.2 %collective-permute-start.10 = (bf16[4,128,256]{2,1,0:T(8,128)(2,1)S(1)}, bf16[4,128,256]{2,1,0:T(8,128)(2,1)S(1)}, u32[]{:S(2)}, u32[]{:S(2)}) collective-permute-start(bf16[4,128,256]{2,1,0:T(8,128)(2,1)S(1)} %collective-permute-done.8.refs_7_), channel_id=1, source_target_pairs={{0,2},{1,5},{2,0},{3,7},{4,6},{5,1},{6,4},{7,3},{8,10},{9,13},{10,... | collective-permute-start | bytes 786440 | tf_op jit(solution)/shard_map/ppermute | solution.py:315
  48.3 37.4 %copy-start.13 = (bf16[4,128,256]{2,1,0:T(8,128)(2,1)}, bf16[4,128,256]{2,1,0:T(8,128)(2,1)S(1)}, u32[]{:S(2)}) copy-start(bf16[4,128,256]{2,1,0:T(8,128)(2,1)S(1)} %collective-permute-done.1.refs_1_) | copy-start | bytes 786436
  48.3 7.0 %collective-permute-start.3 = (bf16[4,128,256]{2,1,0:T(8,128)(2,1)S(1)}, bf16[4,128,256]{2,1,0:T(8,128)(2,1)S(1)}, u32[]{:S(2)}, u32[]{:S(2)}) collective-permute-start(bf16[4,128,256]{2,1,0:T(8,128)(2,1)S(1)} %collective-permute-done.1.refs_1_), channel_id=1, source_target_pairs={{0,4},{1,3},{2,6},{3,1},{4,0},{5,7},{6,2},{7,5},{8,12},{9,11},{10,... | collective-permute-start | bytes 786440 | tf_op jit(solution)/shard_map/ppermute | solution.py:315
  54.0 31.7 %copy-start.14 = (bf16[4,128,256]{2,1,0:T(8,128)(2,1)}, bf16[4,128,256]{2,1,0:T(8,128)(2,1)S(1)}, u32[]{:S(2)}) copy-start(bf16[4,128,256]{2,1,0:T(8,128)(2,1)S(1)} %collective-permute-done.7.refs_6_) | copy-start | bytes 786436
  54.0 6.2 %collective-permute-start.19 = (bf16[4,128,256]{2,1,0:T(8,128)(2,1)S(1)}, bf16[4,128,256]{2,1,0:T(8,128)(2,1)S(1)}, u32[]{:S(2)}, u32[]{:S(2)}) collective-permute-start(bf16[4,128,256]{2,1,0:T(8,128)(2,1)S(1)} %collective-permute-done.7.refs_6_), channel_id=1, source_target_pairs={{0,24},{2,26},{4,28},{6,30},{8,0},{10,2},{12,4},{14,6},{16,8},{18,... | collective-permute-start | bytes 786440 | tf_op jit(solution)/shard_map/ppermute | solution.py:303
  55.1 30.8 %copy-start.5 = (bf16[4,128,256]{2,1,0:T(8,128)(2,1)}, bf16[4,128,256]{2,1,0:T(8,128)(2,1)S(1)}, u32[]{:S(2)}) copy-start(bf16[4,128,256]{2,1,0:T(8,128)(2,1)S(1)} %collective-permute-done.10.refs_9_) | copy-start | bytes 786436
  55.1 15.6 %collective-permute-start.12 = (bf16[8,128,256]{2,1,0:T(8,128)(2,1)S(1)}, bf16[8,128,256]{2,1,0:T(8,128)(2,1)S(1)}, u32[]{:S(2)}, u32[]{:S(2)}) collective-permute-start(bf16[8,128,256]{2,1,0:T(8,128)(2,1)S(1)} %pad_maximum_fusion), channel_id=1, source_target_pairs={{0,4},{1,3},{2,6},{3,1},{4,0},{5,7},{6,2},{7,5},{8,12},{9,11},{10,... | collective-permute-start | bytes 1572872 | tf_op jit(solution)/shard_map/ppermute | solution.py:315
  55.3 30.5 %copy-start.1 = (bf16[8,128,256]{2,1,0:T(8,128)(2,1)}, bf16[8,128,256]{2,1,0:T(8,128)(2,1)S(1)}, u32[]{:S(2)}) copy-start(bf16[8,128,256]{2,1,0:T(8,128)(2,1)S(1)} %constant_dynamic-update-slice_fusion.2.refs_2_) | copy-start | bytes 1572868
  55.3 17.3 %collective-permute-start.11 = (bf16[8,128,256]{2,1,0:T(8,128)(2,1)S(1)}, bf16[8,128,256]{2,1,0:T(8,128)(2,1)S(1)}, u32[]{:S(2)}, u32[]{:S(2)}) collective-permute-start(bf16[8,128,256]{2,1,0:T(8,128)(2,1)S(1)} %constant_dynamic-update-slice_fusion.2.refs_2_), channel_id=1, source_target_pairs={{0,24},{2,26},{4,28},{6,30},{8,0},{10,2},{12,4},{14,6},{16,8},{18,... | collective-permute-start | bytes 1572872 | tf_op jit(solution)/shard_map/ppermute | solution.py:303
  60.2 9.0 %collective-permute-start.20 = (bf16[4,128,256]{2,1,0:T(8,128)(2,1)S(1)}, bf16[4,128,256]{2,1,0:T(8,128)(2,1)S(1)}, u32[]{:S(2)}, u32[]{:S(2)}) collective-permute-start(bf16[4,128,256]{2,1,0:T(8,128)(2,1)S(1)} %collective-permute-done.19), channel_id=1, source_target_pairs={{0,2},{1,5},{2,0},{3,7},{4,6},{5,1},{6,4},{7,3},{8,10},{9,13},{10,... | collective-permute-start | bytes 786440 | tf_op jit(solution)/shard_map/ppermute | solution.py:315
  62.4 13.8 %collective-permute-start.4 = (bf16[4,128,256]{2,1,0:T(8,128)(2,1)S(1)}, bf16[4,128,256]{2,1,0:T(8,128)(2,1)S(1)}, u32[]{:S(2)}, u32[]{:S(2)}) collective-permute-start(bf16[4,128,256]{2,1,0:T(8,128)(2,1)S(1)} %gather_fusion), channel_id=1, source_target_pairs={{0,1},{1,0},{2,3},{3,2},{4,5},{5,4},{6,7},{7,6},{8,9},{9,8},{10,11... | collective-permute-start | bytes 786440 | tf_op jit(solution)/shard_map/ppermute | solution.py:368
  69.1 7.5 %collective-permute-start.9 = (bf16[4,128,256]{2,1,0:T(8,128)(2,1)S(1)}, bf16[4,128,256]{2,1,0:T(8,128)(2,1)S(1)}, u32[]{:S(2)}, u32[]{:S(2)}) collective-permute-start(bf16[4,128,256]{2,1,0:T(8,128)(2,1)S(1)} %collective-permute-done.7.refs_6_), channel_id=1, source_target_pairs={{0,2},{1,5},{2,0},{3,7},{4,6},{5,1},{6,4},{7,3},{8,10},{9,13},{10,... | collective-permute-start | bytes 786440 | tf_op jit(solution)/shard_map/ppermute | solution.py:315
  70.7 15.2 %copy-start.2 = (bf16[8,128,256]{2,1,0:T(8,128)(2,1)}, bf16[8,128,256]{2,1,0:T(8,128)(2,1)S(1)}, u32[]{:S(2)}) copy-start(bf16[8,128,256]{2,1,0:T(8,128)(2,1)S(1)} %constant_dynamic-update-slice_fusion.4.refs_18_) | copy-start | bytes 1572868
  70.7 12.7 %copy-start.6 = (bf16[8,128,256]{2,1,0:T(8,128)(2,1)}, bf16[8,128,256]{2,1,0:T(8,128)(2,1)S(1)}, u32[]{:S(2)}) copy-start(bf16[8,128,256]{2,1,0:T(8,128)(2,1)S(1)} %collective-permute-done.12.refs_11_) | copy-start | bytes 1572868
  70.7 5.5 %collective-permute-start.14 = (bf16[4,128,256]{2,1,0:T(8,128)(2,1)S(1)}, bf16[4,128,256]{2,1,0:T(8,128)(2,1)S(1)}, u32[]{:S(2)}, u32[]{:S(2)}) collective-permute-start(bf16[4,128,256]{2,1,0:T(8,128)(2,1)S(1)} %collective-permute-done.8.refs_7_), channel_id=1, source_target_pairs={{0,1},{1,0},{2,3},{3,2},{4,5},{5,4},{6,7},{7,6},{8,9},{9,8},{10,11... | collective-permute-start | bytes 786440 | tf_op jit(solution)/shard_map/ppermute | solution.py:368
  72.7 11.6 %copy-start.7 = (bf16[8,128,256]{2,1,0:T(8,128)(2,1)}, bf16[8,128,256]{2,1,0:T(8,128)(2,1)S(1)}, u32[]{:S(2)}) copy-start(bf16[8,128,256]{2,1,0:T(8,128)(2,1)S(1)} %collective-permute-done.11.refs_10_) | copy-start | bytes 1572868
  72.7 10.6 %collective-permute-start.21 = (bf16[8,128,256]{2,1,0:T(8,128)(2,1)S(1)}, bf16[8,128,256]{2,1,0:T(8,128)(2,1)S(1)}, u32[]{:S(2)}, u32[]{:S(2)}) collective-permute-start(bf16[8,128,256]{2,1,0:T(8,128)(2,1)S(1)} %constant_dynamic-update-slice_fusion.4.refs_18_), channel_id=1, source_target_pairs={{0,4},{1,3},{2,6},{3,1},{4,0},{5,7},{6,2},{7,5},{8,12},{9,11},{10,... | collective-permute-start | bytes 1572872 | tf_op jit(solution)/shard_map/ppermute | solution.py:315
  73.8 7.0 %collective-permute-start.13 = (bf16[4,128,256]{2,1,0:T(8,128)(2,1)S(1)}, bf16[4,128,256]{2,1,0:T(8,128)(2,1)S(1)}, u32[]{:S(2)}, u32[]{:S(2)}) collective-permute-start(bf16[4,128,256]{2,1,0:T(8,128)(2,1)S(1)} %collective-permute-done.7.refs_6_), channel_id=1, source_target_pairs={{0,1},{1,0},{2,3},{3,2},{4,5},{5,4},{6,7},{7,6},{8,9},{9,8},{10,11... | collective-permute-start | bytes 786440 | tf_op jit(solution)/shard_map/ppermute | solution.py:368
  76.2 9.6 %copy-start.15 = (bf16[4,128,256]{2,1,0:T(8,128)(2,1)}, bf16[4,128,256]{2,1,0:T(8,128)(2,1)S(1)}, u32[]{:S(2)}) copy-start(bf16[4,128,256]{2,1,0:T(8,128)(2,1)S(1)} %collective-permute-done.4.refs_3_) | copy-start | bytes 786436
  76.2 4.7 %collective-permute-start.5 = (bf16[4,128,256]{2,1,0:T(8,128)(2,1)S(1)}, bf16[4,128,256]{2,1,0:T(8,128)(2,1)S(1)}, u32[]{:S(2)}, u32[]{:S(2)}) collective-permute-start(bf16[4,128,256]{2,1,0:T(8,128)(2,1)S(1)} %collective-permute-done.1.refs_1_), channel_id=1, source_target_pairs={{0,1},{1,0},{2,3},{3,2},{4,5},{5,4},{6,7},{7,6},{8,9},{9,8},{10,11... | collective-permute-start | bytes 786440 | tf_op jit(solution)/shard_map/ppermute | solution.py:368
  76.2 9.5 %copy-start.17 = (bf16[4,128,256]{2,1,0:T(8,128)(2,1)}, bf16[4,128,256]{2,1,0:T(8,128)(2,1)S(1)}, u32[]{:S(2)}) copy-start(bf16[4,128,256]{2,1,0:T(8,128)(2,1)S(1)} %collective-permute-done.14.refs_13_) | copy-start | bytes 786436
  76.3 5.1 %collective-permute-start.16 = (bf16[4,128,256]{2,1,0:T(8,128)(2,1)S(1)}, bf16[4,128,256]{2,1,0:T(8,128)(2,1)}, u32[]{:S(2)}, u32[]{:S(2)}) collective-permute-start(bf16[4,128,256]{2,1,0:T(8,128)(2,1)S(1)} %collective-permute-done.10.refs_9_), channel_id=1, source_target_pairs={{0,1},{1,0},{2,3},{3,2},{4,5},{5,4},{6,7},{7,6},{8,9},{9,8},{10,11... | collective-permute-start | bytes 786440 | tf_op jit(solution)/shard_map/ppermute | solution.py:368
  76.7 9.0 %copy-start.16 = (bf16[4,128,256]{2,1,0:T(8,128)(2,1)}, bf16[4,128,256]{2,1,0:T(8,128)(2,1)S(1)}, u32[]{:S(2)}) copy-start(bf16[4,128,256]{2,1,0:T(8,128)(2,1)S(1)} %collective-permute-done.9.refs_8_) | copy-start | bytes 786436
  76.7 5.4 %collective-permute-start.15 = (bf16[4,128,256]{2,1,0:T(8,128)(2,1)S(1)}, bf16[4,128,256]{2,1,0:T(8,128)(2,1)}, u32[]{:S(2)}, u32[]{:S(2)}) collective-permute-start(bf16[4,128,256]{2,1,0:T(8,128)(2,1)S(1)} %collective-permute-done.9.refs_8_), channel_id=1, source_target_pairs={{0,1},{1,0},{2,3},{3,2},{4,5},{5,4},{6,7},{7,6},{8,9},{9,8},{10,11... | collective-permute-start | bytes 786440 | tf_op jit(solution)/shard_map/ppermute | solution.py:368
  80.8 4.9 %copy-start.18 = (bf16[4,128,256]{2,1,0:T(8,128)(2,1)}, bf16[4,128,256]{2,1,0:T(8,128)(2,1)S(1)}, u32[]{:S(2)}) copy-start(bf16[4,128,256]{2,1,0:T(8,128)(2,1)S(1)} %collective-permute-done.13.refs_12_) | copy-start | bytes 786436
  80.8 2.5 %collective-permute-start.6 = (bf16[8,128,256]{2,1,0:T(8,128)(2,1)S(1)}, bf16[8,128,256]{2,1,0:T(8,128)(2,1)S(1)}, u32[]{:S(2)}, u32[]{:S(2)}) collective-permute-start(bf16[8,128,256]{2,1,0:T(8,128)(2,1)S(1)} %constant_dynamic-update-slice_fusion.2.refs_2_), channel_id=1, source_target_pairs={{0,1},{1,0},{2,3},{3,2},{4,5},{5,4},{6,7},{7,6},{8,9},{9,8},{10,11... | collective-permute-start | bytes 1572872 | tf_op jit(solution)/shard_map/ppermute | solution.py:368
  80.9 4.9 %copy-start.19 = (bf16[4,128,256]{2,1,0:T(8,128)(2,1)}, bf16[4,128,256]{2,1,0:T(8,128)(2,1)S(1)}, u32[]{:S(2)}) copy-start(bf16[4,128,256]{2,1,0:T(8,128)(2,1)S(1)} %collective-permute-done.5.refs_4_) | copy-start | bytes 786436
  80.9 2.6 %collective-permute-start.22 = (bf16[8,128,256]{2,1,0:T(8,128)(2,1)S(1)}, bf16[8,128,256]{2,1,0:T(8,128)(2,1)S(1)}, u32[]{:S(2)}, u32[]{:S(2)}) collective-permute-start(bf16[8,128,256]{2,1,0:T(8,128)(2,1)S(1)} %constant_dynamic-update-slice_fusion.4.refs_18_), channel_id=1, source_target_pairs={{0,1},{1,0},{2,3},{3,2},{4,5},{5,4},{6,7},{7,6},{8,9},{9,8},{10,11... | collective-permute-start | bytes 1572872 | tf_op jit(solution)/shard_map/ppermute | solution.py:368
  81.3 2.9 %collective-permute-start.18 = (bf16[8,128,256]{2,1,0:T(8,128)(2,1)S(1)}, bf16[8,128,256]{2,1,0:T(8,128)(2,1)S(1)}, u32[]{:S(2)}, u32[]{:S(2)}) collective-permute-start(bf16[8,128,256]{2,1,0:T(8,128)(2,1)S(1)} %collective-permute-done.12.refs_11_), channel_id=1, source_target_pairs={{0,1},{1,0},{2,3},{3,2},{4,5},{5,4},{6,7},{7,6},{8,9},{9,8},{10,11... | collective-permute-start | bytes 1572872 | tf_op jit(solution)/shard_map/ppermute | solution.py:368
  82.1 3.6 %collective-permute-start.17 = (bf16[8,128,256]{2,1,0:T(8,128)(2,1)S(1)}, bf16[8,128,256]{2,1,0:T(8,128)(2,1)S(1)}, u32[]{:S(2)}, u32[]{:S(2)}) collective-permute-start(bf16[8,128,256]{2,1,0:T(8,128)(2,1)S(1)} %collective-permute-done.11.refs_10_), channel_id=1, source_target_pairs={{0,1},{1,0},{2,3},{3,2},{4,5},{5,4},{6,7},{7,6},{8,9},{9,8},{10,11... | collective-permute-start | bytes 1572872 | tf_op jit(solution)/shard_map/ppermute | solution.py:368
  83.2 2.5 %copy-start.8 = (bf16[8,128,256]{2,1,0:T(8,128)(2,1)}, bf16[8,128,256]{2,1,0:T(8,128)(2,1)S(1)}, u32[]{:S(2)}) copy-start(bf16[8,128,256]{2,1,0:T(8,128)(2,1)S(1)} %collective-permute-done.21.refs_19_) | copy-start | bytes 1572868
  83.2 2.6 %collective-permute-start.23 = (bf16[8,128,256]{2,1,0:T(8,128)(2,1)S(1)}, bf16[8,128,256]{2,1,0:T(8,128)(2,1)}, u32[]{:S(2)}, u32[]{:S(2)}) collective-permute-start(bf16[8,128,256]{2,1,0:T(8,128)(2,1)S(1)} %collective-permute-done.21.refs_19_), channel_id=1, source_target_pairs={{0,1},{1,0},{2,3},{3,2},{4,5},{5,4},{6,7},{7,6},{8,9},{9,8},{10,11... | collective-permute-start | bytes 1572872 | tf_op jit(solution)/shard_map/ppermute | solution.py:368
  83.3 2.6 %copy-start.9 = (bf16[8,128,256]{2,1,0:T(8,128)(2,1)}, bf16[8,128,256]{2,1,0:T(8,128)(2,1)S(1)}, u32[]{:S(2)}) copy-start(bf16[8,128,256]{2,1,0:T(8,128)(2,1)S(1)} %collective-permute-done.6.refs_5_) | copy-start | bytes 1572868
  83.5 2.4 %copy-start.10 = (bf16[8,128,256]{2,1,0:T(8,128)(2,1)}, bf16[8,128,256]{2,1,0:T(8,128)(2,1)S(1)}, u32[]{:S(2)}) copy-start(bf16[8,128,256]{2,1,0:T(8,128)(2,1)S(1)} %collective-permute-done.22.refs_20_) | copy-start | bytes 1572868
  84.2 1.7 %copy-start.11 = (bf16[8,128,256]{2,1,0:T(8,128)(2,1)}, bf16[8,128,256]{2,1,0:T(8,128)(2,1)S(1)}, u32[]{:S(2)}) copy-start(bf16[8,128,256]{2,1,0:T(8,128)(2,1)S(1)} %collective-permute-done.18.refs_17_) | copy-start | bytes 1572868
  85.8 0.8 copy-start.12
